TPU v7x, 32 devices: a whole 2x2x4 slice. The times are simulated.
32 devices in a mesh: parts: 2 (over x), wide: 4 (over y, core), narrow: 4 (over z).
Axes of the slice: x: 2, y: 2, z: 4, core: 2. Of those that a mesh axis runs over, the one named last changes fastest.
Arguments:
- hidden: bfloat16 [512, 2560], P(('parts', 'wide'), 'narrow'), parts along dimension 0, may hold values from -64 to 64
- input_norm_gain: float32 [2560], replicated, may hold values from 0.25 to 1.75
- query_projection_weight: bfloat16 [2560, 4096], P(None, 'narrow'), may hold values from -0.125 to 0.125
- key_projection_weight: bfloat16 [2560, 1024], P(None, 'narrow'), may hold values from -0.125 to 0.125
- value_projection_weight: bfloat16 [2560, 1024], P(None, 'narrow'), may hold values from -0.125 to 0.125
- query_norm_gain: float32 [128], replicated, may hold values from 0.25 to 1.75
- key_norm_gain: float32 [128], replicated, may hold values from 0.25 to 1.75
- output_projection_weight: bfloat16 [4096, 2560], P('narrow'), may hold values from -0.09375 to 0.09375
- stacked_down_factors: bfloat16 [64, 192, 2560], P(('parts', 'wide'), None, 'narrow'), parts along dimension 0, may hold values from -0.125 to 0.125
- query_up_factor: bfloat16 [64, 64, 4096], P(('parts', 'wide'), None, 'narrow'), parts along dimension 0, may hold values from -0.75 to 0.75
- key_up_factor: bfloat16 [64, 64, 1024], P(('parts', 'wide'), None, 'narrow'), parts along dimension 0, may hold values from -0.75 to 0.75
- value_up_factor: bfloat16 [64, 64, 1024], P(('parts', 'wide'), None, 'narrow'), parts along dimension 0, may hold values from -0.75 to 0.75
- output_down_factor: bfloat16 [64, 64, 4096], P(('parts', 'wide'), None, 'narrow'), parts along dimension 0, may hold values from -0.09375 to 0.09375
- output_up_factor: bfloat16 [64, 64, 2560], P(('parts', 'wide'), None, 'narrow'), parts along dimension 0, may hold values from -0.75 to 0.75
- cached_key_rows: bfloat16 [512, 8, 24, 128], P(('parts', 'wide'), 'narrow'), parts along dimension 0, may hold values from -170 to 170
- cached_value_rows: bfloat16 [512, 8, 24, 128], P(('parts', 'wide'), 'narrow'), parts along dimension 0, may hold values from -5 to 5
- cached_length_rows: int32 [512], P(('parts', 'wide')), parts along dimension 0, may hold values from 1 to 24, as said below
- domain_of_row: int32 [512], P('parts'), parts along dimension 0, may hold values from 0 to 31, as said below
- slot_of_domain: int32 [64], P('parts'), parts along dimension 0, may hold values from 0 to 31, as said below
Outputs:
- final_state: bfloat16 [512, 2560], P(('parts', 'wide'), 'narrow'), parts along dimension 0
There are 2 independent parts, one for each index of `parts`. A program takes and returns all parts, laid end to end along the dimension named above; an argument that names none is the same for every part. Nothing has to cross between parts.
Inputs may be any that keep to these rules, and one draw needn't show every extreme that they name: Domain d's adapter sits at slot slot_of_domain[d]; slots g * 8 to (g + 1) * 8 - 1 belong to serving group g. Each slot holds one domain. `domain_of_row`: in each aligned block of 64 rows (the rows of one serving group), at most 16 rows have domains whose slots belong to any one serving group; in every draw one serving group receives exactly 16 rows from every block. `cached_length_rows`: each aligned block of 64 rows holds a row with 24 valid positions.
All inputs are finite; a program needn't handle non-finite values.
Results may differ from a plain program's by a relative error of at most 0.024.
Values may be sent and summed in bfloat16 or wider, within the bound.
No kernel may reach another device: no remote copies, remote signals or barrier semaphores. Data moves between devices by JAX's collectives and lax.ppermute only.
A program may use at most 128 MiB of HBM per device.

v0:
```python
import functools

import jax
import jax.numpy as jnp
from jax import lax
from jax.experimental import pallas as pl
from jax.experimental.pallas import tpu as pltpu
from jax.sharding import PartitionSpec as P

STEPS = 4

epsilon = 1e-06
rope_base = 1000000.0
blocked = -1e30
f32 = jnp.float32
bf16 = jnp.bfloat16

NT = (((1,), (1,)), ((), ()))


def vmem_specs(count):
    return [pl.BlockSpec(memory_space=pltpu.VMEM)] * count


def kernel_params(mib):
    return pltpu.CompilerParams(vmem_limit_bytes=mib * 1024 * 1024)


def pack_kernel(
    domain_ref, slot_ref, key_ref, value_ref, key_out, value_out, target_ref, local_ref, count, sems
):
    rows = key_ref.shape[0]
    groups, _, capacity = key_out.shape[:3]
    per_group = slot_ref.shape[0] // groups
    for group in range(groups):
        count[group] = 0

    def place(row, carry):
        slot = slot_ref[domain_ref[row]]
        dest = lax.div(slot, per_group)
        position = jnp.minimum(count[dest], capacity - 1)
        count[dest] = position + 1
        target_ref[row] = dest * capacity + position
        local_ref[row] = slot - dest * per_group
        pltpu.make_async_copy(
            key_ref.at[row], key_out.at[dest, :, position], sems.at[0, row]
        ).start()
        pltpu.make_async_copy(
            value_ref.at[row], value_out.at[dest, :, position], sems.at[1, row]
        ).start()
        return carry

    lax.fori_loop(0, rows, place, 0)

    def finish(row, carry):
        pltpu.make_async_copy(key_ref.at[row], key_out.at[0, :, 0], sems.at[0, row]).wait()
        pltpu.make_async_copy(value_ref.at[row], value_out.at[0, :, 0], sems.at[1, row]).wait()
        return carry

    lax.fori_loop(0, rows, finish, 0)


def pack_rows(domains, slots, keys, values, groups, capacity):
    rows, kv_local, context, head_dim = keys.shape
    moved = jax.ShapeDtypeStruct((groups, kv_local, capacity, context, head_dim), keys.dtype)
    number = jax.ShapeDtypeStruct((rows,), jnp.int32)
    smem = pl.BlockSpec(memory_space=pltpu.SMEM)
    anywhere = pl.BlockSpec(memory_space=pl.ANY)
    return pl.pallas_call(
        pack_kernel,
        out_shape=(moved, moved, number, number),
        in_specs=[smem, smem, anywhere, anywhere],
        out_specs=(anywhere, anywhere, smem, smem),
        scratch_shapes=[
            pltpu.SMEM((groups,), jnp.int32),
            pltpu.SemaphoreType.DMA((2, rows)),
        ],
        name="pack_rows",
    )(domains, slots, keys, values)


def one_of_slots(slot_column, total):
    ids = lax.broadcasted_iota(jnp.int32, (1, total), 1).astype(f32)
    return slot_column == ids


def spread_over_slots(factor, chosen, total):
    return jnp.concatenate(
        [jnp.where(chosen[:, d : d + 1], factor, 0.0) for d in range(total)], axis=1
    ).astype(bf16)


def pick_slot(product, chosen, total):
    rank = product.shape[1] // total
    picked = jnp.where(chosen[:, 0:1], product[:, :rank], 0.0)
    for d in range(1, total):
        picked = picked + jnp.where(chosen[:, d : d + 1], product[:, d * rank : (d + 1) * rank], 0.0)
    return picked


def partial_low(state, gain, chosen, down_ref, total):
    scaled = (state * gain).astype(bf16)
    product = lax.dot_general(scaled, down_ref[...], NT, preferred_element_type=f32)
    return pick_slot(product, chosen, total).astype(bf16)


def enter_kernel(total, state_ref, gain_ref, down_ref, send_ref):
    width = down_ref.shape[1]
    state = state_ref[:, :width].astype(f32)
    slot = state_ref[:, width + 1 : width + 2].astype(f32)
    chosen = one_of_slots(slot, total)
    low = partial_low(state, gain_ref[...], chosen, down_ref, total)
    for n in range(send_ref.shape[0]):
        send_ref[n, :, :width] = state_ref[:, :width]
        send_ref[n, :, width:] = low


def new_state(total, chosen, received_ref, state_ref, up_ref, width):
    parts = received_ref.shape[0]
    low_out = received_ref[0, :, width:].astype(f32)
    projected = received_ref[0, :, :width].astype(f32)
    for n in range(1, parts):
        low_out = low_out + received_ref[n, :, width:].astype(f32)
        projected = projected + received_ref[n, :, :width].astype(f32)
    spread = spread_over_slots(low_out, chosen, total)
    delta = jnp.dot(spread, up_ref[...], preferred_element_type=f32).astype(bf16)
    return (state_ref[...].astype(f32) + projected + delta.astype(f32)).astype(bf16)


def between_kernel(
    total, received_ref, state_ref, slot_ref, up_ref, gain_ref, down_ref, state_out, send_ref
):
    width = down_ref.shape[1]
    chosen = one_of_slots(slot_ref[:, 1:2].astype(f32), total)
    state = new_state(total, chosen, received_ref, state_ref, up_ref, width)
    state_out[...] = state
    low = partial_low(state.astype(f32), gain_ref[...], chosen, down_ref, total)
    for n in range(send_ref.shape[0]):
        send_ref[n, :, :width] = state
        send_ref[n, :, width:] = low


def leave_kernel(total, received_ref, state_ref, slot_ref, up_ref, state_out):
    width = state_ref.shape[1]
    chosen = one_of_slots(slot_ref[:, 1:2].astype(f32), total)
    state_out[...] = new_state(total, chosen, received_ref, state_ref, up_ref, width)


def norm_and_rotate(vector, gain, cosine, sine):
    head_dim = vector.shape[1]
    mean = jnp.mean(vector * vector, axis=1, keepdims=True)
    scaled = vector * lax.rsqrt(mean + epsilon) * gain
    return (scaled * cosine + pltpu.roll(scaled, head_dim // 2, 1) * sine).astype(bf16)


def step_kernel(total, step, *refs):
    (
        gathered_ref,
        slot_ref,
        gain_ref,
        query_weight,
        key_weight,
        value_weight,
        query_up,
        key_up,
        value_up,
        query_gain,
        key_gain,
        cosine_ref,
        sine_ref,
        bias_ref,
        key_cache,
        value_cache,
    ) = refs[:16]
    earlier = refs[16 : 16 + 2 * step]
    output_weight, output_down = refs[16 + 2 * step : 18 + 2 * step]
    send_ref, key_fresh, value_fresh, attended = refs[18 + 2 * step :]
    parts, rows, wide = gathered_ref.shape
    features = gain_ref.shape[1]
    width = features // parts
    rank = query_up.shape[0] // total
    groups, kv_local, keys_block, head_dim = key_cache.shape
    capacity = rows // groups
    heads = query_weight.shape[1] // head_dim
    per_kv = heads // kv_local

    chosen = one_of_slots(slot_ref[:, 1:2].astype(f32), total)
    state = [gathered_ref[n, :, :width].astype(f32) for n in range(parts)]
    squares = jnp.sum(state[0] * state[0], axis=1, keepdims=True)
    low = gathered_ref[0, :, width:].astype(f32)
    for n in range(1, parts):
        squares = squares + jnp.sum(state[n] * state[n], axis=1, keepdims=True)
        low = low + gathered_ref[n, :, width:].astype(f32)
    inverse = lax.rsqrt(squares / features + epsilon)
    low = low * inverse
    normed = [
        (state[n] * inverse * gain_ref[:, n * width : (n + 1) * width]).astype(bf16)
        for n in range(parts)
    ]

    def project(weight_ref, up_ref, index):
        spread = spread_over_slots(low[:, index * rank : (index + 1) * rank], chosen, total)
        delta = jnp.dot(spread, up_ref[...], preferred_element_type=f32).astype(bf16)
        result = delta.astype(f32)
        for n in range(parts):
            result = result + jnp.dot(
                normed[n],
                weight_ref[n * width : (n + 1) * width, :],
                preferred_element_type=f32,
            )
        return result

    cosine = cosine_ref[step]
    sine = sine_ref[step]
    key = project(key_weight, key_up, 1)
    value = project(value_weight, value_up, 2).astype(bf16)
    for g in range(kv_local):
        columns = slice(g * head_dim, (g + 1) * head_dim)
        key_fresh[g] = norm_and_rotate(key[:, columns], key_gain[...], cosine, sine)
        value_fresh[g] = value[:, columns]
    query = project(query_weight, query_up, 0)
    query_heads = [
        norm_and_rotate(query[:, h * head_dim : (h + 1) * head_dim], query_gain[...], cosine, sine)
        for h in range(heads)
    ]

    scale = head_dim ** (-0.5)
    fresh_count = (step + 1) * capacity
    key_row = lax.broadcasted_iota(jnp.int32, (per_kv * capacity, fresh_count), 1) % capacity
    own_row = lax.broadcasted_iota(jnp.int32, (per_kv * capacity, fresh_count), 0) % capacity
    same_row = key_row == own_row
    for b in range(groups):
        block = slice(b * capacity, (b + 1) * capacity)
        bias = jnp.concatenate([bias_ref[block, :]] * per_kv, axis=0)
        for g in range(kv_local):
            queries = jnp.concatenate(
                [query_heads[g * per_kv + h][block] for h in range(per_kv)], axis=0
            )
            fresh_keys = jnp.concatenate(
                [earlier[2 * t][g, block, :] for t in range(step)] + [key_fresh[g, block, :]], axis=0
            )
            fresh_values = jnp.concatenate(
                [earlier[2 * t + 1][g, block, :] for t in range(step)] + [value_fresh[g, block, :]],
                axis=0,
            )
            cached = (
                lax.dot_general(queries, key_cache[b, g], NT, preferred_element_type=f32) * scale
                + bias
            )
            fresh = lax.dot_general(queries, fresh_keys, NT, preferred_element_type=f32) * scale
            fresh = jnp.where(same_row, fresh, blocked)
            largest = jnp.maximum(
                jnp.max(cached, axis=1, keepdims=True), jnp.max(fresh, axis=1, keepdims=True)
            )
            cached = jnp.exp(cached - largest)
            fresh = jnp.exp(fresh - largest)
            sums = jnp.sum(cached, axis=1, keepdims=True) + jnp.sum(fresh, axis=1, keepdims=True)
            mixed = jnp.dot(cached.astype(bf16), value_cache[b, g], preferred_element_type=f32)
            mixed = mixed + jnp.dot(fresh.astype(bf16), fresh_values, preferred_element_type=f32)
            mixed = (mixed / sums).astype(bf16)
            for h in range(per_kv):
                head = g * per_kv + h
                attended[block, head * head_dim : (head + 1) * head_dim] = mixed[
                    h * capacity : (h + 1) * capacity
                ]

    attended_rows = attended[...]
    product = lax.dot_general(attended_rows, output_down[...], NT, preferred_element_type=f32)
    low_out = pick_slot(product, chosen, total).astype(bf16)
    for n in range(parts):
        term = jnp.dot(
            attended_rows,
            output_weight[:, n * width : (n + 1) * width],
            preferred_element_type=f32,
        )
        send_ref[n, :, :width] = term.astype(bf16)
        send_ref[n, :, width:] = low_out


def exchange(blocks, axis):
    return lax.all_to_all(blocks, axis, split_axis=0, concat_axis=0, tiled=True)


def shards(
    hidden,
    input_norm_gain,
    query_projection_weight,
    key_projection_weight,
    value_projection_weight,
    query_norm_gain,
    key_norm_gain,
    output_projection_weight,
    stacked_down_factors,
    query_up_factor,
    key_up_factor,
    value_up_factor,
    output_down_factor,
    output_up_factor,
    cached_key_rows,
    cached_value_rows,
    cached_length_rows,
    domain_of_row,
    slot_of_domain,
):
    groups = lax.axis_size("wide")
    parts = lax.axis_size("narrow")
    wide_index = lax.axis_index("wide")
    narrow_index = lax.axis_index("narrow")
    row_group, width = hidden.shape
    capacity = row_group // 4
    rows = groups * capacity
    total = stacked_down_factors.shape[0]
    low_width = stacked_down_factors.shape[1]
    rank = output_up_factor.shape[1]
    _, kv_local, context, head_dim = cached_key_rows.shape
    features = input_norm_gain.shape[0]
    query_width = query_projection_weight.shape[1]

    domains = lax.dynamic_slice_in_dim(domain_of_row, wide_index * row_group, row_group)
    key_blocks, value_blocks, target, local = pack_rows(
        domains, slot_of_domain, cached_key_rows, cached_value_rows, groups, capacity
    )
    place = jnp.arange(rows)[:, None] == target[None, :]
    column = jnp.arange(128)[None, :]
    facts = jnp.where(
        column == 0, cached_length_rows[:, None], jnp.where(column == 1, local[:, None], 0)
    ).astype(bf16)
    outgoing = jnp.dot(
        place.astype(bf16), jnp.concatenate([hidden, facts], axis=1), preferred_element_type=f32
    ).astype(bf16)
    arrived = exchange(outgoing.reshape(groups, capacity, width + 128), "wide").reshape(
        rows, width + 128
    )
    key_cache = exchange(key_blocks, "wide").reshape(groups, kv_local, capacity * context, head_dim)
    value_cache = exchange(value_blocks, "wide").reshape(
        groups, kv_local, capacity * context, head_dim
    )

    state = arrived[:, :width]
    facts_here = arrived[:, width:]
    lengths = facts_here[:, 0].astype(f32)
    frequency = rope_base ** (-(jnp.arange(head_dim // 2, dtype=f32) * 2.0) / head_dim)
    positions = lengths[None, :] + jnp.arange(STEPS, dtype=f32)[:, None]
    angles = positions[:, :, None] * frequency
    cosine = jnp.cos(angles)
    sine = jnp.sin(angles)
    cosine = jnp.concatenate([cosine, cosine], axis=-1)
    sine = jnp.concatenate([-sine, sine], axis=-1)
    key_index = jnp.arange(capacity * context)[None, :]
    visible = (key_index // context == (jnp.arange(rows) % capacity)[:, None]) & (
        (key_index % context).astype(f32) < lengths[:, None]
    )
    bias = jnp.where(visible, 0.0, blocked).astype(f32)

    gain_row = input_norm_gain.reshape(1, features)
    gain_slice = lax.dynamic_slice_in_dim(gain_row, narrow_index * width, width, axis=1)
    down = stacked_down_factors.reshape(total * low_width, width)
    query_up = query_up_factor.reshape(total * rank, query_width)
    key_up = key_up_factor.reshape(total * rank, -1)
    value_up = value_up_factor.reshape(total * rank, -1)
    output_down = output_down_factor.reshape(total * rank, query_width)
    output_up = output_up_factor.reshape(total * rank, width)
    query_gain = query_norm_gain.reshape(1, head_dim)
    key_gain = key_norm_gain.reshape(1, head_dim)

    sent_state = jax.ShapeDtypeStruct((parts, rows, width + low_width), bf16)
    sent_terms = jax.ShapeDtypeStruct((parts, rows, width + rank), bf16)
    state_slice = jax.ShapeDtypeStruct((rows, width), bf16)
    fresh = jax.ShapeDtypeStruct((kv_local, rows, head_dim), bf16)

    send = pl.pallas_call(
        functools.partial(enter_kernel, total),
        out_shape=sent_state,
        in_specs=vmem_specs(3),
        out_specs=vmem_specs(1)[0],
        compiler_params=kernel_params(48),
        name="enter",
    )(arrived, gain_slice, down)

    earlier = []
    for step in range(STEPS):
        gathered = exchange(send, "narrow")
        terms, key_fresh, value_fresh = pl.pallas_call(
            functools.partial(step_kernel, total, step),
            out_shape=(sent_terms, fresh, fresh),
            in_specs=vmem_specs(18 + 2 * step),
            out_specs=tuple(vmem_specs(3)),
            scratch_shapes=[pltpu.VMEM((rows, query_width), bf16)],
            compiler_params=kernel_params(48),
            name="attend_step",
        )(
            gathered,
            facts_here,
            gain_row,
            query_projection_weight,
            key_projection_weight,
            value_projection_weight,
            query_up,
            key_up,
            value_up,
            query_gain,
            key_gain,
            cosine,
            sine,
            bias,
            key_cache,
            value_cache,
            *earlier,
            output_projection_weight,
            output_down,
        )
        earlier += [key_fresh, value_fresh]
        received = exchange(terms, "narrow")
        if step < STEPS - 1:
            state, send = pl.pallas_call(
                functools.partial(between_kernel, total),
                out_shape=(state_slice, sent_state),
                in_specs=vmem_specs(6),
                out_specs=tuple(vmem_specs(2)),
                compiler_params=kernel_params(48),
                name="between",
            )(received, state, facts_here, output_up, gain_slice, down)
        else:
            state = pl.pallas_call(
                functools.partial(leave_kernel, total),
                out_shape=state_slice,
                in_specs=vmem_specs(4),
                out_specs=vmem_specs(1)[0],
                compiler_params=kernel_params(48),
                name="leave",
            )(received, state, facts_here, output_up)

    back = exchange(state.reshape(groups, capacity, width), "wide").reshape(rows, width)
    return lax.dot_general(
        place.astype(bf16), back, (((0,), (0,)), ((), ())), preferred_element_type=f32
    ).astype(bf16)


def solution(mesh):
    placed = (
        P(("parts", "wide"), "narrow"),
        P(),
        P(None, "narrow"),
        P(None, "narrow"),
        P(None, "narrow"),
        P(),
        P(),
        P("narrow", None),
        P(("parts", "wide"), None, "narrow"),
        P(("parts", "wide"), None, "narrow"),
        P(("parts", "wide"), None, "narrow"),
        P(("parts", "wide"), None, "narrow"),
        P(("parts", "wide"), None, "narrow"),
        P(("parts", "wide"), None, "narrow"),
        P(("parts", "wide"), "narrow", None, None),
        P(("parts", "wide"), "narrow", None, None),
        P(("parts", "wide")),
        P("parts"),
        P("parts"),
    )
    return jax.shard_map(
        shards,
        mesh=mesh,
        in_specs=placed,
        out_specs=P(("parts", "wide"), "narrow"),
        check_vma=False,
    )
```

profile of v0, /device:TPU:0, one launch (start us, length us, event | category | flops | bytes accessed | tf_op | source)
XLA Modules:
  0.0 279.2 jit_solution(5707624334128147043)
XLA Ops:
  0.0 1.3 dynamic_slice.6.domain_ref
  1.3 51.2 %pack_rows.1 = (bf16[4,2,16,24,128]{4,3,2,1,0:T(8,128)(2,1)}, bf16[4,2,16,24,128]{4,3,2,1,0:T(8,128)(2,1)}, s32[64]{0:T(128)}, s32[64]{0:T(128)}) custom-call(s32[64]{0:T(128)} %dynamic_slice.6.domain_ref, s32[32]{0:T(128)} %slot_ref.1, bf16[64,2,24,128]{3,2,1,0:T(8,128)(2,1)} %key_ref.1, bf16[64,2,24,128]{3,2,1,0:T(8,128)(2,1)} %value_ref.1), custom_call_target="tpu_custom_call" | custom-call | tf_op jit(solution)/shard_map/pack_rows/pallas_call | solution.py:69
  54.4 8.4 %all_to_all.60 = bf16[4,16,768]{2,1,0:T(8,128)(2,1)} all-to-all(bf16[4,16,768]{2,1,0:T(8,128)(2,1)S(1)} %bitcast.60), channel_id=1, replica_groups=mesh['parts'=2,'wide'=4,'narrow'=4] {'wide'}, dimensions={0} | all-to-all | bytes 196608 | tf_op jit(solution)/shard_map/all_to_all | solution.py:281
  62.8 15.1 %all_to_all.61 = bf16[4,2,16,24,128]{4,3,2,1,0:T(8,128)(2,1)S(1)} all-to-all(bf16[4,2,16,24,128]{4,3,2,1,0:T(8,128)(2,1)} %get-tuple-element.27), channel_id=1, replica_groups=mesh['parts'=2,'wide'=4,'narrow'=4] {'wide'}, dimensions={0} | all-to-all | bytes 1572864 | tf_op jit(solution)/shard_map/all_to_all | solution.py:281
  78.0 3.5 %all-to-all-start.3 = ((bf16[4,2,16,24,128]{4,3,2,1,0:T(8,128)(2,1)}), bf16[4,2,16,24,128]{4,3,2,1,0:T(8,128)(2,1)S(1)}, u32[]{:S(2)}, u32[]{:S(2)}) async-start(bf16[4,2,16,24,128]{4,3,2,1,0:T(8,128)(2,1)} %get-tuple-element.28), calls=%async_computation.3 | async-start | bytes 1572864 | tf_op jit(solution)/shard_map/all_to_all | solution.py:281
  88.4 4.7 %all-to-all-done.3 = bf16[4,2,16,24,128]{4,3,2,1,0:T(8,128)(2,1)S(1)} async-done(((bf16[4,2,16,24,128]{4,3,2,1,0:T(8,128)(2,1)}), bf16[4,2,16,24,128]{4,3,2,1,0:T(8,128)(2,1)S(1)}, u32[]{:S(2)}, u32[]{:S(2)}) %all-to-all-start.3) | async-done | bytes 786464 | tf_op jit(solution)/shard_map/all_to_all | solution.py:281
  93.1 5.2 %all-to-all-start.1 = ((bf16[4,64,832]{2,1,0:T(8,128)(2,1)}), bf16[4,64,832]{2,1,0:T(8,128)(2,1)}, u32[]{:S(2)}, u32[]{:S(2)}) async-start(bf16[4,64,832]{2,1,0:T(8,128)(2,1)} %copy-done.17), calls=%async_computation.1 | async-start | bytes 917504 | tf_op jit(solution)/shard_map/all_to_all | solution.py:281
  101.0 1.4 and_select_fusion.refs_13_
  102.5 8.8 %all-to-all-done.1.refs_0_ = bf16[4,64,832]{2,1,0:T(8,128)(2,1)} async-done(((bf16[4,64,832]{2,1,0:T(8,128)(2,1)}), bf16[4,64,832]{2,1,0:T(8,128)(2,1)}, u32[]{:S(2)}, u32[]{:S(2)}) %all-to-all-start.1) | async-done | bytes 426016 | tf_op jit(solution)/shard_map/all_to_all | solution.py:281
  120.4 10.3 %attend_step.4 = (bf16[4,64,704]{2,1,0:T(8,128)(2,1)S(1)}, bf16[2,64,128]{2,1,0:T(8,128)(2,1)S(1)}, bf16[2,64,128]{2,1,0:T(8,128)(2,1)S(1)}) custom-call(bf16[4,64,832]{2,1,0:T(8,128)(2,1)} %all-to-all-done.1.refs_0_, bf16[64,128]{1,0:T(8,128)(2,1)S(1)} %slice.13.refs_1_.slot_ref, f32[1,2560]{1,0:T(1,128)S(1)} %copy-done.25, bf16[2560,1024]{1,0:T(8,128)(2,1)} %refs_3_.7, ...), custom_call_target="tpu_custom_call" | custom-call | tf_op jit(solution)/shard_map/attend_step/pallas_call | solution.py:383
  132.6 4.1 %all-to-all-start.4 = ((bf16[4,64,704]{2,1,0:T(8,128)(2,1)}), bf16[4,64,704]{2,1,0:T(8,128)(2,1)}, u32[]{:S(2)}, u32[]{:S(2)}) async-start(bf16[4,64,704]{2,1,0:T(8,128)(2,1)} %copy-done.19), calls=%async_computation.4 | async-start | bytes 786432 | tf_op jit(solution)/shard_map/all_to_all | solution.py:281
  136.8 1.5 slice.15.state_ref
  138.3 9.7 %all-to-all-done.4.received_ref = bf16[4,64,704]{2,1,0:T(8,128)(2,1)} async-done(((bf16[4,64,704]{2,1,0:T(8,128)(2,1)}), bf16[4,64,704]{2,1,0:T(8,128)(2,1)}, u32[]{:S(2)}, u32[]{:S(2)}) %all-to-all-start.4) | async-done | bytes 360480 | tf_op jit(solution)/shard_map/all_to_all | solution.py:281
  150.7 2.3 between.3
  153.1 14.5 %all_to_all.62.refs_0_ = bf16[4,64,832]{2,1,0:T(8,128)(2,1)S(1)} all-to-all(bf16[4,64,832]{2,1,0:T(8,128)(2,1)S(1)} %get-tuple-element.30), channel_id=1, replica_groups=mesh['parts'=2,'wide'=4,'narrow'=4] {'narrow'}, dimensions={0} | all-to-all | bytes 851968 | tf_op jit(solution)/shard_map/all_to_all | solution.py:281
  167.7 10.3 %attend_step.5 = (bf16[4,64,704]{2,1,0:T(8,128)(2,1)S(1)}, bf16[2,64,128]{2,1,0:T(8,128)(2,1)S(1)}, bf16[2,64,128]{2,1,0:T(8,128)(2,1)S(1)}) custom-call(bf16[4,64,832]{2,1,0:T(8,128)(2,1)S(1)} %all_to_all.62.refs_0_, bf16[64,128]{1,0:T(8,128)(2,1)S(1)} %slice.13.refs_1_.slot_ref, f32[1,2560]{1,0:T(1,128)S(1)} %copy-done.26, bf16[2560,1024]{1,0:T(8,128)(2,1)} %refs_3_.7, ...), custom_call_target="tpu_custom_call" | custom-call | tf_op jit(solution)/shard_map/attend_step/pallas_call | solution.py:383
  178.0 13.4 %all_to_all.63.received_ref = bf16[4,64,704]{2,1,0:T(8,128)(2,1)S(1)} all-to-all(bf16[4,64,704]{2,1,0:T(8,128)(2,1)S(1)} %get-tuple-element.33), channel_id=1, replica_groups=mesh['parts'=2,'wide'=4,'narrow'=4] {'narrow'}, dimensions={0} | all-to-all | bytes 720896 | tf_op jit(solution)/shard_map/all_to_all | solution.py:281
  192.5 15.0 %all_to_all.64.refs_0_ = bf16[4,64,832]{2,1,0:T(8,128)(2,1)S(1)} all-to-all(bf16[4,64,832]{2,1,0:T(8,128)(2,1)S(1)} %get-tuple-element.35), channel_id=1, replica_groups=mesh['parts'=2,'wide'=4,'narrow'=4] {'narrow'}, dimensions={0} | all-to-all | bytes 851968 | tf_op jit(solution)/shard_map/all_to_all | solution.py:281
  207.6 10.2 %attend_step.6 = (bf16[4,64,704]{2,1,0:T(8,128)(2,1)S(1)}, bf16[2,64,128]{2,1,0:T(8,128)(2,1)S(1)}, bf16[2,64,128]{2,1,0:T(8,128)(2,1)S(1)}) custom-call(bf16[4,64,832]{2,1,0:T(8,128)(2,1)S(1)} %all_to_all.64.refs_0_, bf16[64,128]{1,0:T(8,128)(2,1)S(1)} %slice.13.refs_1_.slot_ref, f32[1,2560]{1,0:T(1,128)S(1)} %copy-done.26, bf16[2560,1024]{1,0:T(8,128)(2,1)} %refs_3_.7, ...), custom_call_target="tpu_custom_call" | custom-call | tf_op jit(solution)/shard_map/attend_step/pallas_call | solution.py:383
  217.8 13.5 %all_to_all.65.received_ref = bf16[4,64,704]{2,1,0:T(8,128)(2,1)S(1)} all-to-all(bf16[4,64,704]{2,1,0:T(8,128)(2,1)S(1)} %get-tuple-element.38), channel_id=1, replica_groups=mesh['parts'=2,'wide'=4,'narrow'=4] {'narrow'}, dimensions={0} | all-to-all | bytes 720896 | tf_op jit(solution)/shard_map/all_to_all | solution.py:281
  232.4 15.1 %all_to_all.66.refs_0_ = bf16[4,64,832]{2,1,0:T(8,128)(2,1)S(1)} all-to-all(bf16[4,64,832]{2,1,0:T(8,128)(2,1)S(1)} %get-tuple-element.40), channel_id=1, replica_groups=mesh['parts'=2,'wide'=4,'narrow'=4] {'narrow'}, dimensions={0} | all-to-all | bytes 851968 | tf_op jit(solution)/shard_map/all_to_all | solution.py:281
  247.5 10.3 %attend_step.7 = (bf16[4,64,704]{2,1,0:T(8,128)(2,1)S(1)}, bf16[2,64,128]{2,1,0:T(8,128)(2,1)}, bf16[2,64,128]{2,1,0:T(8,128)(2,1)}) custom-call(bf16[4,64,832]{2,1,0:T(8,128)(2,1)S(1)} %all_to_all.66.refs_0_, bf16[64,128]{1,0:T(8,128)(2,1)S(1)} %slice.13.refs_1_.slot_ref, f32[1,2560]{1,0:T(1,128)S(1)} %copy-done.26, bf16[2560,1024]{1,0:T(8,128)(2,1)} %refs_3_.7, ...), custom_call_target="tpu_custom_call" | custom-call | tf_op jit(solution)/shard_map/attend_step/pallas_call | solution.py:383
  257.9 13.5 %all_to_all.67.received_ref = bf16[4,64,704]{2,1,0:T(8,128)(2,1)S(1)} all-to-all(bf16[4,64,704]{2,1,0:T(8,128)(2,1)S(1)} %get-tuple-element.43), channel_id=1, replica_groups=mesh['parts'=2,'wide'=4,'narrow'=4] {'narrow'}, dimensions={0} | all-to-all | bytes 720896 | tf_op jit(solution)/shard_map/all_to_all | solution.py:281
  271.8 6.6 %all_to_all.68 = bf16[4,16,640]{2,1,0:T(8,128)(2,1)S(1)} all-to-all(bf16[4,16,640]{2,1,0:T(8,128)(2,1)S(1)} %bitcast.51), channel_id=1, replica_groups=mesh['parts'=2,'wide'=4,'narrow'=4] {'wide'}, dimensions={0} | all-to-all | bytes 163840 | tf_op jit(solution)/shard_map/all_to_all | solution.py:281
  (94 shorter events, 28.9 us)
Async XLA Ops:
  52.4 29.6 %copy-start.34 = (f32[2560]{0:T(1024)S(1)}, f32[2560]{0:T(1024)}, u32[]{:S(2)}) copy-start(f32[2560]{0:T(1024)} %param.20) | copy-start | bytes 30724
  52.4 32.1 %copy-start = (bf16[8,192,640]{2,1,0:T(8,128)(2,1)S(1)}, bf16[8,192,640]{2,1,0:T(8,128)(2,1)}, u32[]{:S(2)}) copy-start(bf16[8,192,640]{2,1,0:T(8,128)(2,1)} %param.27) | copy-start | bytes 5898244
  78.0 15.1 %all-to-all-start.3 = ((bf16[4,2,16,24,128]{4,3,2,1,0:T(8,128)(2,1)}), bf16[4,2,16,24,128]{4,3,2,1,0:T(8,128)(2,1)S(1)}, u32[]{:S(2)}, u32[]{:S(2)}) async-start(bf16[4,2,16,24,128]{4,3,2,1,0:T(8,128)(2,1)} %get-tuple-element.28), calls=%async_computation.3 | async-start | bytes 1572864 | tf_op jit(solution)/shard_map/all_to_all | solution.py:281
  82.7 4.5 %copy-start.27 = (f32[1,640]{1,0:T(1,128)}, f32[1,640]{1,0:T(1,128)S(1)}, u32[]{:S(2)}) copy-start(f32[1,640]{1,0:T(1,128)S(1)} %dynamic_slice.7.gain_ref) | copy-start | bytes 7684
  93.1 18.2 %all-to-all-start.1 = ((bf16[4,64,832]{2,1,0:T(8,128)(2,1)}), bf16[4,64,832]{2,1,0:T(8,128)(2,1)}, u32[]{:S(2)}, u32[]{:S(2)}) async-start(bf16[4,64,832]{2,1,0:T(8,128)(2,1)} %copy-done.17), calls=%async_computation.1 | async-start | bytes 917504 | tf_op jit(solution)/shard_map/all_to_all | solution.py:281
  111.3 1.2 copy-start.1
  112.5 1.2 copy-start.3
  132.6 15.3 %all-to-all-start.4 = ((bf16[4,64,704]{2,1,0:T(8,128)(2,1)}), bf16[4,64,704]{2,1,0:T(8,128)(2,1)}, u32[]{:S(2)}, u32[]{:S(2)}) async-start(bf16[4,64,704]{2,1,0:T(8,128)(2,1)} %copy-done.19), calls=%async_computation.4 | async-start | bytes 786432 | tf_op jit(solution)/shard_map/all_to_all | solution.py:281
  148.0 1.1 copy-start.5
  150.6 16.9 %copy-start.2 = (bf16[8,64,1024]{2,1,0:T(8,128)(2,1)S(1)}, bf16[8,64,1024]{2,1,0:T(8,128)(2,1)}, u32[]{:S(2)}) copy-start(bf16[8,64,1024]{2,1,0:T(8,128)(2,1)} %param.28) | copy-start | bytes 3145732
  150.6 16.9 %copy-start.4 = (bf16[8,64,1024]{2,1,0:T(8,128)(2,1)S(1)}, bf16[8,64,1024]{2,1,0:T(8,128)(2,1)}, u32[]{:S(2)}) copy-start(bf16[8,64,1024]{2,1,0:T(8,128)(2,1)} %param.31) | copy-start | bytes 3145732
  150.6 16.9 %copy-start.8 = (bf16[8,64,256]{2,1,0:T(8,128)(2,1)S(1)}, bf16[8,64,256]{2,1,0:T(8,128)(2,1)}, u32[]{:S(2)}) copy-start(bf16[8,64,256]{2,1,0:T(8,128)(2,1)} %param.29) | copy-start | bytes 786436
  150.6 16.9 %copy-start.10 = (bf16[8,64,256]{2,1,0:T(8,128)(2,1)S(1)}, bf16[8,64,256]{2,1,0:T(8,128)(2,1)}, u32[]{:S(2)}) copy-start(bf16[8,64,256]{2,1,0:T(8,128)(2,1)} %param.30) | copy-start | bytes 786436
  150.6 16.9 %copy-start.12 = (f32[4,64,128]{2,1,0:T(8,128)S(1)}, f32[4,64,128]{2,1,0:T(8,128)}, u32[]{:S(2)}) copy-start(f32[4,64,128]{2,1,0:T(8,128)} %pad_maximum_fusion.refs_11_) | copy-start | bytes 393220
  150.6 16.9 %copy-start.14 = (f32[4,64,128]{2,1,0:T(8,128)S(1)}, f32[4,64,128]{2,1,0:T(8,128)}, u32[]{:S(2)}) copy-start(f32[4,64,128]{2,1,0:T(8,128)} %pad_maximum_fusion.1.refs_12_) | copy-start | bytes 393220
  150.7 16.9 %copy-start.16 = (f32[64,384]{1,0:T(8,128)S(1)}, f32[64,384]{1,0:T(8,128)}, u32[]{:S(2)}) copy-start(f32[64,384]{1,0:T(8,128)} %and_select_fusion.refs_13_) | copy-start | bytes 294916
  150.7 16.9 %copy-start.22 = (bf16[2,64,128]{2,1,0:T(8,128)(2,1)S(1)}, bf16[2,64,128]{2,1,0:T(8,128)(2,1)}, u32[]{:S(2)}) copy-start(bf16[2,64,128]{2,1,0:T(8,128)(2,1)} %copy-done.21) | copy-start | bytes 98308
  150.7 16.9 %copy-start.24 = (bf16[2,64,128]{2,1,0:T(8,128)(2,1)S(1)}, bf16[2,64,128]{2,1,0:T(8,128)(2,1)}, u32[]{:S(2)}) copy-start(bf16[2,64,128]{2,1,0:T(8,128)(2,1)} %copy-done.23) | copy-start | bytes 98308
  150.7 16.9 %copy-start.26 = (f32[1,2560]{1,0:T(1,128)S(1)}, f32[1,2560]{1,0:T(1,128)}, u32[]{:S(2)}) copy-start(f32[1,2560]{1,0:T(1,128)} %reshape.141.refs_2_) | copy-start | bytes 30724
  150.7 16.9 %copy-start.31 = (f32[128]{0:T(128)S(1)}, f32[128]{0:T(128)}, u32[]{:S(2)}) copy-start(f32[128]{0:T(128)} %param.24) | copy-start | bytes 1540
  150.7 16.9 %copy-start.33 = (f32[128]{0:T(128)S(1)}, f32[128]{0:T(128)}, u32[]{:S(2)}) copy-start(f32[128]{0:T(128)} %param.25) | copy-start | bytes 1540
  167.7 23.7 %copy-start.6 = (bf16[8,64,640]{2,1,0:T(8,128)(2,1)S(1)}, bf16[8,64,640]{2,1,0:T(8,128)(2,1)}, u32[]{:S(2)}) copy-start(bf16[8,64,640]{2,1,0:T(8,128)(2,1)} %param.32) | copy-start | bytes 1966084
  167.7 23.7 %copy-start.29 = (f32[1,640]{1,0:T(1,128)S(1)}, f32[1,640]{1,0:T(1,128)}, u32[]{:S(2)}) copy-start(f32[1,640]{1,0:T(1,128)} %copy-done.27) | copy-start | bytes 7684
  257.9 20.5 %copy-start.36 = (s32[64]{0:T(128)S(1)}, s32[64]{0:T(128)}, u32[]{:S(2)}) copy-start(s32[64]{0:T(128)} %get-tuple-element.25) | copy-start | bytes 772
  (16 other events, 12.4 us)
where the time goes:
time: 280 us; the launch traced here: 279 us
  blocking collectives  115 us (41%)
  Pallas kernels  98.2 us (35%)
  waiting for transfers between devices  23.3 us (8%)
  local copies, waits for them, and re-layouts  20.2 us (7%)
  starting transfers between devices  12.8 us (5%)
  other arithmetic  7.45 us (3%)
    all_to_all x9, blocking collectives, exchange(): return lax.all_to_all(blocks, axis, split_axis=0, concat_axis=0, tiled=True)  115 us
    pallas_call x1, Pallas kernels, pack_rows(): pl.pallas_call(pack_kernel, out_shape=(moved, moved, number, number), in_...  51.2 us
    pallas_call x4, Pallas kernels, shards(): pl.pallas_call(functools.partial(step_kernel, total, step), out_shape=(se...  41.1 us
    all_to_all x3, waiting for transfers between devices, exchange(): return lax.all_to_all(blocks, axis, split_axis=0, concat_axis=0, tiled=True)  23.3 us
    unnamed x74, local copies, waits for them, and re-layouts  16 us
    all_to_all x3, starting transfers between devices, exchange(): return lax.all_to_all(blocks, axis, split_axis=0, concat_axis=0, tiled=True)  12.8 us
  transfers between devices with their start and end apart: 3, of which 3 were waited for; matrix products, arithmetic and copies ran while one was open for 3% of the time, Pallas kernels for 0%

commit v1 on v0

v1 whole, which is shorter than its diff:
```python
import functools

import jax
import jax.numpy as jnp
from jax import lax
from jax.experimental import pallas as pl
from jax.experimental.pallas import tpu as pltpu
from jax.sharding import PartitionSpec as P

STEPS = 4

epsilon = 1e-06
rope_base = 1000000.0
blocked = -1e30
f32 = jnp.float32
bf16 = jnp.bfloat16

NT = (((1,), (1,)), ((), ()))


def kernel_params(mib):
    return pltpu.CompilerParams(vmem_limit_bytes=mib * 1024 * 1024)


def route_kernel(
    group_ref, domain_ref, slot_ref, length_ref, hidden_ref, target_ref, place_ref, *refs
):
    groups = len(refs) - 3
    outgoing = refs[:groups]
    count, place, facts = refs[groups:]
    rows, width = hidden_ref.shape
    capacity = outgoing[0].shape[0]
    per_group = slot_ref.shape[0] // groups
    here = group_ref[0]
    for group in range(groups):
        count[group] = 0
    places = lax.broadcasted_iota(jnp.int32, (1, groups * capacity), 1)
    columns = lax.broadcasted_iota(jnp.int32, (1, facts.shape[1]), 1)

    def put(row, carry):
        slot = slot_ref[domain_ref[here * rows + row]]
        dest = lax.div(slot, per_group)
        position = jnp.minimum(count[dest], capacity - 1)
        count[dest] = position + 1
        target = lax.rem(dest - here + groups, groups) * capacity + position
        target_ref[row] = target
        place[pl.ds(row, 1), :] = jnp.where(places == target, 1.0, 0.0)
        length = length_ref[row].astype(f32)
        local = (slot - dest * per_group).astype(f32)
        facts[pl.ds(row, 1), :] = jnp.where(
            columns == 0, length, jnp.where(columns == 1, local, 0.0)
        )
        return carry

    lax.fori_loop(0, rows, put, 0)
    chosen = place[...].astype(bf16)
    place_ref[...] = chosen
    across = (((0,), (0,)), ((), ()))
    state = lax.dot_general(chosen, hidden_ref[...], across, preferred_element_type=f32)
    known = lax.dot_general(
        chosen, facts[...].astype(bf16), across, preferred_element_type=f32
    )
    for s in range(groups):
        block = slice(s * capacity, (s + 1) * capacity)
        outgoing[s][:, :width] = state[block].astype(bf16)
        outgoing[s][:, width:] = known[block].astype(bf16)


def pack_kernel(target_ref, key_ref, value_ref, *refs):
    groups = len(refs) - 1
    outgoing, packed = refs[:groups], refs[groups]
    rows, kv_local = key_ref.shape[:2]
    capacity = packed.shape[2]
    if groups * capacity > rows:
        packed[...] = jnp.zeros_like(packed)

    def put(row, carry):
        target = target_ref[row]
        block = lax.div(target, capacity)
        position = target - block * capacity
        for g in range(kv_local):
            packed[block, g, position] = key_ref[row, g]
            packed[block, kv_local + g, position] = value_ref[row, g]
        return carry

    lax.fori_loop(0, rows, put, 0)
    for s in range(groups):
        outgoing[s][...] = packed[s]


def one_of_slots(slot_column, total):
    ids = lax.broadcasted_iota(jnp.int32, (1, total), 1).astype(f32)
    return slot_column == ids


def spread_over_slots(factor, chosen, total):
    return jnp.concatenate(
        [jnp.where(chosen[:, d : d + 1], factor, 0.0) for d in range(total)], axis=1
    ).astype(bf16)


def pick_slot(product, chosen, total):
    rank = product.shape[1] // total
    picked = jnp.where(chosen[:, 0:1], product[:, :rank], 0.0)
    for d in range(1, total):
        picked = picked + jnp.where(chosen[:, d : d + 1], product[:, d * rank : (d + 1) * rank], 0.0)
    return picked


def partial_low(state, gain, chosen, down_ref, total):
    scaled = (state * gain).astype(bf16)
    product = lax.dot_general(scaled, down_ref[...], NT, preferred_element_type=f32)
    return pick_slot(product, chosen, total).astype(bf16)


def enter_kernel(total, state_ref, gain_ref, down_ref, send_ref):
    width = down_ref.shape[1]
    state = state_ref[:, :width].astype(f32)
    slot = state_ref[:, width + 1 : width + 2].astype(f32)
    chosen = one_of_slots(slot, total)
    send_ref[:, :width] = state_ref[:, :width]
    send_ref[:, width:] = partial_low(state, gain_ref[...], chosen, down_ref, total)


def new_state(total, chosen, received, state, up_ref):
    width = state.shape[1]
    low_out = received[0][:, width:].astype(f32)
    projected = received[0][:, :width].astype(f32)
    for part in received[1:]:
        low_out = low_out + part[:, width:].astype(f32)
        projected = projected + part[:, :width].astype(f32)
    spread = spread_over_slots(low_out, chosen, total)
    delta = jnp.dot(spread, up_ref[...], preferred_element_type=f32).astype(bf16)
    return (state.astype(f32) + projected + delta.astype(f32)).astype(bf16)


def between_kernel(total, parts, *refs):
    received = refs[:parts]
    state_ref, slot_ref, up_ref, gain_ref, down_ref, send_ref = refs[parts:]
    width = down_ref.shape[1]
    chosen = one_of_slots(slot_ref[:, 1:2].astype(f32), total)
    state = new_state(total, chosen, received, state_ref[:, :width], up_ref)
    send_ref[:, :width] = state
    send_ref[:, width:] = partial_low(state.astype(f32), gain_ref[...], chosen, down_ref, total)


def leave_kernel(total, parts, *refs):
    received = refs[:parts]
    state_ref, slot_ref, up_ref = refs[parts : parts + 3]
    outgoing = refs[parts + 3 :]
    width = up_ref.shape[1]
    capacity = outgoing[0].shape[0]
    chosen = one_of_slots(slot_ref[:, 1:2].astype(f32), total)
    state = new_state(total, chosen, received, state_ref[:, :width], up_ref)
    for s in range(len(outgoing)):
        outgoing[s][...] = state[s * capacity : (s + 1) * capacity]


def restore_kernel(place_ref, *refs):
    blocks, out_ref = refs[:-1], refs[-1]
    back = jnp.concatenate([block[...] for block in blocks], axis=0)
    out_ref[...] = jnp.dot(place_ref[...], back, preferred_element_type=f32).astype(bf16)


def norm_and_rotate(vector, gain, cosine, sine):
    head_dim = vector.shape[1]
    mean = jnp.mean(vector * vector, axis=1, keepdims=True)
    scaled = vector * lax.rsqrt(mean + epsilon) * gain
    return (scaled * cosine + pltpu.roll(scaled, head_dim // 2, 1) * sine).astype(bf16)


def step_kernel(total, step, parts, groups, *refs):
    refs = list(refs)

    def take(count):
        taken = refs[:count]
        del refs[:count]
        return taken

    gathered = take(parts)
    (
        index_ref,
        slot_ref,
        gain_ref,
        query_weight,
        key_weight,
        value_weight,
        query_up,
        key_up,
        value_up,
        query_gain,
        key_gain,
        cosine_ref,
        sine_ref,
        bias_ref,
    ) = take(14)
    cache = take(groups)
    earlier = take(2 * step)
    output_weight, output_down = take(2)
    outgoing = take(parts)
    key_fresh, value_fresh, attended, terms = refs
    features = parts * gain_ref.shape[2]
    width = features // parts
    rows = gathered[0].shape[0]
    rank = query_up.shape[0] // total
    head_dim = cache[0].shape[2]
    kv_local = cache[0].shape[0] // 2
    capacity = rows // groups
    heads = query_weight.shape[1] // head_dim
    per_kv = heads // kv_local
    here = index_ref[0]

    chosen = one_of_slots(slot_ref[:, 1:2].astype(f32), total)
    state = [gathered[s][:, :width].astype(f32) for s in range(parts)]
    squares = jnp.sum(state[0] * state[0], axis=1, keepdims=True)
    low = gathered[0][:, width:].astype(f32)
    for s in range(1, parts):
        squares = squares + jnp.sum(state[s] * state[s], axis=1, keepdims=True)
        low = low + gathered[s][:, width:].astype(f32)
    inverse = lax.rsqrt(squares / features + epsilon)
    low = low * inverse
    source = [lax.rem(here - s + parts, parts) for s in range(parts)]
    normed = [(state[s] * inverse * gain_ref[source[s]]).astype(bf16) for s in range(parts)]

    def project(weight_ref, up_ref, index):
        spread = spread_over_slots(low[:, index * rank : (index + 1) * rank], chosen, total)
        delta = jnp.dot(spread, up_ref[...], preferred_element_type=f32).astype(bf16)
        result = delta.astype(f32)
        for s in range(parts):
            features_there = pl.ds(pl.multiple_of(source[s] * width, 64), width)
            result = result + jnp.dot(
                normed[s], weight_ref[features_there, :], preferred_element_type=f32
            )
        return result

    cosine = cosine_ref[step]
    sine = sine_ref[step]
    key = project(key_weight, key_up, 1)
    value = project(value_weight, value_up, 2).astype(bf16)
    for g in range(kv_local):
        columns = slice(g * head_dim, (g + 1) * head_dim)
        key_fresh[g] = norm_and_rotate(key[:, columns], key_gain[...], cosine, sine)
        value_fresh[g] = value[:, columns]
    query = project(query_weight, query_up, 0)
    query_heads = [
        norm_and_rotate(query[:, h * head_dim : (h + 1) * head_dim], query_gain[...], cosine, sine)
        for h in range(heads)
    ]

    scale = head_dim ** (-0.5)
    fresh_count = (step + 1) * capacity
    key_row = lax.broadcasted_iota(jnp.int32, (per_kv * capacity, fresh_count), 1) % capacity
    own_row = lax.broadcasted_iota(jnp.int32, (per_kv * capacity, fresh_count), 0) % capacity
    same_row = key_row == own_row
    for b in range(groups):
        block = slice(b * capacity, (b + 1) * capacity)
        bias = jnp.concatenate([bias_ref[block, :]] * per_kv, axis=0)
        for g in range(kv_local):
            queries = jnp.concatenate(
                [query_heads[g * per_kv + h][block] for h in range(per_kv)], axis=0
            )
            fresh_keys = jnp.concatenate(
                [earlier[2 * t][g, block, :] for t in range(step)] + [key_fresh[g, block, :]], axis=0
            )
            fresh_values = jnp.concatenate(
                [earlier[2 * t + 1][g, block, :] for t in range(step)] + [value_fresh[g, block, :]],
                axis=0,
            )
            cached = (
                lax.dot_general(queries, cache[b][g], NT, preferred_element_type=f32) * scale
                + bias
            )
            fresh = lax.dot_general(queries, fresh_keys, NT, preferred_element_type=f32) * scale
            fresh = jnp.where(same_row, fresh, blocked)
            largest = jnp.maximum(
                jnp.max(cached, axis=1, keepdims=True), jnp.max(fresh, axis=1, keepdims=True)
            )
            cached = jnp.exp(cached - largest)
            fresh = jnp.exp(fresh - largest)
            sums = jnp.sum(cached, axis=1, keepdims=True) + jnp.sum(fresh, axis=1, keepdims=True)
            mixed = jnp.dot(cached.astype(bf16), cache[b][kv_local + g], preferred_element_type=f32)
            mixed = mixed + jnp.dot(fresh.astype(bf16), fresh_values, preferred_element_type=f32)
            mixed = (mixed / sums).astype(bf16)
            for h in range(per_kv):
                head = g * per_kv + h
                attended[block, head * head_dim : (head + 1) * head_dim] = mixed[
                    h * capacity : (h + 1) * capacity
                ]

    attended_rows = attended[...]
    product = lax.dot_general(attended_rows, output_down[...], NT, preferred_element_type=f32)
    low_out = pick_slot(product, chosen, total).astype(bf16)
    for n in range(parts):
        term = jnp.dot(
            attended_rows,
            output_weight[:, n * width : (n + 1) * width],
            preferred_element_type=f32,
        )
        terms[lax.rem(n - here + parts, parts)] = term.astype(bf16)
    for s in range(parts):
        outgoing[s][:, :width] = terms[s]
        outgoing[s][:, width:] = low_out


def shift(block, axis, by):
    size = lax.axis_size(axis)
    return lax.ppermute(block, axis, [(i, (i + by) % size) for i in range(size)])


def shards(
    hidden,
    input_norm_gain,
    query_projection_weight,
    key_projection_weight,
    value_projection_weight,
    query_norm_gain,
    key_norm_gain,
    output_projection_weight,
    stacked_down_factors,
    query_up_factor,
    key_up_factor,
    value_up_factor,
    output_down_factor,
    output_up_factor,
    cached_key_rows,
    cached_value_rows,
    cached_length_rows,
    domain_of_row,
    slot_of_domain,
):
    groups = lax.axis_size("wide")
    parts = lax.axis_size("narrow")
    wide_index = lax.axis_index("wide")
    narrow_index = lax.axis_index("narrow")
    row_group, width = hidden.shape
    capacity = row_group // 4
    rows = groups * capacity
    total = stacked_down_factors.shape[0]
    low_width = stacked_down_factors.shape[1]
    rank = output_up_factor.shape[1]
    _, kv_local, context, head_dim = cached_key_rows.shape
    features = input_norm_gain.shape[0]
    query_width = query_projection_weight.shape[1]

    smem = pl.BlockSpec(memory_space=pltpu.SMEM)
    vmem = pl.BlockSpec(memory_space=pltpu.VMEM)
    outgoing_shape = jax.ShapeDtypeStruct((capacity, width + 128), bf16)
    target, place, *outgoing = pl.pallas_call(
        route_kernel,
        out_shape=[
            jax.ShapeDtypeStruct((row_group,), jnp.int32),
            jax.ShapeDtypeStruct((row_group, rows), bf16),
        ]
        + [outgoing_shape] * groups,
        in_specs=[smem] * 4 + [vmem],
        out_specs=[smem] + [vmem] * (groups + 1),
        scratch_shapes=[
            pltpu.SMEM((groups,), jnp.int32),
            pltpu.VMEM((row_group, rows), f32),
            pltpu.VMEM((row_group, 128), f32),
        ],
        compiler_params=kernel_params(8),
        name="route_rows",
    )(wide_index.reshape(1), domain_of_row, slot_of_domain, cached_length_rows, hidden)
    arrived = jnp.concatenate(
        [outgoing[0]] + [shift(outgoing[s], "wide", s) for s in range(1, groups)], axis=0
    )
    packed_shape = (2 * kv_local, capacity, context, head_dim)
    packed = pl.pallas_call(
        pack_kernel,
        out_shape=[jax.ShapeDtypeStruct(packed_shape, bf16)] * groups,
        in_specs=[smem, vmem, vmem],
        out_specs=[vmem] * groups,
        scratch_shapes=[pltpu.VMEM((groups,) + packed_shape, bf16)],
        compiler_params=kernel_params(16),
        name="pack_cache",
    )(target, cached_key_rows, cached_value_rows)
    cache = [packed[0]] + [shift(packed[s], "wide", s) for s in range(1, groups)]
    cache = [block.reshape(2 * kv_local, capacity * context, head_dim) for block in cache]

    facts_here = arrived[:, width:]
    lengths = facts_here[:, 0].astype(f32)
    frequency = rope_base ** (-(jnp.arange(head_dim // 2, dtype=f32) * 2.0) / head_dim)
    positions = lengths[None, :] + jnp.arange(STEPS, dtype=f32)[:, None]
    angles = positions[:, :, None] * frequency
    cosine = jnp.cos(angles)
    sine = jnp.sin(angles)
    cosine = jnp.concatenate([cosine, cosine], axis=-1)
    sine = jnp.concatenate([-sine, sine], axis=-1)
    key_index = jnp.arange(capacity * context)[None, :]
    visible = (key_index // context == (jnp.arange(rows) % capacity)[:, None]) & (
        (key_index % context).astype(f32) < lengths[:, None]
    )
    bias = jnp.where(visible, 0.0, blocked).astype(f32)

    gain_rows = input_norm_gain.reshape(parts, 1, width)
    gain_slice = lax.dynamic_index_in_dim(gain_rows, narrow_index, 0, keepdims=False)
    down = stacked_down_factors.reshape(total * low_width, width)
    query_up = query_up_factor.reshape(total * rank, query_width)
    key_up = key_up_factor.reshape(total * rank, -1)
    value_up = value_up_factor.reshape(total * rank, -1)
    output_down = output_down_factor.reshape(total * rank, query_width)
    output_up = output_up_factor.reshape(total * rank, width)
    query_gain = query_norm_gain.reshape(1, head_dim)
    key_gain = key_norm_gain.reshape(1, head_dim)

    sent_state = jax.ShapeDtypeStruct((rows, width + low_width), bf16)
    sent_terms = jax.ShapeDtypeStruct((rows, width + rank), bf16)
    fresh = jax.ShapeDtypeStruct((kv_local, rows, head_dim), bf16)

    send = pl.pallas_call(
        functools.partial(enter_kernel, total),
        out_shape=sent_state,
        in_specs=[vmem] * 3,
        out_specs=vmem,
        compiler_params=kernel_params(8),
        name="enter",
    )(arrived, gain_slice, down)

    earlier = []
    for step in range(STEPS):
        gathered = [send] + [shift(send, "narrow", s) for s in range(1, parts)]
        *terms, key_fresh, value_fresh = pl.pallas_call(
            functools.partial(step_kernel, total, step, parts, groups),
            out_shape=[sent_terms] * parts + [fresh] * 2,
            in_specs=[vmem] * parts + [smem] + [vmem] * (15 + groups + 2 * step),
            out_specs=[vmem] * (parts + 2),
            scratch_shapes=[
                pltpu.VMEM((rows, query_width), bf16),
                pltpu.VMEM((parts, rows, width), bf16),
            ],
            compiler_params=kernel_params(24),
            name="attend_step",
        )(
            *gathered,
            narrow_index.reshape(1),
            facts_here,
            gain_rows,
            query_projection_weight,
            key_projection_weight,
            value_projection_weight,
            query_up,
            key_up,
            value_up,
            query_gain,
            key_gain,
            cosine,
            sine,
            bias,
            *cache,
            *earlier,
            output_projection_weight,
            output_down,
        )
        earlier += [key_fresh, value_fresh]
        received = [terms[0]] + [shift(terms[s], "narrow", s) for s in range(1, parts)]
        if step < STEPS - 1:
            send = pl.pallas_call(
                functools.partial(between_kernel, total, parts),
                out_shape=sent_state,
                in_specs=[vmem] * (parts + 5),
                out_specs=vmem,
                compiler_params=kernel_params(8),
                name="between",
            )(*received, send, facts_here, output_up, gain_slice, down)
        else:
            leaving = pl.pallas_call(
                functools.partial(leave_kernel, total, parts),
                out_shape=[jax.ShapeDtypeStruct((capacity, width), bf16)] * groups,
                in_specs=[vmem] * (parts + 3),
                out_specs=[vmem] * groups,
                compiler_params=kernel_params(8),
                name="leave",
            )(*received, send, facts_here, output_up)

    back = [leaving[0]] + [shift(leaving[s], "wide", -s) for s in range(1, groups)]
    return pl.pallas_call(
        restore_kernel,
        out_shape=jax.ShapeDtypeStruct((row_group, width), bf16),
        in_specs=[vmem] * (groups + 1),
        out_specs=vmem,
        compiler_params=kernel_params(8),
        name="restore",
    )(place, *back)


def solution(mesh):
    placed = (
        P(("parts", "wide"), "narrow"),
        P(),
        P(None, "narrow"),
        P(None, "narrow"),
        P(None, "narrow"),
        P(),
        P(),
        P("narrow", None),
        P(("parts", "wide"), None, "narrow"),
        P(("parts", "wide"), None, "narrow"),
        P(("parts", "wide"), None, "narrow"),
        P(("parts", "wide"), None, "narrow"),
        P(("parts", "wide"), None, "narrow"),
        P(("parts", "wide"), None, "narrow"),
        P(("parts", "wide"), "narrow", None, None),
        P(("parts", "wide"), "narrow", None, None),
        P(("parts", "wide")),
        P("parts"),
        P("parts"),
    )
    return jax.shard_map(
        shards,
        mesh=mesh,
        in_specs=placed,
        out_specs=P(("parts", "wide"), "narrow"),
        check_vma=False,
    )
```

time: 280 us -> 165 us (0.59)
  blocking collectives: 115 us -> 0 us
  Pallas kernels: 98.2 us -> 32.8 us
  waiting for transfers between devices: 23.3 us -> 58.6 us
  starting transfers between devices: 12.8 us -> 42.6 us
  local copies, waits for them, and re-layouts: 20.2 us -> 26.1 us
  other arithmetic: 7.45 us -> 4.15 us
    all_to_all x9 -> x0, blocking collectives: 115 us -> none  [exchange(): return lax.all_to_all(blocks, axis, split_axis=0, concat_axis=0, tiled=True)]
    pallas_call x9 -> x11, Pallas kernels: 97.4 us -> 32 us  [the longest x4 22.5 us: shards(): pl.pallas_call(functools.partial(step_kernel, total, step, parts, groups)...]
    ppermute x0 -> x33, waiting for transfers between devices: none -> 58.6 us  [shift(): lax.ppermute(block, axis, [(i, (i + by) % size) for i in range(size)])]
    ppermute x0 -> x33, starting transfers between devices: none -> 42.6 us  [shift(): lax.ppermute(block, axis, [(i, (i + by) % size) for i in range(size)])]
    all_to_all x3 -> x0, waiting for transfers between devices: 23.3 us -> none  [exchange(): return lax.all_to_all(blocks, axis, split_axis=0, concat_axis=0, tiled=True)]
    all_to_all x3 -> x0, starting transfers between devices: 12.8 us -> none  [exchange(): return lax.all_to_all(blocks, axis, split_axis=0, concat_axis=0, tiled=True)]
    unnamed x74 -> x63, local copies, waits for them, and re-layouts: 16 us -> 23.3 us
  transfers between devices with their start and end apart: 3 -> 33, of which waited for: 3 -> 18; matrix products, arithmetic and copies ran while one was open for 3% -> 7% of each run, Pallas kernels for 0% -> 2%
where the time goes in v1:
time: 165 us
  waiting for transfers between devices  58.6 us (36%)
  starting transfers between devices  42.6 us (26%)
  Pallas kernels  32.8 us (20%)
  local copies, waits for them, and re-layouts  26.1 us (16%)
  other arithmetic  4.15 us (3%)
    ppermute x33, waiting for transfers between devices, shift(): lax.ppermute(block, axis, [(i, (i + by) % size) for i in range(size)])  58.6 us
    ppermute x33, starting transfers between devices, shift(): lax.ppermute(block, axis, [(i, (i + by) % size) for i in range(size)])  42.6 us
    unnamed x63, local copies, waits for them, and re-layouts  23.3 us
    pallas_call x4, Pallas kernels, shards(): pl.pallas_call(functools.partial(step_kernel, total, step, parts, groups)...  22.5 us
    pallas_call x3, Pallas kernels, shards(): pl.pallas_call(functools.partial(between_kernel, total, parts), out_shape...  3.53 us
  transfers between devices with their start and end apart: 33, of which 18 were waited for; matrix products, arithmetic and copies ran while one was open for 7% of the time, Pallas kernels for 2%

profile of v1, /device:TPU:0, one launch (start us, length us, event | category | flops | bytes accessed | tf_op | source)
XLA Modules:
  0.0 164.5 jit_solution(5606333507265948771)
XLA Ops:
  6.5 2.5 %collective-permute-start.1 = (bf16[16,768]{1,0:T(8,128)(2,1)}, bf16[16,768]{1,0:T(8,128)(2,1)}, u32[]{:S(2)}, u32[]{:S(2)}) collective-permute-start(bf16[16,768]{1,0:T(8,128)(2,1)} %get-tuple-element.44), channel_id=1, source_target_pairs={{0,8},{4,12},{8,0},{12,4},{1,9},{5,13},{9,1},{13,5},{2,10},{6,14},... | collective-permute-start | bytes 73736 | tf_op jit(solution)/shard_map/ppermute | solution.py:307
  28.3 3.8 %collective-permute-start.5 = (bf16[64,832]{1,0:T(8,128)(2,1)S(1)}, bf16[64,832]{1,0:T(8,128)(2,1)S(1)}, u32[]{:S(2)}, u32[]{:S(2)}) collective-permute-start(bf16[64,832]{1,0:T(8,128)(2,1)S(1)} %enter.1.refs_0_.refs_4_), channel_id=1, source_target_pairs={{0,3},{1,0},{2,1},{3,2},{4,7},{5,4},{6,5},{7,6},{8,11},{9,8},{10,9... | collective-permute-start | bytes 319496 | tf_op jit(solution)/shard_map/ppermute | solution.py:307
  36.0 7.2 %collective-permute-done.4.refs_2_ = bf16[64,832]{1,0:T(8,128)(2,1)S(1)} collective-permute-done((bf16[64,832]{1,0:T(8,128)(2,1)S(1)}, bf16[64,832]{1,0:T(8,128)(2,1)S(1)}, u32[]{:S(2)}, u32[]{:S(2)}) %collective-permute-start.4) | collective-permute-done | bytes 106528 | tf_op jit(solution)/shard_map/ppermute | solution.py:307
  51.0 5.6 %attend_step.4 = (bf16[64,704]{1,0:T(8,128)(2,1)S(1)}, bf16[64,704]{1,0:T(8,128)(2,1)S(1)}, bf16[64,704]{1,0:T(8,128)(2,1)S(1)}, bf16[64,704]{1,0:T(8,128)(2,1)S...) custom-call(bf16[64,832]{1,0:T(8,128)(2,1)S(1)} %enter.1.refs_0_.refs_4_, ...), custom_call_target="tpu_custom_call" | custom-call | tf_op jit(solution)/shard_map/attend_step/pallas_call | solution.py:423
  59.2 2.5 %collective-permute-start.11 = (bf16[64,704]{1,0:T(8,128)(2,1)S(1)}, bf16[64,704]{1,0:T(8,128)(2,1)S(1)}, u32[]{:S(2)}, u32[]{:S(2)}) collective-permute-start(bf16[64,704]{1,0:T(8,128)(2,1)S(1)} %get-tuple-element.54), channel_id=1, source_target_pairs={{0,3},{1,0},{2,1},{3,2},{4,7},{5,4},{6,5},{7,6},{8,11},{9,8},{10,9... | collective-permute-start | bytes 270344 | tf_op jit(solution)/shard_map/ppermute | solution.py:307
  64.2 2.7 %collective-permute-done.10.refs_2_ = bf16[64,704]{1,0:T(8,128)(2,1)S(1)} collective-permute-done((bf16[64,704]{1,0:T(8,128)(2,1)S(1)}, bf16[64,704]{1,0:T(8,128)(2,1)S(1)}, u32[]{:S(2)}, u32[]{:S(2)}) %collective-permute-start.10) | collective-permute-done | bytes 90144 | tf_op jit(solution)/shard_map/ppermute | solution.py:307
  68.1 3.7 %collective-permute-start.14 = (bf16[64,832]{1,0:T(8,128)(2,1)S(1)}, bf16[64,832]{1,0:T(8,128)(2,1)S(1)}, u32[]{:S(2)}, u32[]{:S(2)}) collective-permute-start(bf16[64,832]{1,0:T(8,128)(2,1)S(1)} %between.3.refs_0_.refs_4_), channel_id=1, source_target_pairs={{0,3},{1,0},{2,1},{3,2},{4,7},{5,4},{6,5},{7,6},{8,11},{9,8},{10,9... | collective-permute-start | bytes 319496 | tf_op jit(solution)/shard_map/ppermute | solution.py:307
  72.5 3.0 %collective-permute-done.14.refs_3_ = bf16[64,832]{1,0:T(8,128)(2,1)S(1)} collective-permute-done((bf16[64,832]{1,0:T(8,128)(2,1)S(1)}, bf16[64,832]{1,0:T(8,128)(2,1)S(1)}, u32[]{:S(2)}, u32[]{:S(2)}) %collective-permute-start.14) | collective-permute-done | bytes 106528 | tf_op jit(solution)/shard_map/ppermute | solution.py:307
  75.5 6.1 %collective-permute-done.13.refs_2_ = bf16[64,832]{1,0:T(8,128)(2,1)S(1)} collective-permute-done((bf16[64,832]{1,0:T(8,128)(2,1)S(1)}, bf16[64,832]{1,0:T(8,128)(2,1)S(1)}, u32[]{:S(2)}, u32[]{:S(2)}) %collective-permute-start.13) | collective-permute-done | bytes 106528 | tf_op jit(solution)/shard_map/ppermute | solution.py:307
  84.1 5.6 %attend_step.5 = (bf16[64,704]{1,0:T(8,128)(2,1)S(1)}, bf16[64,704]{1,0:T(8,128)(2,1)S(1)}, bf16[64,704]{1,0:T(8,128)(2,1)S(1)}, bf16[64,704]{1,0:T(8,128)(2,1)S...) custom-call(bf16[64,832]{1,0:T(8,128)(2,1)S(1)} %between.3.refs_0_.refs_4_, ...), custom_call_target="tpu_custom_call" | custom-call | tf_op jit(solution)/shard_map/attend_step/pallas_call | solution.py:423
  91.3 2.8 %collective-permute-start.17 = (bf16[64,704]{1,0:T(8,128)(2,1)S(1)}, bf16[64,704]{1,0:T(8,128)(2,1)S(1)}, u32[]{:S(2)}, u32[]{:S(2)}) collective-permute-start(bf16[64,704]{1,0:T(8,128)(2,1)S(1)} %get-tuple-element.60), channel_id=1, source_target_pairs={{0,3},{1,0},{2,1},{3,2},{4,7},{5,4},{6,5},{7,6},{8,11},{9,8},{10,9... | collective-permute-start | bytes 270344 | tf_op jit(solution)/shard_map/ppermute | solution.py:307
  94.1 3.1 %collective-permute-done.15.refs_1_ = bf16[64,704]{1,0:T(8,128)(2,1)S(1)} collective-permute-done((bf16[64,704]{1,0:T(8,128)(2,1)S(1)}, bf16[64,704]{1,0:T(8,128)(2,1)S(1)}, u32[]{:S(2)}, u32[]{:S(2)}) %collective-permute-start.15) | collective-permute-done | bytes 90144 | tf_op jit(solution)/shard_map/ppermute | solution.py:307
  100.7 3.0 %collective-permute-start.20 = (bf16[64,832]{1,0:T(8,128)(2,1)S(1)}, bf16[64,832]{1,0:T(8,128)(2,1)S(1)}, u32[]{:S(2)}, u32[]{:S(2)}) collective-permute-start(bf16[64,832]{1,0:T(8,128)(2,1)S(1)} %between.4.refs_0_.refs_4_), channel_id=1, source_target_pairs={{0,3},{1,0},{2,1},{3,2},{4,7},{5,4},{6,5},{7,6},{8,11},{9,8},{10,9... | collective-permute-start | bytes 319496 | tf_op jit(solution)/shard_map/ppermute | solution.py:307
  104.4 3.0 %collective-permute-done.20.refs_3_ = bf16[64,832]{1,0:T(8,128)(2,1)S(1)} collective-permute-done((bf16[64,832]{1,0:T(8,128)(2,1)S(1)}, bf16[64,832]{1,0:T(8,128)(2,1)S(1)}, u32[]{:S(2)}, u32[]{:S(2)}) %collective-permute-start.20) | collective-permute-done | bytes 106528 | tf_op jit(solution)/shard_map/ppermute | solution.py:307
  107.3 6.2 %collective-permute-done.19.refs_2_ = bf16[64,832]{1,0:T(8,128)(2,1)S(1)} collective-permute-done((bf16[64,832]{1,0:T(8,128)(2,1)S(1)}, bf16[64,832]{1,0:T(8,128)(2,1)S(1)}, u32[]{:S(2)}, u32[]{:S(2)}) %collective-permute-start.19) | collective-permute-done | bytes 106528 | tf_op jit(solution)/shard_map/ppermute | solution.py:307
  113.6 5.6 %attend_step.6 = (bf16[64,704]{1,0:T(8,128)(2,1)S(1)}, bf16[64,704]{1,0:T(8,128)(2,1)S(1)}, bf16[64,704]{1,0:T(8,128)(2,1)S(1)}, bf16[64,704]{1,0:T(8,128)(2,1)S...) custom-call(bf16[64,832]{1,0:T(8,128)(2,1)S(1)} %between.4.refs_0_.refs_4_, ...), custom_call_target="tpu_custom_call" | custom-call | tf_op jit(solution)/shard_map/attend_step/pallas_call | solution.py:423
  121.1 2.8 %collective-permute-start.23 = (bf16[64,704]{1,0:T(8,128)(2,1)S(1)}, bf16[64,704]{1,0:T(8,128)(2,1)S(1)}, u32[]{:S(2)}, u32[]{:S(2)}) collective-permute-start(bf16[64,704]{1,0:T(8,128)(2,1)S(1)} %get-tuple-element.66), channel_id=1, source_target_pairs={{0,3},{1,0},{2,1},{3,2},{4,7},{5,4},{6,5},{7,6},{8,11},{9,8},{10,9... | collective-permute-start | bytes 270344 | tf_op jit(solution)/shard_map/ppermute | solution.py:307
  123.9 2.8 %collective-permute-done.21.refs_1_ = bf16[64,704]{1,0:T(8,128)(2,1)S(1)} collective-permute-done((bf16[64,704]{1,0:T(8,128)(2,1)S(1)}, bf16[64,704]{1,0:T(8,128)(2,1)S(1)}, u32[]{:S(2)}, u32[]{:S(2)}) %collective-permute-start.21) | collective-permute-done | bytes 90144 | tf_op jit(solution)/shard_map/ppermute | solution.py:307
  130.4 3.2 %collective-permute-start.26 = (bf16[64,832]{1,0:T(8,128)(2,1)S(1)}, bf16[64,832]{1,0:T(8,128)(2,1)S(1)}, u32[]{:S(2)}, u32[]{:S(2)}) collective-permute-start(bf16[64,832]{1,0:T(8,128)(2,1)S(1)} %between.5.refs_0_.refs_4_), channel_id=1, source_target_pairs={{0,3},{1,0},{2,1},{3,2},{4,7},{5,4},{6,5},{7,6},{8,11},{9,8},{10,9... | collective-permute-start | bytes 319496 | tf_op jit(solution)/shard_map/ppermute | solution.py:307
  134.3 3.0 %collective-permute-done.26.refs_3_ = bf16[64,832]{1,0:T(8,128)(2,1)S(1)} collective-permute-done((bf16[64,832]{1,0:T(8,128)(2,1)S(1)}, bf16[64,832]{1,0:T(8,128)(2,1)S(1)}, u32[]{:S(2)}, u32[]{:S(2)}) %collective-permute-start.26) | collective-permute-done | bytes 106528 | tf_op jit(solution)/shard_map/ppermute | solution.py:307
  137.2 5.9 %collective-permute-done.25.refs_2_ = bf16[64,832]{1,0:T(8,128)(2,1)S(1)} collective-permute-done((bf16[64,832]{1,0:T(8,128)(2,1)S(1)}, bf16[64,832]{1,0:T(8,128)(2,1)S(1)}, u32[]{:S(2)}, u32[]{:S(2)}) %collective-permute-start.25) | collective-permute-done | bytes 106528 | tf_op jit(solution)/shard_map/ppermute | solution.py:307
  143.2 5.8 %attend_step.7 = (bf16[64,704]{1,0:T(8,128)(2,1)S(1)}, bf16[64,704]{1,0:T(8,128)(2,1)S(1)}, bf16[64,704]{1,0:T(8,128)(2,1)S(1)}, bf16[64,704]{1,0:T(8,128)(2,1)S...) custom-call(bf16[64,832]{1,0:T(8,128)(2,1)S(1)} %between.5.refs_0_.refs_4_, ...), custom_call_target="tpu_custom_call" | custom-call | tf_op jit(solution)/shard_map/attend_step/pallas_call | solution.py:423
  150.7 2.9 %collective-permute-start.29 = (bf16[64,704]{1,0:T(8,128)(2,1)S(1)}, bf16[64,704]{1,0:T(8,128)(2,1)S(1)}, u32[]{:S(2)}, u32[]{:S(2)}) collective-permute-start(bf16[64,704]{1,0:T(8,128)(2,1)S(1)} %get-tuple-element.72), channel_id=1, source_target_pairs={{0,3},{1,0},{2,1},{3,2},{4,7},{5,4},{6,5},{7,6},{8,11},{9,8},{10,9... | collective-permute-start | bytes 270344 | tf_op jit(solution)/shard_map/ppermute | solution.py:307
  153.5 3.0 %collective-permute-done.27.refs_1_ = bf16[64,704]{1,0:T(8,128)(2,1)S(1)} collective-permute-done((bf16[64,704]{1,0:T(8,128)(2,1)S(1)}, bf16[64,704]{1,0:T(8,128)(2,1)S(1)}, u32[]{:S(2)}, u32[]{:S(2)}) %collective-permute-start.27) | collective-permute-done | bytes 90144 | tf_op jit(solution)/shard_map/ppermute | solution.py:307
  (130 shorter events, 68.3 us)
Async XLA Ops:
  6.0 13.3 %collective-permute-start = (bf16[16,768]{1,0:T(8,128)(2,1)}, bf16[16,768]{1,0:T(8,128)(2,1)}, u32[]{:S(2)}, u32[]{:S(2)}) collective-permute-start(bf16[16,768]{1,0:T(8,128)(2,1)} %get-tuple-element.43), channel_id=1, source_target_pairs={{0,4},{4,8},{8,12},{12,0},{1,5},{5,9},{9,13},{13,1},{2,6},{6,10},{... | collective-permute-start | bytes 73736 | tf_op jit(solution)/shard_map/ppermute | solution.py:307
  6.5 15.0 %collective-permute-start.1 = (bf16[16,768]{1,0:T(8,128)(2,1)}, bf16[16,768]{1,0:T(8,128)(2,1)}, u32[]{:S(2)}, u32[]{:S(2)}) collective-permute-start(bf16[16,768]{1,0:T(8,128)(2,1)} %get-tuple-element.44), channel_id=1, source_target_pairs={{0,8},{4,12},{8,0},{12,4},{1,9},{5,13},{9,1},{13,5},{2,10},{6,14},... | collective-permute-start | bytes 73736 | tf_op jit(solution)/shard_map/ppermute | solution.py:307
  9.0 13.8 %collective-permute-start.2 = (bf16[16,768]{1,0:T(8,128)(2,1)}, bf16[16,768]{1,0:T(8,128)(2,1)}, u32[]{:S(2)}, u32[]{:S(2)}) collective-permute-start(bf16[16,768]{1,0:T(8,128)(2,1)} %get-tuple-element.45), channel_id=1, source_target_pairs={{0,12},{4,0},{8,4},{12,8},{1,13},{5,1},{9,5},{13,9},{2,14},{6,2},{... | collective-permute-start | bytes 73736 | tf_op jit(solution)/shard_map/ppermute | solution.py:307
  15.0 28.2 %collective-permute-start.6 = (bf16[4,16,24,128]{3,2,1,0:T(8,128)(2,1)}, bf16[4,16,24,128]{3,2,1,0:T(8,128)(2,1)S(1)}, u32[]{:S(2)}, u32[]{:S(2)}) collective-permute-start(bf16[4,16,24,128]{3,2,1,0:T(8,128)(2,1)} %get-tuple-element.48), channel_id=1, source_target_pairs={{0,4},{4,8},{8,12},{12,0},{1,5},{5,9},{9,13},{13,1},{2,6},{6,10},{... | collective-permute-start | bytes 1179656 | tf_op jit(solution)/shard_map/ppermute | solution.py:307
  15.8 27.4 %collective-permute-start.7 = (bf16[4,16,24,128]{3,2,1,0:T(8,128)(2,1)}, bf16[4,16,24,128]{3,2,1,0:T(8,128)(2,1)S(1)}, u32[]{:S(2)}, u32[]{:S(2)}) collective-permute-start(bf16[4,16,24,128]{3,2,1,0:T(8,128)(2,1)} %get-tuple-element.49), channel_id=1, source_target_pairs={{0,8},{4,12},{8,0},{12,4},{1,9},{5,13},{9,1},{13,5},{2,10},{6,14},... | collective-permute-start | bytes 1179656 | tf_op jit(solution)/shard_map/ppermute | solution.py:307
  19.4 23.8 %collective-permute-start.8 = (bf16[4,16,24,128]{3,2,1,0:T(8,128)(2,1)}, bf16[4,16,24,128]{3,2,1,0:T(8,128)(2,1)S(1)}, u32[]{:S(2)}, u32[]{:S(2)}) collective-permute-start(bf16[4,16,24,128]{3,2,1,0:T(8,128)(2,1)} %copy-done.27), channel_id=1, source_target_pairs={{0,12},{4,0},{8,4},{12,8},{1,13},{5,1},{9,5},{13,9},{2,14},{6,2},{... | collective-permute-start | bytes 1179656 | tf_op jit(solution)/shard_map/ppermute | solution.py:307
  34.8 8.3 %collective-permute-start.4 = (bf16[64,832]{1,0:T(8,128)(2,1)S(1)}, bf16[64,832]{1,0:T(8,128)(2,1)S(1)}, u32[]{:S(2)}, u32[]{:S(2)}) collective-permute-start(bf16[64,832]{1,0:T(8,128)(2,1)S(1)} %enter.1.refs_0_.refs_4_), channel_id=1, source_target_pairs={{0,2},{1,3},{2,0},{3,1},{4,6},{5,7},{6,4},{7,5},{8,10},{9,11},{10,... | collective-permute-start | bytes 319496 | tf_op jit(solution)/shard_map/ppermute | solution.py:307
  34.8 8.3 %collective-permute-start.3 = (bf16[64,832]{1,0:T(8,128)(2,1)S(1)}, bf16[64,832]{1,0:T(8,128)(2,1)S(1)}, u32[]{:S(2)}, u32[]{:S(2)}) collective-permute-start(bf16[64,832]{1,0:T(8,128)(2,1)S(1)} %enter.1.refs_0_.refs_4_), channel_id=1, source_target_pairs={{0,1},{1,2},{2,3},{3,0},{4,5},{5,6},{6,7},{7,4},{8,9},{9,10},{10,1... | collective-permute-start | bytes 319496 | tf_op jit(solution)/shard_map/ppermute | solution.py:307
  56.9 10.0 %collective-permute-start.10 = (bf16[64,704]{1,0:T(8,128)(2,1)S(1)}, bf16[64,704]{1,0:T(8,128)(2,1)S(1)}, u32[]{:S(2)}, u32[]{:S(2)}) collective-permute-start(bf16[64,704]{1,0:T(8,128)(2,1)S(1)} %get-tuple-element.53), channel_id=1, source_target_pairs={{0,2},{1,3},{2,0},{3,1},{4,6},{5,7},{6,4},{7,5},{8,10},{9,11},{10,... | collective-permute-start | bytes 270344 | tf_op jit(solution)/shard_map/ppermute | solution.py:307
  59.2 7.7 %collective-permute-start.11 = (bf16[64,704]{1,0:T(8,128)(2,1)S(1)}, bf16[64,704]{1,0:T(8,128)(2,1)S(1)}, u32[]{:S(2)}, u32[]{:S(2)}) collective-permute-start(bf16[64,704]{1,0:T(8,128)(2,1)S(1)} %get-tuple-element.54), channel_id=1, source_target_pairs={{0,3},{1,0},{2,1},{3,2},{4,7},{5,4},{6,5},{7,6},{8,11},{9,8},{10,9... | collective-permute-start | bytes 270344 | tf_op jit(solution)/shard_map/ppermute | solution.py:307
  71.9 9.7 %collective-permute-start.13 = (bf16[64,832]{1,0:T(8,128)(2,1)S(1)}, bf16[64,832]{1,0:T(8,128)(2,1)S(1)}, u32[]{:S(2)}, u32[]{:S(2)}) collective-permute-start(bf16[64,832]{1,0:T(8,128)(2,1)S(1)} %between.3.refs_0_.refs_4_), channel_id=1, source_target_pairs={{0,2},{1,3},{2,0},{3,1},{4,6},{5,7},{6,4},{7,5},{8,10},{9,11},{10,... | collective-permute-start | bytes 319496 | tf_op jit(solution)/shard_map/ppermute | solution.py:307
  71.9 9.7 %collective-permute-start.12 = (bf16[64,832]{1,0:T(8,128)(2,1)S(1)}, bf16[64,832]{1,0:T(8,128)(2,1)S(1)}, u32[]{:S(2)}, u32[]{:S(2)}) collective-permute-start(bf16[64,832]{1,0:T(8,128)(2,1)S(1)} %between.3.refs_0_.refs_4_), channel_id=1, source_target_pairs={{0,1},{1,2},{2,3},{3,0},{4,5},{5,6},{6,7},{7,4},{8,9},{9,10},{10,1... | collective-permute-start | bytes 319496 | tf_op jit(solution)/shard_map/ppermute | solution.py:307
  89.7 7.6 %collective-permute-start.15 = (bf16[64,704]{1,0:T(8,128)(2,1)S(1)}, bf16[64,704]{1,0:T(8,128)(2,1)S(1)}, u32[]{:S(2)}, u32[]{:S(2)}) collective-permute-start(bf16[64,704]{1,0:T(8,128)(2,1)S(1)} %get-tuple-element.58), channel_id=1, source_target_pairs={{0,1},{1,2},{2,3},{3,0},{4,5},{5,6},{6,7},{7,4},{8,9},{9,10},{10,1... | collective-permute-start | bytes 270344 | tf_op jit(solution)/shard_map/ppermute | solution.py:307
  89.7 9.8 %collective-permute-start.16 = (bf16[64,704]{1,0:T(8,128)(2,1)S(1)}, bf16[64,704]{1,0:T(8,128)(2,1)S(1)}, u32[]{:S(2)}, u32[]{:S(2)}) collective-permute-start(bf16[64,704]{1,0:T(8,128)(2,1)S(1)} %get-tuple-element.59), channel_id=1, source_target_pairs={{0,2},{1,3},{2,0},{3,1},{4,6},{5,7},{6,4},{7,5},{8,10},{9,11},{10,... | collective-permute-start | bytes 270344 | tf_op jit(solution)/shard_map/ppermute | solution.py:307
  91.3 8.3 %collective-permute-start.17 = (bf16[64,704]{1,0:T(8,128)(2,1)S(1)}, bf16[64,704]{1,0:T(8,128)(2,1)S(1)}, u32[]{:S(2)}, u32[]{:S(2)}) collective-permute-start(bf16[64,704]{1,0:T(8,128)(2,1)S(1)} %get-tuple-element.60), channel_id=1, source_target_pairs={{0,3},{1,0},{2,1},{3,2},{4,7},{5,4},{6,5},{7,6},{8,11},{9,8},{10,9... | collective-permute-start | bytes 270344 | tf_op jit(solution)/shard_map/ppermute | solution.py:307
  103.7 9.8 %collective-permute-start.19 = (bf16[64,832]{1,0:T(8,128)(2,1)S(1)}, bf16[64,832]{1,0:T(8,128)(2,1)S(1)}, u32[]{:S(2)}, u32[]{:S(2)}) collective-permute-start(bf16[64,832]{1,0:T(8,128)(2,1)S(1)} %between.4.refs_0_.refs_4_), channel_id=1, source_target_pairs={{0,2},{1,3},{2,0},{3,1},{4,6},{5,7},{6,4},{7,5},{8,10},{9,11},{10,... | collective-permute-start | bytes 319496 | tf_op jit(solution)/shard_map/ppermute | solution.py:307
  103.9 9.6 %collective-permute-start.18 = (bf16[64,832]{1,0:T(8,128)(2,1)S(1)}, bf16[64,832]{1,0:T(8,128)(2,1)S(1)}, u32[]{:S(2)}, u32[]{:S(2)}) collective-permute-start(bf16[64,832]{1,0:T(8,128)(2,1)S(1)} %between.4.refs_0_.refs_4_), channel_id=1, source_target_pairs={{0,1},{1,2},{2,3},{3,0},{4,5},{5,6},{6,7},{7,4},{8,9},{9,10},{10,1... | collective-permute-start | bytes 319496 | tf_op jit(solution)/shard_map/ppermute | solution.py:307
  119.2 7.6 %collective-permute-start.21 = (bf16[64,704]{1,0:T(8,128)(2,1)S(1)}, bf16[64,704]{1,0:T(8,128)(2,1)S(1)}, u32[]{:S(2)}, u32[]{:S(2)}) collective-permute-start(bf16[64,704]{1,0:T(8,128)(2,1)S(1)} %get-tuple-element.64), channel_id=1, source_target_pairs={{0,1},{1,2},{2,3},{3,0},{4,5},{5,6},{6,7},{7,4},{8,9},{9,10},{10,1... | collective-permute-start | bytes 270344 | tf_op jit(solution)/shard_map/ppermute | solution.py:307
  119.2 10.0 %collective-permute-start.22 = (bf16[64,704]{1,0:T(8,128)(2,1)S(1)}, bf16[64,704]{1,0:T(8,128)(2,1)S(1)}, u32[]{:S(2)}, u32[]{:S(2)}) collective-permute-start(bf16[64,704]{1,0:T(8,128)(2,1)S(1)} %get-tuple-element.65), channel_id=1, source_target_pairs={{0,2},{1,3},{2,0},{3,1},{4,6},{5,7},{6,4},{7,5},{8,10},{9,11},{10,... | collective-permute-start | bytes 270344 | tf_op jit(solution)/shard_map/ppermute | solution.py:307
  121.1 8.2 %collective-permute-start.23 = (bf16[64,704]{1,0:T(8,128)(2,1)S(1)}, bf16[64,704]{1,0:T(8,128)(2,1)S(1)}, u32[]{:S(2)}, u32[]{:S(2)}) collective-permute-start(bf16[64,704]{1,0:T(8,128)(2,1)S(1)} %get-tuple-element.66), channel_id=1, source_target_pairs={{0,3},{1,0},{2,1},{3,2},{4,7},{5,4},{6,5},{7,6},{8,11},{9,8},{10,9... | collective-permute-start | bytes 270344 | tf_op jit(solution)/shard_map/ppermute | solution.py:307
  133.6 9.5 %collective-permute-start.25 = (bf16[64,832]{1,0:T(8,128)(2,1)S(1)}, bf16[64,832]{1,0:T(8,128)(2,1)S(1)}, u32[]{:S(2)}, u32[]{:S(2)}) collective-permute-start(bf16[64,832]{1,0:T(8,128)(2,1)S(1)} %between.5.refs_0_.refs_4_), channel_id=1, source_target_pairs={{0,2},{1,3},{2,0},{3,1},{4,6},{5,7},{6,4},{7,5},{8,10},{9,11},{10,... | collective-permute-start | bytes 319496 | tf_op jit(solution)/shard_map/ppermute | solution.py:307
  133.6 9.5 %collective-permute-start.24 = (bf16[64,832]{1,0:T(8,128)(2,1)S(1)}, bf16[64,832]{1,0:T(8,128)(2,1)S(1)}, u32[]{:S(2)}, u32[]{:S(2)}) collective-permute-start(bf16[64,832]{1,0:T(8,128)(2,1)S(1)} %between.5.refs_0_.refs_4_), channel_id=1, source_target_pairs={{0,1},{1,2},{2,3},{3,0},{4,5},{5,6},{6,7},{7,4},{8,9},{9,10},{10,1... | collective-permute-start | bytes 319496 | tf_op jit(solution)/shard_map/ppermute | solution.py:307
  149.0 9.8 %collective-permute-start.28 = (bf16[64,704]{1,0:T(8,128)(2,1)S(1)}, bf16[64,704]{1,0:T(8,128)(2,1)S(1)}, u32[]{:S(2)}, u32[]{:S(2)}) collective-permute-start(bf16[64,704]{1,0:T(8,128)(2,1)S(1)} %get-tuple-element.71), channel_id=1, source_target_pairs={{0,2},{1,3},{2,0},{3,1},{4,6},{5,7},{6,4},{7,5},{8,10},{9,11},{10,... | collective-permute-start | bytes 270344 | tf_op jit(solution)/shard_map/ppermute | solution.py:307
  150.7 8.1 %collective-permute-start.29 = (bf16[64,704]{1,0:T(8,128)(2,1)S(1)}, bf16[64,704]{1,0:T(8,128)(2,1)S(1)}, u32[]{:S(2)}, u32[]{:S(2)}) collective-permute-start(bf16[64,704]{1,0:T(8,128)(2,1)S(1)} %get-tuple-element.72), channel_id=1, source_target_pairs={{0,3},{1,0},{2,1},{3,2},{4,7},{5,4},{6,5},{7,6},{8,11},{9,8},{10,9... | collective-permute-start | bytes 270344 | tf_op jit(solution)/shard_map/ppermute | solution.py:307
  (39 other events, 403.1 us)

commit v2 on v1

v2 whole, which is shorter than its diff:
```python
import functools

import jax
import jax.numpy as jnp
from jax import lax
from jax.experimental import pallas as pl
from jax.experimental.pallas import tpu as pltpu
from jax.sharding import PartitionSpec as P

STEPS = 4

epsilon = 1e-06
rope_base = 1000000.0
blocked = -1e30
f32 = jnp.float32
bf16 = jnp.bfloat16

NT = (((1,), (1,)), ((), ()))


def kernel_params(mib):
    return pltpu.CompilerParams(vmem_limit_bytes=mib * 1024 * 1024)


def copy_all(pairs, sems):
    copies = [
        pltpu.make_async_copy(source, target, sems.at[index])
        for index, (source, target) in enumerate(pairs)
    ]
    for copy in copies:
        copy.start()
    return copies


def route_kernel(
    group_ref, domain_hbm, slot_hbm, length_hbm, hidden_hbm, target_ref, place_ref, *refs
):
    groups = len(refs) - 8
    outgoing = refs[:groups]
    count, place, facts, domain_ref, slot_ref, length_ref, hidden_ref, sems = refs[groups:]
    rows, width = hidden_ref.shape
    capacity = outgoing[0].shape[0]
    per_group = slot_ref.shape[0] // groups
    here = group_ref[0]
    *tables, hidden_copy = copy_all(
        [
            (domain_hbm, domain_ref),
            (slot_hbm, slot_ref),
            (length_hbm, length_ref),
            (hidden_hbm, hidden_ref),
        ],
        sems,
    )
    for group in range(groups):
        count[group] = 0
    places = lax.broadcasted_iota(jnp.int32, (1, groups * capacity), 1)
    columns = lax.broadcasted_iota(jnp.int32, (1, facts.shape[1]), 1)
    for copy in tables:
        copy.wait()

    def put(row, carry):
        slot = slot_ref[domain_ref[here * rows + row]]
        dest = lax.div(slot, per_group)
        position = jnp.minimum(count[dest], capacity - 1)
        count[dest] = position + 1
        target = lax.rem(dest - here + groups, groups) * capacity + position
        target_ref[row] = target
        place[pl.ds(row, 1), :] = jnp.where(places == target, 1.0, 0.0)
        length = length_ref[row].astype(f32)
        local = (slot - dest * per_group).astype(f32)
        facts[pl.ds(row, 1), :] = jnp.where(
            columns == 0, length, jnp.where(columns == 1, local, 0.0)
        )
        return carry

    lax.fori_loop(0, rows, put, 0)
    chosen = place[...].astype(bf16)
    place_ref[...] = chosen
    across = (((0,), (0,)), ((), ()))
    known = lax.dot_general(
        chosen, facts[...].astype(bf16), across, preferred_element_type=f32
    ).astype(bf16)
    hidden_copy.wait()
    state = lax.dot_general(
        chosen, hidden_ref[...], across, preferred_element_type=f32
    ).astype(bf16)
    for s in range(groups):
        block = slice(s * capacity, (s + 1) * capacity)
        outgoing[s][:, :width] = state[block]
        outgoing[s][:, width:] = known[block]


def pack_kernel(target_ref, key_hbm, value_hbm, *refs):
    groups = len(refs) - 4
    outgoing = refs[:groups]
    packed, key_ref, value_ref, sems = refs[groups:]
    rows, kv_local = key_ref.shape[:2]
    capacity = packed.shape[2]
    copies = copy_all([(key_hbm, key_ref), (value_hbm, value_ref)], sems)
    if groups * capacity > rows:
        packed[...] = jnp.zeros_like(packed)
    for copy in copies:
        copy.wait()

    def put(row, carry):
        target = target_ref[row]
        block = lax.div(target, capacity)
        position = target - block * capacity
        for g in range(kv_local):
            packed[block, g, position] = key_ref[row, g]
            packed[block, kv_local + g, position] = value_ref[row, g]
        return carry

    lax.fori_loop(0, rows, put, 0)
    for s in range(groups):
        outgoing[s][...] = packed[s]


def load_kernel(rank, *refs):
    query, key, value, query_up, key_up, value_up, output, output_down, output_up, down = refs[:10]
    inputs, *same, down_out = refs[10:18]
    sems = refs[18]
    total, kinds = down.shape[0], down.shape[1] // rank
    pairs = []
    column = 0
    for weight in (query, key, value):
        width = weight.shape[1]
        pairs.append((weight, inputs.at[:, column : column + width]))
        column += width
    pairs += zip((query_up, key_up, value_up, output, output_down, output_up), same)
    for kind in range(kinds):
        for d in range(total):
            pairs.append(
                (
                    down.at[d, kind * rank : (kind + 1) * rank, :],
                    down_out.at[kind, d * rank : (d + 1) * rank, :],
                )
            )
    for copy in copy_all(pairs, sems):
        copy.wait()


def own_slots(slot, total, rank):
    lane = lax.broadcasted_iota(jnp.int32, (1, 2 * rank), 1)
    second = (lane >= rank).astype(f32)
    return [slot == 2.0 * j + second for j in range(total // 2)]


def spread_over_slots(factor, own):
    twice = jnp.concatenate([factor, factor], axis=1)
    return jnp.concatenate([jnp.where(mask, twice, 0.0).astype(bf16) for mask in own], axis=1)


def pick_slot(product, own):
    wide = own[0].shape[1]
    picked = jnp.where(own[0], product[:, :wide], 0.0)
    for j in range(1, len(own)):
        picked = picked + jnp.where(own[j], product[:, j * wide : (j + 1) * wide], 0.0)
    return picked[:, : wide // 2] + picked[:, wide // 2 :]


def partial_low(state, gain, own, down_ref):
    scaled = (state * gain).astype(bf16)
    picked = []
    for kind in range(down_ref.shape[0]):
        product = lax.dot_general(scaled, down_ref[kind], NT, preferred_element_type=f32)
        picked.append(pick_slot(product, own).astype(bf16))
    return jnp.concatenate(picked, axis=1)


def enter_kernel(total, rank, groups, *refs):
    blocks = refs[:groups]
    gain_ref, down_ref, send_ref, facts_ref = refs[groups:]
    width = down_ref.shape[2]
    everything = jnp.concatenate([block[...] for block in blocks], axis=0)
    facts = everything[:, width:].astype(f32)
    own = own_slots(facts[:, 1:2], total, rank)
    facts_ref[...] = facts
    send_ref[:, :width] = everything[:, :width]
    send_ref[:, width:] = partial_low(
        everything[:, :width].astype(f32), gain_ref[...], own, down_ref
    )


def new_state(own, received, state, up_ref):
    width = state.shape[1]
    low_out = received[0][:, width:].astype(f32)
    projected = received[0][:, :width].astype(f32)
    for part in received[1:]:
        low_out = low_out + part[:, width:].astype(f32)
        projected = projected + part[:, :width].astype(f32)
    spread = spread_over_slots(low_out, own)
    delta = jnp.dot(spread, up_ref[...], preferred_element_type=f32).astype(bf16)
    return (state.astype(f32) + projected + delta.astype(f32)).astype(bf16)


def between_kernel(total, rank, parts, *refs):
    received = refs[:parts]
    state_ref, facts_ref, up_ref, gain_ref, down_ref, send_ref = refs[parts:]
    width = down_ref.shape[2]
    own = own_slots(facts_ref[:, 1:2], total, rank)
    state = new_state(own, received, state_ref[:, :width], up_ref)
    send_ref[:, :width] = state
    send_ref[:, width:] = partial_low(state.astype(f32), gain_ref[...], own, down_ref)


def leave_kernel(total, rank, parts, *refs):
    received = refs[:parts]
    state_ref, facts_ref, up_ref = refs[parts : parts + 3]
    outgoing = refs[parts + 3 :]
    width = up_ref.shape[1]
    capacity = outgoing[0].shape[0]
    own = own_slots(facts_ref[:, 1:2], total, rank)
    state = new_state(own, received, state_ref[:, :width], up_ref)
    for s in range(len(outgoing)):
        outgoing[s][...] = state[s * capacity : (s + 1) * capacity]


def restore_kernel(place_ref, *refs):
    blocks, out_ref = refs[:-1], refs[-1]
    back = jnp.concatenate([block[...] for block in blocks], axis=0)
    out_ref[...] = jnp.dot(place_ref[...], back, preferred_element_type=f32).astype(bf16)


def norm_and_rotate(vector, gain, cosine, sine):
    head_dim = vector.shape[1]
    mean = jnp.mean(vector * vector, axis=1, keepdims=True)
    scaled = vector * lax.rsqrt(mean + epsilon) * gain
    return (scaled * cosine + pltpu.roll(scaled, head_dim // 2, 1) * sine).astype(bf16)


def project_slices(slices, masks, here, gain_ref, weight_ref):
    width = gain_ref.shape[2]
    products, squares, low = None, None, None
    for piece, mask in zip(slices, masks):
        source = jnp.bitwise_xor(here, mask)
        state = piece[:, :width].astype(f32)
        scaled = (state * gain_ref[source]).astype(bf16)
        features_there = pl.ds(pl.multiple_of(source * width, 64), width)
        product = jnp.dot(scaled, weight_ref[features_there, :], preferred_element_type=f32)
        square = jnp.sum(state * state, axis=1, keepdims=True)
        part = piece[:, width:].astype(f32)
        products = product if products is None else products + product
        squares = square if squares is None else squares + square
        low = part if low is None else low + part
    return products, squares, low


def early_kernel(masks, *refs):
    slices = refs[: len(masks)]
    index_ref, gain_ref, weight_ref, products_ref, squares_ref, low_ref = refs[len(masks) :]
    products, squares, low = project_slices(slices, masks, index_ref[0], gain_ref, weight_ref)
    products_ref[...] = products
    squares_ref[...] = jnp.broadcast_to(squares, squares_ref.shape)
    low_ref[...] = low


def step_kernel(total, rank, step, parts, masks, groups, *refs):
    refs = list(refs)

    def take(count):
        taken = refs[:count]
        del refs[:count]
        return taken

    slices = take(len(masks))
    (
        index_ref,
        products_ref,
        squares_ref,
        low_ref,
        facts_ref,
        gain_ref,
        weight_ref,
        query_up,
        key_up,
        value_up,
        query_gain,
        key_gain,
        cosine_ref,
        sine_ref,
        bias_ref,
    ) = take(15)
    cache = take(groups)
    earlier = take(2 * step)
    output_weight, output_down = take(2)
    outgoing = take(parts)
    key_fresh, value_fresh, attended, terms = refs
    features = weight_ref.shape[0]
    width = features // parts
    rows = products_ref.shape[0]
    head_dim = cache[0].shape[2]
    kv_local = cache[0].shape[0] // 2
    capacity = rows // groups
    query_width = query_up.shape[1]
    key_width = key_up.shape[1]
    heads = query_width // head_dim
    per_kv = heads // kv_local
    here = index_ref[0]

    own = own_slots(facts_ref[:, 1:2], total, rank)
    products, squares, low = project_slices(slices, masks, here, gain_ref, weight_ref)
    inverse = lax.rsqrt((squares_ref[:, :1] + squares) / features + epsilon)
    low = (low_ref[...] + low) * inverse

    def project(columns, up_ref, index):
        spread = spread_over_slots(low[:, index * rank : (index + 1) * rank], own)
        delta = jnp.dot(spread, up_ref[...], preferred_element_type=f32).astype(bf16)
        whole = (products_ref[:, columns] + products[:, columns]) * inverse
        return whole + delta.astype(f32)

    cosine = cosine_ref[step]
    sine = sine_ref[step]
    key = project(slice(query_width, query_width + key_width), key_up, 1)
    value = project(slice(query_width + key_width, None), value_up, 2).astype(bf16)
    for g in range(kv_local):
        columns = slice(g * head_dim, (g + 1) * head_dim)
        key_fresh[g] = norm_and_rotate(key[:, columns], key_gain[...], cosine, sine)
        value_fresh[g] = value[:, columns]
    query = project(slice(0, query_width), query_up, 0)
    query_heads = [
        norm_and_rotate(query[:, h * head_dim : (h + 1) * head_dim], query_gain[...], cosine, sine)
        for h in range(heads)
    ]

    scale = head_dim ** (-0.5)
    fresh_count = (step + 1) * capacity
    lanes = 128 * (-(-fresh_count // 128))
    filler = jnp.zeros((lanes - fresh_count, head_dim), bf16)
    key_place = lax.broadcasted_iota(jnp.int32, (per_kv * capacity, lanes), 1)
    own_row = lax.broadcasted_iota(jnp.int32, (per_kv * capacity, lanes), 0) % capacity
    same_row = (key_place % capacity == own_row) & (key_place < fresh_count)
    cached_count = bias_ref.shape[1]
    for b in range(groups):
        block = slice(b * capacity, (b + 1) * capacity)
        bias = jnp.concatenate([bias_ref[block, :]] * per_kv, axis=0)
        for g in range(kv_local):
            queries = jnp.concatenate(
                [query_heads[g * per_kv + h][block] for h in range(per_kv)], axis=0
            )
            fresh_keys = jnp.concatenate(
                [earlier[2 * t][g, block, :] for t in range(step)]
                + [key_fresh[g, block, :], filler],
                axis=0,
            )
            fresh_values = jnp.concatenate(
                [earlier[2 * t + 1][g, block, :] for t in range(step)]
                + [value_fresh[g, block, :], filler],
                axis=0,
            )
            cached = (
                lax.dot_general(queries, cache[b][g], NT, preferred_element_type=f32) * scale + bias
            )
            fresh = lax.dot_general(queries, fresh_keys, NT, preferred_element_type=f32) * scale
            fresh = jnp.where(same_row, fresh, blocked)
            scores = jnp.concatenate([cached, fresh], axis=1)
            largest = jnp.max(scores, axis=1, keepdims=True)
            weights = jnp.exp(scores - largest).astype(bf16)
            values = jnp.concatenate([cache[b][kv_local + g], fresh_values], axis=0)
            summing = jnp.concatenate([values, jnp.ones_like(values)], axis=1)
            mixed = jnp.dot(weights, summing, preferred_element_type=f32)
            mixed = (mixed[:, :head_dim] / mixed[:, head_dim:]).astype(bf16)
            for h in range(per_kv):
                head = g * per_kv + h
                attended[block, head * head_dim : (head + 1) * head_dim] = mixed[
                    h * capacity : (h + 1) * capacity
                ]

    attended_rows = attended[...]
    product = lax.dot_general(attended_rows, output_down[...], NT, preferred_element_type=f32)
    low_out = pick_slot(product, own).astype(bf16)
    for n in range(parts):
        term = jnp.dot(
            attended_rows,
            output_weight[:, n * width : (n + 1) * width],
            preferred_element_type=f32,
        )
        terms[jnp.bitwise_xor(here, n)] = term.astype(bf16)
    for mask in range(parts):
        outgoing[mask][:, :width] = terms[mask]
        outgoing[mask][:, width:] = low_out


def shift(block, axis, by):
    size = lax.axis_size(axis)
    return lax.ppermute(block, axis, [(i, (i + by) % size) for i in range(size)])


def swap(block, axis, mask):
    return lax.ppermute(block, axis, [(i, i ^ mask) for i in range(lax.axis_size(axis))])


def shards(
    hidden,
    input_norm_gain,
    query_projection_weight,
    key_projection_weight,
    value_projection_weight,
    query_norm_gain,
    key_norm_gain,
    output_projection_weight,
    stacked_down_factors,
    query_up_factor,
    key_up_factor,
    value_up_factor,
    output_down_factor,
    output_up_factor,
    cached_key_rows,
    cached_value_rows,
    cached_length_rows,
    domain_of_row,
    slot_of_domain,
):
    groups = lax.axis_size("wide")
    parts = lax.axis_size("narrow")
    wide_index = lax.axis_index("wide")
    narrow_index = lax.axis_index("narrow")
    row_group, width = hidden.shape
    capacity = row_group // 4
    rows = groups * capacity
    total = stacked_down_factors.shape[0]
    low_width = stacked_down_factors.shape[1]
    rank = output_up_factor.shape[1]
    _, kv_local, context, head_dim = cached_key_rows.shape
    features = input_norm_gain.shape[0]
    query_width = query_projection_weight.shape[1]

    smem = pl.BlockSpec(memory_space=pltpu.SMEM)
    vmem = pl.BlockSpec(memory_space=pltpu.VMEM)
    hbm = pl.BlockSpec(memory_space=pltpu.HBM)
    outgoing_shape = jax.ShapeDtypeStruct((capacity, width + 128), bf16)
    target, place, *outgoing = pl.pallas_call(
        route_kernel,
        out_shape=[
            jax.ShapeDtypeStruct((row_group,), jnp.int32),
            jax.ShapeDtypeStruct((row_group, rows), bf16),
        ]
        + [outgoing_shape] * groups,
        in_specs=[smem] + [hbm] * 4,
        out_specs=[smem] + [vmem] * (groups + 1),
        scratch_shapes=[
            pltpu.SMEM((groups,), jnp.int32),
            pltpu.VMEM((row_group, rows), f32),
            pltpu.VMEM((row_group, 128), f32),
            pltpu.SMEM(domain_of_row.shape, jnp.int32),
            pltpu.SMEM(slot_of_domain.shape, jnp.int32),
            pltpu.SMEM(cached_length_rows.shape, jnp.int32),
            pltpu.VMEM(hidden.shape, bf16),
            pltpu.SemaphoreType.DMA((4,)),
        ],
        compiler_params=kernel_params(8),
        name="route_rows",
    )(wide_index.reshape(1), domain_of_row, slot_of_domain, cached_length_rows, hidden)
    arrived = [outgoing[0]] + [shift(outgoing[s], "wide", s) for s in range(1, groups)]
    packed_shape = (2 * kv_local, capacity, context, head_dim)
    packed = pl.pallas_call(
        pack_kernel,
        out_shape=[jax.ShapeDtypeStruct(packed_shape, bf16)] * groups,
        in_specs=[smem, hbm, hbm],
        out_specs=[vmem] * groups,
        scratch_shapes=[
            pltpu.VMEM((groups,) + packed_shape, bf16),
            pltpu.VMEM(cached_key_rows.shape, bf16),
            pltpu.VMEM(cached_value_rows.shape, bf16),
            pltpu.SemaphoreType.DMA((2,)),
        ],
        compiler_params=kernel_params(16),
        name="pack_cache",
    )(target, cached_key_rows, cached_value_rows)
    cache = [packed[0]] + [shift(packed[s], "wide", s) for s in range(1, groups)]
    cache = [block.reshape(2 * kv_local, capacity * context, head_dim) for block in cache]

    key_width = key_projection_weight.shape[1]
    stored = [
        (features, query_width + 2 * key_width),
        (total * rank, query_width),
        (total * rank, key_width),
        (total * rank, key_width),
        output_projection_weight.shape,
        (total * rank, query_width),
        (total * rank, width),
        (low_width // rank, total * rank, width),
    ]
    weights = pl.pallas_call(
        functools.partial(load_kernel, rank),
        out_shape=[jax.ShapeDtypeStruct(shape, bf16) for shape in stored],
        in_specs=[hbm] * 10,
        out_specs=[vmem] * 8,
        scratch_shapes=[pltpu.SemaphoreType.DMA((9 + total * low_width // rank,))],
        compiler_params=kernel_params(24),
        cost_estimate=pl.CostEstimate(flops=0, bytes_accessed=40000000, transcendentals=0),
        name="load_weights",
    )(
        query_projection_weight,
        key_projection_weight,
        value_projection_weight,
        query_up_factor.reshape(total * rank, query_width),
        key_up_factor.reshape(total * rank, key_width),
        value_up_factor.reshape(total * rank, key_width),
        output_projection_weight,
        output_down_factor.reshape(total * rank, query_width),
        output_up_factor.reshape(total * rank, width),
        stacked_down_factors,
    )
    input_weight, query_up, key_up, value_up, output_weight, output_down, output_up, down = weights

    gain_rows = input_norm_gain.reshape(parts, 1, width)
    gain_slice = lax.dynamic_index_in_dim(gain_rows, narrow_index, 0, keepdims=False)
    sent_state = jax.ShapeDtypeStruct((rows, width + low_width), bf16)
    send, facts_here = pl.pallas_call(
        functools.partial(enter_kernel, total, rank, groups),
        out_shape=[sent_state, jax.ShapeDtypeStruct((rows, 128), f32)],
        in_specs=[vmem] * (groups + 2),
        out_specs=[vmem] * 2,
        compiler_params=kernel_params(8),
        name="enter",
    )(*arrived, gain_slice, down)
    lengths = facts_here[:, 0]
    frequency = rope_base ** (-(jnp.arange(head_dim // 2, dtype=f32) * 2.0) / head_dim)
    positions = lengths[None, :] + jnp.arange(STEPS, dtype=f32)[:, None]
    angles = positions[:, :, None] * frequency
    cosine = jnp.cos(angles)
    sine = jnp.sin(angles)
    cosine = jnp.concatenate([cosine, cosine], axis=-1)
    sine = jnp.concatenate([-sine, sine], axis=-1)
    key_index = jnp.arange(capacity * context)[None, :]
    visible = (key_index // context == (jnp.arange(rows) % capacity)[:, None]) & (
        (key_index % context).astype(f32) < lengths[:, None]
    )
    bias = jnp.where(visible, 0.0, blocked).astype(f32)

    query_gain = query_norm_gain.reshape(1, head_dim)
    key_gain = key_norm_gain.reshape(1, head_dim)
    index_here = narrow_index.reshape(1)
    sent_terms = jax.ShapeDtypeStruct((rows, width + rank), bf16)
    fresh = jax.ShapeDtypeStruct((kv_local, rows, head_dim), bf16)
    far = [mask for mask in range(parts - 1, 1, -1) if mask % 2 == 1]
    early = [0, 1] + far
    late = [mask ^ 1 for mask in far]

    earlier = []
    for step in range(STEPS):
        from_far = [swap(send, "narrow", mask) for mask in far]
        slices = [send, swap(send, "narrow", 1)] + from_far
        passed_on = [swap(piece, "narrow", 1) for piece in from_far]
        sums = pl.pallas_call(
            functools.partial(early_kernel, early),
            out_shape=[
                jax.ShapeDtypeStruct((rows, input_weight.shape[1]), f32),
                jax.ShapeDtypeStruct((rows, 128), f32),
                jax.ShapeDtypeStruct((rows, low_width), f32),
            ],
            in_specs=[vmem] * len(early) + [smem] + [vmem] * 2,
            out_specs=[vmem] * 3,
            compiler_params=kernel_params(16),
            cost_estimate=pl.CostEstimate(
                flops=2 * rows * features * input_weight.shape[1],
                bytes_accessed=10000000,
                transcendentals=0,
            ),
            name="project_early",
        )(*slices, index_here, gain_rows, input_weight)
        *terms, key_fresh, value_fresh = pl.pallas_call(
            functools.partial(step_kernel, total, rank, step, parts, late, groups),
            out_shape=[sent_terms] * parts + [fresh] * 2,
            in_specs=[vmem] * len(late) + [smem] + [vmem] * (16 + groups + 2 * step),
            out_specs=[vmem] * (parts + 2),
            scratch_shapes=[
                pltpu.VMEM((rows, query_width), bf16),
                pltpu.VMEM((parts, rows, width), bf16),
            ],
            compiler_params=kernel_params(24),
            name="attend_step",
        )(
            *passed_on,
            index_here,
            *sums,
            facts_here,
            gain_rows,
            input_weight,
            query_up,
            key_up,
            value_up,
            query_gain,
            key_gain,
            cosine,
            sine,
            bias,
            *cache,
            *earlier,
            output_weight,
            output_down,
        )
        earlier += [key_fresh, value_fresh]
        received = [terms[0]] + [swap(terms[mask], "narrow", mask) for mask in range(parts - 1, 0, -1)]
        if step < STEPS - 1:
            send = pl.pallas_call(
                functools.partial(between_kernel, total, rank, parts),
                out_shape=sent_state,
                in_specs=[vmem] * (parts + 5),
                out_specs=vmem,
                compiler_params=kernel_params(8),
                name="between",
            )(*received, send, facts_here, output_up, gain_slice, down)
        else:
            leaving = pl.pallas_call(
                functools.partial(leave_kernel, total, rank, parts),
                out_shape=[jax.ShapeDtypeStruct((capacity, width), bf16)] * groups,
                in_specs=[vmem] * (parts + 3),
                out_specs=[vmem] * groups,
                compiler_params=kernel_params(8),
                name="leave",
            )(*received, send, facts_here, output_up)

    back = [leaving[0]] + [shift(leaving[s], "wide", -s) for s in range(1, groups)]
    return pl.pallas_call(
        restore_kernel,
        out_shape=jax.ShapeDtypeStruct((row_group, width), bf16),
        in_specs=[vmem] * (groups + 1),
        out_specs=vmem,
        compiler_params=kernel_params(8),
        name="restore",
    )(place, *back)


def solution(mesh):
    placed = (
        P(("parts", "wide"), "narrow"),
        P(),
        P(None, "narrow"),
        P(None, "narrow"),
        P(None, "narrow"),
        P(),
        P(),
        P("narrow", None),
        P(("parts", "wide"), None, "narrow"),
        P(("parts", "wide"), None, "narrow"),
        P(("parts", "wide"), None, "narrow"),
        P(("parts", "wide"), None, "narrow"),
        P(("parts", "wide"), None, "narrow"),
        P(("parts", "wide"), None, "narrow"),
        P(("parts", "wide"), "narrow", None, None),
        P(("parts", "wide"), "narrow", None, None),
        P(("parts", "wide")),
        P("parts"),
        P("parts"),
    )
    return jax.shard_map(
        shards,
        mesh=mesh,
        in_specs=placed,
        out_specs=P(("parts", "wide"), "narrow"),
        check_vma=False,
    )
```

time: 165 us -> 155 us (0.939)
  starting transfers between devices: 42.6 us -> 36.4 us
  waiting for transfers between devices: 58.6 us -> 53.8 us
  Pallas kernels: 32.8 us -> 36.9 us
  other arithmetic: 4.15 us -> 0.79 us
    ppermute x33 -> x9, waiting for transfers between devices: 58.6 us -> 3.37 us  [shift(): lax.ppermute(block, axis, [(i, (i + by) % size) for i in range(size)])]
    ppermute x0 -> x24, waiting for transfers between devices: none -> 50.4 us  [swap(): lax.ppermute(block, axis, [(i, i ^ mask) for i in range(lax.axis_size(axi...]
    ppermute x33 -> x9, starting transfers between devices: 42.6 us -> 6.92 us  [shift(): lax.ppermute(block, axis, [(i, (i + by) % size) for i in range(size)])]
    ppermute x0 -> x24, starting transfers between devices: none -> 29.5 us  [swap(): lax.ppermute(block, axis, [(i, i ^ mask) for i in range(lax.axis_size(axi...]
    pallas_call x9 -> x14, Pallas kernels: 27.3 us -> 32.1 us  [the longest x4 15.8 us: shards(): pl.pallas_call(functools.partial(step_kernel, total, rank, step, parts, l...]
    unnamed x63 -> x40, local copies, waits for them, and re-layouts: 23.3 us -> 25 us
  transfers between devices with their start and end apart: 33 -> 33, of which waited for: 18 -> 20; matrix products, arithmetic and copies ran while one was open for 7% -> 1% of each run, Pallas kernels for 2% -> 9%
where the time goes in v2:
time: 155 us; the launch traced here: 154 us
  waiting for transfers between devices  53.8 us (35%)
  Pallas kernels  36.9 us (24%)
  starting transfers between devices  36.4 us (23%)
  local copies, waits for them, and re-layouts  25.8 us (17%)
    ppermute x24, waiting for transfers between devices, swap(): lax.ppermute(block, axis, [(i, i ^ mask) for i in range(lax.axis_size(axi...  50.4 us
    ppermute x24, starting transfers between devices, swap(): lax.ppermute(block, axis, [(i, i ^ mask) for i in range(lax.axis_size(axi...  29.5 us
    unnamed x40, local copies, waits for them, and re-layouts  25 us
    pallas_call x4, Pallas kernels, shards(): pl.pallas_call(functools.partial(step_kernel, total, rank, step, parts, l...  15.8 us
    pallas_call x1, Pallas kernels, shards(): pl.pallas_call(functools.partial(load_kernel, rank), out_shape=[jax.Shape...  7.61 us
    ppermute x9, starting transfers between devices, shift(): lax.ppermute(block, axis, [(i, (i + by) % size) for i in range(size)])  6.92 us
    pallas_call x4, Pallas kernels, shards(): pl.pallas_call(functools.partial(early_kernel, early), out_shape=[jax.Sha...  4.63 us
    ppermute x9, waiting for transfers between devices, shift(): lax.ppermute(block, axis, [(i, (i + by) % size) for i in range(size)])  3.37 us
  transfers between devices with their start and end apart: 33, of which 20 were waited for; matrix products, arithmetic and copies ran while one was open for 1% of the time, Pallas kernels for 9%

profile of v2, /device:TPU:0, one launch (start us, length us, event | category | flops | bytes accessed | tf_op | source)
XLA Modules:
  0.0 154.0 jit_solution(8728816442288683952)
XLA Ops:
  2.9 2.5 %route_rows.1 = (s32[64]{0:T(128)S(1)}, bf16[64,64]{1,0:T(8,128)(2,1)S(1)}, bf16[16,768]{1,0:T(8,128)(2,1)S(1)}, bf16[16,768]{1,0:T(8,128)(2,1)S(1)}, bf16[16,76...) custom-call(s32[1]{0:T(128)} %bitcast.group_ref, s32[256]{0:T(256)S(1)} %copy-done.17, s32[32]{0:T(128)S(1)} %copy-done.18, ...), custom_call_target="tpu_custom_call" | custom-call | tf_op jit(solution)/shard_map/route_rows/pallas_call | solution.py:432
  5.9 2.6 %collective-permute-start.1 = (bf16[16,768]{1,0:T(8,128)(2,1)S(1)}, bf16[16,768]{1,0:T(8,128)(2,1)S(1)}, u32[]{:S(2)}, u32[]{:S(2)}) collective-permute-start(bf16[16,768]{1,0:T(8,128)(2,1)S(1)} %get-tuple-element.66), channel_id=1, source_target_pairs={{0,8},{4,12},{8,0},{12,4},{1,9},{5,13},{9,1},{13,5},{2,10},{6,14},... | collective-permute-start | bytes 73736 | tf_op jit(solution)/shard_map/ppermute | solution.py:386
  14.9 2.5 %copy-done.2 = bf16[2560,1024]{1,0:T(8,128)(2,1)S(1)} copy-done((bf16[2560,1024]{1,0:T(8,128)(2,1)S(1)}, bf16[2560,1024]{1,0:T(8,128)(2,1)}, u32[]{:S(2)}) %copy-start.2) | copy-done | bytes 5242904
  17.4 2.5 %copy-done.3 = bf16[1024,2560]{1,0:T(8,128)(2,1)S(1)} copy-done((bf16[1024,2560]{1,0:T(8,128)(2,1)S(1)}, bf16[1024,2560]{1,0:T(8,128)(2,1)}, u32[]{:S(2)}) %copy-start.3) | copy-done | bytes 5242904
  29.5 7.6 %load_weights.1 = (bf16[2560,1536]{1,0:T(8,128)(2,1)}, bf16[512,1024]{1,0:T(8,128)(2,1)S(1)}, bf16[512,256]{1,0:T(8,128)(2,1)S(1)}, bf16[512,256]{1,0:T(8,128)(2...) custom-call(bf16[2560,1024]{1,0:T(8,128)(2,1)S(1)} %copy-done.2, ...), custom_call_target="tpu_custom_call" | custom-call | bytes 40000000 | tf_op jit(solution)/shard_map/load_weights/pallas_call | solution.py:484
  41.2 2.5 %collective-permute-start.3 = (bf16[64,832]{1,0:T(8,128)(2,1)S(1)}, bf16[64,832]{1,0:T(8,128)(2,1)S(1)}, u32[]{:S(2)}, u32[]{:S(2)}) collective-permute-start(bf16[64,832]{1,0:T(8,128)(2,1)S(1)} %get-tuple-element.69.refs_0_.refs_4_), channel_id=1, source_target_pairs={{0,3},{1,2},{2,1},{3,0},{4,7},{5,6},{6,5},{7,4},{8,11},{9,10},{10,... | collective-permute-start | bytes 319496 | tf_op jit(solution)/shard_map/ppermute | solution.py:390
  44.4 4.7 %collective-permute-done.3.refs_2_ = bf16[64,832]{1,0:T(8,128)(2,1)S(1)} collective-permute-done((bf16[64,832]{1,0:T(8,128)(2,1)S(1)}, bf16[64,832]{1,0:T(8,128)(2,1)S(1)}, u32[]{:S(2)}, u32[]{:S(2)}) %collective-permute-start.3) | collective-permute-done | bytes 106528 | tf_op jit(solution)/shard_map/ppermute | solution.py:390
  49.9 3.2 %copy-done = bf16[2560,1536]{1,0:T(8,128)(2,1)S(1)} copy-done((bf16[2560,1536]{1,0:T(8,128)(2,1)S(1)}, bf16[2560,1536]{1,0:T(8,128)(2,1)}, u32[]{:S(2)}) %copy-start) | copy-done | bytes 7864344
  56.4 3.8 %attend_step.4 = (bf16[64,704]{1,0:T(8,128)(2,1)S(1)}, bf16[64,704]{1,0:T(8,128)(2,1)S(1)}, bf16[64,704]{1,0:T(8,128)(2,1)S(1)}, bf16[64,704]{1,0:T(8,128)(2,1)S...) custom-call(bf16[64,832]{1,0:T(8,128)(2,1)S(1)} %collective-permute-done.4.refs_0_, ...), custom_call_target="tpu_custom_call" | custom-call | tf_op jit(solution)/shard_map/attend_step/pallas_call | solution.py:563
  60.2 2.7 %collective-permute-start.9 = (bf16[64,704]{1,0:T(8,128)(2,1)S(1)}, bf16[64,704]{1,0:T(8,128)(2,1)S(1)}, u32[]{:S(2)}, u32[]{:S(2)}) collective-permute-start(bf16[64,704]{1,0:T(8,128)(2,1)S(1)} %get-tuple-element.86), channel_id=1, source_target_pairs={{0,3},{1,2},{2,1},{3,0},{4,7},{5,6},{6,5},{7,4},{8,11},{9,10},{10,... | collective-permute-start | bytes 270344 | tf_op jit(solution)/shard_map/ppermute | solution.py:390
  64.6 2.8 %collective-permute-done.9.refs_1_ = bf16[64,704]{1,0:T(8,128)(2,1)S(1)} collective-permute-done((bf16[64,704]{1,0:T(8,128)(2,1)S(1)}, bf16[64,704]{1,0:T(8,128)(2,1)S(1)}, u32[]{:S(2)}, u32[]{:S(2)}) %collective-permute-start.9) | collective-permute-done | bytes 90144 | tf_op jit(solution)/shard_map/ppermute | solution.py:390
  67.4 3.4 %collective-permute-done.10.refs_2_ = bf16[64,704]{1,0:T(8,128)(2,1)S(1)} collective-permute-done((bf16[64,704]{1,0:T(8,128)(2,1)S(1)}, bf16[64,704]{1,0:T(8,128)(2,1)S(1)}, u32[]{:S(2)}, u32[]{:S(2)}) %collective-permute-start.10) | collective-permute-done | bytes 90144 | tf_op jit(solution)/shard_map/ppermute | solution.py:390
  74.1 5.5 %collective-permute-done.12.refs_2_ = bf16[64,832]{1,0:T(8,128)(2,1)S(1)} collective-permute-done((bf16[64,832]{1,0:T(8,128)(2,1)S(1)}, bf16[64,832]{1,0:T(8,128)(2,1)S(1)}, u32[]{:S(2)}, u32[]{:S(2)}) %collective-permute-start.12) | collective-permute-done | bytes 106528 | tf_op jit(solution)/shard_map/ppermute | solution.py:390
  81.5 2.9 %collective-permute-done.13.refs_0_ = bf16[64,832]{1,0:T(8,128)(2,1)S(1)} collective-permute-done((bf16[64,832]{1,0:T(8,128)(2,1)S(1)}, bf16[64,832]{1,0:T(8,128)(2,1)S(1)}, u32[]{:S(2)}, u32[]{:S(2)}) %collective-permute-start.13) | collective-permute-done | bytes 106528 | tf_op jit(solution)/shard_map/ppermute | solution.py:390
  84.4 3.8 %attend_step.5 = (bf16[64,704]{1,0:T(8,128)(2,1)S(1)}, bf16[64,704]{1,0:T(8,128)(2,1)S(1)}, bf16[64,704]{1,0:T(8,128)(2,1)S(1)}, bf16[64,704]{1,0:T(8,128)(2,1)S...) custom-call(bf16[64,832]{1,0:T(8,128)(2,1)S(1)} %collective-permute-done.13.refs_0_, ...), custom_call_target="tpu_custom_call" | custom-call | tf_op jit(solution)/shard_map/attend_step/pallas_call | solution.py:563
  89.7 2.9 %collective-permute-start.17 = (bf16[64,704]{1,0:T(8,128)(2,1)S(1)}, bf16[64,704]{1,0:T(8,128)(2,1)S(1)}, u32[]{:S(2)}, u32[]{:S(2)}) collective-permute-start(bf16[64,704]{1,0:T(8,128)(2,1)S(1)} %get-tuple-element.98), channel_id=1, source_target_pairs={{0,1},{1,0},{2,3},{3,2},{4,5},{5,4},{6,7},{7,6},{8,9},{9,8},{10,11... | collective-permute-start | bytes 270344 | tf_op jit(solution)/shard_map/ppermute | solution.py:390
  99.9 4.7 %collective-permute-done.18.refs_2_ = bf16[64,832]{1,0:T(8,128)(2,1)S(1)} collective-permute-done((bf16[64,832]{1,0:T(8,128)(2,1)S(1)}, bf16[64,832]{1,0:T(8,128)(2,1)S(1)}, u32[]{:S(2)}, u32[]{:S(2)}) %collective-permute-start.18) | collective-permute-done | bytes 106528 | tf_op jit(solution)/shard_map/ppermute | solution.py:390
  109.3 4.0 %attend_step.6 = (bf16[64,704]{1,0:T(8,128)(2,1)S(1)}, bf16[64,704]{1,0:T(8,128)(2,1)S(1)}, bf16[64,704]{1,0:T(8,128)(2,1)S(1)}, bf16[64,704]{1,0:T(8,128)(2,1)S...) custom-call(bf16[64,832]{1,0:T(8,128)(2,1)S(1)} %collective-permute-done.19.refs_0_, ...), custom_call_target="tpu_custom_call" | custom-call | tf_op jit(solution)/shard_map/attend_step/pallas_call | solution.py:563
  113.3 3.3 %collective-permute-start.21 = (bf16[64,704]{1,0:T(8,128)(2,1)S(1)}, bf16[64,704]{1,0:T(8,128)(2,1)S(1)}, u32[]{:S(2)}, u32[]{:S(2)}) collective-permute-start(bf16[64,704]{1,0:T(8,128)(2,1)S(1)} %get-tuple-element.105), channel_id=1, source_target_pairs={{0,3},{1,2},{2,1},{3,0},{4,7},{5,6},{6,5},{7,4},{8,11},{9,10},{10,... | collective-permute-start | bytes 270344 | tf_op jit(solution)/shard_map/ppermute | solution.py:390
  119.9 2.5 %collective-permute-done.22.refs_2_ = bf16[64,704]{1,0:T(8,128)(2,1)S(1)} collective-permute-done((bf16[64,704]{1,0:T(8,128)(2,1)S(1)}, bf16[64,704]{1,0:T(8,128)(2,1)S(1)}, u32[]{:S(2)}, u32[]{:S(2)}) %collective-permute-start.22) | collective-permute-done | bytes 90144 | tf_op jit(solution)/shard_map/ppermute | solution.py:390
  125.9 5.5 %collective-permute-done.24.refs_2_ = bf16[64,832]{1,0:T(8,128)(2,1)S(1)} collective-permute-done((bf16[64,832]{1,0:T(8,128)(2,1)S(1)}, bf16[64,832]{1,0:T(8,128)(2,1)S(1)}, u32[]{:S(2)}, u32[]{:S(2)}) %collective-permute-start.24) | collective-permute-done | bytes 106528 | tf_op jit(solution)/shard_map/ppermute | solution.py:390
  133.7 2.5 %collective-permute-done.25.refs_0_ = bf16[64,832]{1,0:T(8,128)(2,1)S(1)} collective-permute-done((bf16[64,832]{1,0:T(8,128)(2,1)S(1)}, bf16[64,832]{1,0:T(8,128)(2,1)S(1)}, u32[]{:S(2)}, u32[]{:S(2)}) %collective-permute-start.25) | collective-permute-done | bytes 106528 | tf_op jit(solution)/shard_map/ppermute | solution.py:390
  136.2 4.2 %attend_step.7 = (bf16[64,704]{1,0:T(8,128)(2,1)S(1)}, bf16[64,704]{1,0:T(8,128)(2,1)S(1)}, bf16[64,704]{1,0:T(8,128)(2,1)S(1)}, bf16[64,704]{1,0:T(8,128)(2,1)S...) custom-call(bf16[64,832]{1,0:T(8,128)(2,1)S(1)} %collective-permute-done.25.refs_0_, ...), custom_call_target="tpu_custom_call" | custom-call | tf_op jit(solution)/shard_map/attend_step/pallas_call | solution.py:563
  142.0 2.9 %collective-permute-start.29 = (bf16[64,704]{1,0:T(8,128)(2,1)S(1)}, bf16[64,704]{1,0:T(8,128)(2,1)S(1)}, u32[]{:S(2)}, u32[]{:S(2)}) collective-permute-start(bf16[64,704]{1,0:T(8,128)(2,1)S(1)} %get-tuple-element.116), channel_id=1, source_target_pairs={{0,1},{1,0},{2,3},{3,2},{4,5},{5,4},{6,7},{7,6},{8,9},{9,8},{10,11... | collective-permute-start | bytes 270344 | tf_op jit(solution)/shard_map/ppermute | solution.py:390
  (109 shorter events, 68.2 us)
Async XLA Ops:
  5.4 31.7 %collective-permute-start = (bf16[16,768]{1,0:T(8,128)(2,1)S(1)}, bf16[16,768]{1,0:T(8,128)(2,1)S(1)}, u32[]{:S(2)}, u32[]{:S(2)}) collective-permute-start(bf16[16,768]{1,0:T(8,128)(2,1)S(1)} %get-tuple-element.65), channel_id=1, source_target_pairs={{0,4},{4,8},{8,12},{12,0},{1,5},{5,9},{9,13},{13,1},{2,6},{6,10},{... | collective-permute-start | bytes 73736 | tf_op jit(solution)/shard_map/ppermute | solution.py:386
  5.9 32.7 %collective-permute-start.1 = (bf16[16,768]{1,0:T(8,128)(2,1)S(1)}, bf16[16,768]{1,0:T(8,128)(2,1)S(1)}, u32[]{:S(2)}, u32[]{:S(2)}) collective-permute-start(bf16[16,768]{1,0:T(8,128)(2,1)S(1)} %get-tuple-element.66), channel_id=1, source_target_pairs={{0,8},{4,12},{8,0},{12,4},{1,9},{5,13},{9,1},{13,5},{2,10},{6,14},... | collective-permute-start | bytes 73736 | tf_op jit(solution)/shard_map/ppermute | solution.py:386
  8.5 30.1 %collective-permute-start.2 = (bf16[16,768]{1,0:T(8,128)(2,1)S(1)}, bf16[16,768]{1,0:T(8,128)(2,1)S(1)}, u32[]{:S(2)}, u32[]{:S(2)}) collective-permute-start(bf16[16,768]{1,0:T(8,128)(2,1)S(1)} %get-tuple-element.67), channel_id=1, source_target_pairs={{0,12},{4,0},{8,4},{12,8},{1,13},{5,1},{9,5},{13,9},{2,14},{6,2},{... | collective-permute-start | bytes 73736 | tf_op jit(solution)/shard_map/ppermute | solution.py:386
  13.6 40.7 %collective-permute-start.6 = (bf16[4,16,24,128]{3,2,1,0:T(8,128)(2,1)S(1)}, bf16[4,16,24,128]{3,2,1,0:T(8,128)(2,1)S(1)}, u32[]{:S(2)}, u32[]{:S(2)}) collective-permute-start(bf16[4,16,24,128]{3,2,1,0:T(8,128)(2,1)S(1)} %get-tuple-element.80), channel_id=1, source_target_pairs={{0,4},{4,8},{8,12},{12,0},{1,5},{5,9},{9,13},{13,1},{2,6},{6,10},{... | collective-permute-start | bytes 1179656 | tf_op jit(solution)/shard_map/ppermute | solution.py:386
  13.7 40.6 %collective-permute-start.7 = (bf16[4,16,24,128]{3,2,1,0:T(8,128)(2,1)S(1)}, bf16[4,16,24,128]{3,2,1,0:T(8,128)(2,1)S(1)}, u32[]{:S(2)}, u32[]{:S(2)}) collective-permute-start(bf16[4,16,24,128]{3,2,1,0:T(8,128)(2,1)S(1)} %get-tuple-element.81), channel_id=1, source_target_pairs={{0,8},{4,12},{8,0},{12,4},{1,9},{5,13},{9,1},{13,5},{2,10},{6,14},... | collective-permute-start | bytes 1179656 | tf_op jit(solution)/shard_map/ppermute | solution.py:386
  37.1 17.2 %collective-permute-start.8 = (bf16[4,16,24,128]{3,2,1,0:T(8,128)(2,1)S(1)}, bf16[4,16,24,128]{3,2,1,0:T(8,128)(2,1)S(1)}, u32[]{:S(2)}, u32[]{:S(2)}) collective-permute-start(bf16[4,16,24,128]{3,2,1,0:T(8,128)(2,1)S(1)} %get-tuple-element.82), channel_id=1, source_target_pairs={{0,12},{4,0},{8,4},{12,8},{1,13},{5,1},{9,5},{13,9},{2,14},{6,2},{... | collective-permute-start | bytes 1179656 | tf_op jit(solution)/shard_map/ppermute | solution.py:386
  39.4 10.5 %collective-permute-start.5 = (bf16[64,832]{1,0:T(8,128)(2,1)S(1)}, bf16[64,832]{1,0:T(8,128)(2,1)S(1)}, u32[]{:S(2)}, u32[]{:S(2)}) collective-permute-start(bf16[64,832]{1,0:T(8,128)(2,1)S(1)} %get-tuple-element.69.refs_0_.refs_4_), channel_id=1, source_target_pairs={{0,1},{1,0},{2,3},{3,2},{4,5},{5,4},{6,7},{7,6},{8,9},{9,8},{10,11... | collective-permute-start | bytes 319496 | tf_op jit(solution)/shard_map/ppermute | solution.py:390
  41.2 8.0 %collective-permute-start.3 = (bf16[64,832]{1,0:T(8,128)(2,1)S(1)}, bf16[64,832]{1,0:T(8,128)(2,1)S(1)}, u32[]{:S(2)}, u32[]{:S(2)}) collective-permute-start(bf16[64,832]{1,0:T(8,128)(2,1)S(1)} %get-tuple-element.69.refs_0_.refs_4_), channel_id=1, source_target_pairs={{0,3},{1,2},{2,1},{3,0},{4,7},{5,6},{6,5},{7,4},{8,11},{9,10},{10,... | collective-permute-start | bytes 319496 | tf_op jit(solution)/shard_map/ppermute | solution.py:390
  60.2 7.2 %collective-permute-start.9 = (bf16[64,704]{1,0:T(8,128)(2,1)S(1)}, bf16[64,704]{1,0:T(8,128)(2,1)S(1)}, u32[]{:S(2)}, u32[]{:S(2)}) collective-permute-start(bf16[64,704]{1,0:T(8,128)(2,1)S(1)} %get-tuple-element.86), channel_id=1, source_target_pairs={{0,3},{1,2},{2,1},{3,0},{4,7},{5,6},{6,5},{7,4},{8,11},{9,10},{10,... | collective-permute-start | bytes 270344 | tf_op jit(solution)/shard_map/ppermute | solution.py:390
  62.9 7.9 %collective-permute-start.10 = (bf16[64,704]{1,0:T(8,128)(2,1)S(1)}, bf16[64,704]{1,0:T(8,128)(2,1)S(1)}, u32[]{:S(2)}, u32[]{:S(2)}) collective-permute-start(bf16[64,704]{1,0:T(8,128)(2,1)S(1)} %get-tuple-element.87), channel_id=1, source_target_pairs={{0,2},{1,3},{2,0},{3,1},{4,6},{5,7},{6,4},{7,5},{8,10},{9,11},{10,... | collective-permute-start | bytes 270344 | tf_op jit(solution)/shard_map/ppermute | solution.py:390
  63.2 7.7 %collective-permute-start.11 = (bf16[64,704]{1,0:T(8,128)(2,1)S(1)}, bf16[64,704]{1,0:T(8,128)(2,1)S(1)}, u32[]{:S(2)}, u32[]{:S(2)}) collective-permute-start(bf16[64,704]{1,0:T(8,128)(2,1)S(1)} %get-tuple-element.88), channel_id=1, source_target_pairs={{0,1},{1,0},{2,3},{3,2},{4,5},{5,4},{6,7},{7,6},{8,9},{9,8},{10,11... | collective-permute-start | bytes 270344 | tf_op jit(solution)/shard_map/ppermute | solution.py:390
  71.8 7.8 %collective-permute-start.12 = (bf16[64,832]{1,0:T(8,128)(2,1)S(1)}, bf16[64,832]{1,0:T(8,128)(2,1)S(1)}, u32[]{:S(2)}, u32[]{:S(2)}) collective-permute-start(bf16[64,832]{1,0:T(8,128)(2,1)S(1)} %between.3.refs_0_.refs_4_), channel_id=1, source_target_pairs={{0,3},{1,2},{2,1},{3,0},{4,7},{5,6},{6,5},{7,4},{8,11},{9,10},{10,... | collective-permute-start | bytes 319496 | tf_op jit(solution)/shard_map/ppermute | solution.py:390
  74.1 6.2 %collective-permute-start.14 = (bf16[64,832]{1,0:T(8,128)(2,1)S(1)}, bf16[64,832]{1,0:T(8,128)(2,1)S(1)}, u32[]{:S(2)}, u32[]{:S(2)}) collective-permute-start(bf16[64,832]{1,0:T(8,128)(2,1)S(1)} %between.3.refs_0_.refs_4_), channel_id=1, source_target_pairs={{0,1},{1,0},{2,3},{3,2},{4,5},{5,4},{6,7},{7,6},{8,9},{9,8},{10,11... | collective-permute-start | bytes 319496 | tf_op jit(solution)/shard_map/ppermute | solution.py:390
  88.2 6.6 %collective-permute-start.15 = (bf16[64,704]{1,0:T(8,128)(2,1)S(1)}, bf16[64,704]{1,0:T(8,128)(2,1)S(1)}, u32[]{:S(2)}, u32[]{:S(2)}) collective-permute-start(bf16[64,704]{1,0:T(8,128)(2,1)S(1)} %get-tuple-element.96), channel_id=1, source_target_pairs={{0,3},{1,2},{2,1},{3,0},{4,7},{5,6},{6,5},{7,4},{8,11},{9,10},{10,... | collective-permute-start | bytes 270344 | tf_op jit(solution)/shard_map/ppermute | solution.py:390
  89.5 7.3 %collective-permute-start.16 = (bf16[64,704]{1,0:T(8,128)(2,1)S(1)}, bf16[64,704]{1,0:T(8,128)(2,1)S(1)}, u32[]{:S(2)}, u32[]{:S(2)}) collective-permute-start(bf16[64,704]{1,0:T(8,128)(2,1)S(1)} %get-tuple-element.97), channel_id=1, source_target_pairs={{0,2},{1,3},{2,0},{3,1},{4,6},{5,7},{6,4},{7,5},{8,10},{9,11},{10,... | collective-permute-start | bytes 270344 | tf_op jit(solution)/shard_map/ppermute | solution.py:390
  89.7 7.1 %collective-permute-start.17 = (bf16[64,704]{1,0:T(8,128)(2,1)S(1)}, bf16[64,704]{1,0:T(8,128)(2,1)S(1)}, u32[]{:S(2)}, u32[]{:S(2)}) collective-permute-start(bf16[64,704]{1,0:T(8,128)(2,1)S(1)} %get-tuple-element.98), channel_id=1, source_target_pairs={{0,1},{1,0},{2,3},{3,2},{4,5},{5,4},{6,7},{7,6},{8,9},{9,8},{10,11... | collective-permute-start | bytes 270344 | tf_op jit(solution)/shard_map/ppermute | solution.py:390
  97.8 6.8 %collective-permute-start.18 = (bf16[64,832]{1,0:T(8,128)(2,1)S(1)}, bf16[64,832]{1,0:T(8,128)(2,1)S(1)}, u32[]{:S(2)}, u32[]{:S(2)}) collective-permute-start(bf16[64,832]{1,0:T(8,128)(2,1)S(1)} %between.4.refs_0_.refs_4_), channel_id=1, source_target_pairs={{0,3},{1,2},{2,1},{3,0},{4,7},{5,6},{6,5},{7,4},{8,11},{9,10},{10,... | collective-permute-start | bytes 319496 | tf_op jit(solution)/shard_map/ppermute | solution.py:390
  99.9 6.9 %collective-permute-start.20 = (bf16[64,832]{1,0:T(8,128)(2,1)S(1)}, bf16[64,832]{1,0:T(8,128)(2,1)S(1)}, u32[]{:S(2)}, u32[]{:S(2)}) collective-permute-start(bf16[64,832]{1,0:T(8,128)(2,1)S(1)} %between.4.refs_0_.refs_4_), channel_id=1, source_target_pairs={{0,1},{1,0},{2,3},{3,2},{4,5},{5,4},{6,7},{7,6},{8,9},{9,8},{10,11... | collective-permute-start | bytes 319496 | tf_op jit(solution)/shard_map/ppermute | solution.py:390
  113.3 6.6 %collective-permute-start.21 = (bf16[64,704]{1,0:T(8,128)(2,1)S(1)}, bf16[64,704]{1,0:T(8,128)(2,1)S(1)}, u32[]{:S(2)}, u32[]{:S(2)}) collective-permute-start(bf16[64,704]{1,0:T(8,128)(2,1)S(1)} %get-tuple-element.105), channel_id=1, source_target_pairs={{0,3},{1,2},{2,1},{3,0},{4,7},{5,6},{6,5},{7,4},{8,11},{9,10},{10,... | collective-permute-start | bytes 270344 | tf_op jit(solution)/shard_map/ppermute | solution.py:390
  123.4 8.0 %collective-permute-start.24 = (bf16[64,832]{1,0:T(8,128)(2,1)S(1)}, bf16[64,832]{1,0:T(8,128)(2,1)S(1)}, u32[]{:S(2)}, u32[]{:S(2)}) collective-permute-start(bf16[64,832]{1,0:T(8,128)(2,1)S(1)} %between.5.refs_0_.refs_4_), channel_id=1, source_target_pairs={{0,3},{1,2},{2,1},{3,0},{4,7},{5,6},{6,5},{7,4},{8,11},{9,10},{10,... | collective-permute-start | bytes 319496 | tf_op jit(solution)/shard_map/ppermute | solution.py:390
  125.9 6.6 %collective-permute-start.26 = (bf16[64,832]{1,0:T(8,128)(2,1)S(1)}, bf16[64,832]{1,0:T(8,128)(2,1)S(1)}, u32[]{:S(2)}, u32[]{:S(2)}) collective-permute-start(bf16[64,832]{1,0:T(8,128)(2,1)S(1)} %between.5.refs_0_.refs_4_), channel_id=1, source_target_pairs={{0,1},{1,0},{2,3},{3,2},{4,5},{5,4},{6,7},{7,6},{8,9},{9,8},{10,11... | collective-permute-start | bytes 319496 | tf_op jit(solution)/shard_map/ppermute | solution.py:390
  140.4 6.6 %collective-permute-start.27 = (bf16[64,704]{1,0:T(8,128)(2,1)S(1)}, bf16[64,704]{1,0:T(8,128)(2,1)S(1)}, u32[]{:S(2)}, u32[]{:S(2)}) collective-permute-start(bf16[64,704]{1,0:T(8,128)(2,1)S(1)} %get-tuple-element.114), channel_id=1, source_target_pairs={{0,3},{1,2},{2,1},{3,0},{4,7},{5,6},{6,5},{7,4},{8,11},{9,10},{10,... | collective-permute-start | bytes 270344 | tf_op jit(solution)/shard_map/ppermute | solution.py:390
  141.7 7.3 %collective-permute-start.28 = (bf16[64,704]{1,0:T(8,128)(2,1)S(1)}, bf16[64,704]{1,0:T(8,128)(2,1)S(1)}, u32[]{:S(2)}, u32[]{:S(2)}) collective-permute-start(bf16[64,704]{1,0:T(8,128)(2,1)S(1)} %get-tuple-element.115), channel_id=1, source_target_pairs={{0,2},{1,3},{2,0},{3,1},{4,6},{5,7},{6,4},{7,5},{8,10},{9,11},{10,... | collective-permute-start | bytes 270344 | tf_op jit(solution)/shard_map/ppermute | solution.py:390
  142.0 7.1 %collective-permute-start.29 = (bf16[64,704]{1,0:T(8,128)(2,1)S(1)}, bf16[64,704]{1,0:T(8,128)(2,1)S(1)}, u32[]{:S(2)}, u32[]{:S(2)}) collective-permute-start(bf16[64,704]{1,0:T(8,128)(2,1)S(1)} %get-tuple-element.116), channel_id=1, source_target_pairs={{0,1},{1,0},{2,3},{3,2},{4,5},{5,4},{6,7},{7,6},{8,9},{9,8},{10,11... | collective-permute-start | bytes 270344 | tf_op jit(solution)/shard_map/ppermute | solution.py:390
  (29 other events, 96.5 us)

commit v3 on v2

--- a/solution.py
+++ b/solution.py
@@ -20,6 +20,10 @@
 
 def kernel_params(mib):
     return pltpu.CompilerParams(vmem_limit_bytes=mib * 1024 * 1024)
+
+
+def in_hbm(array):
+    return pltpu.with_memory_space_constraint(array, pltpu.HBM)
 
 
 def copy_all(pairs, sems):
@@ -450,7 +454,13 @@
         ],
         compiler_params=kernel_params(8),
         name="route_rows",
-    )(wide_index.reshape(1), domain_of_row, slot_of_domain, cached_length_rows, hidden)
+    )(
+        wide_index.reshape(1),
+        in_hbm(domain_of_row),
+        in_hbm(slot_of_domain),
+        in_hbm(cached_length_rows),
+        in_hbm(hidden),
+    )
     arrived = [outgoing[0]] + [shift(outgoing[s], "wide", s) for s in range(1, groups)]
     packed_shape = (2 * kv_local, capacity, context, head_dim)
     packed = pl.pallas_call(
@@ -466,7 +476,7 @@
         ],
         compiler_params=kernel_params(16),
         name="pack_cache",
-    )(target, cached_key_rows, cached_value_rows)
+    )(target, in_hbm(cached_key_rows), in_hbm(cached_value_rows))
     cache = [packed[0]] + [shift(packed[s], "wide", s) for s in range(1, groups)]
     cache = [block.reshape(2 * kv_local, capacity * context, head_dim) for block in cache]
 
@@ -491,16 +501,16 @@
         cost_estimate=pl.CostEstimate(flops=0, bytes_accessed=40000000, transcendentals=0),
         name="load_weights",
     )(
-        query_projection_weight,
-        key_projection_weight,
-        value_projection_weight,
-        query_up_factor.reshape(total * rank, query_width),
-        key_up_factor.reshape(total * rank, key_width),
-        value_up_factor.reshape(total * rank, key_width),
-        output_projection_weight,
-        output_down_factor.reshape(total * rank, query_width),
-        output_up_factor.reshape(total * rank, width),
-        stacked_down_factors,
+        in_hbm(query_projection_weight),
+        in_hbm(key_projection_weight),
+        in_hbm(value_projection_weight),
+        in_hbm(query_up_factor.reshape(total * rank, query_width)),
+        in_hbm(key_up_factor.reshape(total * rank, key_width)),
+        in_hbm(value_up_factor.reshape(total * rank, key_width)),
+        in_hbm(output_projection_weight),
+        in_hbm(output_down_factor.reshape(total * rank, query_width)),
+        in_hbm(output_up_factor.reshape(total * rank, width)),
+        in_hbm(stacked_down_factors),
     )
     input_weight, query_up, key_up, value_up, output_weight, output_down, output_up, down = weights
 

time: 155 us -> 134 us (0.86)
  local copies, waits for them, and re-layouts: 25.8 us -> 0.85 us
  starting transfers between devices: 36.4 us -> 38.9 us
  waiting for transfers between devices: 53.8 us -> 55.8 us
    unnamed x40 -> x4, local copies, waits for them, and re-layouts: 25 us -> 0.01 us
    ppermute x9, starting transfers between devices: 6.92 us -> 10.3 us  [shift(): lax.ppermute(block, axis, [(i, (i + by) % size) for i in range(size)])]
    ppermute x24, waiting for transfers between devices: 50.4 us -> 52.8 us  [swap(): lax.ppermute(block, axis, [(i, i ^ mask) for i in range(lax.axis_size(axi...]
  transfers between devices with their start and end apart: 33 -> 33, of which waited for: 20 -> 21; matrix products, arithmetic and copies ran while one was open for 1% -> 1% of each run, Pallas kernels for 9% -> 11%
where the time goes in v3:
time: 134 us
  waiting for transfers between devices  55.8 us (42%)
  starting transfers between devices  38.9 us (29%)
  Pallas kernels  37.2 us (28%)
    ppermute x24, waiting for transfers between devices, swap(): lax.ppermute(block, axis, [(i, i ^ mask) for i in range(lax.axis_size(axi...  52.8 us
    ppermute x24, starting transfers between devices, swap(): lax.ppermute(block, axis, [(i, i ^ mask) for i in range(lax.axis_size(axi...  28.7 us
    pallas_call x4, Pallas kernels, shards(): pl.pallas_call(functools.partial(step_kernel, total, rank, step, parts, l...  15.9 us
    ppermute x9, starting transfers between devices, shift(): lax.ppermute(block, axis, [(i, (i + by) % size) for i in range(size)])  10.3 us
    pallas_call x1, Pallas kernels, shards(): pl.pallas_call(functools.partial(load_kernel, rank), out_shape=[jax.Shape...  6.51 us
    pallas_call x4, Pallas kernels, shards(): pl.pallas_call(functools.partial(early_kernel, early), out_shape=[jax.Sha...  4.62 us
    ppermute x9, waiting for transfers between devices, shift(): lax.ppermute(block, axis, [(i, (i + by) % size) for i in range(size)])  3.06 us
    pallas_call x3, Pallas kernels, shards(): pl.pallas_call(functools.partial(between_kernel, total, rank, parts), out...  2.97 us
  transfers between devices with their start and end apart: 33, of which 21 were waited for; matrix products, arithmetic and copies ran while one was open for 1% of the time, Pallas kernels for 11%

profile of v3, /device:TPU:0, one launch (start us, length us, event | category | flops | bytes accessed | tf_op | source)
XLA Modules:
  0.0 133.9 jit_solution(8762663022911525367)
XLA Ops:
  0.0 2.6 %route_rows.1 = (s32[64]{0:T(128)S(1)}, bf16[64,64]{1,0:T(8,128)(2,1)S(1)}, bf16[16,768]{1,0:T(8,128)(2,1)S(1)}, bf16[16,768]{1,0:T(8,128)(2,1)S(1)}, bf16[16,76...) custom-call(s32[1]{0:T(128)} %bitcast.group_ref, s32[256]{0:T(256)} %domain_hbm.1, s32[32]{0:T(128)} %slot_hbm.1, ...), custom_call_target="tpu_custom_call" | custom-call | tf_op jit(solution)/shard_map/route_rows/pallas_call | solution.py:436
  3.1 2.6 %collective-permute-start.1 = (bf16[16,768]{1,0:T(8,128)(2,1)S(1)}, bf16[16,768]{1,0:T(8,128)(2,1)S(1)}, u32[]{:S(2)}, u32[]{:S(2)}) collective-permute-start(bf16[16,768]{1,0:T(8,128)(2,1)S(1)} %get-tuple-element.66), channel_id=1, source_target_pairs={{0,8},{4,12},{8,0},{12,4},{1,9},{5,13},{9,1},{13,5},{2,10},{6,14},... | collective-permute-start | bytes 73736 | tf_op jit(solution)/shard_map/ppermute | solution.py:390
  7.1 2.7 %pack_cache.1 = (bf16[4,16,24,128]{3,2,1,0:T(8,128)(2,1)S(1)}, bf16[4,16,24,128]{3,2,1,0:T(8,128)(2,1)S(1)}, bf16[4,16,24,128]{3,2,1,0:T(8,128)(2,1)S(1)}, bf16[4,16,24,128]{3,2,1,0:T(8,128)(2,1)S(1)}) custom-call(s32[64]{0:T(128)S(1)} %get-tuple-element.78.target_ref, bf16[64,2,24,128]{3,2,1,0:T(8,128)(2,1)} %key_hbm.1, bf16[64,2,24,128]{3,2,1,0:T(8,128)(2,1)} %value_hbm.1), custom_call_target="tpu_custom_call" | custom-call | tf_op jit(solution)/shard_map/pack_cache/pallas_call | solution.py:466
  11.1 6.5 %load_weights.1 = (bf16[2560,1536]{1,0:T(8,128)(2,1)S(1)}, bf16[512,1024]{1,0:T(8,128)(2,1)S(1)}, bf16[512,256]{1,0:T(8,128)(2,1)S(1)}, bf16[512,256]{1,0:T(8,12...) custom-call(bf16[2560,1024]{1,0:T(8,128)(2,1)} %refs_0_.1, ...), custom_call_target="tpu_custom_call" | custom-call | bytes 40000000 | tf_op jit(solution)/shard_map/load_weights/pallas_call | solution.py:494
  21.7 2.5 %collective-permute-start.3 = (bf16[64,832]{1,0:T(8,128)(2,1)S(1)}, bf16[64,832]{1,0:T(8,128)(2,1)S(1)}, u32[]{:S(2)}, u32[]{:S(2)}) collective-permute-start(bf16[64,832]{1,0:T(8,128)(2,1)S(1)} %get-tuple-element.69.refs_0_.refs_4_), channel_id=1, source_target_pairs={{0,3},{1,2},{2,1},{3,0},{4,7},{5,6},{6,5},{7,4},{8,11},{9,10},{10,... | collective-permute-start | bytes 319496 | tf_op jit(solution)/shard_map/ppermute | solution.py:394
  25.0 4.7 %collective-permute-done.3.refs_2_ = bf16[64,832]{1,0:T(8,128)(2,1)S(1)} collective-permute-done((bf16[64,832]{1,0:T(8,128)(2,1)S(1)}, bf16[64,832]{1,0:T(8,128)(2,1)S(1)}, u32[]{:S(2)}, u32[]{:S(2)}) %collective-permute-start.3) | collective-permute-done | bytes 106528 | tf_op jit(solution)/shard_map/ppermute | solution.py:394
  31.6 2.9 %collective-permute-done.4.refs_0_ = bf16[64,832]{1,0:T(8,128)(2,1)S(1)} collective-permute-done((bf16[64,832]{1,0:T(8,128)(2,1)S(1)}, bf16[64,832]{1,0:T(8,128)(2,1)S(1)}, u32[]{:S(2)}, u32[]{:S(2)}) %collective-permute-start.4) | collective-permute-done | bytes 106528 | tf_op jit(solution)/shard_map/ppermute | solution.py:394
  34.5 3.8 %attend_step.4 = (bf16[64,704]{1,0:T(8,128)(2,1)S(1)}, bf16[64,704]{1,0:T(8,128)(2,1)S(1)}, bf16[64,704]{1,0:T(8,128)(2,1)S(1)}, bf16[64,704]{1,0:T(8,128)(2,1)S...) custom-call(bf16[64,832]{1,0:T(8,128)(2,1)S(1)} %collective-permute-done.4.refs_0_, ...), custom_call_target="tpu_custom_call" | custom-call | tf_op jit(solution)/shard_map/attend_step/pallas_call | solution.py:573
  40.5 2.4 %collective-permute-start.11 = (bf16[64,704]{1,0:T(8,128)(2,1)S(1)}, bf16[64,704]{1,0:T(8,128)(2,1)S(1)}, u32[]{:S(2)}, u32[]{:S(2)}) collective-permute-start(bf16[64,704]{1,0:T(8,128)(2,1)S(1)} %get-tuple-element.88), channel_id=1, source_target_pairs={{0,1},{1,0},{2,3},{3,2},{4,5},{5,4},{6,7},{7,6},{8,9},{9,8},{10,11... | collective-permute-start | bytes 270344 | tf_op jit(solution)/shard_map/ppermute | solution.py:394
  42.8 2.2 %collective-permute-done.9.refs_1_ = bf16[64,704]{1,0:T(8,128)(2,1)S(1)} collective-permute-done((bf16[64,704]{1,0:T(8,128)(2,1)S(1)}, bf16[64,704]{1,0:T(8,128)(2,1)S(1)}, u32[]{:S(2)}, u32[]{:S(2)}) %collective-permute-start.9) | collective-permute-done | bytes 90144 | tf_op jit(solution)/shard_map/ppermute | solution.py:394
  45.0 3.0 %collective-permute-done.10.refs_2_ = bf16[64,704]{1,0:T(8,128)(2,1)S(1)} collective-permute-done((bf16[64,704]{1,0:T(8,128)(2,1)S(1)}, bf16[64,704]{1,0:T(8,128)(2,1)S(1)}, u32[]{:S(2)}, u32[]{:S(2)}) %collective-permute-start.10) | collective-permute-done | bytes 90144 | tf_op jit(solution)/shard_map/ppermute | solution.py:394
  51.0 4.9 %collective-permute-done.12.refs_2_ = bf16[64,832]{1,0:T(8,128)(2,1)S(1)} collective-permute-done((bf16[64,832]{1,0:T(8,128)(2,1)S(1)}, bf16[64,832]{1,0:T(8,128)(2,1)S(1)}, u32[]{:S(2)}, u32[]{:S(2)}) %collective-permute-start.12) | collective-permute-done | bytes 106528 | tf_op jit(solution)/shard_map/ppermute | solution.py:394
  60.7 3.8 %attend_step.5 = (bf16[64,704]{1,0:T(8,128)(2,1)S(1)}, bf16[64,704]{1,0:T(8,128)(2,1)S(1)}, bf16[64,704]{1,0:T(8,128)(2,1)S(1)}, bf16[64,704]{1,0:T(8,128)(2,1)S...) custom-call(bf16[64,832]{1,0:T(8,128)(2,1)S(1)} %collective-permute-done.13.refs_0_, ...), custom_call_target="tpu_custom_call" | custom-call | tf_op jit(solution)/shard_map/attend_step/pallas_call | solution.py:573
  66.6 2.4 %collective-permute-start.17 = (bf16[64,704]{1,0:T(8,128)(2,1)S(1)}, bf16[64,704]{1,0:T(8,128)(2,1)S(1)}, u32[]{:S(2)}, u32[]{:S(2)}) collective-permute-start(bf16[64,704]{1,0:T(8,128)(2,1)S(1)} %get-tuple-element.98), channel_id=1, source_target_pairs={{0,1},{1,0},{2,3},{3,2},{4,5},{5,4},{6,7},{7,6},{8,9},{9,8},{10,11... | collective-permute-start | bytes 270344 | tf_op jit(solution)/shard_map/ppermute | solution.py:394
  71.2 2.6 %collective-permute-done.16.refs_2_ = bf16[64,704]{1,0:T(8,128)(2,1)S(1)} collective-permute-done((bf16[64,704]{1,0:T(8,128)(2,1)S(1)}, bf16[64,704]{1,0:T(8,128)(2,1)S(1)}, u32[]{:S(2)}, u32[]{:S(2)}) %collective-permute-start.16) | collective-permute-done | bytes 90144 | tf_op jit(solution)/shard_map/ppermute | solution.py:394
  76.7 5.1 %collective-permute-done.18.refs_2_ = bf16[64,832]{1,0:T(8,128)(2,1)S(1)} collective-permute-done((bf16[64,832]{1,0:T(8,128)(2,1)S(1)}, bf16[64,832]{1,0:T(8,128)(2,1)S(1)}, u32[]{:S(2)}, u32[]{:S(2)}) %collective-permute-start.18) | collective-permute-done | bytes 106528 | tf_op jit(solution)/shard_map/ppermute | solution.py:394
  86.6 4.0 %attend_step.6 = (bf16[64,704]{1,0:T(8,128)(2,1)S(1)}, bf16[64,704]{1,0:T(8,128)(2,1)S(1)}, bf16[64,704]{1,0:T(8,128)(2,1)S(1)}, bf16[64,704]{1,0:T(8,128)(2,1)S...) custom-call(bf16[64,832]{1,0:T(8,128)(2,1)S(1)} %collective-permute-done.19.refs_0_, ...), custom_call_target="tpu_custom_call" | custom-call | tf_op jit(solution)/shard_map/attend_step/pallas_call | solution.py:573
  92.5 2.6 %collective-permute-start.23 = (bf16[64,704]{1,0:T(8,128)(2,1)S(1)}, bf16[64,704]{1,0:T(8,128)(2,1)S(1)}, u32[]{:S(2)}, u32[]{:S(2)}) collective-permute-start(bf16[64,704]{1,0:T(8,128)(2,1)S(1)} %get-tuple-element.107), channel_id=1, source_target_pairs={{0,1},{1,0},{2,3},{3,2},{4,5},{5,4},{6,7},{7,6},{8,9},{9,8},{10,11... | collective-permute-start | bytes 270344 | tf_op jit(solution)/shard_map/ppermute | solution.py:394
  97.2 2.3 %collective-permute-done.22.refs_2_ = bf16[64,704]{1,0:T(8,128)(2,1)S(1)} collective-permute-done((bf16[64,704]{1,0:T(8,128)(2,1)S(1)}, bf16[64,704]{1,0:T(8,128)(2,1)S(1)}, u32[]{:S(2)}, u32[]{:S(2)}) %collective-permute-start.22) | collective-permute-done | bytes 90144 | tf_op jit(solution)/shard_map/ppermute | solution.py:394
  102.7 4.9 %collective-permute-done.24.refs_2_ = bf16[64,832]{1,0:T(8,128)(2,1)S(1)} collective-permute-done((bf16[64,832]{1,0:T(8,128)(2,1)S(1)}, bf16[64,832]{1,0:T(8,128)(2,1)S(1)}, u32[]{:S(2)}, u32[]{:S(2)}) %collective-permute-start.24) | collective-permute-done | bytes 106528 | tf_op jit(solution)/shard_map/ppermute | solution.py:394
  112.4 4.3 %attend_step.7 = (bf16[64,704]{1,0:T(8,128)(2,1)S(1)}, bf16[64,704]{1,0:T(8,128)(2,1)S(1)}, bf16[64,704]{1,0:T(8,128)(2,1)S(1)}, bf16[64,704]{1,0:T(8,128)(2,1)S...) custom-call(bf16[64,832]{1,0:T(8,128)(2,1)S(1)} %collective-permute-done.25.refs_0_, ...), custom_call_target="tpu_custom_call" | custom-call | tf_op jit(solution)/shard_map/attend_step/pallas_call | solution.py:573
  118.7 2.4 %collective-permute-start.29 = (bf16[64,704]{1,0:T(8,128)(2,1)S(1)}, bf16[64,704]{1,0:T(8,128)(2,1)S(1)}, u32[]{:S(2)}, u32[]{:S(2)}) collective-permute-start(bf16[64,704]{1,0:T(8,128)(2,1)S(1)} %get-tuple-element.116), channel_id=1, source_target_pairs={{0,1},{1,0},{2,3},{3,2},{4,5},{5,4},{6,7},{7,6},{8,9},{9,8},{10,11... | collective-permute-start | bytes 270344 | tf_op jit(solution)/shard_map/ppermute | solution.py:394
  123.3 2.6 %collective-permute-done.28.refs_2_ = bf16[64,704]{1,0:T(8,128)(2,1)S(1)} collective-permute-done((bf16[64,704]{1,0:T(8,128)(2,1)S(1)}, bf16[64,704]{1,0:T(8,128)(2,1)S(1)}, u32[]{:S(2)}, u32[]{:S(2)}) %collective-permute-start.28) | collective-permute-done | bytes 90144 | tf_op jit(solution)/shard_map/ppermute | solution.py:394
  126.2 3.7 %collective-permute-start.31 = (bf16[16,640]{1,0:T(8,128)(2,1)S(1)}, bf16[16,640]{1,0:T(8,128)(2,1)S(1)}, u32[]{:S(2)}, u32[]{:S(2)}) collective-permute-start(bf16[16,640]{1,0:T(8,128)(2,1)S(1)} %get-tuple-element.119), channel_id=1, source_target_pairs={{0,8},{4,12},{8,0},{12,4},{1,9},{5,13},{9,1},{13,5},{2,10},{6,14},... | collective-permute-start | bytes 61448 | tf_op jit(solution)/shard_map/ppermute | solution.py:390
  (73 shorter events, 52.2 us)
Async XLA Ops:
  2.6 15.0 %collective-permute-start = (bf16[16,768]{1,0:T(8,128)(2,1)S(1)}, bf16[16,768]{1,0:T(8,128)(2,1)S(1)}, u32[]{:S(2)}, u32[]{:S(2)}) collective-permute-start(bf16[16,768]{1,0:T(8,128)(2,1)S(1)} %get-tuple-element.65), channel_id=1, source_target_pairs={{0,4},{4,8},{8,12},{12,0},{1,5},{5,9},{9,13},{13,1},{2,6},{6,10},{... | collective-permute-start | bytes 73736 | tf_op jit(solution)/shard_map/ppermute | solution.py:390
  3.1 15.9 %collective-permute-start.1 = (bf16[16,768]{1,0:T(8,128)(2,1)S(1)}, bf16[16,768]{1,0:T(8,128)(2,1)S(1)}, u32[]{:S(2)}, u32[]{:S(2)}) collective-permute-start(bf16[16,768]{1,0:T(8,128)(2,1)S(1)} %get-tuple-element.66), channel_id=1, source_target_pairs={{0,8},{4,12},{8,0},{12,4},{1,9},{5,13},{9,1},{13,5},{2,10},{6,14},... | collective-permute-start | bytes 73736 | tf_op jit(solution)/shard_map/ppermute | solution.py:390
  5.7 13.3 %collective-permute-start.2 = (bf16[16,768]{1,0:T(8,128)(2,1)S(1)}, bf16[16,768]{1,0:T(8,128)(2,1)S(1)}, u32[]{:S(2)}, u32[]{:S(2)}) collective-permute-start(bf16[16,768]{1,0:T(8,128)(2,1)S(1)} %get-tuple-element.67), channel_id=1, source_target_pairs={{0,12},{4,0},{8,4},{12,8},{1,13},{5,1},{9,5},{13,9},{2,14},{6,2},{... | collective-permute-start | bytes 73736 | tf_op jit(solution)/shard_map/ppermute | solution.py:390
  9.9 24.6 %collective-permute-start.6 = (bf16[4,16,24,128]{3,2,1,0:T(8,128)(2,1)S(1)}, bf16[4,16,24,128]{3,2,1,0:T(8,128)(2,1)S(1)}, u32[]{:S(2)}, u32[]{:S(2)}) collective-permute-start(bf16[4,16,24,128]{3,2,1,0:T(8,128)(2,1)S(1)} %get-tuple-element.80), channel_id=1, source_target_pairs={{0,4},{4,8},{8,12},{12,0},{1,5},{5,9},{9,13},{13,1},{2,6},{6,10},{... | collective-permute-start | bytes 1179656 | tf_op jit(solution)/shard_map/ppermute | solution.py:390
  9.9 24.6 %collective-permute-start.7 = (bf16[4,16,24,128]{3,2,1,0:T(8,128)(2,1)S(1)}, bf16[4,16,24,128]{3,2,1,0:T(8,128)(2,1)S(1)}, u32[]{:S(2)}, u32[]{:S(2)}) collective-permute-start(bf16[4,16,24,128]{3,2,1,0:T(8,128)(2,1)S(1)} %get-tuple-element.81), channel_id=1, source_target_pairs={{0,8},{4,12},{8,0},{12,4},{1,9},{5,13},{9,1},{13,5},{2,10},{6,14},... | collective-permute-start | bytes 1179656 | tf_op jit(solution)/shard_map/ppermute | solution.py:390
  17.6 16.9 %collective-permute-start.8 = (bf16[4,16,24,128]{3,2,1,0:T(8,128)(2,1)S(1)}, bf16[4,16,24,128]{3,2,1,0:T(8,128)(2,1)S(1)}, u32[]{:S(2)}, u32[]{:S(2)}) collective-permute-start(bf16[4,16,24,128]{3,2,1,0:T(8,128)(2,1)S(1)} %get-tuple-element.82), channel_id=1, source_target_pairs={{0,12},{4,0},{8,4},{12,8},{1,13},{5,1},{9,5},{13,9},{2,14},{6,2},{... | collective-permute-start | bytes 1179656 | tf_op jit(solution)/shard_map/ppermute | solution.py:390
  19.9 10.5 %collective-permute-start.5 = (bf16[64,832]{1,0:T(8,128)(2,1)S(1)}, bf16[64,832]{1,0:T(8,128)(2,1)S(1)}, u32[]{:S(2)}, u32[]{:S(2)}) collective-permute-start(bf16[64,832]{1,0:T(8,128)(2,1)S(1)} %get-tuple-element.69.refs_0_.refs_4_), channel_id=1, source_target_pairs={{0,1},{1,0},{2,3},{3,2},{4,5},{5,4},{6,7},{7,6},{8,9},{9,8},{10,11... | collective-permute-start | bytes 319496 | tf_op jit(solution)/shard_map/ppermute | solution.py:394
  21.7 8.0 %collective-permute-start.3 = (bf16[64,832]{1,0:T(8,128)(2,1)S(1)}, bf16[64,832]{1,0:T(8,128)(2,1)S(1)}, u32[]{:S(2)}, u32[]{:S(2)}) collective-permute-start(bf16[64,832]{1,0:T(8,128)(2,1)S(1)} %get-tuple-element.69.refs_0_.refs_4_), channel_id=1, source_target_pairs={{0,3},{1,2},{2,1},{3,0},{4,7},{5,6},{6,5},{7,4},{8,11},{9,10},{10,... | collective-permute-start | bytes 319496 | tf_op jit(solution)/shard_map/ppermute | solution.py:394
  38.4 6.7 %collective-permute-start.9 = (bf16[64,704]{1,0:T(8,128)(2,1)S(1)}, bf16[64,704]{1,0:T(8,128)(2,1)S(1)}, u32[]{:S(2)}, u32[]{:S(2)}) collective-permute-start(bf16[64,704]{1,0:T(8,128)(2,1)S(1)} %get-tuple-element.86), channel_id=1, source_target_pairs={{0,3},{1,2},{2,1},{3,0},{4,7},{5,6},{6,5},{7,4},{8,11},{9,10},{10,... | collective-permute-start | bytes 270344 | tf_op jit(solution)/shard_map/ppermute | solution.py:394
  39.8 8.2 %collective-permute-start.10 = (bf16[64,704]{1,0:T(8,128)(2,1)S(1)}, bf16[64,704]{1,0:T(8,128)(2,1)S(1)}, u32[]{:S(2)}, u32[]{:S(2)}) collective-permute-start(bf16[64,704]{1,0:T(8,128)(2,1)S(1)} %get-tuple-element.87), channel_id=1, source_target_pairs={{0,2},{1,3},{2,0},{3,1},{4,6},{5,7},{6,4},{7,5},{8,10},{9,11},{10,... | collective-permute-start | bytes 270344 | tf_op jit(solution)/shard_map/ppermute | solution.py:394
  40.5 7.5 %collective-permute-start.11 = (bf16[64,704]{1,0:T(8,128)(2,1)S(1)}, bf16[64,704]{1,0:T(8,128)(2,1)S(1)}, u32[]{:S(2)}, u32[]{:S(2)}) collective-permute-start(bf16[64,704]{1,0:T(8,128)(2,1)S(1)} %get-tuple-element.88), channel_id=1, source_target_pairs={{0,1},{1,0},{2,3},{3,2},{4,5},{5,4},{6,7},{7,6},{8,9},{9,8},{10,11... | collective-permute-start | bytes 270344 | tf_op jit(solution)/shard_map/ppermute | solution.py:394
  49.0 7.0 %collective-permute-start.12 = (bf16[64,832]{1,0:T(8,128)(2,1)S(1)}, bf16[64,832]{1,0:T(8,128)(2,1)S(1)}, u32[]{:S(2)}, u32[]{:S(2)}) collective-permute-start(bf16[64,832]{1,0:T(8,128)(2,1)S(1)} %between.3.refs_0_.refs_4_), channel_id=1, source_target_pairs={{0,3},{1,2},{2,1},{3,0},{4,7},{5,6},{6,5},{7,4},{8,11},{9,10},{10,... | collective-permute-start | bytes 319496 | tf_op jit(solution)/shard_map/ppermute | solution.py:394
  51.0 7.0 %collective-permute-start.14 = (bf16[64,832]{1,0:T(8,128)(2,1)S(1)}, bf16[64,832]{1,0:T(8,128)(2,1)S(1)}, u32[]{:S(2)}, u32[]{:S(2)}) collective-permute-start(bf16[64,832]{1,0:T(8,128)(2,1)S(1)} %between.3.refs_0_.refs_4_), channel_id=1, source_target_pairs={{0,1},{1,0},{2,3},{3,2},{4,5},{5,4},{6,7},{7,6},{8,9},{9,8},{10,11... | collective-permute-start | bytes 319496 | tf_op jit(solution)/shard_map/ppermute | solution.py:394
  64.6 6.6 %collective-permute-start.15 = (bf16[64,704]{1,0:T(8,128)(2,1)S(1)}, bf16[64,704]{1,0:T(8,128)(2,1)S(1)}, u32[]{:S(2)}, u32[]{:S(2)}) collective-permute-start(bf16[64,704]{1,0:T(8,128)(2,1)S(1)} %get-tuple-element.96), channel_id=1, source_target_pairs={{0,3},{1,2},{2,1},{3,0},{4,7},{5,6},{6,5},{7,4},{8,11},{9,10},{10,... | collective-permute-start | bytes 270344 | tf_op jit(solution)/shard_map/ppermute | solution.py:394
  66.6 7.1 %collective-permute-start.16 = (bf16[64,704]{1,0:T(8,128)(2,1)S(1)}, bf16[64,704]{1,0:T(8,128)(2,1)S(1)}, u32[]{:S(2)}, u32[]{:S(2)}) collective-permute-start(bf16[64,704]{1,0:T(8,128)(2,1)S(1)} %get-tuple-element.97), channel_id=1, source_target_pairs={{0,2},{1,3},{2,0},{3,1},{4,6},{5,7},{6,4},{7,5},{8,10},{9,11},{10,... | collective-permute-start | bytes 270344 | tf_op jit(solution)/shard_map/ppermute | solution.py:394
  66.6 7.1 %collective-permute-start.17 = (bf16[64,704]{1,0:T(8,128)(2,1)S(1)}, bf16[64,704]{1,0:T(8,128)(2,1)S(1)}, u32[]{:S(2)}, u32[]{:S(2)}) collective-permute-start(bf16[64,704]{1,0:T(8,128)(2,1)S(1)} %get-tuple-element.98), channel_id=1, source_target_pairs={{0,1},{1,0},{2,3},{3,2},{4,5},{5,4},{6,7},{7,6},{8,9},{9,8},{10,11... | collective-permute-start | bytes 270344 | tf_op jit(solution)/shard_map/ppermute | solution.py:394
  74.8 7.0 %collective-permute-start.18 = (bf16[64,832]{1,0:T(8,128)(2,1)S(1)}, bf16[64,832]{1,0:T(8,128)(2,1)S(1)}, u32[]{:S(2)}, u32[]{:S(2)}) collective-permute-start(bf16[64,832]{1,0:T(8,128)(2,1)S(1)} %between.4.refs_0_.refs_4_), channel_id=1, source_target_pairs={{0,3},{1,2},{2,1},{3,0},{4,7},{5,6},{6,5},{7,4},{8,11},{9,10},{10,... | collective-permute-start | bytes 319496 | tf_op jit(solution)/shard_map/ppermute | solution.py:394
  76.7 6.9 %collective-permute-start.20 = (bf16[64,832]{1,0:T(8,128)(2,1)S(1)}, bf16[64,832]{1,0:T(8,128)(2,1)S(1)}, u32[]{:S(2)}, u32[]{:S(2)}) collective-permute-start(bf16[64,832]{1,0:T(8,128)(2,1)S(1)} %between.4.refs_0_.refs_4_), channel_id=1, source_target_pairs={{0,1},{1,0},{2,3},{3,2},{4,5},{5,4},{6,7},{7,6},{8,9},{9,8},{10,11... | collective-permute-start | bytes 319496 | tf_op jit(solution)/shard_map/ppermute | solution.py:394
  92.5 7.1 %collective-permute-start.22 = (bf16[64,704]{1,0:T(8,128)(2,1)S(1)}, bf16[64,704]{1,0:T(8,128)(2,1)S(1)}, u32[]{:S(2)}, u32[]{:S(2)}) collective-permute-start(bf16[64,704]{1,0:T(8,128)(2,1)S(1)} %get-tuple-element.106), channel_id=1, source_target_pairs={{0,2},{1,3},{2,0},{3,1},{4,6},{5,7},{6,4},{7,5},{8,10},{9,11},{10,... | collective-permute-start | bytes 270344 | tf_op jit(solution)/shard_map/ppermute | solution.py:394
  92.5 7.1 %collective-permute-start.23 = (bf16[64,704]{1,0:T(8,128)(2,1)S(1)}, bf16[64,704]{1,0:T(8,128)(2,1)S(1)}, u32[]{:S(2)}, u32[]{:S(2)}) collective-permute-start(bf16[64,704]{1,0:T(8,128)(2,1)S(1)} %get-tuple-element.107), channel_id=1, source_target_pairs={{0,1},{1,0},{2,3},{3,2},{4,5},{5,4},{6,7},{7,6},{8,9},{9,8},{10,11... | collective-permute-start | bytes 270344 | tf_op jit(solution)/shard_map/ppermute | solution.py:394
  100.6 7.0 %collective-permute-start.24 = (bf16[64,832]{1,0:T(8,128)(2,1)S(1)}, bf16[64,832]{1,0:T(8,128)(2,1)S(1)}, u32[]{:S(2)}, u32[]{:S(2)}) collective-permute-start(bf16[64,832]{1,0:T(8,128)(2,1)S(1)} %between.5.refs_0_.refs_4_), channel_id=1, source_target_pairs={{0,3},{1,2},{2,1},{3,0},{4,7},{5,6},{6,5},{7,4},{8,11},{9,10},{10,... | collective-permute-start | bytes 319496 | tf_op jit(solution)/shard_map/ppermute | solution.py:394
  102.6 7.0 %collective-permute-start.26 = (bf16[64,832]{1,0:T(8,128)(2,1)S(1)}, bf16[64,832]{1,0:T(8,128)(2,1)S(1)}, u32[]{:S(2)}, u32[]{:S(2)}) collective-permute-start(bf16[64,832]{1,0:T(8,128)(2,1)S(1)} %between.5.refs_0_.refs_4_), channel_id=1, source_target_pairs={{0,1},{1,0},{2,3},{3,2},{4,5},{5,4},{6,7},{7,6},{8,9},{9,8},{10,11... | collective-permute-start | bytes 319496 | tf_op jit(solution)/shard_map/ppermute | solution.py:394
  118.7 7.1 %collective-permute-start.28 = (bf16[64,704]{1,0:T(8,128)(2,1)S(1)}, bf16[64,704]{1,0:T(8,128)(2,1)S(1)}, u32[]{:S(2)}, u32[]{:S(2)}) collective-permute-start(bf16[64,704]{1,0:T(8,128)(2,1)S(1)} %get-tuple-element.115), channel_id=1, source_target_pairs={{0,2},{1,3},{2,0},{3,1},{4,6},{5,7},{6,4},{7,5},{8,10},{9,11},{10,... | collective-permute-start | bytes 270344 | tf_op jit(solution)/shard_map/ppermute | solution.py:394
  118.7 7.1 %collective-permute-start.29 = (bf16[64,704]{1,0:T(8,128)(2,1)S(1)}, bf16[64,704]{1,0:T(8,128)(2,1)S(1)}, u32[]{:S(2)}, u32[]{:S(2)}) collective-permute-start(bf16[64,704]{1,0:T(8,128)(2,1)S(1)} %get-tuple-element.116), channel_id=1, source_target_pairs={{0,1},{1,0},{2,3},{3,2},{4,5},{5,4},{6,7},{7,6},{8,9},{9,8},{10,11... | collective-permute-start | bytes 270344 | tf_op jit(solution)/shard_map/ppermute | solution.py:394
  (11 other events, 74.5 us)

commit v4 on v3

--- a/solution.py
+++ b/solution.py
@@ -24,6 +24,10 @@
 
 def in_hbm(array):
     return pltpu.with_memory_space_constraint(array, pltpu.HBM)
+
+
+def in_order(refs, order):
+    return [refs[order.index(block)] for block in range(len(order))]
 
 
 def copy_all(pairs, sems):
@@ -67,7 +71,7 @@
         dest = lax.div(slot, per_group)
         position = jnp.minimum(count[dest], capacity - 1)
         count[dest] = position + 1
-        target = lax.rem(dest - here + groups, groups) * capacity + position
+        target = jnp.bitwise_xor(dest, here) * capacity + position
         target_ref[row] = target
         place[pl.ds(row, 1), :] = jnp.where(places == target, 1.0, 0.0)
         length = length_ref[row].astype(f32)
@@ -120,27 +124,20 @@
         outgoing[s][...] = packed[s]
 
 
-def load_kernel(rank, *refs):
-    query, key, value, query_up, key_up, value_up, output, output_down, output_up, down = refs[:10]
-    inputs, *same, down_out = refs[10:18]
-    sems = refs[18]
-    total, kinds = down.shape[0], down.shape[1] // rank
+def load_inputs_kernel(query, key, value, after, inputs, sems):
     pairs = []
     column = 0
     for weight in (query, key, value):
         width = weight.shape[1]
         pairs.append((weight, inputs.at[:, column : column + width]))
         column += width
-    pairs += zip((query_up, key_up, value_up, output, output_down, output_up), same)
-    for kind in range(kinds):
-        for d in range(total):
-            pairs.append(
-                (
-                    down.at[d, kind * rank : (kind + 1) * rank, :],
-                    down_out.at[kind, d * rank : (d + 1) * rank, :],
-                )
-            )
     for copy in copy_all(pairs, sems):
+        copy.wait()
+
+
+def load_others_kernel(*refs):
+    count = (len(refs) - 2) // 2
+    for copy in copy_all(zip(refs[:count], refs[count + 1 : -1]), refs[-1]):
         copy.wait()
 
 
@@ -172,15 +169,28 @@
     return jnp.concatenate(picked, axis=1)
 
 
-def enter_kernel(total, rank, groups, *refs):
-    blocks = refs[:groups]
-    gain_ref, down_ref, send_ref, facts_ref = refs[groups:]
+def enter_kernel(total, rank, order, *refs):
+    groups = len(order)
+    blocks = in_order(refs[:groups], order)
+    gain_ref, down_hbm, send_ref, facts_ref, down_ref, sems = refs[groups:]
     width = down_ref.shape[2]
+    pairs = []
+    for kind in range(down_ref.shape[0]):
+        for d in range(total):
+            pairs.append(
+                (
+                    down_hbm.at[d, kind * rank : (kind + 1) * rank, :],
+                    down_ref.at[kind, d * rank : (d + 1) * rank, :],
+                )
+            )
+    copies = copy_all(pairs, sems)
     everything = jnp.concatenate([block[...] for block in blocks], axis=0)
     facts = everything[:, width:].astype(f32)
     own = own_slots(facts[:, 1:2], total, rank)
     facts_ref[...] = facts
     send_ref[:, :width] = everything[:, :width]
+    for copy in copies:
+        copy.wait()
     send_ref[:, width:] = partial_low(
         everything[:, :width].astype(f32), gain_ref[...], own, down_ref
     )
@@ -220,8 +230,8 @@
         outgoing[s][...] = state[s * capacity : (s + 1) * capacity]
 
 
-def restore_kernel(place_ref, *refs):
-    blocks, out_ref = refs[:-1], refs[-1]
+def restore_kernel(order, place_ref, *refs):
+    blocks, out_ref = in_order(refs[:-1], order), refs[-1]
     back = jnp.concatenate([block[...] for block in blocks], axis=0)
     out_ref[...] = jnp.dot(place_ref[...], back, preferred_element_type=f32).astype(bf16)
 
@@ -259,7 +269,8 @@
     low_ref[...] = low
 
 
-def step_kernel(total, rank, step, parts, masks, groups, *refs):
+def step_kernel(total, rank, step, parts, masks, order, *refs):
+    groups = len(order)
     refs = list(refs)
 
     def take(count):
@@ -285,7 +296,7 @@
         sine_ref,
         bias_ref,
     ) = take(15)
-    cache = take(groups)
+    cache = in_order(take(groups), order)
     earlier = take(2 * step)
     output_weight, output_down = take(2)
     outgoing = take(parts)
@@ -385,13 +396,12 @@
         outgoing[mask][:, width:] = low_out
 
 
-def shift(block, axis, by):
-    size = lax.axis_size(axis)
-    return lax.ppermute(block, axis, [(i, (i + by) % size) for i in range(size)])
-
-
 def swap(block, axis, mask):
     return lax.ppermute(block, axis, [(i, i ^ mask) for i in range(lax.axis_size(axis))])
+
+
+def swap_all(blocks, axis, order):
+    return [blocks[0]] + [swap(blocks[mask], axis, mask) for mask in order[1:]]
 
 
 def shards(
@@ -429,6 +439,7 @@
     features = input_norm_gain.shape[0]
     query_width = query_projection_weight.shape[1]
 
+    load_cost = pl.CostEstimate(flops=0, bytes_accessed=20000000, transcendentals=0)
     smem = pl.BlockSpec(memory_space=pltpu.SMEM)
     vmem = pl.BlockSpec(memory_space=pltpu.VMEM)
     hbm = pl.BlockSpec(memory_space=pltpu.HBM)
@@ -461,7 +472,8 @@
         in_hbm(cached_length_rows),
         in_hbm(hidden),
     )
-    arrived = [outgoing[0]] + [shift(outgoing[s], "wide", s) for s in range(1, groups)]
+    by_group = [0] + list(range(groups - 1, 0, -1))
+    arrived = swap_all(outgoing, "wide", by_group)
     packed_shape = (2 * kv_local, capacity, context, head_dim)
     packed = pl.pallas_call(
         pack_kernel,
@@ -477,54 +489,67 @@
         compiler_params=kernel_params(16),
         name="pack_cache",
     )(target, in_hbm(cached_key_rows), in_hbm(cached_value_rows))
-    cache = [packed[0]] + [shift(packed[s], "wide", s) for s in range(1, groups)]
+    cache = swap_all(packed, "wide", by_group)
     cache = [block.reshape(2 * kv_local, capacity * context, head_dim) for block in cache]
-
-    key_width = key_projection_weight.shape[1]
-    stored = [
-        (features, query_width + 2 * key_width),
-        (total * rank, query_width),
-        (total * rank, key_width),
-        (total * rank, key_width),
-        output_projection_weight.shape,
-        (total * rank, query_width),
-        (total * rank, width),
-        (low_width // rank, total * rank, width),
-    ]
-    weights = pl.pallas_call(
-        functools.partial(load_kernel, rank),
-        out_shape=[jax.ShapeDtypeStruct(shape, bf16) for shape in stored],
-        in_specs=[hbm] * 10,
-        out_specs=[vmem] * 8,
-        scratch_shapes=[pltpu.SemaphoreType.DMA((9 + total * low_width // rank,))],
-        compiler_params=kernel_params(24),
-        cost_estimate=pl.CostEstimate(flops=0, bytes_accessed=40000000, transcendentals=0),
-        name="load_weights",
-    )(
-        in_hbm(query_projection_weight),
-        in_hbm(key_projection_weight),
-        in_hbm(value_projection_weight),
-        in_hbm(query_up_factor.reshape(total * rank, query_width)),
-        in_hbm(key_up_factor.reshape(total * rank, key_width)),
-        in_hbm(value_up_factor.reshape(total * rank, key_width)),
-        in_hbm(output_projection_weight),
-        in_hbm(output_down_factor.reshape(total * rank, query_width)),
-        in_hbm(output_up_factor.reshape(total * rank, width)),
-        in_hbm(stacked_down_factors),
-    )
-    input_weight, query_up, key_up, value_up, output_weight, output_down, output_up, down = weights
 
     gain_rows = input_norm_gain.reshape(parts, 1, width)
     gain_slice = lax.dynamic_index_in_dim(gain_rows, narrow_index, 0, keepdims=False)
     sent_state = jax.ShapeDtypeStruct((rows, width + low_width), bf16)
-    send, facts_here = pl.pallas_call(
-        functools.partial(enter_kernel, total, rank, groups),
-        out_shape=[sent_state, jax.ShapeDtypeStruct((rows, 128), f32)],
-        in_specs=[vmem] * (groups + 2),
-        out_specs=[vmem] * 2,
+    kinds = low_width // rank
+    send, facts_here, down = pl.pallas_call(
+        functools.partial(enter_kernel, total, rank, by_group),
+        out_shape=[
+            sent_state,
+            jax.ShapeDtypeStruct((rows, 128), f32),
+            jax.ShapeDtypeStruct((kinds, total * rank, width), bf16),
+        ],
+        in_specs=[vmem] * (groups + 1) + [hbm],
+        out_specs=[vmem] * 3,
+        scratch_shapes=[pltpu.SemaphoreType.DMA((kinds * total,))],
         compiler_params=kernel_params(8),
         name="enter",
-    )(*arrived, gain_slice, down)
+    )(*arrived, gain_slice, in_hbm(stacked_down_factors))
+
+    key_width = key_projection_weight.shape[1]
+    input_width = query_width + 2 * key_width
+
+    def load_inputs(after):
+        return pl.pallas_call(
+            load_inputs_kernel,
+            out_shape=jax.ShapeDtypeStruct((features, input_width), bf16),
+            in_specs=[hbm] * 3 + [vmem],
+            out_specs=vmem,
+            scratch_shapes=[pltpu.SemaphoreType.DMA((3,))],
+            compiler_params=kernel_params(16),
+            cost_estimate=load_cost,
+            name="load_inputs",
+        )(
+            in_hbm(query_projection_weight),
+            in_hbm(key_projection_weight),
+            in_hbm(value_projection_weight),
+            after,
+        )
+
+    def load_others(after):
+        others = [
+            query_up_factor.reshape(total * rank, query_width),
+            key_up_factor.reshape(total * rank, key_width),
+            value_up_factor.reshape(total * rank, key_width),
+            output_projection_weight,
+            output_down_factor.reshape(total * rank, query_width),
+            output_up_factor.reshape(total * rank, width),
+        ]
+        return pl.pallas_call(
+            load_others_kernel,
+            out_shape=[jax.ShapeDtypeStruct(array.shape, bf16) for array in others],
+            in_specs=[hbm] * len(others) + [vmem],
+            out_specs=[vmem] * len(others),
+            scratch_shapes=[pltpu.SemaphoreType.DMA((len(others),))],
+            compiler_params=kernel_params(16),
+            cost_estimate=load_cost,
+            name="load_others",
+        )(*[in_hbm(array) for array in others], after)
+
     lengths = facts_here[:, 0]
     frequency = rope_base ** (-(jnp.arange(head_dim // 2, dtype=f32) * 2.0) / head_dim)
     positions = lengths[None, :] + jnp.arange(STEPS, dtype=f32)[:, None]
@@ -544,7 +569,7 @@
     index_here = narrow_index.reshape(1)
     sent_terms = jax.ShapeDtypeStruct((rows, width + rank), bf16)
     fresh = jax.ShapeDtypeStruct((kv_local, rows, head_dim), bf16)
-    far = [mask for mask in range(parts - 1, 1, -1) if mask % 2 == 1]
+    far = [mask for mask in range(2, parts) if mask % 2 == 0]
     early = [0, 1] + far
     late = [mask ^ 1 for mask in far]
 
@@ -553,10 +578,15 @@
         from_far = [swap(send, "narrow", mask) for mask in far]
         slices = [send, swap(send, "narrow", 1)] + from_far
         passed_on = [swap(piece, "narrow", 1) for piece in from_far]
+        if step == 0:
+            input_weight = load_inputs(facts_here)
+            query_up, key_up, value_up, output_weight, output_down, output_up = load_others(
+                from_far[0]
+            )
         sums = pl.pallas_call(
             functools.partial(early_kernel, early),
             out_shape=[
-                jax.ShapeDtypeStruct((rows, input_weight.shape[1]), f32),
+                jax.ShapeDtypeStruct((rows, input_width), f32),
                 jax.ShapeDtypeStruct((rows, 128), f32),
                 jax.ShapeDtypeStruct((rows, low_width), f32),
             ],
@@ -564,14 +594,14 @@
             out_specs=[vmem] * 3,
             compiler_params=kernel_params(16),
             cost_estimate=pl.CostEstimate(
-                flops=2 * rows * features * input_weight.shape[1],
+                flops=2 * rows * features * input_width,
                 bytes_accessed=10000000,
                 transcendentals=0,
             ),
             name="project_early",
         )(*slices, index_here, gain_rows, input_weight)
         *terms, key_fresh, value_fresh = pl.pallas_call(
-            functools.partial(step_kernel, total, rank, step, parts, late, groups),
+            functools.partial(step_kernel, total, rank, step, parts, late, by_group),
             out_shape=[sent_terms] * parts + [fresh] * 2,
             in_specs=[vmem] * len(late) + [smem] + [vmem] * (16 + groups + 2 * step),
             out_specs=[vmem] * (parts + 2),
@@ -602,7 +632,9 @@
             output_down,
         )
         earlier += [key_fresh, value_fresh]
-        received = [terms[0]] + [swap(terms[mask], "narrow", mask) for mask in range(parts - 1, 0, -1)]
+        received = swap_all(
+            terms, "narrow", [0] + far + [mask + 1 for mask in far] + [1]
+        )
         if step < STEPS - 1:
             send = pl.pallas_call(
                 functools.partial(between_kernel, total, rank, parts),
@@ -622,9 +654,9 @@
                 name="leave",
             )(*received, send, facts_here, output_up)
 
-    back = [leaving[0]] + [shift(leaving[s], "wide", -s) for s in range(1, groups)]
+    back = swap_all(leaving, "wide", by_group)
     return pl.pallas_call(
-        restore_kernel,
+        functools.partial(restore_kernel, by_group),
         out_shape=jax.ShapeDtypeStruct((row_group, width), bf16),
         in_specs=[vmem] * (groups + 1),
         out_specs=vmem,

time: 134 us -> 133 us (level)
  waiting for transfers between devices: 55.8 us -> 53.2 us
  Pallas kernels: 37.2 us -> 39.2 us
    ppermute x9 -> x0, starting transfers between devices: 10.3 us -> none  [shift(): lax.ppermute(block, axis, [(i, (i + by) % size) for i in range(size)])]
    ppermute x24 -> x33, starting transfers between devices: 28.7 us -> 37.7 us  [swap(): lax.ppermute(block, axis, [(i, i ^ mask) for i in range(lax.axis_size(axi...]
    ppermute x9 -> x0, waiting for transfers between devices: 3.06 us -> none  [shift(): lax.ppermute(block, axis, [(i, (i + by) % size) for i in range(size)])]
    pallas_call x3 -> x4, Pallas kernels: 8.09 us -> 10 us  [the longest x1 3.41 us: load_others(): pl.pallas_call(load_others_kernel, out_shape=[jax.ShapeDtypeStruct(array....]
    ppermute x24 -> x33, waiting for transfers between devices: 52.8 us -> 53.2 us  [swap(): lax.ppermute(block, axis, [(i, i ^ mask) for i in range(lax.axis_size(axi...]
  transfers between devices with their start and end apart: 33 -> 33, of which waited for: 21 -> 20; matrix products, arithmetic and copies ran while one was open for 1% -> 1% of each run, Pallas kernels for 11% -> 13%
where the time goes in v4:
time: 133 us; the launch traced here: 132 us
  waiting for transfers between devices  53.2 us (40%)
  Pallas kernels  39.2 us (29%)
  starting transfers between devices  37.7 us (28%)
    ppermute x33, waiting for transfers between devices, swap(): lax.ppermute(block, axis, [(i, i ^ mask) for i in range(lax.axis_size(axi...  53.2 us
    ppermute x33, starting transfers between devices, swap(): lax.ppermute(block, axis, [(i, i ^ mask) for i in range(lax.axis_size(axi...  37.7 us
    pallas_call x4, Pallas kernels, shards(): pl.pallas_call(functools.partial(step_kernel, total, rank, step, parts, l...  15.9 us
    pallas_call x4, Pallas kernels, shards(): pl.pallas_call(functools.partial(early_kernel, early), out_shape=[jax.Sha...  4.62 us
    pallas_call x1, Pallas kernels, load_others(): pl.pallas_call(load_others_kernel, out_shape=[jax.ShapeDtypeStruct(array....  3.41 us
    pallas_call x1, Pallas kernels, load_inputs(): pl.pallas_call(load_inputs_kernel, out_shape=jax.ShapeDtypeStruct((featur...  3.28 us
    pallas_call x3, Pallas kernels, shards(): pl.pallas_call(functools.partial(between_kernel, total, rank, parts), out...  2.97 us
    pallas_call x1, Pallas kernels, shards(): pl.pallas_call(pack_kernel, out_shape=[jax.ShapeDtypeStruct(packed_shape,...  2.74 us
  transfers between devices with their start and end apart: 33, of which 20 were waited for; matrix products, arithmetic and copies ran while one was open for 1% of the time, Pallas kernels for 13%

profile of v4, /device:TPU:0, one launch (start us, length us, event | category | flops | bytes accessed | tf_op | source)
XLA Modules:
  0.0 132.0 jit_solution(17820394530669677733)
XLA Ops:
  0.0 2.6 %route_rows.1 = (s32[64]{0:T(128)S(1)}, bf16[64,64]{1,0:T(8,128)(2,1)S(1)}, bf16[16,768]{1,0:T(8,128)(2,1)S(1)}, bf16[16,768]{1,0:T(8,128)(2,1)S(1)}, bf16[16,76...) custom-call(s32[1]{0:T(128)} %bitcast.group_ref, s32[256]{0:T(256)} %domain_hbm.1, s32[32]{0:T(128)} %slot_hbm.1, ...), custom_call_target="tpu_custom_call" | custom-call | tf_op jit(solution)/shard_map/route_rows/pallas_call | solution.py:447
  2.6 2.5 %collective-permute-start = (bf16[16,768]{1,0:T(8,128)(2,1)S(1)}, bf16[16,768]{1,0:T(8,128)(2,1)S(1)}, u32[]{:S(2)}, u32[]{:S(2)}) collective-permute-start(bf16[16,768]{1,0:T(8,128)(2,1)S(1)} %get-tuple-element.64), channel_id=1, source_target_pairs={{0,12},{4,8},{8,4},{12,0},{1,13},{5,9},{9,5},{13,1},{2,14},{6,10},... | collective-permute-start | bytes 73736 | tf_op jit(solution)/shard_map/ppermute | solution.py:400
  5.8 2.7 %pack_cache.1 = (bf16[4,16,24,128]{3,2,1,0:T(8,128)(2,1)S(1)}, bf16[4,16,24,128]{3,2,1,0:T(8,128)(2,1)S(1)}, bf16[4,16,24,128]{3,2,1,0:T(8,128)(2,1)S(1)}, bf16[4,16,24,128]{3,2,1,0:T(8,128)(2,1)S(1)}) custom-call(s32[64]{0:T(128)S(1)} %get-tuple-element.75.target_ref, bf16[64,2,24,128]{3,2,1,0:T(8,128)(2,1)} %key_hbm.1, bf16[64,2,24,128]{3,2,1,0:T(8,128)(2,1)} %value_hbm.1), custom_call_target="tpu_custom_call" | custom-call | tf_op jit(solution)/shard_map/pack_cache/pallas_call | solution.py:478
  11.6 2.6 %enter.1 = (bf16[64,832]{1,0:T(8,128)(2,1)S(1)}, f32[64,128]{1,0:T(8,128)S(1)}, bf16[3,512,640]{2,1,0:T(8,128)(2,1)S(1)}) custom-call(bf16[16,768]{1,0:T(8,128)(2,1)S(1)} %get-tuple-element.63.refs_0_, bf16[16,768]{1,0:T(8,128)(2,1)S(1)} %collective-permute-done.refs_1_, bf16[16,768]{1,0:T(8,128)(2,1)S(1)} %collective-permute-done.1.refs_2_, ...), custom_call_target="tpu_custom_call" | custom-call | tf_op jit(solution)/shard_map/enter/pallas_call | solution.py:499
  15.8 2.6 %collective-permute-start.3 = (bf16[64,832]{1,0:T(8,128)(2,1)S(1)}, bf16[64,832]{1,0:T(8,128)(2,1)S(1)}, u32[]{:S(2)}, u32[]{:S(2)}) collective-permute-start(bf16[64,832]{1,0:T(8,128)(2,1)S(1)} %get-tuple-element.67.refs_0_.refs_4_), channel_id=1, source_target_pairs={{0,2},{1,3},{2,0},{3,1},{4,6},{5,7},{6,4},{7,5},{8,10},{9,11},{10,... | collective-permute-start | bytes 319496 | tf_op jit(solution)/shard_map/ppermute | solution.py:400
  19.2 5.3 %collective-permute-done.3.refs_2_.refs_6_ = bf16[64,832]{1,0:T(8,128)(2,1)S(1)} collective-permute-done((bf16[64,832]{1,0:T(8,128)(2,1)S(1)}, bf16[64,832]{1,0:T(8,128)(2,1)S(1)}, u32[]{:S(2)}, u32[]{:S(2)}) %collective-permute-start.3) | collective-permute-done | bytes 106528 | tf_op jit(solution)/shard_map/ppermute | solution.py:400
  25.1 3.3 %load_inputs.1.refs_5_.refs_7_ = bf16[2560,1536]{1,0:T(8,128)(2,1)S(1)} custom-call(bf16[2560,1024]{1,0:T(8,128)(2,1)} %query.1, bf16[2560,256]{1,0:T(8,128)(2,1)} %key.1, bf16[2560,256]{1,0:T(8,128)(2,1)} %value.1, f32[64,128]{1,0:T(8,128)S(1)} %get-tuple-element.68.after.refs_5_), custom_call_target="tpu_custom_call" | custom-call | bytes 20000000 | tf_op jit(solution)/shard_map/load_inputs/pallas_call | solution.py:517
  28.3 3.4 %load_others.1 = (bf16[512,1024]{1,0:T(8,128)(2,1)S(1)}, bf16[512,256]{1,0:T(8,128)(2,1)S(1)}, bf16[512,256]{1,0:T(8,128)(2,1)S(1)}, bf16[1024,2560]{1,0:T(8,128...) custom-call(bf16[512,1024]{1,0:T(8,128)(2,1)} %bitcast.39, bf16[512,256]{1,0:T(8,128)(2,1)} %bitcast.42, ...), custom_call_target="tpu_custom_call" | custom-call | bytes 20000000 | tf_op jit(solution)/shard_map/load_others/pallas_call | solution.py:542
  33.0 3.8 %attend_step.4 = (bf16[64,704]{1,0:T(8,128)(2,1)S(1)}, bf16[64,704]{1,0:T(8,128)(2,1)S(1)}, bf16[64,704]{1,0:T(8,128)(2,1)S(1)}, bf16[64,704]{1,0:T(8,128)(2,1)S...) custom-call(bf16[64,832]{1,0:T(8,128)(2,1)S(1)} %collective-permute-done.4.refs_0_, ...), custom_call_target="tpu_custom_call" | custom-call | tf_op jit(solution)/shard_map/attend_step/pallas_call | solution.py:603
  36.8 2.7 %collective-permute-start.9 = (bf16[64,704]{1,0:T(8,128)(2,1)S(1)}, bf16[64,704]{1,0:T(8,128)(2,1)S(1)}, u32[]{:S(2)}, u32[]{:S(2)}) collective-permute-start(bf16[64,704]{1,0:T(8,128)(2,1)S(1)} %get-tuple-element.83), channel_id=1, source_target_pairs={{0,2},{1,3},{2,0},{3,1},{4,6},{5,7},{6,4},{7,5},{8,10},{9,11},{10,... | collective-permute-start | bytes 270344 | tf_op jit(solution)/shard_map/ppermute | solution.py:400
  40.8 5.9 %collective-permute-done.9.refs_1_ = bf16[64,704]{1,0:T(8,128)(2,1)S(1)} collective-permute-done((bf16[64,704]{1,0:T(8,128)(2,1)S(1)}, bf16[64,704]{1,0:T(8,128)(2,1)S(1)}, u32[]{:S(2)}, u32[]{:S(2)}) %collective-permute-start.9) | collective-permute-done | bytes 90144 | tf_op jit(solution)/shard_map/ppermute | solution.py:400
  51.3 3.4 %collective-permute-done.12.refs_2_ = bf16[64,832]{1,0:T(8,128)(2,1)S(1)} collective-permute-done((bf16[64,832]{1,0:T(8,128)(2,1)S(1)}, bf16[64,832]{1,0:T(8,128)(2,1)S(1)}, u32[]{:S(2)}, u32[]{:S(2)}) %collective-permute-start.12) | collective-permute-done | bytes 106528 | tf_op jit(solution)/shard_map/ppermute | solution.py:400
  59.6 3.8 %attend_step.5 = (bf16[64,704]{1,0:T(8,128)(2,1)S(1)}, bf16[64,704]{1,0:T(8,128)(2,1)S(1)}, bf16[64,704]{1,0:T(8,128)(2,1)S(1)}, bf16[64,704]{1,0:T(8,128)(2,1)S...) custom-call(bf16[64,832]{1,0:T(8,128)(2,1)S(1)} %collective-permute-done.13.refs_0_, ...), custom_call_target="tpu_custom_call" | custom-call | tf_op jit(solution)/shard_map/attend_step/pallas_call | solution.py:603
  67.0 3.5 %collective-permute-done.15.refs_1_ = bf16[64,704]{1,0:T(8,128)(2,1)S(1)} collective-permute-done((bf16[64,704]{1,0:T(8,128)(2,1)S(1)}, bf16[64,704]{1,0:T(8,128)(2,1)S(1)}, u32[]{:S(2)}, u32[]{:S(2)}) %collective-permute-start.15) | collective-permute-done | bytes 90144 | tf_op jit(solution)/shard_map/ppermute | solution.py:400
  76.4 4.3 %collective-permute-done.18.refs_2_ = bf16[64,832]{1,0:T(8,128)(2,1)S(1)} collective-permute-done((bf16[64,832]{1,0:T(8,128)(2,1)S(1)}, bf16[64,832]{1,0:T(8,128)(2,1)S(1)}, u32[]{:S(2)}, u32[]{:S(2)}) %collective-permute-start.18) | collective-permute-done | bytes 106528 | tf_op jit(solution)/shard_map/ppermute | solution.py:400
  83.1 2.4 %collective-permute-done.19.refs_0_ = bf16[64,832]{1,0:T(8,128)(2,1)S(1)} collective-permute-done((bf16[64,832]{1,0:T(8,128)(2,1)S(1)}, bf16[64,832]{1,0:T(8,128)(2,1)S(1)}, u32[]{:S(2)}, u32[]{:S(2)}) %collective-permute-start.19) | collective-permute-done | bytes 106528 | tf_op jit(solution)/shard_map/ppermute | solution.py:400
  85.5 4.0 %attend_step.6 = (bf16[64,704]{1,0:T(8,128)(2,1)S(1)}, bf16[64,704]{1,0:T(8,128)(2,1)S(1)}, bf16[64,704]{1,0:T(8,128)(2,1)S(1)}, bf16[64,704]{1,0:T(8,128)(2,1)S...) custom-call(bf16[64,832]{1,0:T(8,128)(2,1)S(1)} %collective-permute-done.19.refs_0_, ...), custom_call_target="tpu_custom_call" | custom-call | tf_op jit(solution)/shard_map/attend_step/pallas_call | solution.py:603
  93.0 4.2 %collective-permute-done.21.refs_1_ = bf16[64,704]{1,0:T(8,128)(2,1)S(1)} collective-permute-done((bf16[64,704]{1,0:T(8,128)(2,1)S(1)}, bf16[64,704]{1,0:T(8,128)(2,1)S(1)}, u32[]{:S(2)}, u32[]{:S(2)}) %collective-permute-start.21) | collective-permute-done | bytes 90144 | tf_op jit(solution)/shard_map/ppermute | solution.py:400
  97.2 2.7 %collective-permute-done.23.refs_3_ = bf16[64,704]{1,0:T(8,128)(2,1)S(1)} collective-permute-done((bf16[64,704]{1,0:T(8,128)(2,1)S(1)}, bf16[64,704]{1,0:T(8,128)(2,1)S(1)}, u32[]{:S(2)}, u32[]{:S(2)}) %collective-permute-start.23) | collective-permute-done | bytes 90144 | tf_op jit(solution)/shard_map/ppermute | solution.py:400
  103.2 4.6 %collective-permute-done.24.refs_2_ = bf16[64,832]{1,0:T(8,128)(2,1)S(1)} collective-permute-done((bf16[64,832]{1,0:T(8,128)(2,1)S(1)}, bf16[64,832]{1,0:T(8,128)(2,1)S(1)}, u32[]{:S(2)}, u32[]{:S(2)}) %collective-permute-start.24) | collective-permute-done | bytes 106528 | tf_op jit(solution)/shard_map/ppermute | solution.py:400
  109.0 4.5 %collective-permute-done.25.refs_0_ = bf16[64,832]{1,0:T(8,128)(2,1)S(1)} collective-permute-done((bf16[64,832]{1,0:T(8,128)(2,1)S(1)}, bf16[64,832]{1,0:T(8,128)(2,1)S(1)}, u32[]{:S(2)}, u32[]{:S(2)}) %collective-permute-start.25) | collective-permute-done | bytes 106528 | tf_op jit(solution)/shard_map/ppermute | solution.py:400
  113.5 4.3 %attend_step.7 = (bf16[64,704]{1,0:T(8,128)(2,1)S(1)}, bf16[64,704]{1,0:T(8,128)(2,1)S(1)}, bf16[64,704]{1,0:T(8,128)(2,1)S(1)}, bf16[64,704]{1,0:T(8,128)(2,1)S...) custom-call(bf16[64,832]{1,0:T(8,128)(2,1)S(1)} %collective-permute-done.25.refs_0_, ...), custom_call_target="tpu_custom_call" | custom-call | tf_op jit(solution)/shard_map/attend_step/pallas_call | solution.py:603
  121.3 3.8 %collective-permute-done.27.refs_1_ = bf16[64,704]{1,0:T(8,128)(2,1)S(1)} collective-permute-done((bf16[64,704]{1,0:T(8,128)(2,1)S(1)}, bf16[64,704]{1,0:T(8,128)(2,1)S(1)}, u32[]{:S(2)}, u32[]{:S(2)}) %collective-permute-start.27) | collective-permute-done | bytes 90144 | tf_op jit(solution)/shard_map/ppermute | solution.py:400
  126.4 2.9 %collective-permute-start.31 = (bf16[16,640]{1,0:T(8,128)(2,1)S(1)}, bf16[16,640]{1,0:T(8,128)(2,1)S(1)}, u32[]{:S(2)}, u32[]{:S(2)}) collective-permute-start(bf16[16,640]{1,0:T(8,128)(2,1)S(1)} %get-tuple-element.117), channel_id=1, source_target_pairs={{0,8},{4,12},{8,0},{12,4},{1,9},{5,13},{9,1},{13,5},{2,10},{6,14},... | collective-permute-start | bytes 61448 | tf_op jit(solution)/shard_map/ppermute | solution.py:400
  (74 shorter events, 46.1 us)
Async XLA Ops:
  2.6 8.8 %collective-permute-start = (bf16[16,768]{1,0:T(8,128)(2,1)S(1)}, bf16[16,768]{1,0:T(8,128)(2,1)S(1)}, u32[]{:S(2)}, u32[]{:S(2)}) collective-permute-start(bf16[16,768]{1,0:T(8,128)(2,1)S(1)} %get-tuple-element.64), channel_id=1, source_target_pairs={{0,12},{4,8},{8,4},{12,0},{1,13},{5,9},{9,5},{13,1},{2,14},{6,10},... | collective-permute-start | bytes 73736 | tf_op jit(solution)/shard_map/ppermute | solution.py:400
  5.1 6.5 %collective-permute-start.1 = (bf16[16,768]{1,0:T(8,128)(2,1)S(1)}, bf16[16,768]{1,0:T(8,128)(2,1)S(1)}, u32[]{:S(2)}, u32[]{:S(2)}) collective-permute-start(bf16[16,768]{1,0:T(8,128)(2,1)S(1)} %get-tuple-element.65), channel_id=1, source_target_pairs={{0,8},{4,12},{8,0},{12,4},{1,9},{5,13},{9,1},{13,5},{2,10},{6,14},... | collective-permute-start | bytes 73736 | tf_op jit(solution)/shard_map/ppermute | solution.py:400
  5.7 5.8 %collective-permute-start.2 = (bf16[16,768]{1,0:T(8,128)(2,1)S(1)}, bf16[16,768]{1,0:T(8,128)(2,1)S(1)}, u32[]{:S(2)}, u32[]{:S(2)}) collective-permute-start(bf16[16,768]{1,0:T(8,128)(2,1)S(1)} %get-tuple-element.66), channel_id=1, source_target_pairs={{0,4},{4,0},{8,12},{12,8},{1,5},{5,1},{9,13},{13,9},{2,6},{6,2},{1... | collective-permute-start | bytes 73736 | tf_op jit(solution)/shard_map/ppermute | solution.py:400
  8.5 24.4 %collective-permute-start.6 = (bf16[4,16,24,128]{3,2,1,0:T(8,128)(2,1)S(1)}, bf16[4,16,24,128]{3,2,1,0:T(8,128)(2,1)S(1)}, u32[]{:S(2)}, u32[]{:S(2)}) collective-permute-start(bf16[4,16,24,128]{3,2,1,0:T(8,128)(2,1)S(1)} %get-tuple-element.77), channel_id=1, source_target_pairs={{0,12},{4,8},{8,4},{12,0},{1,13},{5,9},{9,5},{13,1},{2,14},{6,10},... | collective-permute-start | bytes 1179656 | tf_op jit(solution)/shard_map/ppermute | solution.py:400
  10.1 22.9 %collective-permute-start.7 = (bf16[4,16,24,128]{3,2,1,0:T(8,128)(2,1)S(1)}, bf16[4,16,24,128]{3,2,1,0:T(8,128)(2,1)S(1)}, u32[]{:S(2)}, u32[]{:S(2)}) collective-permute-start(bf16[4,16,24,128]{3,2,1,0:T(8,128)(2,1)S(1)} %get-tuple-element.78), channel_id=1, source_target_pairs={{0,8},{4,12},{8,0},{12,4},{1,9},{5,13},{9,1},{13,5},{2,10},{6,14},... | collective-permute-start | bytes 1179656 | tf_op jit(solution)/shard_map/ppermute | solution.py:400
  11.5 21.5 %collective-permute-start.8 = (bf16[4,16,24,128]{3,2,1,0:T(8,128)(2,1)S(1)}, bf16[4,16,24,128]{3,2,1,0:T(8,128)(2,1)S(1)}, u32[]{:S(2)}, u32[]{:S(2)}) collective-permute-start(bf16[4,16,24,128]{3,2,1,0:T(8,128)(2,1)S(1)} %get-tuple-element.79), channel_id=1, source_target_pairs={{0,4},{4,0},{8,12},{12,8},{1,5},{5,1},{9,13},{13,9},{2,6},{6,2},{1... | collective-permute-start | bytes 1179656 | tf_op jit(solution)/shard_map/ppermute | solution.py:400
  14.2 17.6 %collective-permute-start.5 = (bf16[64,832]{1,0:T(8,128)(2,1)S(1)}, bf16[64,832]{1,0:T(8,128)(2,1)S(1)}, u32[]{:S(2)}, u32[]{:S(2)}) collective-permute-start(bf16[64,832]{1,0:T(8,128)(2,1)S(1)} %get-tuple-element.67.refs_0_.refs_4_), channel_id=1, source_target_pairs={{0,1},{1,0},{2,3},{3,2},{4,5},{5,4},{6,7},{7,6},{8,9},{9,8},{10,11... | collective-permute-start | bytes 319496 | tf_op jit(solution)/shard_map/ppermute | solution.py:400
  15.8 8.6 %collective-permute-start.3 = (bf16[64,832]{1,0:T(8,128)(2,1)S(1)}, bf16[64,832]{1,0:T(8,128)(2,1)S(1)}, u32[]{:S(2)}, u32[]{:S(2)}) collective-permute-start(bf16[64,832]{1,0:T(8,128)(2,1)S(1)} %get-tuple-element.67.refs_0_.refs_4_), channel_id=1, source_target_pairs={{0,2},{1,3},{2,0},{3,1},{4,6},{5,7},{6,4},{7,5},{8,10},{9,11},{10,... | collective-permute-start | bytes 319496 | tf_op jit(solution)/shard_map/ppermute | solution.py:400
  24.5 8.5 %collective-permute-start.4 = (bf16[64,832]{1,0:T(8,128)(2,1)S(1)}, bf16[64,832]{1,0:T(8,128)(2,1)S(1)}, u32[]{:S(2)}, u32[]{:S(2)}) collective-permute-start(bf16[64,832]{1,0:T(8,128)(2,1)S(1)} %collective-permute-done.3.refs_2_.refs_6_), channel_id=1, source_target_pairs={{0,1},{1,0},{2,3},{3,2},{4,5},{5,4},{6,7},{7,6},{8,9},{9,8},{10,11... | collective-permute-start | bytes 319496 | tf_op jit(solution)/shard_map/ppermute | solution.py:400
  36.8 9.9 %collective-permute-start.9 = (bf16[64,704]{1,0:T(8,128)(2,1)S(1)}, bf16[64,704]{1,0:T(8,128)(2,1)S(1)}, u32[]{:S(2)}, u32[]{:S(2)}) collective-permute-start(bf16[64,704]{1,0:T(8,128)(2,1)S(1)} %get-tuple-element.83), channel_id=1, source_target_pairs={{0,2},{1,3},{2,0},{3,1},{4,6},{5,7},{6,4},{7,5},{8,10},{9,11},{10,... | collective-permute-start | bytes 270344 | tf_op jit(solution)/shard_map/ppermute | solution.py:400
  39.5 7.2 %collective-permute-start.10 = (bf16[64,704]{1,0:T(8,128)(2,1)S(1)}, bf16[64,704]{1,0:T(8,128)(2,1)S(1)}, u32[]{:S(2)}, u32[]{:S(2)}) collective-permute-start(bf16[64,704]{1,0:T(8,128)(2,1)S(1)} %get-tuple-element.84), channel_id=1, source_target_pairs={{0,3},{1,2},{2,1},{3,0},{4,7},{5,6},{6,5},{7,4},{8,11},{9,10},{10,... | collective-permute-start | bytes 270344 | tf_op jit(solution)/shard_map/ppermute | solution.py:400
  40.8 6.4 %collective-permute-start.11 = (bf16[64,704]{1,0:T(8,128)(2,1)S(1)}, bf16[64,704]{1,0:T(8,128)(2,1)S(1)}, u32[]{:S(2)}, u32[]{:S(2)}) collective-permute-start(bf16[64,704]{1,0:T(8,128)(2,1)S(1)} %get-tuple-element.85), channel_id=1, source_target_pairs={{0,1},{1,0},{2,3},{3,2},{4,5},{5,4},{6,7},{7,6},{8,9},{9,8},{10,11... | collective-permute-start | bytes 270344 | tf_op jit(solution)/shard_map/ppermute | solution.py:400
  48.2 6.5 %collective-permute-start.12 = (bf16[64,832]{1,0:T(8,128)(2,1)S(1)}, bf16[64,832]{1,0:T(8,128)(2,1)S(1)}, u32[]{:S(2)}, u32[]{:S(2)}) collective-permute-start(bf16[64,832]{1,0:T(8,128)(2,1)S(1)} %between.3.refs_0_.refs_4_), channel_id=1, source_target_pairs={{0,2},{1,3},{2,0},{3,1},{4,6},{5,7},{6,4},{7,5},{8,10},{9,11},{10,... | collective-permute-start | bytes 319496 | tf_op jit(solution)/shard_map/ppermute | solution.py:400
  50.4 6.3 %collective-permute-start.14 = (bf16[64,832]{1,0:T(8,128)(2,1)S(1)}, bf16[64,832]{1,0:T(8,128)(2,1)S(1)}, u32[]{:S(2)}, u32[]{:S(2)}) collective-permute-start(bf16[64,832]{1,0:T(8,128)(2,1)S(1)} %between.3.refs_0_.refs_4_), channel_id=1, source_target_pairs={{0,1},{1,0},{2,3},{3,2},{4,5},{5,4},{6,7},{7,6},{8,9},{9,8},{10,11... | collective-permute-start | bytes 319496 | tf_op jit(solution)/shard_map/ppermute | solution.py:400
  63.4 7.2 %collective-permute-start.15 = (bf16[64,704]{1,0:T(8,128)(2,1)S(1)}, bf16[64,704]{1,0:T(8,128)(2,1)S(1)}, u32[]{:S(2)}, u32[]{:S(2)}) collective-permute-start(bf16[64,704]{1,0:T(8,128)(2,1)S(1)} %get-tuple-element.94), channel_id=1, source_target_pairs={{0,2},{1,3},{2,0},{3,1},{4,6},{5,7},{6,4},{7,5},{8,10},{9,11},{10,... | collective-permute-start | bytes 270344 | tf_op jit(solution)/shard_map/ppermute | solution.py:400
  65.1 6.6 %collective-permute-start.16 = (bf16[64,704]{1,0:T(8,128)(2,1)S(1)}, bf16[64,704]{1,0:T(8,128)(2,1)S(1)}, u32[]{:S(2)}, u32[]{:S(2)}) collective-permute-start(bf16[64,704]{1,0:T(8,128)(2,1)S(1)} %get-tuple-element.95), channel_id=1, source_target_pairs={{0,3},{1,2},{2,1},{3,0},{4,7},{5,6},{6,5},{7,4},{8,11},{9,10},{10,... | collective-permute-start | bytes 270344 | tf_op jit(solution)/shard_map/ppermute | solution.py:400
  73.6 7.1 %collective-permute-start.18 = (bf16[64,832]{1,0:T(8,128)(2,1)S(1)}, bf16[64,832]{1,0:T(8,128)(2,1)S(1)}, u32[]{:S(2)}, u32[]{:S(2)}) collective-permute-start(bf16[64,832]{1,0:T(8,128)(2,1)S(1)} %between.4.refs_0_.refs_4_), channel_id=1, source_target_pairs={{0,2},{1,3},{2,0},{3,1},{4,6},{5,7},{6,4},{7,5},{8,10},{9,11},{10,... | collective-permute-start | bytes 319496 | tf_op jit(solution)/shard_map/ppermute | solution.py:400
  74.9 7.0 %collective-permute-start.20 = (bf16[64,832]{1,0:T(8,128)(2,1)S(1)}, bf16[64,832]{1,0:T(8,128)(2,1)S(1)}, u32[]{:S(2)}, u32[]{:S(2)}) collective-permute-start(bf16[64,832]{1,0:T(8,128)(2,1)S(1)} %between.4.refs_0_.refs_4_), channel_id=1, source_target_pairs={{0,1},{1,0},{2,3},{3,2},{4,5},{5,4},{6,7},{7,6},{8,9},{9,8},{10,11... | collective-permute-start | bytes 319496 | tf_op jit(solution)/shard_map/ppermute | solution.py:400
  89.5 7.7 %collective-permute-start.21 = (bf16[64,704]{1,0:T(8,128)(2,1)S(1)}, bf16[64,704]{1,0:T(8,128)(2,1)S(1)}, u32[]{:S(2)}, u32[]{:S(2)}) collective-permute-start(bf16[64,704]{1,0:T(8,128)(2,1)S(1)} %get-tuple-element.103), channel_id=1, source_target_pairs={{0,2},{1,3},{2,0},{3,1},{4,6},{5,7},{6,4},{7,5},{8,10},{9,11},{10,... | collective-permute-start | bytes 270344 | tf_op jit(solution)/shard_map/ppermute | solution.py:400
  90.5 6.7 %collective-permute-start.22 = (bf16[64,704]{1,0:T(8,128)(2,1)S(1)}, bf16[64,704]{1,0:T(8,128)(2,1)S(1)}, u32[]{:S(2)}, u32[]{:S(2)}) collective-permute-start(bf16[64,704]{1,0:T(8,128)(2,1)S(1)} %get-tuple-element.104), channel_id=1, source_target_pairs={{0,3},{1,2},{2,1},{3,0},{4,7},{5,6},{6,5},{7,4},{8,11},{9,10},{10,... | collective-permute-start | bytes 270344 | tf_op jit(solution)/shard_map/ppermute | solution.py:400
  92.4 7.5 %collective-permute-start.23 = (bf16[64,704]{1,0:T(8,128)(2,1)S(1)}, bf16[64,704]{1,0:T(8,128)(2,1)S(1)}, u32[]{:S(2)}, u32[]{:S(2)}) collective-permute-start(bf16[64,704]{1,0:T(8,128)(2,1)S(1)} %get-tuple-element.105), channel_id=1, source_target_pairs={{0,1},{1,0},{2,3},{3,2},{4,5},{5,4},{6,7},{7,6},{8,9},{9,8},{10,11... | collective-permute-start | bytes 270344 | tf_op jit(solution)/shard_map/ppermute | solution.py:400
  100.9 7.0 %collective-permute-start.24 = (bf16[64,832]{1,0:T(8,128)(2,1)S(1)}, bf16[64,832]{1,0:T(8,128)(2,1)S(1)}, u32[]{:S(2)}, u32[]{:S(2)}) collective-permute-start(bf16[64,832]{1,0:T(8,128)(2,1)S(1)} %between.5.refs_0_.refs_4_), channel_id=1, source_target_pairs={{0,2},{1,3},{2,0},{3,1},{4,6},{5,7},{6,4},{7,5},{8,10},{9,11},{10,... | collective-permute-start | bytes 319496 | tf_op jit(solution)/shard_map/ppermute | solution.py:400
  117.8 7.3 %collective-permute-start.27 = (bf16[64,704]{1,0:T(8,128)(2,1)S(1)}, bf16[64,704]{1,0:T(8,128)(2,1)S(1)}, u32[]{:S(2)}, u32[]{:S(2)}) collective-permute-start(bf16[64,704]{1,0:T(8,128)(2,1)S(1)} %get-tuple-element.112), channel_id=1, source_target_pairs={{0,2},{1,3},{2,0},{3,1},{4,6},{5,7},{6,4},{7,5},{8,10},{9,11},{10,... | collective-permute-start | bytes 270344 | tf_op jit(solution)/shard_map/ppermute | solution.py:400
  118.3 6.8 %collective-permute-start.28 = (bf16[64,704]{1,0:T(8,128)(2,1)S(1)}, bf16[64,704]{1,0:T(8,128)(2,1)S(1)}, u32[]{:S(2)}, u32[]{:S(2)}) collective-permute-start(bf16[64,704]{1,0:T(8,128)(2,1)S(1)} %get-tuple-element.113), channel_id=1, source_target_pairs={{0,3},{1,2},{2,1},{3,0},{4,7},{5,6},{6,5},{7,4},{8,11},{9,10},{10,... | collective-permute-start | bytes 270344 | tf_op jit(solution)/shard_map/ppermute | solution.py:400
  (11 other events, 44.7 us)

commit v5 on v4

--- a/solution.py
+++ b/solution.py
@@ -16,6 +16,7 @@
 bf16 = jnp.bfloat16
 
 NT = (((1,), (1,)), ((), ()))
+NN = (((1,), (0,)), ((), ()))
 
 
 def kernel_params(mib):
@@ -98,16 +99,28 @@
         outgoing[s][:, width:] = known[block]
 
 
-def pack_kernel(target_ref, key_hbm, value_hbm, *refs):
-    groups = len(refs) - 4
+def pack_kernel(target_ref, key_hbm, value_hbm, down_hbm, *refs):
+    groups = len(refs) - 5
     outgoing = refs[:groups]
-    packed, key_ref, value_ref, sems = refs[groups:]
+    down_ref, packed, key_ref, value_ref, sems = refs[groups:]
     rows, kv_local = key_ref.shape[:2]
     capacity = packed.shape[2]
-    copies = copy_all([(key_hbm, key_ref), (value_hbm, value_ref)], sems)
+    kinds = down_ref.shape[0]
+    total = down_hbm.shape[0]
+    rank = down_hbm.shape[1] // kinds
+    pairs = [(key_hbm, key_ref), (value_hbm, value_ref)]
+    for kind in range(kinds):
+        for d in range(total):
+            pairs.append(
+                (
+                    down_hbm.at[d, kind * rank : (kind + 1) * rank, :],
+                    down_ref.at[kind, d * rank : (d + 1) * rank, :],
+                )
+            )
+    copies = copy_all(pairs, sems)
     if groups * capacity > rows:
         packed[...] = jnp.zeros_like(packed)
-    for copy in copies:
+    for copy in copies[:2]:
         copy.wait()
 
     def put(row, carry):
@@ -122,6 +135,8 @@
     lax.fori_loop(0, rows, put, 0)
     for s in range(groups):
         outgoing[s][...] = packed[s]
+    for copy in copies[2:]:
+        copy.wait()
 
 
 def load_inputs_kernel(query, key, value, after, inputs, sems):
@@ -136,8 +151,16 @@
 
 
 def load_others_kernel(*refs):
-    count = (len(refs) - 2) // 2
-    for copy in copy_all(zip(refs[:count], refs[count + 1 : -1]), refs[-1]):
+    count = (len(refs) - 4) // 2 - 1
+    sources, output_down, down, _ = refs[:count], *refs[count : count + 3]
+    targets = refs[count + 3 : 2 * count + 3]
+    output_down_across, down_across, held, sems = refs[2 * count + 3 :]
+    copies = copy_all([(output_down, held), *zip(sources, targets)], sems)
+    for kind in range(down.shape[0]):
+        down_across[kind] = down[kind].T
+    copies[0].wait()
+    output_down_across[...] = held[...].T
+    for copy in copies[1:]:
         copy.wait()
 
 
@@ -160,11 +183,11 @@
     return picked[:, : wide // 2] + picked[:, wide // 2 :]
 
 
-def partial_low(state, gain, own, down_ref):
+def partial_low(state, gain, own, down_ref, form):
     scaled = (state * gain).astype(bf16)
     picked = []
     for kind in range(down_ref.shape[0]):
-        product = lax.dot_general(scaled, down_ref[kind], NT, preferred_element_type=f32)
+        product = lax.dot_general(scaled, down_ref[kind], form, preferred_element_type=f32)
         picked.append(pick_slot(product, own).astype(bf16))
     return jnp.concatenate(picked, axis=1)
 
@@ -172,27 +195,15 @@
 def enter_kernel(total, rank, order, *refs):
     groups = len(order)
     blocks = in_order(refs[:groups], order)
-    gain_ref, down_hbm, send_ref, facts_ref, down_ref, sems = refs[groups:]
+    gain_ref, down_ref, send_ref, facts_ref = refs[groups:]
     width = down_ref.shape[2]
-    pairs = []
-    for kind in range(down_ref.shape[0]):
-        for d in range(total):
-            pairs.append(
-                (
-                    down_hbm.at[d, kind * rank : (kind + 1) * rank, :],
-                    down_ref.at[kind, d * rank : (d + 1) * rank, :],
-                )
-            )
-    copies = copy_all(pairs, sems)
     everything = jnp.concatenate([block[...] for block in blocks], axis=0)
     facts = everything[:, width:].astype(f32)
     own = own_slots(facts[:, 1:2], total, rank)
     facts_ref[...] = facts
     send_ref[:, :width] = everything[:, :width]
-    for copy in copies:
-        copy.wait()
     send_ref[:, width:] = partial_low(
-        everything[:, :width].astype(f32), gain_ref[...], own, down_ref
+        everything[:, :width].astype(f32), gain_ref[...], own, down_ref, NT
     )
 
 
@@ -211,11 +222,11 @@
 def between_kernel(total, rank, parts, *refs):
     received = refs[:parts]
     state_ref, facts_ref, up_ref, gain_ref, down_ref, send_ref = refs[parts:]
-    width = down_ref.shape[2]
+    width = down_ref.shape[1]
     own = own_slots(facts_ref[:, 1:2], total, rank)
     state = new_state(own, received, state_ref[:, :width], up_ref)
     send_ref[:, :width] = state
-    send_ref[:, width:] = partial_low(state.astype(f32), gain_ref[...], own, down_ref)
+    send_ref[:, width:] = partial_low(state.astype(f32), gain_ref[...], own, down_ref, NN)
 
 
 def leave_kernel(total, rank, parts, *refs):
@@ -345,35 +356,43 @@
     key_place = lax.broadcasted_iota(jnp.int32, (per_kv * capacity, lanes), 1)
     own_row = lax.broadcasted_iota(jnp.int32, (per_kv * capacity, lanes), 0) % capacity
     same_row = (key_place % capacity == own_row) & (key_place < fresh_count)
-    cached_count = bias_ref.shape[1]
-    for b in range(groups):
-        block = slice(b * capacity, (b + 1) * capacity)
-        bias = jnp.concatenate([bias_ref[block, :]] * per_kv, axis=0)
-        for g in range(kv_local):
+    def fresh_rows(now, which, g, block):
+        return jnp.concatenate(
+            [earlier[2 * t + which][g, block, :] for t in range(step)] + [now[g, block, :], filler],
+            axis=0,
+        )
+
+    together = 4
+    for first in range(0, groups, together):
+        blocks = [
+            (b, slice(b * capacity, (b + 1) * capacity), g)
+            for g in range(kv_local)
+            for b in range(first, min(first + together, groups))
+        ]
+        scores = []
+        for b, block, g in blocks:
             queries = jnp.concatenate(
                 [query_heads[g * per_kv + h][block] for h in range(per_kv)], axis=0
             )
-            fresh_keys = jnp.concatenate(
-                [earlier[2 * t][g, block, :] for t in range(step)]
-                + [key_fresh[g, block, :], filler],
-                axis=0,
+            bias = jnp.concatenate([bias_ref[block, :]] * per_kv, axis=0)
+            cached = lax.dot_general(queries, cache[b][g], NT, preferred_element_type=f32)
+            fresh = lax.dot_general(
+                queries, fresh_rows(key_fresh, 0, g, block), NT, preferred_element_type=f32
             )
-            fresh_values = jnp.concatenate(
-                [earlier[2 * t + 1][g, block, :] for t in range(step)]
-                + [value_fresh[g, block, :], filler],
-                axis=0,
+            fresh = jnp.where(same_row, fresh * scale, blocked)
+            scores.append(jnp.concatenate([cached * scale + bias, fresh], axis=1))
+        largest = [jnp.max(score, axis=1, keepdims=True) for score in scores]
+        weights = [
+            jnp.exp(score - top).astype(bf16) for score, top in zip(scores, largest)
+        ]
+        mixes = []
+        for (b, block, g), weight in zip(blocks, weights):
+            values = jnp.concatenate(
+                [cache[b][kv_local + g], fresh_rows(value_fresh, 1, g, block)], axis=0
             )
-            cached = (
-                lax.dot_general(queries, cache[b][g], NT, preferred_element_type=f32) * scale + bias
-            )
-            fresh = lax.dot_general(queries, fresh_keys, NT, preferred_element_type=f32) * scale
-            fresh = jnp.where(same_row, fresh, blocked)
-            scores = jnp.concatenate([cached, fresh], axis=1)
-            largest = jnp.max(scores, axis=1, keepdims=True)
-            weights = jnp.exp(scores - largest).astype(bf16)
-            values = jnp.concatenate([cache[b][kv_local + g], fresh_values], axis=0)
             summing = jnp.concatenate([values, jnp.ones_like(values)], axis=1)
-            mixed = jnp.dot(weights, summing, preferred_element_type=f32)
+            mixes.append(jnp.dot(weight, summing, preferred_element_type=f32))
+        for (b, block, g), mixed in zip(blocks, mixes):
             mixed = (mixed[:, :head_dim] / mixed[:, head_dim:]).astype(bf16)
             for h in range(per_kv):
                 head = g * per_kv + h
@@ -382,7 +401,7 @@
                 ]
 
     attended_rows = attended[...]
-    product = lax.dot_general(attended_rows, output_down[...], NT, preferred_element_type=f32)
+    product = jnp.dot(attended_rows, output_down[...], preferred_element_type=f32)
     low_out = pick_slot(product, own).astype(bf16)
     for n in range(parts):
         term = jnp.dot(
@@ -475,40 +494,36 @@
     by_group = [0] + list(range(groups - 1, 0, -1))
     arrived = swap_all(outgoing, "wide", by_group)
     packed_shape = (2 * kv_local, capacity, context, head_dim)
-    packed = pl.pallas_call(
+    kinds = low_width // rank
+    *packed, down = pl.pallas_call(
         pack_kernel,
-        out_shape=[jax.ShapeDtypeStruct(packed_shape, bf16)] * groups,
-        in_specs=[smem, hbm, hbm],
-        out_specs=[vmem] * groups,
+        out_shape=[jax.ShapeDtypeStruct(packed_shape, bf16)] * groups
+        + [jax.ShapeDtypeStruct((kinds, total * rank, width), bf16)],
+        in_specs=[smem, hbm, hbm, hbm],
+        out_specs=[vmem] * (groups + 1),
         scratch_shapes=[
             pltpu.VMEM((groups,) + packed_shape, bf16),
             pltpu.VMEM(cached_key_rows.shape, bf16),
             pltpu.VMEM(cached_value_rows.shape, bf16),
-            pltpu.SemaphoreType.DMA((2,)),
+            pltpu.SemaphoreType.DMA((2 + kinds * total,)),
         ],
         compiler_params=kernel_params(16),
         name="pack_cache",
-    )(target, in_hbm(cached_key_rows), in_hbm(cached_value_rows))
+    )(target, in_hbm(cached_key_rows), in_hbm(cached_value_rows), in_hbm(stacked_down_factors))
     cache = swap_all(packed, "wide", by_group)
     cache = [block.reshape(2 * kv_local, capacity * context, head_dim) for block in cache]
 
     gain_rows = input_norm_gain.reshape(parts, 1, width)
     gain_slice = lax.dynamic_index_in_dim(gain_rows, narrow_index, 0, keepdims=False)
     sent_state = jax.ShapeDtypeStruct((rows, width + low_width), bf16)
-    kinds = low_width // rank
-    send, facts_here, down = pl.pallas_call(
+    send, facts_here = pl.pallas_call(
         functools.partial(enter_kernel, total, rank, by_group),
-        out_shape=[
-            sent_state,
-            jax.ShapeDtypeStruct((rows, 128), f32),
-            jax.ShapeDtypeStruct((kinds, total * rank, width), bf16),
-        ],
-        in_specs=[vmem] * (groups + 1) + [hbm],
-        out_specs=[vmem] * 3,
-        scratch_shapes=[pltpu.SemaphoreType.DMA((kinds * total,))],
+        out_shape=[sent_state, jax.ShapeDtypeStruct((rows, 128), f32)],
+        in_specs=[vmem] * (groups + 2),
+        out_specs=[vmem] * 2,
         compiler_params=kernel_params(8),
         name="enter",
-    )(*arrived, gain_slice, in_hbm(stacked_down_factors))
+    )(*arrived, gain_slice, down)
 
     key_width = key_projection_weight.shape[1]
     input_width = query_width + 2 * key_width
@@ -536,19 +551,30 @@
             key_up_factor.reshape(total * rank, key_width),
             value_up_factor.reshape(total * rank, key_width),
             output_projection_weight,
-            output_down_factor.reshape(total * rank, query_width),
             output_up_factor.reshape(total * rank, width),
+        ]
+        turned = [
+            jax.ShapeDtypeStruct((query_width, total * rank), bf16),
+            jax.ShapeDtypeStruct((kinds, width, total * rank), bf16),
         ]
         return pl.pallas_call(
             load_others_kernel,
-            out_shape=[jax.ShapeDtypeStruct(array.shape, bf16) for array in others],
-            in_specs=[hbm] * len(others) + [vmem],
-            out_specs=[vmem] * len(others),
-            scratch_shapes=[pltpu.SemaphoreType.DMA((len(others),))],
-            compiler_params=kernel_params(16),
+            out_shape=[jax.ShapeDtypeStruct(array.shape, bf16) for array in others] + turned,
+            in_specs=[hbm] * (len(others) + 1) + [vmem] * 2,
+            out_specs=[vmem] * (len(others) + 2),
+            scratch_shapes=[
+                pltpu.VMEM((total * rank, query_width), bf16),
+                pltpu.SemaphoreType.DMA((len(others) + 1,)),
+            ],
+            compiler_params=kernel_params(20),
             cost_estimate=load_cost,
             name="load_others",
-        )(*[in_hbm(array) for array in others], after)
+        )(
+            *[in_hbm(array) for array in others],
+            in_hbm(output_down_factor.reshape(total * rank, query_width)),
+            down,
+            after,
+        )
 
     lengths = facts_here[:, 0]
     frequency = rope_base ** (-(jnp.arange(head_dim // 2, dtype=f32) * 2.0) / head_dim)
@@ -576,13 +602,14 @@
     earlier = []
     for step in range(STEPS):
         from_far = [swap(send, "narrow", mask) for mask in far]
-        slices = [send, swap(send, "narrow", 1)] + from_far
+        from_near = swap(send, "narrow", 1)
+        if step == 0:
+            input_weight = load_inputs(facts_here)
+            input_weight, *from_far = lax.optimization_barrier((input_weight, *from_far))
         passed_on = [swap(piece, "narrow", 1) for piece in from_far]
         if step == 0:
-            input_weight = load_inputs(facts_here)
-            query_up, key_up, value_up, output_weight, output_down, output_up = load_others(
-                from_far[0]
-            )
+            *others, output_down, down_across = load_others(from_far[0])
+            query_up, key_up, value_up, output_weight, output_up = others
         sums = pl.pallas_call(
             functools.partial(early_kernel, early),
             out_shape=[
@@ -599,7 +626,7 @@
                 transcendentals=0,
             ),
             name="project_early",
-        )(*slices, index_here, gain_rows, input_weight)
+        )(send, from_near, *from_far, index_here, gain_rows, input_weight)
         *terms, key_fresh, value_fresh = pl.pallas_call(
             functools.partial(step_kernel, total, rank, step, parts, late, by_group),
             out_shape=[sent_terms] * parts + [fresh] * 2,
@@ -643,7 +670,7 @@
                 out_specs=vmem,
                 compiler_params=kernel_params(8),
                 name="between",
-            )(*received, send, facts_here, output_up, gain_slice, down)
+            )(*received, send, facts_here, output_up, gain_slice, down_across)
         else:
             leaving = pl.pallas_call(
                 functools.partial(leave_kernel, total, rank, parts),

time: 133 us -> 129 us (0.970)
  Pallas kernels: 39.2 us -> 33.8 us
  waiting for transfers between devices: 53.2 us -> 56.4 us
    pallas_call x4, Pallas kernels: 15.9 us -> 11.6 us  [shards(): pl.pallas_call(functools.partial(step_kernel, total, rank, step, parts, l...]
    ppermute x33, waiting for transfers between devices: 53.2 us -> 56.4 us  [swap(): lax.ppermute(block, axis, [(i, i ^ mask) for i in range(lax.axis_size(axi...]
    pallas_call x1, Pallas kernels: 2.57 us -> 0.79 us  [shards(): pl.pallas_call(functools.partial(enter_kernel, total, rank, by_group), ou...]
where the time goes in v5:
time: 129 us
  waiting for transfers between devices  56.4 us (44%)
  starting transfers between devices  36.5 us (28%)
  Pallas kernels  33.8 us (26%)
    ppermute x33, waiting for transfers between devices, swap(): lax.ppermute(block, axis, [(i, i ^ mask) for i in range(lax.axis_size(axi...  56.4 us
    ppermute x33, starting transfers between devices, swap(): lax.ppermute(block, axis, [(i, i ^ mask) for i in range(lax.axis_size(axi...  36.5 us
    pallas_call x4, Pallas kernels, shards(): pl.pallas_call(functools.partial(step_kernel, total, rank, step, parts, l...  11.6 us
    pallas_call x4, Pallas kernels, shards(): pl.pallas_call(functools.partial(early_kernel, early), out_shape=[jax.Sha...  4.7 us
    pallas_call x1, Pallas kernels, shards(): pl.pallas_call(pack_kernel, out_shape=[jax.ShapeDtypeStruct(packed_shape,...  3.9 us
    pallas_call x1, Pallas kernels, load_others(): pl.pallas_call(load_others_kernel, out_shape=[jax.ShapeDtypeStruct(array....  3.44 us
    pallas_call x1, Pallas kernels, load_inputs(): pl.pallas_call(load_inputs_kernel, out_shape=jax.ShapeDtypeStruct((featur...  3.28 us
    pallas_call x1, Pallas kernels, shards(): pl.pallas_call(route_kernel, out_shape=[jax.ShapeDtypeStruct((row_group,)...  2.76 us
  transfers between devices with their start and end apart: 33, of which 20 were waited for; matrix products, arithmetic and copies ran while one was open for 1% of the time, Pallas kernels for 13%

profile of v5, /device:TPU:0, one launch (start us, length us, event | category | flops | bytes accessed | tf_op | source)
XLA Modules:
  0.0 128.7 jit_solution(8072853181655037142)
XLA Ops:
  0.0 2.8 %route_rows.1 = (s32[64]{0:T(128)S(1)}, bf16[64,64]{1,0:T(8,128)(2,1)S(1)}, bf16[16,768]{1,0:T(8,128)(2,1)S(1)}, bf16[16,768]{1,0:T(8,128)(2,1)S(1)}, bf16[16,76...) custom-call(s32[1]{0:T(128)} %bitcast.group_ref, s32[256]{0:T(256)} %domain_hbm.1, s32[32]{0:T(128)} %slot_hbm.1, ...), custom_call_target="tpu_custom_call" | custom-call | tf_op jit(solution)/shard_map/route_rows/pallas_call | solution.py:466
  2.8 2.5 %collective-permute-start = (bf16[16,768]{1,0:T(8,128)(2,1)S(1)}, bf16[16,768]{1,0:T(8,128)(2,1)S(1)}, u32[]{:S(2)}, u32[]{:S(2)}) collective-permute-start(bf16[16,768]{1,0:T(8,128)(2,1)S(1)} %get-tuple-element.67), channel_id=1, source_target_pairs={{0,12},{4,8},{8,4},{12,0},{1,13},{5,9},{9,5},{13,1},{2,14},{6,10},... | collective-permute-start | bytes 73736 | tf_op jit(solution)/shard_map/ppermute | solution.py:419
  5.9 3.9 %pack_cache.1 = (bf16[4,16,24,128]{3,2,1,0:T(8,128)(2,1)S(1)}, bf16[4,16,24,128]{3,2,1,0:T(8,128)(2,1)S(1)}, bf16[4,16,24,128]{3,2,1,0:T(8,128)(2,1)}, bf16[4,16...) custom-call(s32[64]{0:T(128)S(1)} %get-tuple-element.70.target_ref, bf16[64,2,24,128]{3,2,1,0:T(8,128)(2,1)} %key_hbm.1, ...), custom_call_target="tpu_custom_call" | custom-call | tf_op jit(solution)/shard_map/pack_cache/pallas_call | solution.py:498
  13.7 2.7 %collective-permute-start.3 = (bf16[64,832]{1,0:T(8,128)(2,1)S(1)}, bf16[64,832]{1,0:T(8,128)(2,1)S(1)}, u32[]{:S(2)}, u32[]{:S(2)}) collective-permute-start(bf16[64,832]{1,0:T(8,128)(2,1)S(1)} %get-tuple-element.73.refs_0_.refs_4_), channel_id=1, source_target_pairs={{0,2},{1,3},{2,0},{3,1},{4,6},{5,7},{6,4},{7,5},{8,10},{9,11},{10,... | collective-permute-start | bytes 319496 | tf_op jit(solution)/shard_map/ppermute | solution.py:419
  18.7 3.3 %load_inputs.1.refs_5_.refs_7_ = bf16[2560,1536]{1,0:T(8,128)(2,1)S(1)} custom-call(bf16[2560,1024]{1,0:T(8,128)(2,1)} %query.1, bf16[2560,256]{1,0:T(8,128)(2,1)} %key.1, bf16[2560,256]{1,0:T(8,128)(2,1)} %value.1, f32[64,128]{1,0:T(8,128)S(1)} %get-tuple-element.72.after.refs_5_), custom_call_target="tpu_custom_call" | custom-call | bytes 20000000 | tf_op jit(solution)/shard_map/load_inputs/pallas_call | solution.py:532
  23.5 3.4 %load_others.1 = (bf16[512,1024]{1,0:T(8,128)(2,1)S(1)}, bf16[512,256]{1,0:T(8,128)(2,1)S(1)}, bf16[512,256]{1,0:T(8,128)(2,1)S(1)}, bf16[1024,2560]{1,0:T(8,128...) custom-call(bf16[512,1024]{1,0:T(8,128)(2,1)} %bitcast.39, ...), custom_call_target="tpu_custom_call" | custom-call | bytes 20000000 | tf_op jit(solution)/shard_map/load_others/pallas_call | solution.py:560
  28.1 2.5 %collective-permute-done.7 = bf16[4,16,24,128]{3,2,1,0:T(8,128)(2,1)S(1)} collective-permute-done((bf16[4,16,24,128]{3,2,1,0:T(8,128)(2,1)}, bf16[4,16,24,128]{3,2,1,0:T(8,128)(2,1)S(1)}, u32[]{:S(2)}, u32[]{:S(2)}) %collective-permute-start.7) | collective-permute-done | bytes 393248 | tf_op jit(solution)/shard_map/ppermute | solution.py:419
  30.7 2.9 %attend_step.4 = (bf16[64,704]{1,0:T(8,128)(2,1)S(1)}, bf16[64,704]{1,0:T(8,128)(2,1)S(1)}, bf16[64,704]{1,0:T(8,128)(2,1)S(1)}, bf16[64,704]{1,0:T(8,128)(2,1)S...) custom-call(bf16[64,832]{1,0:T(8,128)(2,1)S(1)} %collective-permute-done.4.refs_0_, ...), custom_call_target="tpu_custom_call" | custom-call | tf_op jit(solution)/shard_map/attend_step/pallas_call | solution.py:630
  33.6 2.9 %collective-permute-start.9 = (bf16[64,704]{1,0:T(8,128)(2,1)S(1)}, bf16[64,704]{1,0:T(8,128)(2,1)S(1)}, u32[]{:S(2)}, u32[]{:S(2)}) collective-permute-start(bf16[64,704]{1,0:T(8,128)(2,1)S(1)} %get-tuple-element.89), channel_id=1, source_target_pairs={{0,2},{1,3},{2,0},{3,1},{4,6},{5,7},{6,4},{7,5},{8,10},{9,11},{10,... | collective-permute-start | bytes 270344 | tf_op jit(solution)/shard_map/ppermute | solution.py:419
  38.0 6.3 %collective-permute-done.9.refs_1_ = bf16[64,704]{1,0:T(8,128)(2,1)S(1)} collective-permute-done((bf16[64,704]{1,0:T(8,128)(2,1)S(1)}, bf16[64,704]{1,0:T(8,128)(2,1)S(1)}, u32[]{:S(2)}, u32[]{:S(2)}) %collective-permute-start.9) | collective-permute-done | bytes 90144 | tf_op jit(solution)/shard_map/ppermute | solution.py:419
  45.5 3.5 %collective-permute-start.12 = (bf16[64,832]{1,0:T(8,128)(2,1)S(1)}, bf16[64,832]{1,0:T(8,128)(2,1)S(1)}, u32[]{:S(2)}, u32[]{:S(2)}) collective-permute-start(bf16[64,832]{1,0:T(8,128)(2,1)S(1)} %between.3.refs_0_.refs_4_), channel_id=1, source_target_pairs={{0,2},{1,3},{2,0},{3,1},{4,6},{5,7},{6,4},{7,5},{8,10},{9,11},{10,... | collective-permute-start | bytes 319496 | tf_op jit(solution)/shard_map/ppermute | solution.py:419
  49.5 5.4 %collective-permute-done.12.refs_2_ = bf16[64,832]{1,0:T(8,128)(2,1)S(1)} collective-permute-done((bf16[64,832]{1,0:T(8,128)(2,1)S(1)}, bf16[64,832]{1,0:T(8,128)(2,1)S(1)}, u32[]{:S(2)}, u32[]{:S(2)}) %collective-permute-start.12) | collective-permute-done | bytes 106528 | tf_op jit(solution)/shard_map/ppermute | solution.py:419
  57.2 2.6 %collective-permute-done.13.refs_0_ = bf16[64,832]{1,0:T(8,128)(2,1)S(1)} collective-permute-done((bf16[64,832]{1,0:T(8,128)(2,1)S(1)}, bf16[64,832]{1,0:T(8,128)(2,1)S(1)}, u32[]{:S(2)}, u32[]{:S(2)}) %collective-permute-start.13) | collective-permute-done | bytes 106528 | tf_op jit(solution)/shard_map/ppermute | solution.py:419
  59.7 2.8 %attend_step.5 = (bf16[64,704]{1,0:T(8,128)(2,1)S(1)}, bf16[64,704]{1,0:T(8,128)(2,1)S(1)}, bf16[64,704]{1,0:T(8,128)(2,1)S(1)}, bf16[64,704]{1,0:T(8,128)(2,1)S...) custom-call(bf16[64,832]{1,0:T(8,128)(2,1)S(1)} %collective-permute-done.13.refs_0_, ...), custom_call_target="tpu_custom_call" | custom-call | tf_op jit(solution)/shard_map/attend_step/pallas_call | solution.py:630
  66.1 5.4 %collective-permute-done.15.refs_1_ = bf16[64,704]{1,0:T(8,128)(2,1)S(1)} collective-permute-done((bf16[64,704]{1,0:T(8,128)(2,1)S(1)}, bf16[64,704]{1,0:T(8,128)(2,1)S(1)}, u32[]{:S(2)}, u32[]{:S(2)}) %collective-permute-start.15) | collective-permute-done | bytes 90144 | tf_op jit(solution)/shard_map/ppermute | solution.py:419
  75.4 6.1 %collective-permute-done.18.refs_2_ = bf16[64,832]{1,0:T(8,128)(2,1)S(1)} collective-permute-done((bf16[64,832]{1,0:T(8,128)(2,1)S(1)}, bf16[64,832]{1,0:T(8,128)(2,1)S(1)}, u32[]{:S(2)}, u32[]{:S(2)}) %collective-permute-start.18) | collective-permute-done | bytes 106528 | tf_op jit(solution)/shard_map/ppermute | solution.py:419
  83.0 3.3 %collective-permute-done.19.refs_0_ = bf16[64,832]{1,0:T(8,128)(2,1)S(1)} collective-permute-done((bf16[64,832]{1,0:T(8,128)(2,1)S(1)}, bf16[64,832]{1,0:T(8,128)(2,1)S(1)}, u32[]{:S(2)}, u32[]{:S(2)}) %collective-permute-start.19) | collective-permute-done | bytes 106528 | tf_op jit(solution)/shard_map/ppermute | solution.py:419
  86.3 3.0 %attend_step.6 = (bf16[64,704]{1,0:T(8,128)(2,1)S(1)}, bf16[64,704]{1,0:T(8,128)(2,1)S(1)}, bf16[64,704]{1,0:T(8,128)(2,1)S(1)}, bf16[64,704]{1,0:T(8,128)(2,1)S...) custom-call(bf16[64,832]{1,0:T(8,128)(2,1)S(1)} %collective-permute-done.19.refs_0_, ...), custom_call_target="tpu_custom_call" | custom-call | tf_op jit(solution)/shard_map/attend_step/pallas_call | solution.py:630
  92.9 4.5 %collective-permute-done.21.refs_1_ = bf16[64,704]{1,0:T(8,128)(2,1)S(1)} collective-permute-done((bf16[64,704]{1,0:T(8,128)(2,1)S(1)}, bf16[64,704]{1,0:T(8,128)(2,1)S(1)}, u32[]{:S(2)}, u32[]{:S(2)}) %collective-permute-start.21) | collective-permute-done | bytes 90144 | tf_op jit(solution)/shard_map/ppermute | solution.py:419
  99.2 2.3 %collective-permute-start.24 = (bf16[64,832]{1,0:T(8,128)(2,1)S(1)}, bf16[64,832]{1,0:T(8,128)(2,1)S(1)}, u32[]{:S(2)}, u32[]{:S(2)}) collective-permute-start(bf16[64,832]{1,0:T(8,128)(2,1)S(1)} %between.5.refs_0_.refs_4_), channel_id=1, source_target_pairs={{0,2},{1,3},{2,0},{3,1},{4,6},{5,7},{6,4},{7,5},{8,10},{9,11},{10,... | collective-permute-start | bytes 319496 | tf_op jit(solution)/shard_map/ppermute | solution.py:419
  101.9 5.1 %collective-permute-done.24.refs_2_ = bf16[64,832]{1,0:T(8,128)(2,1)S(1)} collective-permute-done((bf16[64,832]{1,0:T(8,128)(2,1)S(1)}, bf16[64,832]{1,0:T(8,128)(2,1)S(1)}, u32[]{:S(2)}, u32[]{:S(2)}) %collective-permute-start.24) | collective-permute-done | bytes 106528 | tf_op jit(solution)/shard_map/ppermute | solution.py:419
  109.2 2.5 %collective-permute-done.25.refs_0_ = bf16[64,832]{1,0:T(8,128)(2,1)S(1)} collective-permute-done((bf16[64,832]{1,0:T(8,128)(2,1)S(1)}, bf16[64,832]{1,0:T(8,128)(2,1)S(1)}, u32[]{:S(2)}, u32[]{:S(2)}) %collective-permute-start.25) | collective-permute-done | bytes 106528 | tf_op jit(solution)/shard_map/ppermute | solution.py:419
  111.7 2.8 %attend_step.7 = (bf16[64,704]{1,0:T(8,128)(2,1)S(1)}, bf16[64,704]{1,0:T(8,128)(2,1)S(1)}, bf16[64,704]{1,0:T(8,128)(2,1)S(1)}, bf16[64,704]{1,0:T(8,128)(2,1)S...) custom-call(bf16[64,832]{1,0:T(8,128)(2,1)S(1)} %collective-permute-done.25.refs_0_, ...), custom_call_target="tpu_custom_call" | custom-call | tf_op jit(solution)/shard_map/attend_step/pallas_call | solution.py:630
  118.1 5.0 %collective-permute-done.27.refs_1_ = bf16[64,704]{1,0:T(8,128)(2,1)S(1)} collective-permute-done((bf16[64,704]{1,0:T(8,128)(2,1)S(1)}, bf16[64,704]{1,0:T(8,128)(2,1)S(1)}, u32[]{:S(2)}, u32[]{:S(2)}) %collective-permute-start.27) | collective-permute-done | bytes 90144 | tf_op jit(solution)/shard_map/ppermute | solution.py:419
  (78 shorter events, 41.1 us)
Async XLA Ops:
  2.8 10.0 %collective-permute-start = (bf16[16,768]{1,0:T(8,128)(2,1)S(1)}, bf16[16,768]{1,0:T(8,128)(2,1)S(1)}, u32[]{:S(2)}, u32[]{:S(2)}) collective-permute-start(bf16[16,768]{1,0:T(8,128)(2,1)S(1)} %get-tuple-element.67), channel_id=1, source_target_pairs={{0,12},{4,8},{8,4},{12,0},{1,13},{5,9},{9,5},{13,1},{2,14},{6,10},... | collective-permute-start | bytes 73736 | tf_op jit(solution)/shard_map/ppermute | solution.py:419
  5.2 7.6 %collective-permute-start.1 = (bf16[16,768]{1,0:T(8,128)(2,1)S(1)}, bf16[16,768]{1,0:T(8,128)(2,1)S(1)}, u32[]{:S(2)}, u32[]{:S(2)}) collective-permute-start(bf16[16,768]{1,0:T(8,128)(2,1)S(1)} %get-tuple-element.68), channel_id=1, source_target_pairs={{0,8},{4,12},{8,0},{12,4},{1,9},{5,13},{9,1},{13,5},{2,10},{6,14},... | collective-permute-start | bytes 73736 | tf_op jit(solution)/shard_map/ppermute | solution.py:419
  5.9 7.0 %collective-permute-start.2 = (bf16[16,768]{1,0:T(8,128)(2,1)S(1)}, bf16[16,768]{1,0:T(8,128)(2,1)S(1)}, u32[]{:S(2)}, u32[]{:S(2)}) collective-permute-start(bf16[16,768]{1,0:T(8,128)(2,1)S(1)} %get-tuple-element.69), channel_id=1, source_target_pairs={{0,4},{4,0},{8,12},{12,8},{1,5},{5,1},{9,13},{13,9},{2,6},{6,2},{1... | collective-permute-start | bytes 73736 | tf_op jit(solution)/shard_map/ppermute | solution.py:419
  10.6 17.6 %collective-permute-start.6 = (bf16[4,16,24,128]{3,2,1,0:T(8,128)(2,1)}, bf16[4,16,24,128]{3,2,1,0:T(8,128)(2,1)S(1)}, u32[]{:S(2)}, u32[]{:S(2)}) collective-permute-start(bf16[4,16,24,128]{3,2,1,0:T(8,128)(2,1)} %get-tuple-element.83), channel_id=1, source_target_pairs={{0,12},{4,8},{8,4},{12,0},{1,13},{5,9},{9,5},{13,1},{2,14},{6,10},... | collective-permute-start | bytes 1179656 | tf_op jit(solution)/shard_map/ppermute | solution.py:419
  12.1 18.6 %collective-permute-start.7 = (bf16[4,16,24,128]{3,2,1,0:T(8,128)(2,1)}, bf16[4,16,24,128]{3,2,1,0:T(8,128)(2,1)S(1)}, u32[]{:S(2)}, u32[]{:S(2)}) collective-permute-start(bf16[4,16,24,128]{3,2,1,0:T(8,128)(2,1)} %get-tuple-element.84), channel_id=1, source_target_pairs={{0,8},{4,12},{8,0},{12,4},{1,9},{5,13},{9,1},{13,5},{2,10},{6,14},... | collective-permute-start | bytes 1179656 | tf_op jit(solution)/shard_map/ppermute | solution.py:419
  12.8 17.9 %collective-permute-start.8 = (bf16[4,16,24,128]{3,2,1,0:T(8,128)(2,1)}, bf16[4,16,24,128]{3,2,1,0:T(8,128)(2,1)S(1)}, u32[]{:S(2)}, u32[]{:S(2)}) collective-permute-start(bf16[4,16,24,128]{3,2,1,0:T(8,128)(2,1)} %copy-done.2), channel_id=1, source_target_pairs={{0,4},{4,0},{8,12},{12,8},{1,5},{5,1},{9,13},{13,9},{2,6},{6,2},{1... | collective-permute-start | bytes 1179656 | tf_op jit(solution)/shard_map/ppermute | solution.py:419
  13.7 9.1 %collective-permute-start.3 = (bf16[64,832]{1,0:T(8,128)(2,1)S(1)}, bf16[64,832]{1,0:T(8,128)(2,1)S(1)}, u32[]{:S(2)}, u32[]{:S(2)}) collective-permute-start(bf16[64,832]{1,0:T(8,128)(2,1)S(1)} %get-tuple-element.73.refs_0_.refs_4_), channel_id=1, source_target_pairs={{0,2},{1,3},{2,0},{3,1},{4,6},{5,7},{6,4},{7,5},{8,10},{9,11},{10,... | collective-permute-start | bytes 319496 | tf_op jit(solution)/shard_map/ppermute | solution.py:419
  16.3 10.6 %collective-permute-start.5 = (bf16[64,832]{1,0:T(8,128)(2,1)S(1)}, bf16[64,832]{1,0:T(8,128)(2,1)S(1)}, u32[]{:S(2)}, u32[]{:S(2)}) collective-permute-start(bf16[64,832]{1,0:T(8,128)(2,1)S(1)} %get-tuple-element.73.refs_0_.refs_4_), channel_id=1, source_target_pairs={{0,1},{1,0},{2,3},{3,2},{4,5},{5,4},{6,7},{7,6},{8,9},{9,8},{10,11... | collective-permute-start | bytes 319496 | tf_op jit(solution)/shard_map/ppermute | solution.py:419
  33.6 10.7 %collective-permute-start.9 = (bf16[64,704]{1,0:T(8,128)(2,1)S(1)}, bf16[64,704]{1,0:T(8,128)(2,1)S(1)}, u32[]{:S(2)}, u32[]{:S(2)}) collective-permute-start(bf16[64,704]{1,0:T(8,128)(2,1)S(1)} %get-tuple-element.89), channel_id=1, source_target_pairs={{0,2},{1,3},{2,0},{3,1},{4,6},{5,7},{6,4},{7,5},{8,10},{9,11},{10,... | collective-permute-start | bytes 270344 | tf_op jit(solution)/shard_map/ppermute | solution.py:419
  36.4 7.8 %collective-permute-start.10 = (bf16[64,704]{1,0:T(8,128)(2,1)S(1)}, bf16[64,704]{1,0:T(8,128)(2,1)S(1)}, u32[]{:S(2)}, u32[]{:S(2)}) collective-permute-start(bf16[64,704]{1,0:T(8,128)(2,1)S(1)} %get-tuple-element.90), channel_id=1, source_target_pairs={{0,3},{1,2},{2,1},{3,0},{4,7},{5,6},{6,5},{7,4},{8,11},{9,10},{10,... | collective-permute-start | bytes 270344 | tf_op jit(solution)/shard_map/ppermute | solution.py:419
  37.8 6.9 %collective-permute-start.11 = (bf16[64,704]{1,0:T(8,128)(2,1)S(1)}, bf16[64,704]{1,0:T(8,128)(2,1)S(1)}, u32[]{:S(2)}, u32[]{:S(2)}) collective-permute-start(bf16[64,704]{1,0:T(8,128)(2,1)S(1)} %get-tuple-element.91), channel_id=1, source_target_pairs={{0,1},{1,0},{2,3},{3,2},{4,5},{5,4},{6,7},{7,6},{8,9},{9,8},{10,11... | collective-permute-start | bytes 270344 | tf_op jit(solution)/shard_map/ppermute | solution.py:419
  45.5 9.4 %collective-permute-start.12 = (bf16[64,832]{1,0:T(8,128)(2,1)S(1)}, bf16[64,832]{1,0:T(8,128)(2,1)S(1)}, u32[]{:S(2)}, u32[]{:S(2)}) collective-permute-start(bf16[64,832]{1,0:T(8,128)(2,1)S(1)} %between.3.refs_0_.refs_4_), channel_id=1, source_target_pairs={{0,2},{1,3},{2,0},{3,1},{4,6},{5,7},{6,4},{7,5},{8,10},{9,11},{10,... | collective-permute-start | bytes 319496 | tf_op jit(solution)/shard_map/ppermute | solution.py:419
  49.0 7.0 %collective-permute-start.14 = (bf16[64,832]{1,0:T(8,128)(2,1)S(1)}, bf16[64,832]{1,0:T(8,128)(2,1)S(1)}, u32[]{:S(2)}, u32[]{:S(2)}) collective-permute-start(bf16[64,832]{1,0:T(8,128)(2,1)S(1)} %between.3.refs_0_.refs_4_), channel_id=1, source_target_pairs={{0,1},{1,0},{2,3},{3,2},{4,5},{5,4},{6,7},{7,6},{8,9},{9,8},{10,11... | collective-permute-start | bytes 319496 | tf_op jit(solution)/shard_map/ppermute | solution.py:419
  62.6 8.9 %collective-permute-start.15 = (bf16[64,704]{1,0:T(8,128)(2,1)S(1)}, bf16[64,704]{1,0:T(8,128)(2,1)S(1)}, u32[]{:S(2)}, u32[]{:S(2)}) collective-permute-start(bf16[64,704]{1,0:T(8,128)(2,1)S(1)} %get-tuple-element.100), channel_id=1, source_target_pairs={{0,2},{1,3},{2,0},{3,1},{4,6},{5,7},{6,4},{7,5},{8,10},{9,11},{10,... | collective-permute-start | bytes 270344 | tf_op jit(solution)/shard_map/ppermute | solution.py:419
  63.7 7.8 %collective-permute-start.16 = (bf16[64,704]{1,0:T(8,128)(2,1)S(1)}, bf16[64,704]{1,0:T(8,128)(2,1)S(1)}, u32[]{:S(2)}, u32[]{:S(2)}) collective-permute-start(bf16[64,704]{1,0:T(8,128)(2,1)S(1)} %get-tuple-element.101), channel_id=1, source_target_pairs={{0,3},{1,2},{2,1},{3,0},{4,7},{5,6},{6,5},{7,4},{8,11},{9,10},{10,... | collective-permute-start | bytes 270344 | tf_op jit(solution)/shard_map/ppermute | solution.py:419
  65.3 7.1 %collective-permute-start.17 = (bf16[64,704]{1,0:T(8,128)(2,1)S(1)}, bf16[64,704]{1,0:T(8,128)(2,1)S(1)}, u32[]{:S(2)}, u32[]{:S(2)}) collective-permute-start(bf16[64,704]{1,0:T(8,128)(2,1)S(1)} %get-tuple-element.102), channel_id=1, source_target_pairs={{0,1},{1,0},{2,3},{3,2},{4,5},{5,4},{6,7},{7,6},{8,9},{9,8},{10,11... | collective-permute-start | bytes 270344 | tf_op jit(solution)/shard_map/ppermute | solution.py:419
  73.2 8.3 %collective-permute-start.18 = (bf16[64,832]{1,0:T(8,128)(2,1)S(1)}, bf16[64,832]{1,0:T(8,128)(2,1)S(1)}, u32[]{:S(2)}, u32[]{:S(2)}) collective-permute-start(bf16[64,832]{1,0:T(8,128)(2,1)S(1)} %between.4.refs_0_.refs_4_), channel_id=1, source_target_pairs={{0,2},{1,3},{2,0},{3,1},{4,6},{5,7},{6,4},{7,5},{8,10},{9,11},{10,... | collective-permute-start | bytes 319496 | tf_op jit(solution)/shard_map/ppermute | solution.py:419
  74.0 7.9 %collective-permute-start.20 = (bf16[64,832]{1,0:T(8,128)(2,1)S(1)}, bf16[64,832]{1,0:T(8,128)(2,1)S(1)}, u32[]{:S(2)}, u32[]{:S(2)}) collective-permute-start(bf16[64,832]{1,0:T(8,128)(2,1)S(1)} %between.4.refs_0_.refs_4_), channel_id=1, source_target_pairs={{0,1},{1,0},{2,3},{3,2},{4,5},{5,4},{6,7},{7,6},{8,9},{9,8},{10,11... | collective-permute-start | bytes 319496 | tf_op jit(solution)/shard_map/ppermute | solution.py:419
  89.3 8.1 %collective-permute-start.21 = (bf16[64,704]{1,0:T(8,128)(2,1)S(1)}, bf16[64,704]{1,0:T(8,128)(2,1)S(1)}, u32[]{:S(2)}, u32[]{:S(2)}) collective-permute-start(bf16[64,704]{1,0:T(8,128)(2,1)S(1)} %get-tuple-element.109), channel_id=1, source_target_pairs={{0,2},{1,3},{2,0},{3,1},{4,6},{5,7},{6,4},{7,5},{8,10},{9,11},{10,... | collective-permute-start | bytes 270344 | tf_op jit(solution)/shard_map/ppermute | solution.py:419
  89.8 7.6 %collective-permute-start.22 = (bf16[64,704]{1,0:T(8,128)(2,1)S(1)}, bf16[64,704]{1,0:T(8,128)(2,1)S(1)}, u32[]{:S(2)}, u32[]{:S(2)}) collective-permute-start(bf16[64,704]{1,0:T(8,128)(2,1)S(1)} %get-tuple-element.110), channel_id=1, source_target_pairs={{0,3},{1,2},{2,1},{3,0},{4,7},{5,6},{6,5},{7,4},{8,11},{9,10},{10,... | collective-permute-start | bytes 270344 | tf_op jit(solution)/shard_map/ppermute | solution.py:419
  99.2 7.8 %collective-permute-start.24 = (bf16[64,832]{1,0:T(8,128)(2,1)S(1)}, bf16[64,832]{1,0:T(8,128)(2,1)S(1)}, u32[]{:S(2)}, u32[]{:S(2)}) collective-permute-start(bf16[64,832]{1,0:T(8,128)(2,1)S(1)} %between.5.refs_0_.refs_4_), channel_id=1, source_target_pairs={{0,2},{1,3},{2,0},{3,1},{4,6},{5,7},{6,4},{7,5},{8,10},{9,11},{10,... | collective-permute-start | bytes 319496 | tf_op jit(solution)/shard_map/ppermute | solution.py:419
  101.5 6.6 %collective-permute-start.26 = (bf16[64,832]{1,0:T(8,128)(2,1)S(1)}, bf16[64,832]{1,0:T(8,128)(2,1)S(1)}, u32[]{:S(2)}, u32[]{:S(2)}) collective-permute-start(bf16[64,832]{1,0:T(8,128)(2,1)S(1)} %between.5.refs_0_.refs_4_), channel_id=1, source_target_pairs={{0,1},{1,0},{2,3},{3,2},{4,5},{5,4},{6,7},{7,6},{8,9},{9,8},{10,11... | collective-permute-start | bytes 319496 | tf_op jit(solution)/shard_map/ppermute | solution.py:419
  114.5 8.5 %collective-permute-start.27 = (bf16[64,704]{1,0:T(8,128)(2,1)S(1)}, bf16[64,704]{1,0:T(8,128)(2,1)S(1)}, u32[]{:S(2)}, u32[]{:S(2)}) collective-permute-start(bf16[64,704]{1,0:T(8,128)(2,1)S(1)} %get-tuple-element.118), channel_id=1, source_target_pairs={{0,2},{1,3},{2,0},{3,1},{4,6},{5,7},{6,4},{7,5},{8,10},{9,11},{10,... | collective-permute-start | bytes 270344 | tf_op jit(solution)/shard_map/ppermute | solution.py:419
  116.0 7.1 %collective-permute-start.28 = (bf16[64,704]{1,0:T(8,128)(2,1)S(1)}, bf16[64,704]{1,0:T(8,128)(2,1)S(1)}, u32[]{:S(2)}, u32[]{:S(2)}) collective-permute-start(bf16[64,704]{1,0:T(8,128)(2,1)S(1)} %get-tuple-element.119), channel_id=1, source_target_pairs={{0,3},{1,2},{2,1},{3,0},{4,7},{5,6},{6,5},{7,4},{8,11},{9,10},{10,... | collective-permute-start | bytes 270344 | tf_op jit(solution)/shard_map/ppermute | solution.py:419
  (13 other events, 62.7 us)

commit v6 on v5

--- a/solution.py
+++ b/solution.py
@@ -139,15 +139,27 @@
         copy.wait()
 
 
-def load_inputs_kernel(query, key, value, after, inputs, sems):
-    pairs = []
-    column = 0
-    for weight in (query, key, value):
-        width = weight.shape[1]
-        pairs.append((weight, inputs.at[:, column : column + width]))
-        column += width
-    for copy in copy_all(pairs, sems):
-        copy.wait()
+def load_inputs_kernel(turn, turn_ref, query, key, value, after, *refs):
+    inputs, sems = refs[-2:]
+
+    @pl.when(turn_ref[0] == turn)
+    def _():
+        pairs = []
+        column = 0
+        for weight in (query, key, value):
+            width = weight.shape[1]
+            pairs.append((weight, inputs.at[:, column : column + width]))
+            column += width
+        for copy in copy_all(pairs, sems):
+            copy.wait()
+
+    for held in refs[:-2]:
+
+        @pl.when(turn_ref[0] != turn)
+        def _():
+            copy = pltpu.make_async_copy(held, inputs, sems.at[0])
+            copy.start()
+            copy.wait()
 
 
 def load_others_kernel(*refs):
@@ -516,6 +528,30 @@
     gain_rows = input_norm_gain.reshape(parts, 1, width)
     gain_slice = lax.dynamic_index_in_dim(gain_rows, narrow_index, 0, keepdims=False)
     sent_state = jax.ShapeDtypeStruct((rows, width + low_width), bf16)
+    key_width = key_projection_weight.shape[1]
+    input_width = query_width + 2 * key_width
+
+    def load_inputs(turn, after, *held):
+        return pl.pallas_call(
+            functools.partial(load_inputs_kernel, turn),
+            out_shape=jax.ShapeDtypeStruct((features, input_width), bf16),
+            in_specs=[smem] + [hbm] * 3 + [vmem] * (1 + len(held)),
+            out_specs=vmem,
+            scratch_shapes=[pltpu.SemaphoreType.DMA((3,))],
+            compiler_params=kernel_params(18),
+            cost_estimate=load_cost,
+            name="load_inputs",
+        )(
+            lax.rem(wide_index, 2).reshape(1),
+            in_hbm(query_projection_weight),
+            in_hbm(key_projection_weight),
+            in_hbm(value_projection_weight),
+            after,
+            *held,
+        )
+
+    input_weight = load_inputs(1, arrived[-1])
+    input_weight, *arrived = lax.optimization_barrier((input_weight, *arrived))
     send, facts_here = pl.pallas_call(
         functools.partial(enter_kernel, total, rank, by_group),
         out_shape=[sent_state, jax.ShapeDtypeStruct((rows, 128), f32)],
@@ -524,26 +560,6 @@
         compiler_params=kernel_params(8),
         name="enter",
     )(*arrived, gain_slice, down)
-
-    key_width = key_projection_weight.shape[1]
-    input_width = query_width + 2 * key_width
-
-    def load_inputs(after):
-        return pl.pallas_call(
-            load_inputs_kernel,
-            out_shape=jax.ShapeDtypeStruct((features, input_width), bf16),
-            in_specs=[hbm] * 3 + [vmem],
-            out_specs=vmem,
-            scratch_shapes=[pltpu.SemaphoreType.DMA((3,))],
-            compiler_params=kernel_params(16),
-            cost_estimate=load_cost,
-            name="load_inputs",
-        )(
-            in_hbm(query_projection_weight),
-            in_hbm(key_projection_weight),
-            in_hbm(value_projection_weight),
-            after,
-        )
 
     def load_others(after):
         others = [
@@ -604,7 +620,7 @@
         from_far = [swap(send, "narrow", mask) for mask in far]
         from_near = swap(send, "narrow", 1)
         if step == 0:
-            input_weight = load_inputs(facts_here)
+            input_weight = load_inputs(0, facts_here, input_weight)
             input_weight, *from_far = lax.optimization_barrier((input_weight, *from_far))
         passed_on = [swap(piece, "narrow", 1) for piece in from_far]
         if step == 0:

time: 129 us -> 126 us (0.977)
  waiting for transfers between devices: 56.4 us -> 52.3 us
    ppermute x33, waiting for transfers between devices: 56.4 us -> 52.3 us  [swap(): lax.ppermute(block, axis, [(i, i ^ mask) for i in range(lax.axis_size(axi...]
    pallas_call x1 -> x2, Pallas kernels: 3.28 us -> 3.31 us  [load_inputs(): pl.pallas_call(functools.partial(load_inputs_kernel, turn), out_shape=jax...]
  transfers between devices with their start and end apart: 33 -> 33, of which waited for: 20 -> 21; matrix products, arithmetic and copies ran while one was open for 1% -> 1% of each run, Pallas kernels for 13% -> 13%
where the time goes in v6:
time: 126 us; the launch traced here: 125 us
  waiting for transfers between devices  52.3 us (42%)
  starting transfers between devices  37 us (29%)
  Pallas kernels  33.5 us (27%)
  local copies, waits for them, and re-layouts  1.59 us (1%)
    ppermute x33, waiting for transfers between devices, swap(): lax.ppermute(block, axis, [(i, i ^ mask) for i in range(lax.axis_size(axi...  52.3 us
    ppermute x33, starting transfers between devices, swap(): lax.ppermute(block, axis, [(i, i ^ mask) for i in range(lax.axis_size(axi...  37 us
    pallas_call x4, Pallas kernels, shards(): pl.pallas_call(functools.partial(step_kernel, total, rank, step, parts, l...  11.3 us
    pallas_call x4, Pallas kernels, shards(): pl.pallas_call(functools.partial(early_kernel, early), out_shape=[jax.Sha...  4.63 us
    pallas_call x1, Pallas kernels, shards(): pl.pallas_call(pack_kernel, out_shape=[jax.ShapeDtypeStruct(packed_shape,...  3.89 us
    pallas_call x1, Pallas kernels, load_others(): pl.pallas_call(load_others_kernel, out_shape=[jax.ShapeDtypeStruct(array....  3.44 us
    pallas_call x2, Pallas kernels, load_inputs(): pl.pallas_call(functools.partial(load_inputs_kernel, turn), out_shape=jax...  3.31 us
    pallas_call x1, Pallas kernels, shards(): pl.pallas_call(route_kernel, out_shape=[jax.ShapeDtypeStruct((row_group,)...  2.63 us
  transfers between devices with their start and end apart: 33, of which 21 were waited for; matrix products, arithmetic and copies ran while one was open for 1% of the time, Pallas kernels for 13%

profile of v6, /device:TPU:0, one launch (start us, length us, event | category | flops | bytes accessed | tf_op | source)
XLA Modules:
  0.0 125.5 jit_solution(16665677163969902437)
XLA Ops:
  0.0 2.6 %route_rows.1 = (s32[64]{0:T(128)S(1)}, bf16[64,64]{1,0:T(8,128)(2,1)S(1)}, bf16[16,768]{1,0:T(8,128)(2,1)S(1)}, bf16[16,768]{1,0:T(8,128)(2,1)S(1)}, bf16[16,76...) custom-call(s32[1]{0:T(128)} %bitcast.group_ref, s32[256]{0:T(256)} %domain_hbm.1, s32[32]{0:T(128)} %slot_hbm.1, ...), custom_call_target="tpu_custom_call" | custom-call | tf_op jit(solution)/shard_map/route_rows/pallas_call | solution.py:478
  3.2 2.6 %collective-permute-start.1 = (bf16[16,768]{1,0:T(8,128)(2,1)S(1)}, bf16[16,768]{1,0:T(8,128)(2,1)S(1)}, u32[]{:S(2)}, u32[]{:S(2)}) collective-permute-start(bf16[16,768]{1,0:T(8,128)(2,1)S(1)} %get-tuple-element.73), channel_id=1, source_target_pairs={{0,12},{4,8},{8,4},{12,0},{1,13},{5,9},{9,5},{13,1},{2,14},{6,10},... | collective-permute-start | bytes 73736 | tf_op jit(solution)/shard_map/ppermute | solution.py:431
  5.8 3.9 %pack_cache.1 = (bf16[4,16,24,128]{3,2,1,0:T(8,128)(2,1)S(1)}, bf16[4,16,24,128]{3,2,1,0:T(8,128)(2,1)S(1)}, bf16[4,16,24,128]{3,2,1,0:T(8,128)(2,1)}, bf16[4,16...) custom-call(s32[64]{0:T(128)S(1)} %get-tuple-element.79.target_ref, bf16[64,2,24,128]{3,2,1,0:T(8,128)(2,1)} %key_hbm.1, ...), custom_call_target="tpu_custom_call" | custom-call | tf_op jit(solution)/shard_map/pack_cache/pallas_call | solution.py:510
  14.3 2.9 %collective-permute-start.3 = (bf16[64,832]{1,0:T(8,128)(2,1)S(1)}, bf16[64,832]{1,0:T(8,128)(2,1)S(1)}, u32[]{:S(2)}, u32[]{:S(2)}) collective-permute-start(bf16[64,832]{1,0:T(8,128)(2,1)S(1)} %get-tuple-element.83.refs_0_.refs_4_), channel_id=1, source_target_pairs={{0,2},{1,3},{2,0},{3,1},{4,6},{5,7},{6,4},{7,5},{8,10},{9,11},{10,... | collective-permute-start | bytes 319496 | tf_op jit(solution)/shard_map/ppermute | solution.py:431
  19.5 3.3 %load_inputs.3.refs_5_.refs_7_ = bf16[2560,1536]{1,0:T(8,128)(2,1)S(1)} custom-call(s32[1]{0:T(128)} %bitcast.1.turn_ref, bf16[2560,1024]{1,0:T(8,128)(2,1)} %query.3, bf16[2560,256]{1,0:T(8,128)(2,1)} %key.3, bf16[2560,256]{1,0:T(8,128)(2,1)} %value.3, f32[64,128]{1,0:T(8,128)S(1)} %get-tuple-element.81.after.refs_5_, bf16[2560,1536]{1,0:T(8,128)(2,1)S(1)} %load_inputs.2.refs_0_), custom_call_target="tpu_custom_call" | custom-call | bytes 20000000 | tf_op jit(solution)/shard_map/load_inputs/pallas_call | solution.py:535
  23.5 3.4 %load_others.1 = (bf16[512,1024]{1,0:T(8,128)(2,1)S(1)}, bf16[512,256]{1,0:T(8,128)(2,1)S(1)}, bf16[512,256]{1,0:T(8,128)(2,1)S(1)}, bf16[1024,2560]{1,0:T(8,128...) custom-call(bf16[512,1024]{1,0:T(8,128)(2,1)} %bitcast.40, ...), custom_call_target="tpu_custom_call" | custom-call | bytes 20000000 | tf_op jit(solution)/shard_map/load_others/pallas_call | solution.py:576
  30.5 2.9 %attend_step.4 = (bf16[64,704]{1,0:T(8,128)(2,1)S(1)}, bf16[64,704]{1,0:T(8,128)(2,1)S(1)}, bf16[64,704]{1,0:T(8,128)(2,1)S(1)}, bf16[64,704]{1,0:T(8,128)(2,1)S...) custom-call(bf16[64,832]{1,0:T(8,128)(2,1)S(1)} %collective-permute-done.4.refs_0_, ...), custom_call_target="tpu_custom_call" | custom-call | tf_op jit(solution)/shard_map/attend_step/pallas_call | solution.py:646
  33.4 4.1 %collective-permute-start.10 = (bf16[64,704]{1,0:T(8,128)(2,1)S(1)}, bf16[64,704]{1,0:T(8,128)(2,1)S(1)}, u32[]{:S(2)}, u32[]{:S(2)}) collective-permute-start(bf16[64,704]{1,0:T(8,128)(2,1)S(1)} %get-tuple-element.100), channel_id=1, source_target_pairs={{0,3},{1,2},{2,1},{3,0},{4,7},{5,6},{6,5},{7,4},{8,11},{9,10},{10,... | collective-permute-start | bytes 270344 | tf_op jit(solution)/shard_map/ppermute | solution.py:431
  38.2 3.0 %collective-permute-done.10.refs_2_ = bf16[64,704]{1,0:T(8,128)(2,1)S(1)} collective-permute-done((bf16[64,704]{1,0:T(8,128)(2,1)S(1)}, bf16[64,704]{1,0:T(8,128)(2,1)S(1)}, u32[]{:S(2)}, u32[]{:S(2)}) %collective-permute-start.10) | collective-permute-done | bytes 90144 | tf_op jit(solution)/shard_map/ppermute | solution.py:431
  41.2 2.6 %collective-permute-done.11.refs_3_ = bf16[64,704]{1,0:T(8,128)(2,1)S(1)} collective-permute-done((bf16[64,704]{1,0:T(8,128)(2,1)S(1)}, bf16[64,704]{1,0:T(8,128)(2,1)S(1)}, u32[]{:S(2)}, u32[]{:S(2)}) %collective-permute-start.11) | collective-permute-done | bytes 90144 | tf_op jit(solution)/shard_map/ppermute | solution.py:431
  49.9 4.8 %collective-permute-done.12.refs_2_ = bf16[64,832]{1,0:T(8,128)(2,1)S(1)} collective-permute-done((bf16[64,832]{1,0:T(8,128)(2,1)S(1)}, bf16[64,832]{1,0:T(8,128)(2,1)S(1)}, u32[]{:S(2)}, u32[]{:S(2)}) %collective-permute-start.12) | collective-permute-done | bytes 106528 | tf_op jit(solution)/shard_map/ppermute | solution.py:431
  56.0 3.5 %collective-permute-done.13.refs_0_ = bf16[64,832]{1,0:T(8,128)(2,1)S(1)} collective-permute-done((bf16[64,832]{1,0:T(8,128)(2,1)S(1)}, bf16[64,832]{1,0:T(8,128)(2,1)S(1)}, u32[]{:S(2)}, u32[]{:S(2)}) %collective-permute-start.13) | collective-permute-done | bytes 106528 | tf_op jit(solution)/shard_map/ppermute | solution.py:431
  59.5 2.8 %attend_step.5 = (bf16[64,704]{1,0:T(8,128)(2,1)S(1)}, bf16[64,704]{1,0:T(8,128)(2,1)S(1)}, bf16[64,704]{1,0:T(8,128)(2,1)S(1)}, bf16[64,704]{1,0:T(8,128)(2,1)S...) custom-call(bf16[64,832]{1,0:T(8,128)(2,1)S(1)} %collective-permute-done.13.refs_0_, ...), custom_call_target="tpu_custom_call" | custom-call | tf_op jit(solution)/shard_map/attend_step/pallas_call | solution.py:646
  65.8 5.2 %collective-permute-done.15.refs_1_ = bf16[64,704]{1,0:T(8,128)(2,1)S(1)} collective-permute-done((bf16[64,704]{1,0:T(8,128)(2,1)S(1)}, bf16[64,704]{1,0:T(8,128)(2,1)S(1)}, u32[]{:S(2)}, u32[]{:S(2)}) %collective-permute-start.15) | collective-permute-done | bytes 90144 | tf_op jit(solution)/shard_map/ppermute | solution.py:431
  72.1 2.3 %collective-permute-start.18 = (bf16[64,832]{1,0:T(8,128)(2,1)S(1)}, bf16[64,832]{1,0:T(8,128)(2,1)S(1)}, u32[]{:S(2)}, u32[]{:S(2)}) collective-permute-start(bf16[64,832]{1,0:T(8,128)(2,1)S(1)} %between.4.refs_0_.refs_4_), channel_id=1, source_target_pairs={{0,2},{1,3},{2,0},{3,1},{4,6},{5,7},{6,4},{7,5},{8,10},{9,11},{10,... | collective-permute-start | bytes 319496 | tf_op jit(solution)/shard_map/ppermute | solution.py:431
  74.8 5.0 %collective-permute-done.18.refs_2_ = bf16[64,832]{1,0:T(8,128)(2,1)S(1)} collective-permute-done((bf16[64,832]{1,0:T(8,128)(2,1)S(1)}, bf16[64,832]{1,0:T(8,128)(2,1)S(1)}, u32[]{:S(2)}, u32[]{:S(2)}) %collective-permute-start.18) | collective-permute-done | bytes 106528 | tf_op jit(solution)/shard_map/ppermute | solution.py:431
  81.7 2.8 %collective-permute-done.19.refs_0_ = bf16[64,832]{1,0:T(8,128)(2,1)S(1)} collective-permute-done((bf16[64,832]{1,0:T(8,128)(2,1)S(1)}, bf16[64,832]{1,0:T(8,128)(2,1)S(1)}, u32[]{:S(2)}, u32[]{:S(2)}) %collective-permute-start.19) | collective-permute-done | bytes 106528 | tf_op jit(solution)/shard_map/ppermute | solution.py:431
  84.5 2.8 %attend_step.6 = (bf16[64,704]{1,0:T(8,128)(2,1)S(1)}, bf16[64,704]{1,0:T(8,128)(2,1)S(1)}, bf16[64,704]{1,0:T(8,128)(2,1)S(1)}, bf16[64,704]{1,0:T(8,128)(2,1)S...) custom-call(bf16[64,832]{1,0:T(8,128)(2,1)S(1)} %collective-permute-done.19.refs_0_, ...), custom_call_target="tpu_custom_call" | custom-call | tf_op jit(solution)/shard_map/attend_step/pallas_call | solution.py:646
  90.9 5.0 %collective-permute-done.21.refs_1_ = bf16[64,704]{1,0:T(8,128)(2,1)S(1)} collective-permute-done((bf16[64,704]{1,0:T(8,128)(2,1)S(1)}, bf16[64,704]{1,0:T(8,128)(2,1)S(1)}, u32[]{:S(2)}, u32[]{:S(2)}) %collective-permute-start.21) | collective-permute-done | bytes 90144 | tf_op jit(solution)/shard_map/ppermute | solution.py:431
  99.5 4.5 %collective-permute-done.24.refs_2_ = bf16[64,832]{1,0:T(8,128)(2,1)S(1)} collective-permute-done((bf16[64,832]{1,0:T(8,128)(2,1)S(1)}, bf16[64,832]{1,0:T(8,128)(2,1)S(1)}, u32[]{:S(2)}, u32[]{:S(2)}) %collective-permute-start.24) | collective-permute-done | bytes 106528 | tf_op jit(solution)/shard_map/ppermute | solution.py:431
  106.3 2.5 %collective-permute-done.25.refs_0_ = bf16[64,832]{1,0:T(8,128)(2,1)S(1)} collective-permute-done((bf16[64,832]{1,0:T(8,128)(2,1)S(1)}, bf16[64,832]{1,0:T(8,128)(2,1)S(1)}, u32[]{:S(2)}, u32[]{:S(2)}) %collective-permute-start.25) | collective-permute-done | bytes 106528 | tf_op jit(solution)/shard_map/ppermute | solution.py:431
  108.9 2.8 %attend_step.7 = (bf16[64,704]{1,0:T(8,128)(2,1)S(1)}, bf16[64,704]{1,0:T(8,128)(2,1)S(1)}, bf16[64,704]{1,0:T(8,128)(2,1)S(1)}, bf16[64,704]{1,0:T(8,128)(2,1)S...) custom-call(bf16[64,832]{1,0:T(8,128)(2,1)S(1)} %collective-permute-done.25.refs_0_, ...), custom_call_target="tpu_custom_call" | custom-call | tf_op jit(solution)/shard_map/attend_step/pallas_call | solution.py:646
  112.5 2.8 %collective-permute-start.28 = (bf16[64,704]{1,0:T(8,128)(2,1)S(1)}, bf16[64,704]{1,0:T(8,128)(2,1)S(1)}, u32[]{:S(2)}, u32[]{:S(2)}) collective-permute-start(bf16[64,704]{1,0:T(8,128)(2,1)S(1)} %get-tuple-element.129), channel_id=1, source_target_pairs={{0,3},{1,2},{2,1},{3,0},{4,7},{5,6},{6,5},{7,4},{8,11},{9,10},{10,... | collective-permute-start | bytes 270344 | tf_op jit(solution)/shard_map/ppermute | solution.py:431
  115.3 4.2 %collective-permute-done.27.refs_1_ = bf16[64,704]{1,0:T(8,128)(2,1)S(1)} collective-permute-done((bf16[64,704]{1,0:T(8,128)(2,1)S(1)}, bf16[64,704]{1,0:T(8,128)(2,1)S(1)}, u32[]{:S(2)}, u32[]{:S(2)}) %collective-permute-start.27) | collective-permute-done | bytes 90144 | tf_op jit(solution)/shard_map/ppermute | solution.py:431
  (77 shorter events, 42.9 us)
Async XLA Ops:
  2.6 10.6 %collective-permute-start = (bf16[16,768]{1,0:T(8,128)(2,1)S(1)}, bf16[16,768]{1,0:T(8,128)(2,1)S(1)}, u32[]{:S(2)}, u32[]{:S(2)}) collective-permute-start(bf16[16,768]{1,0:T(8,128)(2,1)S(1)} %get-tuple-element.71), channel_id=1, source_target_pairs={{0,4},{4,0},{8,12},{12,8},{1,5},{5,1},{9,13},{13,9},{2,6},{6,2},{1... | collective-permute-start | bytes 73736 | tf_op jit(solution)/shard_map/ppermute | solution.py:431
  3.2 10.3 %collective-permute-start.1 = (bf16[16,768]{1,0:T(8,128)(2,1)S(1)}, bf16[16,768]{1,0:T(8,128)(2,1)S(1)}, u32[]{:S(2)}, u32[]{:S(2)}) collective-permute-start(bf16[16,768]{1,0:T(8,128)(2,1)S(1)} %get-tuple-element.73), channel_id=1, source_target_pairs={{0,12},{4,8},{8,4},{12,0},{1,13},{5,9},{9,5},{13,1},{2,14},{6,10},... | collective-permute-start | bytes 73736 | tf_op jit(solution)/shard_map/ppermute | solution.py:431
  5.8 7.7 %collective-permute-start.2 = (bf16[16,768]{1,0:T(8,128)(2,1)S(1)}, bf16[16,768]{1,0:T(8,128)(2,1)S(1)}, u32[]{:S(2)}, u32[]{:S(2)}) collective-permute-start(bf16[16,768]{1,0:T(8,128)(2,1)S(1)} %get-tuple-element.74), channel_id=1, source_target_pairs={{0,8},{4,12},{8,0},{12,4},{1,9},{5,13},{9,1},{13,5},{2,10},{6,14},... | collective-permute-start | bytes 73736 | tf_op jit(solution)/shard_map/ppermute | solution.py:431
  10.5 18.3 %collective-permute-start.6 = (bf16[4,16,24,128]{3,2,1,0:T(8,128)(2,1)}, bf16[4,16,24,128]{3,2,1,0:T(8,128)(2,1)S(1)}, u32[]{:S(2)}, u32[]{:S(2)}) collective-permute-start(bf16[4,16,24,128]{3,2,1,0:T(8,128)(2,1)} %get-tuple-element.93), channel_id=1, source_target_pairs={{0,12},{4,8},{8,4},{12,0},{1,13},{5,9},{9,5},{13,1},{2,14},{6,10},... | collective-permute-start | bytes 1179656 | tf_op jit(solution)/shard_map/ppermute | solution.py:431
  11.9 18.7 %collective-permute-start.7 = (bf16[4,16,24,128]{3,2,1,0:T(8,128)(2,1)}, bf16[4,16,24,128]{3,2,1,0:T(8,128)(2,1)S(1)}, u32[]{:S(2)}, u32[]{:S(2)}) collective-permute-start(bf16[4,16,24,128]{3,2,1,0:T(8,128)(2,1)} %get-tuple-element.94), channel_id=1, source_target_pairs={{0,8},{4,12},{8,0},{12,4},{1,9},{5,13},{9,1},{13,5},{2,10},{6,14},... | collective-permute-start | bytes 1179656 | tf_op jit(solution)/shard_map/ppermute | solution.py:431
  13.3 17.3 %collective-permute-start.8 = (bf16[4,16,24,128]{3,2,1,0:T(8,128)(2,1)}, bf16[4,16,24,128]{3,2,1,0:T(8,128)(2,1)S(1)}, u32[]{:S(2)}, u32[]{:S(2)}) collective-permute-start(bf16[4,16,24,128]{3,2,1,0:T(8,128)(2,1)} %copy-done.2), channel_id=1, source_target_pairs={{0,4},{4,0},{8,12},{12,8},{1,5},{5,1},{9,13},{13,9},{2,6},{6,2},{1... | collective-permute-start | bytes 1179656 | tf_op jit(solution)/shard_map/ppermute | solution.py:431
  14.3 8.5 %collective-permute-start.3 = (bf16[64,832]{1,0:T(8,128)(2,1)S(1)}, bf16[64,832]{1,0:T(8,128)(2,1)S(1)}, u32[]{:S(2)}, u32[]{:S(2)}) collective-permute-start(bf16[64,832]{1,0:T(8,128)(2,1)S(1)} %get-tuple-element.83.refs_0_.refs_4_), channel_id=1, source_target_pairs={{0,2},{1,3},{2,0},{3,1},{4,6},{5,7},{6,4},{7,5},{8,10},{9,11},{10,... | collective-permute-start | bytes 319496 | tf_op jit(solution)/shard_map/ppermute | solution.py:431
  17.2 9.8 %collective-permute-start.5 = (bf16[64,832]{1,0:T(8,128)(2,1)S(1)}, bf16[64,832]{1,0:T(8,128)(2,1)S(1)}, u32[]{:S(2)}, u32[]{:S(2)}) collective-permute-start(bf16[64,832]{1,0:T(8,128)(2,1)S(1)} %get-tuple-element.83.refs_0_.refs_4_), channel_id=1, source_target_pairs={{0,1},{1,0},{2,3},{3,2},{4,5},{5,4},{6,7},{7,6},{8,9},{9,8},{10,11... | collective-permute-start | bytes 319496 | tf_op jit(solution)/shard_map/ppermute | solution.py:431
  33.4 7.8 %collective-permute-start.10 = (bf16[64,704]{1,0:T(8,128)(2,1)S(1)}, bf16[64,704]{1,0:T(8,128)(2,1)S(1)}, u32[]{:S(2)}, u32[]{:S(2)}) collective-permute-start(bf16[64,704]{1,0:T(8,128)(2,1)S(1)} %get-tuple-element.100), channel_id=1, source_target_pairs={{0,3},{1,2},{2,1},{3,0},{4,7},{5,6},{6,5},{7,4},{8,11},{9,10},{10,... | collective-permute-start | bytes 270344 | tf_op jit(solution)/shard_map/ppermute | solution.py:431
  37.6 6.2 %collective-permute-start.11 = (bf16[64,704]{1,0:T(8,128)(2,1)S(1)}, bf16[64,704]{1,0:T(8,128)(2,1)S(1)}, u32[]{:S(2)}, u32[]{:S(2)}) collective-permute-start(bf16[64,704]{1,0:T(8,128)(2,1)S(1)} %get-tuple-element.101), channel_id=1, source_target_pairs={{0,1},{1,0},{2,3},{3,2},{4,5},{5,4},{6,7},{7,6},{8,9},{9,8},{10,11... | collective-permute-start | bytes 270344 | tf_op jit(solution)/shard_map/ppermute | solution.py:431
  37.6 8.5 %collective-permute-start.9 = (bf16[64,704]{1,0:T(8,128)(2,1)S(1)}, bf16[64,704]{1,0:T(8,128)(2,1)S(1)}, u32[]{:S(2)}, u32[]{:S(2)}) collective-permute-start(bf16[64,704]{1,0:T(8,128)(2,1)S(1)} %get-tuple-element.99), channel_id=1, source_target_pairs={{0,2},{1,3},{2,0},{3,1},{4,6},{5,7},{6,4},{7,5},{8,10},{9,11},{10,... | collective-permute-start | bytes 270344 | tf_op jit(solution)/shard_map/ppermute | solution.py:431
  46.8 7.9 %collective-permute-start.12 = (bf16[64,832]{1,0:T(8,128)(2,1)S(1)}, bf16[64,832]{1,0:T(8,128)(2,1)S(1)}, u32[]{:S(2)}, u32[]{:S(2)}) collective-permute-start(bf16[64,832]{1,0:T(8,128)(2,1)S(1)} %between.3.refs_0_.refs_4_), channel_id=1, source_target_pairs={{0,2},{1,3},{2,0},{3,1},{4,6},{5,7},{6,4},{7,5},{8,10},{9,11},{10,... | collective-permute-start | bytes 319496 | tf_op jit(solution)/shard_map/ppermute | solution.py:431
  48.3 6.6 %collective-permute-start.14 = (bf16[64,832]{1,0:T(8,128)(2,1)S(1)}, bf16[64,832]{1,0:T(8,128)(2,1)S(1)}, u32[]{:S(2)}, u32[]{:S(2)}) collective-permute-start(bf16[64,832]{1,0:T(8,128)(2,1)S(1)} %between.3.refs_0_.refs_4_), channel_id=1, source_target_pairs={{0,1},{1,0},{2,3},{3,2},{4,5},{5,4},{6,7},{7,6},{8,9},{9,8},{10,11... | collective-permute-start | bytes 319496 | tf_op jit(solution)/shard_map/ppermute | solution.py:431
  62.3 8.8 %collective-permute-start.15 = (bf16[64,704]{1,0:T(8,128)(2,1)S(1)}, bf16[64,704]{1,0:T(8,128)(2,1)S(1)}, u32[]{:S(2)}, u32[]{:S(2)}) collective-permute-start(bf16[64,704]{1,0:T(8,128)(2,1)S(1)} %get-tuple-element.110), channel_id=1, source_target_pairs={{0,2},{1,3},{2,0},{3,1},{4,6},{5,7},{6,4},{7,5},{8,10},{9,11},{10,... | collective-permute-start | bytes 270344 | tf_op jit(solution)/shard_map/ppermute | solution.py:431
  63.1 8.0 %collective-permute-start.16 = (bf16[64,704]{1,0:T(8,128)(2,1)S(1)}, bf16[64,704]{1,0:T(8,128)(2,1)S(1)}, u32[]{:S(2)}, u32[]{:S(2)}) collective-permute-start(bf16[64,704]{1,0:T(8,128)(2,1)S(1)} %get-tuple-element.111), channel_id=1, source_target_pairs={{0,3},{1,2},{2,1},{3,0},{4,7},{5,6},{6,5},{7,4},{8,11},{9,10},{10,... | collective-permute-start | bytes 270344 | tf_op jit(solution)/shard_map/ppermute | solution.py:431
  64.7 6.6 %collective-permute-start.17 = (bf16[64,704]{1,0:T(8,128)(2,1)S(1)}, bf16[64,704]{1,0:T(8,128)(2,1)S(1)}, u32[]{:S(2)}, u32[]{:S(2)}) collective-permute-start(bf16[64,704]{1,0:T(8,128)(2,1)S(1)} %get-tuple-element.112), channel_id=1, source_target_pairs={{0,1},{1,0},{2,3},{3,2},{4,5},{5,4},{6,7},{7,6},{8,9},{9,8},{10,11... | collective-permute-start | bytes 270344 | tf_op jit(solution)/shard_map/ppermute | solution.py:431
  72.1 7.7 %collective-permute-start.18 = (bf16[64,832]{1,0:T(8,128)(2,1)S(1)}, bf16[64,832]{1,0:T(8,128)(2,1)S(1)}, u32[]{:S(2)}, u32[]{:S(2)}) collective-permute-start(bf16[64,832]{1,0:T(8,128)(2,1)S(1)} %between.4.refs_0_.refs_4_), channel_id=1, source_target_pairs={{0,2},{1,3},{2,0},{3,1},{4,6},{5,7},{6,4},{7,5},{8,10},{9,11},{10,... | collective-permute-start | bytes 319496 | tf_op jit(solution)/shard_map/ppermute | solution.py:431
  87.4 8.6 %collective-permute-start.21 = (bf16[64,704]{1,0:T(8,128)(2,1)S(1)}, bf16[64,704]{1,0:T(8,128)(2,1)S(1)}, u32[]{:S(2)}, u32[]{:S(2)}) collective-permute-start(bf16[64,704]{1,0:T(8,128)(2,1)S(1)} %get-tuple-element.119), channel_id=1, source_target_pairs={{0,2},{1,3},{2,0},{3,1},{4,6},{5,7},{6,4},{7,5},{8,10},{9,11},{10,... | collective-permute-start | bytes 270344 | tf_op jit(solution)/shard_map/ppermute | solution.py:431
  88.7 7.2 %collective-permute-start.22 = (bf16[64,704]{1,0:T(8,128)(2,1)S(1)}, bf16[64,704]{1,0:T(8,128)(2,1)S(1)}, u32[]{:S(2)}, u32[]{:S(2)}) collective-permute-start(bf16[64,704]{1,0:T(8,128)(2,1)S(1)} %get-tuple-element.120), channel_id=1, source_target_pairs={{0,3},{1,2},{2,1},{3,0},{4,7},{5,6},{6,5},{7,4},{8,11},{9,10},{10,... | collective-permute-start | bytes 270344 | tf_op jit(solution)/shard_map/ppermute | solution.py:431
  89.8 6.4 %collective-permute-start.23 = (bf16[64,704]{1,0:T(8,128)(2,1)S(1)}, bf16[64,704]{1,0:T(8,128)(2,1)S(1)}, u32[]{:S(2)}, u32[]{:S(2)}) collective-permute-start(bf16[64,704]{1,0:T(8,128)(2,1)S(1)} %get-tuple-element.121), channel_id=1, source_target_pairs={{0,1},{1,0},{2,3},{3,2},{4,5},{5,4},{6,7},{7,6},{8,9},{9,8},{10,11... | collective-permute-start | bytes 270344 | tf_op jit(solution)/shard_map/ppermute | solution.py:431
  97.1 7.0 %collective-permute-start.24 = (bf16[64,832]{1,0:T(8,128)(2,1)S(1)}, bf16[64,832]{1,0:T(8,128)(2,1)S(1)}, u32[]{:S(2)}, u32[]{:S(2)}) collective-permute-start(bf16[64,832]{1,0:T(8,128)(2,1)S(1)} %between.5.refs_0_.refs_4_), channel_id=1, source_target_pairs={{0,2},{1,3},{2,0},{3,1},{4,6},{5,7},{6,4},{7,5},{8,10},{9,11},{10,... | collective-permute-start | bytes 319496 | tf_op jit(solution)/shard_map/ppermute | solution.py:431
  98.1 7.1 %collective-permute-start.26 = (bf16[64,832]{1,0:T(8,128)(2,1)S(1)}, bf16[64,832]{1,0:T(8,128)(2,1)S(1)}, u32[]{:S(2)}, u32[]{:S(2)}) collective-permute-start(bf16[64,832]{1,0:T(8,128)(2,1)S(1)} %between.5.refs_0_.refs_4_), channel_id=1, source_target_pairs={{0,1},{1,0},{2,3},{3,2},{4,5},{5,4},{6,7},{7,6},{8,9},{9,8},{10,11... | collective-permute-start | bytes 319496 | tf_op jit(solution)/shard_map/ppermute | solution.py:431
  111.7 7.7 %collective-permute-start.27 = (bf16[64,704]{1,0:T(8,128)(2,1)S(1)}, bf16[64,704]{1,0:T(8,128)(2,1)S(1)}, u32[]{:S(2)}, u32[]{:S(2)}) collective-permute-start(bf16[64,704]{1,0:T(8,128)(2,1)S(1)} %get-tuple-element.128), channel_id=1, source_target_pairs={{0,2},{1,3},{2,0},{3,1},{4,6},{5,7},{6,4},{7,5},{8,10},{9,11},{10,... | collective-permute-start | bytes 270344 | tf_op jit(solution)/shard_map/ppermute | solution.py:431
  112.5 7.0 %collective-permute-start.28 = (bf16[64,704]{1,0:T(8,128)(2,1)S(1)}, bf16[64,704]{1,0:T(8,128)(2,1)S(1)}, u32[]{:S(2)}, u32[]{:S(2)}) collective-permute-start(bf16[64,704]{1,0:T(8,128)(2,1)S(1)} %get-tuple-element.129), channel_id=1, source_target_pairs={{0,3},{1,2},{2,1},{3,0},{4,7},{5,6},{6,5},{7,4},{8,11},{9,10},{10,... | collective-permute-start | bytes 270344 | tf_op jit(solution)/shard_map/ppermute | solution.py:431
  (12 other events, 50.4 us)

commit v7 on v6

--- a/solution.py
+++ b/solution.py
@@ -31,10 +31,10 @@
     return [refs[order.index(block)] for block in range(len(order))]
 
 
-def copy_all(pairs, sems):
+def copy_all(pairs, sems, first=0):
     copies = [
         pltpu.make_async_copy(source, target, sems.at[index])
-        for index, (source, target) in enumerate(pairs)
+        for index, (source, target) in enumerate(pairs, first)
     ]
     for copy in copies:
         copy.start()
@@ -82,7 +82,7 @@
         )
         return carry
 
-    lax.fori_loop(0, rows, put, 0)
+    lax.fori_loop(0, rows, put, 0, unroll=8)
     chosen = place[...].astype(bf16)
     place_ref[...] = chosen
     across = (((0,), (0,)), ((), ()))
@@ -108,7 +108,12 @@
     kinds = down_ref.shape[0]
     total = down_hbm.shape[0]
     rank = down_hbm.shape[1] // kinds
-    pairs = [(key_hbm, key_ref), (value_hbm, value_ref)]
+    copies = copy_all([(key_hbm, key_ref), (value_hbm, value_ref)], sems)
+    if groups * capacity > rows:
+        packed[...] = jnp.zeros_like(packed)
+    for copy in copies:
+        copy.wait()
+    pairs = []
     for kind in range(kinds):
         for d in range(total):
             pairs.append(
@@ -117,11 +122,7 @@
                     down_ref.at[kind, d * rank : (d + 1) * rank, :],
                 )
             )
-    copies = copy_all(pairs, sems)
-    if groups * capacity > rows:
-        packed[...] = jnp.zeros_like(packed)
-    for copy in copies[:2]:
-        copy.wait()
+    down_copies = copy_all(pairs, sems, len(copies))
 
     def put(row, carry):
         target = target_ref[row]
@@ -132,10 +133,10 @@
             packed[block, kv_local + g, position] = value_ref[row, g]
         return carry
 
-    lax.fori_loop(0, rows, put, 0)
+    lax.fori_loop(0, rows, put, 0, unroll=4)
     for s in range(groups):
         outgoing[s][...] = packed[s]
-    for copy in copies[2:]:
+    for copy in down_copies:
         copy.wait()
 
 

time: 126 us -> 126 us (level)
  no operation moved by 1% of the time
where the time goes in v7:
time: 126 us
  waiting for transfers between devices  52.3 us (42%)
  starting transfers between devices  37 us (29%)
  Pallas kernels  33.6 us (27%)
  local copies, waits for them, and re-layouts  1.59 us (1%)
    ppermute x33, waiting for transfers between devices, swap(): lax.ppermute(block, axis, [(i, i ^ mask) for i in range(lax.axis_size(axi...  52.3 us
    ppermute x33, starting transfers between devices, swap(): lax.ppermute(block, axis, [(i, i ^ mask) for i in range(lax.axis_size(axi...  37 us
    pallas_call x4, Pallas kernels, shards(): pl.pallas_call(functools.partial(step_kernel, total, rank, step, parts, l...  11.3 us
    pallas_call x4, Pallas kernels, shards(): pl.pallas_call(functools.partial(early_kernel, early), out_shape=[jax.Sha...  4.63 us
    pallas_call x1, Pallas kernels, shards(): pl.pallas_call(pack_kernel, out_shape=[jax.ShapeDtypeStruct(packed_shape,...  4.59 us
    pallas_call x1, Pallas kernels, load_others(): pl.pallas_call(load_others_kernel, out_shape=[jax.ShapeDtypeStruct(array....  3.44 us
    pallas_call x2, Pallas kernels, load_inputs(): pl.pallas_call(functools.partial(load_inputs_kernel, turn), out_shape=jax...  3.31 us
  transfers between devices with their start and end apart: 33, of which 21 were waited for; matrix products, arithmetic and copies ran while one was open for 1% of the time, Pallas kernels for 13%

profile of v7, /device:TPU:0, one launch (start us, length us, event | category | flops | bytes accessed | tf_op | source)
XLA Modules:
  0.0 125.6 jit_solution(13478551946514081523)
XLA Ops:
  2.5 2.6 %collective-permute-start.1 = (bf16[16,768]{1,0:T(8,128)(2,1)S(1)}, bf16[16,768]{1,0:T(8,128)(2,1)S(1)}, u32[]{:S(2)}, u32[]{:S(2)}) collective-permute-start(bf16[16,768]{1,0:T(8,128)(2,1)S(1)} %get-tuple-element.73), channel_id=1, source_target_pairs={{0,12},{4,8},{8,4},{12,0},{1,13},{5,9},{9,5},{13,1},{2,14},{6,10},... | collective-permute-start | bytes 73736 | tf_op jit(solution)/shard_map/ppermute | solution.py:432
  5.2 4.6 %pack_cache.1 = (bf16[4,16,24,128]{3,2,1,0:T(8,128)(2,1)S(1)}, bf16[4,16,24,128]{3,2,1,0:T(8,128)(2,1)S(1)}, bf16[4,16,24,128]{3,2,1,0:T(8,128)(2,1)}, bf16[4,16...) custom-call(s32[64]{0:T(128)S(1)} %get-tuple-element.79.target_ref, bf16[64,2,24,128]{3,2,1,0:T(8,128)(2,1)} %key_hbm.1, ...), custom_call_target="tpu_custom_call" | custom-call | tf_op jit(solution)/shard_map/pack_cache/pallas_call | solution.py:511
  14.4 2.9 %collective-permute-start.3 = (bf16[64,832]{1,0:T(8,128)(2,1)S(1)}, bf16[64,832]{1,0:T(8,128)(2,1)S(1)}, u32[]{:S(2)}, u32[]{:S(2)}) collective-permute-start(bf16[64,832]{1,0:T(8,128)(2,1)S(1)} %get-tuple-element.83.refs_0_.refs_4_), channel_id=1, source_target_pairs={{0,2},{1,3},{2,0},{3,1},{4,6},{5,7},{6,4},{7,5},{8,10},{9,11},{10,... | collective-permute-start | bytes 319496 | tf_op jit(solution)/shard_map/ppermute | solution.py:432
  19.6 3.3 %load_inputs.3.refs_5_.refs_7_ = bf16[2560,1536]{1,0:T(8,128)(2,1)S(1)} custom-call(s32[1]{0:T(128)} %bitcast.1.turn_ref, bf16[2560,1024]{1,0:T(8,128)(2,1)} %query.3, bf16[2560,256]{1,0:T(8,128)(2,1)} %key.3, bf16[2560,256]{1,0:T(8,128)(2,1)} %value.3, f32[64,128]{1,0:T(8,128)S(1)} %get-tuple-element.81.after.refs_5_, bf16[2560,1536]{1,0:T(8,128)(2,1)S(1)} %load_inputs.2.refs_0_), custom_call_target="tpu_custom_call" | custom-call | bytes 20000000 | tf_op jit(solution)/shard_map/load_inputs/pallas_call | solution.py:536
  23.6 3.4 %load_others.1 = (bf16[512,1024]{1,0:T(8,128)(2,1)S(1)}, bf16[512,256]{1,0:T(8,128)(2,1)S(1)}, bf16[512,256]{1,0:T(8,128)(2,1)S(1)}, bf16[1024,2560]{1,0:T(8,128...) custom-call(bf16[512,1024]{1,0:T(8,128)(2,1)} %bitcast.40, ...), custom_call_target="tpu_custom_call" | custom-call | bytes 20000000 | tf_op jit(solution)/shard_map/load_others/pallas_call | solution.py:577
  30.6 2.9 %attend_step.4 = (bf16[64,704]{1,0:T(8,128)(2,1)S(1)}, bf16[64,704]{1,0:T(8,128)(2,1)S(1)}, bf16[64,704]{1,0:T(8,128)(2,1)S(1)}, bf16[64,704]{1,0:T(8,128)(2,1)S...) custom-call(bf16[64,832]{1,0:T(8,128)(2,1)S(1)} %collective-permute-done.4.refs_0_, ...), custom_call_target="tpu_custom_call" | custom-call | tf_op jit(solution)/shard_map/attend_step/pallas_call | solution.py:647
  33.5 4.1 %collective-permute-start.10 = (bf16[64,704]{1,0:T(8,128)(2,1)S(1)}, bf16[64,704]{1,0:T(8,128)(2,1)S(1)}, u32[]{:S(2)}, u32[]{:S(2)}) collective-permute-start(bf16[64,704]{1,0:T(8,128)(2,1)S(1)} %get-tuple-element.100), channel_id=1, source_target_pairs={{0,3},{1,2},{2,1},{3,0},{4,7},{5,6},{6,5},{7,4},{8,11},{9,10},{10,... | collective-permute-start | bytes 270344 | tf_op jit(solution)/shard_map/ppermute | solution.py:432
  38.3 3.0 %collective-permute-done.10.refs_2_ = bf16[64,704]{1,0:T(8,128)(2,1)S(1)} collective-permute-done((bf16[64,704]{1,0:T(8,128)(2,1)S(1)}, bf16[64,704]{1,0:T(8,128)(2,1)S(1)}, u32[]{:S(2)}, u32[]{:S(2)}) %collective-permute-start.10) | collective-permute-done | bytes 90144 | tf_op jit(solution)/shard_map/ppermute | solution.py:432
  41.3 2.6 %collective-permute-done.11.refs_3_ = bf16[64,704]{1,0:T(8,128)(2,1)S(1)} collective-permute-done((bf16[64,704]{1,0:T(8,128)(2,1)S(1)}, bf16[64,704]{1,0:T(8,128)(2,1)S(1)}, u32[]{:S(2)}, u32[]{:S(2)}) %collective-permute-start.11) | collective-permute-done | bytes 90144 | tf_op jit(solution)/shard_map/ppermute | solution.py:432
  43.9 2.3 %collective-permute-done.9.refs_1_ = bf16[64,704]{1,0:T(8,128)(2,1)S(1)} collective-permute-done((bf16[64,704]{1,0:T(8,128)(2,1)S(1)}, bf16[64,704]{1,0:T(8,128)(2,1)S(1)}, u32[]{:S(2)}, u32[]{:S(2)}) %collective-permute-start.9) | collective-permute-done | bytes 90144 | tf_op jit(solution)/shard_map/ppermute | solution.py:432
  50.0 4.8 %collective-permute-done.12.refs_2_ = bf16[64,832]{1,0:T(8,128)(2,1)S(1)} collective-permute-done((bf16[64,832]{1,0:T(8,128)(2,1)S(1)}, bf16[64,832]{1,0:T(8,128)(2,1)S(1)}, u32[]{:S(2)}, u32[]{:S(2)}) %collective-permute-start.12) | collective-permute-done | bytes 106528 | tf_op jit(solution)/shard_map/ppermute | solution.py:432
  56.1 3.5 %collective-permute-done.13.refs_0_ = bf16[64,832]{1,0:T(8,128)(2,1)S(1)} collective-permute-done((bf16[64,832]{1,0:T(8,128)(2,1)S(1)}, bf16[64,832]{1,0:T(8,128)(2,1)S(1)}, u32[]{:S(2)}, u32[]{:S(2)}) %collective-permute-start.13) | collective-permute-done | bytes 106528 | tf_op jit(solution)/shard_map/ppermute | solution.py:432
  59.6 2.8 %attend_step.5 = (bf16[64,704]{1,0:T(8,128)(2,1)S(1)}, bf16[64,704]{1,0:T(8,128)(2,1)S(1)}, bf16[64,704]{1,0:T(8,128)(2,1)S(1)}, bf16[64,704]{1,0:T(8,128)(2,1)S...) custom-call(bf16[64,832]{1,0:T(8,128)(2,1)S(1)} %collective-permute-done.13.refs_0_, ...), custom_call_target="tpu_custom_call" | custom-call | tf_op jit(solution)/shard_map/attend_step/pallas_call | solution.py:647
  65.9 5.2 %collective-permute-done.15.refs_1_ = bf16[64,704]{1,0:T(8,128)(2,1)S(1)} collective-permute-done((bf16[64,704]{1,0:T(8,128)(2,1)S(1)}, bf16[64,704]{1,0:T(8,128)(2,1)S(1)}, u32[]{:S(2)}, u32[]{:S(2)}) %collective-permute-start.15) | collective-permute-done | bytes 90144 | tf_op jit(solution)/shard_map/ppermute | solution.py:432
  72.1 2.3 %collective-permute-start.18 = (bf16[64,832]{1,0:T(8,128)(2,1)S(1)}, bf16[64,832]{1,0:T(8,128)(2,1)S(1)}, u32[]{:S(2)}, u32[]{:S(2)}) collective-permute-start(bf16[64,832]{1,0:T(8,128)(2,1)S(1)} %between.4.refs_0_.refs_4_), channel_id=1, source_target_pairs={{0,2},{1,3},{2,0},{3,1},{4,6},{5,7},{6,4},{7,5},{8,10},{9,11},{10,... | collective-permute-start | bytes 319496 | tf_op jit(solution)/shard_map/ppermute | solution.py:432
  74.9 5.0 %collective-permute-done.18.refs_2_ = bf16[64,832]{1,0:T(8,128)(2,1)S(1)} collective-permute-done((bf16[64,832]{1,0:T(8,128)(2,1)S(1)}, bf16[64,832]{1,0:T(8,128)(2,1)S(1)}, u32[]{:S(2)}, u32[]{:S(2)}) %collective-permute-start.18) | collective-permute-done | bytes 106528 | tf_op jit(solution)/shard_map/ppermute | solution.py:432
  81.8 2.8 %collective-permute-done.19.refs_0_ = bf16[64,832]{1,0:T(8,128)(2,1)S(1)} collective-permute-done((bf16[64,832]{1,0:T(8,128)(2,1)S(1)}, bf16[64,832]{1,0:T(8,128)(2,1)S(1)}, u32[]{:S(2)}, u32[]{:S(2)}) %collective-permute-start.19) | collective-permute-done | bytes 106528 | tf_op jit(solution)/shard_map/ppermute | solution.py:432
  84.6 2.8 %attend_step.6 = (bf16[64,704]{1,0:T(8,128)(2,1)S(1)}, bf16[64,704]{1,0:T(8,128)(2,1)S(1)}, bf16[64,704]{1,0:T(8,128)(2,1)S(1)}, bf16[64,704]{1,0:T(8,128)(2,1)S...) custom-call(bf16[64,832]{1,0:T(8,128)(2,1)S(1)} %collective-permute-done.19.refs_0_, ...), custom_call_target="tpu_custom_call" | custom-call | tf_op jit(solution)/shard_map/attend_step/pallas_call | solution.py:647
  91.0 5.0 %collective-permute-done.21.refs_1_ = bf16[64,704]{1,0:T(8,128)(2,1)S(1)} collective-permute-done((bf16[64,704]{1,0:T(8,128)(2,1)S(1)}, bf16[64,704]{1,0:T(8,128)(2,1)S(1)}, u32[]{:S(2)}, u32[]{:S(2)}) %collective-permute-start.21) | collective-permute-done | bytes 90144 | tf_op jit(solution)/shard_map/ppermute | solution.py:432
  99.6 4.5 %collective-permute-done.24.refs_2_ = bf16[64,832]{1,0:T(8,128)(2,1)S(1)} collective-permute-done((bf16[64,832]{1,0:T(8,128)(2,1)S(1)}, bf16[64,832]{1,0:T(8,128)(2,1)S(1)}, u32[]{:S(2)}, u32[]{:S(2)}) %collective-permute-start.24) | collective-permute-done | bytes 106528 | tf_op jit(solution)/shard_map/ppermute | solution.py:432
  106.4 2.5 %collective-permute-done.25.refs_0_ = bf16[64,832]{1,0:T(8,128)(2,1)S(1)} collective-permute-done((bf16[64,832]{1,0:T(8,128)(2,1)S(1)}, bf16[64,832]{1,0:T(8,128)(2,1)S(1)}, u32[]{:S(2)}, u32[]{:S(2)}) %collective-permute-start.25) | collective-permute-done | bytes 106528 | tf_op jit(solution)/shard_map/ppermute | solution.py:432
  109.0 2.8 %attend_step.7 = (bf16[64,704]{1,0:T(8,128)(2,1)S(1)}, bf16[64,704]{1,0:T(8,128)(2,1)S(1)}, bf16[64,704]{1,0:T(8,128)(2,1)S(1)}, bf16[64,704]{1,0:T(8,128)(2,1)S...) custom-call(bf16[64,832]{1,0:T(8,128)(2,1)S(1)} %collective-permute-done.25.refs_0_, ...), custom_call_target="tpu_custom_call" | custom-call | tf_op jit(solution)/shard_map/attend_step/pallas_call | solution.py:647
  112.6 2.8 %collective-permute-start.28 = (bf16[64,704]{1,0:T(8,128)(2,1)S(1)}, bf16[64,704]{1,0:T(8,128)(2,1)S(1)}, u32[]{:S(2)}, u32[]{:S(2)}) collective-permute-start(bf16[64,704]{1,0:T(8,128)(2,1)S(1)} %get-tuple-element.129), channel_id=1, source_target_pairs={{0,3},{1,2},{2,1},{3,0},{4,7},{5,6},{6,5},{7,4},{8,11},{9,10},{10,... | collective-permute-start | bytes 270344 | tf_op jit(solution)/shard_map/ppermute | solution.py:432
  115.4 4.2 %collective-permute-done.27.refs_1_ = bf16[64,704]{1,0:T(8,128)(2,1)S(1)} collective-permute-done((bf16[64,704]{1,0:T(8,128)(2,1)S(1)}, bf16[64,704]{1,0:T(8,128)(2,1)S(1)}, u32[]{:S(2)}, u32[]{:S(2)}) %collective-permute-start.27) | collective-permute-done | bytes 90144 | tf_op jit(solution)/shard_map/ppermute | solution.py:432
  (77 shorter events, 42.6 us)
Async XLA Ops:
  2.0 11.3 %collective-permute-start = (bf16[16,768]{1,0:T(8,128)(2,1)S(1)}, bf16[16,768]{1,0:T(8,128)(2,1)S(1)}, u32[]{:S(2)}, u32[]{:S(2)}) collective-permute-start(bf16[16,768]{1,0:T(8,128)(2,1)S(1)} %get-tuple-element.71), channel_id=1, source_target_pairs={{0,4},{4,0},{8,12},{12,8},{1,5},{5,1},{9,13},{13,9},{2,6},{6,2},{1... | collective-permute-start | bytes 73736 | tf_op jit(solution)/shard_map/ppermute | solution.py:432
  2.5 11.0 %collective-permute-start.1 = (bf16[16,768]{1,0:T(8,128)(2,1)S(1)}, bf16[16,768]{1,0:T(8,128)(2,1)S(1)}, u32[]{:S(2)}, u32[]{:S(2)}) collective-permute-start(bf16[16,768]{1,0:T(8,128)(2,1)S(1)} %get-tuple-element.73), channel_id=1, source_target_pairs={{0,12},{4,8},{8,4},{12,0},{1,13},{5,9},{9,5},{13,1},{2,14},{6,10},... | collective-permute-start | bytes 73736 | tf_op jit(solution)/shard_map/ppermute | solution.py:432
  5.2 8.4 %collective-permute-start.2 = (bf16[16,768]{1,0:T(8,128)(2,1)S(1)}, bf16[16,768]{1,0:T(8,128)(2,1)S(1)}, u32[]{:S(2)}, u32[]{:S(2)}) collective-permute-start(bf16[16,768]{1,0:T(8,128)(2,1)S(1)} %get-tuple-element.74), channel_id=1, source_target_pairs={{0,8},{4,12},{8,0},{12,4},{1,9},{5,13},{9,1},{13,5},{2,10},{6,14},... | collective-permute-start | bytes 73736 | tf_op jit(solution)/shard_map/ppermute | solution.py:432
  10.6 18.3 %collective-permute-start.6 = (bf16[4,16,24,128]{3,2,1,0:T(8,128)(2,1)}, bf16[4,16,24,128]{3,2,1,0:T(8,128)(2,1)S(1)}, u32[]{:S(2)}, u32[]{:S(2)}) collective-permute-start(bf16[4,16,24,128]{3,2,1,0:T(8,128)(2,1)} %get-tuple-element.93), channel_id=1, source_target_pairs={{0,12},{4,8},{8,4},{12,0},{1,13},{5,9},{9,5},{13,1},{2,14},{6,10},... | collective-permute-start | bytes 1179656 | tf_op jit(solution)/shard_map/ppermute | solution.py:432
  11.9 18.7 %collective-permute-start.7 = (bf16[4,16,24,128]{3,2,1,0:T(8,128)(2,1)}, bf16[4,16,24,128]{3,2,1,0:T(8,128)(2,1)S(1)}, u32[]{:S(2)}, u32[]{:S(2)}) collective-permute-start(bf16[4,16,24,128]{3,2,1,0:T(8,128)(2,1)} %get-tuple-element.94), channel_id=1, source_target_pairs={{0,8},{4,12},{8,0},{12,4},{1,9},{5,13},{9,1},{13,5},{2,10},{6,14},... | collective-permute-start | bytes 1179656 | tf_op jit(solution)/shard_map/ppermute | solution.py:432
  13.4 17.3 %collective-permute-start.8 = (bf16[4,16,24,128]{3,2,1,0:T(8,128)(2,1)}, bf16[4,16,24,128]{3,2,1,0:T(8,128)(2,1)S(1)}, u32[]{:S(2)}, u32[]{:S(2)}) collective-permute-start(bf16[4,16,24,128]{3,2,1,0:T(8,128)(2,1)} %copy-done.2), channel_id=1, source_target_pairs={{0,4},{4,0},{8,12},{12,8},{1,5},{5,1},{9,13},{13,9},{2,6},{6,2},{1... | collective-permute-start | bytes 1179656 | tf_op jit(solution)/shard_map/ppermute | solution.py:432
  14.4 8.5 %collective-permute-start.3 = (bf16[64,832]{1,0:T(8,128)(2,1)S(1)}, bf16[64,832]{1,0:T(8,128)(2,1)S(1)}, u32[]{:S(2)}, u32[]{:S(2)}) collective-permute-start(bf16[64,832]{1,0:T(8,128)(2,1)S(1)} %get-tuple-element.83.refs_0_.refs_4_), channel_id=1, source_target_pairs={{0,2},{1,3},{2,0},{3,1},{4,6},{5,7},{6,4},{7,5},{8,10},{9,11},{10,... | collective-permute-start | bytes 319496 | tf_op jit(solution)/shard_map/ppermute | solution.py:432
  17.3 9.8 %collective-permute-start.5 = (bf16[64,832]{1,0:T(8,128)(2,1)S(1)}, bf16[64,832]{1,0:T(8,128)(2,1)S(1)}, u32[]{:S(2)}, u32[]{:S(2)}) collective-permute-start(bf16[64,832]{1,0:T(8,128)(2,1)S(1)} %get-tuple-element.83.refs_0_.refs_4_), channel_id=1, source_target_pairs={{0,1},{1,0},{2,3},{3,2},{4,5},{5,4},{6,7},{7,6},{8,9},{9,8},{10,11... | collective-permute-start | bytes 319496 | tf_op jit(solution)/shard_map/ppermute | solution.py:432
  33.5 7.8 %collective-permute-start.10 = (bf16[64,704]{1,0:T(8,128)(2,1)S(1)}, bf16[64,704]{1,0:T(8,128)(2,1)S(1)}, u32[]{:S(2)}, u32[]{:S(2)}) collective-permute-start(bf16[64,704]{1,0:T(8,128)(2,1)S(1)} %get-tuple-element.100), channel_id=1, source_target_pairs={{0,3},{1,2},{2,1},{3,0},{4,7},{5,6},{6,5},{7,4},{8,11},{9,10},{10,... | collective-permute-start | bytes 270344 | tf_op jit(solution)/shard_map/ppermute | solution.py:432
  37.6 6.2 %collective-permute-start.11 = (bf16[64,704]{1,0:T(8,128)(2,1)S(1)}, bf16[64,704]{1,0:T(8,128)(2,1)S(1)}, u32[]{:S(2)}, u32[]{:S(2)}) collective-permute-start(bf16[64,704]{1,0:T(8,128)(2,1)S(1)} %get-tuple-element.101), channel_id=1, source_target_pairs={{0,1},{1,0},{2,3},{3,2},{4,5},{5,4},{6,7},{7,6},{8,9},{9,8},{10,11... | collective-permute-start | bytes 270344 | tf_op jit(solution)/shard_map/ppermute | solution.py:432
  37.7 8.5 %collective-permute-start.9 = (bf16[64,704]{1,0:T(8,128)(2,1)S(1)}, bf16[64,704]{1,0:T(8,128)(2,1)S(1)}, u32[]{:S(2)}, u32[]{:S(2)}) collective-permute-start(bf16[64,704]{1,0:T(8,128)(2,1)S(1)} %get-tuple-element.99), channel_id=1, source_target_pairs={{0,2},{1,3},{2,0},{3,1},{4,6},{5,7},{6,4},{7,5},{8,10},{9,11},{10,... | collective-permute-start | bytes 270344 | tf_op jit(solution)/shard_map/ppermute | solution.py:432
  46.9 7.9 %collective-permute-start.12 = (bf16[64,832]{1,0:T(8,128)(2,1)S(1)}, bf16[64,832]{1,0:T(8,128)(2,1)S(1)}, u32[]{:S(2)}, u32[]{:S(2)}) collective-permute-start(bf16[64,832]{1,0:T(8,128)(2,1)S(1)} %between.3.refs_0_.refs_4_), channel_id=1, source_target_pairs={{0,2},{1,3},{2,0},{3,1},{4,6},{5,7},{6,4},{7,5},{8,10},{9,11},{10,... | collective-permute-start | bytes 319496 | tf_op jit(solution)/shard_map/ppermute | solution.py:432
  48.4 6.6 %collective-permute-start.14 = (bf16[64,832]{1,0:T(8,128)(2,1)S(1)}, bf16[64,832]{1,0:T(8,128)(2,1)S(1)}, u32[]{:S(2)}, u32[]{:S(2)}) collective-permute-start(bf16[64,832]{1,0:T(8,128)(2,1)S(1)} %between.3.refs_0_.refs_4_), channel_id=1, source_target_pairs={{0,1},{1,0},{2,3},{3,2},{4,5},{5,4},{6,7},{7,6},{8,9},{9,8},{10,11... | collective-permute-start | bytes 319496 | tf_op jit(solution)/shard_map/ppermute | solution.py:432
  62.4 8.8 %collective-permute-start.15 = (bf16[64,704]{1,0:T(8,128)(2,1)S(1)}, bf16[64,704]{1,0:T(8,128)(2,1)S(1)}, u32[]{:S(2)}, u32[]{:S(2)}) collective-permute-start(bf16[64,704]{1,0:T(8,128)(2,1)S(1)} %get-tuple-element.110), channel_id=1, source_target_pairs={{0,2},{1,3},{2,0},{3,1},{4,6},{5,7},{6,4},{7,5},{8,10},{9,11},{10,... | collective-permute-start | bytes 270344 | tf_op jit(solution)/shard_map/ppermute | solution.py:432
  63.1 8.0 %collective-permute-start.16 = (bf16[64,704]{1,0:T(8,128)(2,1)S(1)}, bf16[64,704]{1,0:T(8,128)(2,1)S(1)}, u32[]{:S(2)}, u32[]{:S(2)}) collective-permute-start(bf16[64,704]{1,0:T(8,128)(2,1)S(1)} %get-tuple-element.111), channel_id=1, source_target_pairs={{0,3},{1,2},{2,1},{3,0},{4,7},{5,6},{6,5},{7,4},{8,11},{9,10},{10,... | collective-permute-start | bytes 270344 | tf_op jit(solution)/shard_map/ppermute | solution.py:432
  64.8 6.6 %collective-permute-start.17 = (bf16[64,704]{1,0:T(8,128)(2,1)S(1)}, bf16[64,704]{1,0:T(8,128)(2,1)S(1)}, u32[]{:S(2)}, u32[]{:S(2)}) collective-permute-start(bf16[64,704]{1,0:T(8,128)(2,1)S(1)} %get-tuple-element.112), channel_id=1, source_target_pairs={{0,1},{1,0},{2,3},{3,2},{4,5},{5,4},{6,7},{7,6},{8,9},{9,8},{10,11... | collective-permute-start | bytes 270344 | tf_op jit(solution)/shard_map/ppermute | solution.py:432
  72.1 7.7 %collective-permute-start.18 = (bf16[64,832]{1,0:T(8,128)(2,1)S(1)}, bf16[64,832]{1,0:T(8,128)(2,1)S(1)}, u32[]{:S(2)}, u32[]{:S(2)}) collective-permute-start(bf16[64,832]{1,0:T(8,128)(2,1)S(1)} %between.4.refs_0_.refs_4_), channel_id=1, source_target_pairs={{0,2},{1,3},{2,0},{3,1},{4,6},{5,7},{6,4},{7,5},{8,10},{9,11},{10,... | collective-permute-start | bytes 319496 | tf_op jit(solution)/shard_map/ppermute | solution.py:432
  87.5 8.6 %collective-permute-start.21 = (bf16[64,704]{1,0:T(8,128)(2,1)S(1)}, bf16[64,704]{1,0:T(8,128)(2,1)S(1)}, u32[]{:S(2)}, u32[]{:S(2)}) collective-permute-start(bf16[64,704]{1,0:T(8,128)(2,1)S(1)} %get-tuple-element.119), channel_id=1, source_target_pairs={{0,2},{1,3},{2,0},{3,1},{4,6},{5,7},{6,4},{7,5},{8,10},{9,11},{10,... | collective-permute-start | bytes 270344 | tf_op jit(solution)/shard_map/ppermute | solution.py:432
  88.8 7.2 %collective-permute-start.22 = (bf16[64,704]{1,0:T(8,128)(2,1)S(1)}, bf16[64,704]{1,0:T(8,128)(2,1)S(1)}, u32[]{:S(2)}, u32[]{:S(2)}) collective-permute-start(bf16[64,704]{1,0:T(8,128)(2,1)S(1)} %get-tuple-element.120), channel_id=1, source_target_pairs={{0,3},{1,2},{2,1},{3,0},{4,7},{5,6},{6,5},{7,4},{8,11},{9,10},{10,... | collective-permute-start | bytes 270344 | tf_op jit(solution)/shard_map/ppermute | solution.py:432
  89.9 6.4 %collective-permute-start.23 = (bf16[64,704]{1,0:T(8,128)(2,1)S(1)}, bf16[64,704]{1,0:T(8,128)(2,1)S(1)}, u32[]{:S(2)}, u32[]{:S(2)}) collective-permute-start(bf16[64,704]{1,0:T(8,128)(2,1)S(1)} %get-tuple-element.121), channel_id=1, source_target_pairs={{0,1},{1,0},{2,3},{3,2},{4,5},{5,4},{6,7},{7,6},{8,9},{9,8},{10,11... | collective-permute-start | bytes 270344 | tf_op jit(solution)/shard_map/ppermute | solution.py:432
  97.2 7.0 %collective-permute-start.24 = (bf16[64,832]{1,0:T(8,128)(2,1)S(1)}, bf16[64,832]{1,0:T(8,128)(2,1)S(1)}, u32[]{:S(2)}, u32[]{:S(2)}) collective-permute-start(bf16[64,832]{1,0:T(8,128)(2,1)S(1)} %between.5.refs_0_.refs_4_), channel_id=1, source_target_pairs={{0,2},{1,3},{2,0},{3,1},{4,6},{5,7},{6,4},{7,5},{8,10},{9,11},{10,... | collective-permute-start | bytes 319496 | tf_op jit(solution)/shard_map/ppermute | solution.py:432
  98.2 7.1 %collective-permute-start.26 = (bf16[64,832]{1,0:T(8,128)(2,1)S(1)}, bf16[64,832]{1,0:T(8,128)(2,1)S(1)}, u32[]{:S(2)}, u32[]{:S(2)}) collective-permute-start(bf16[64,832]{1,0:T(8,128)(2,1)S(1)} %between.5.refs_0_.refs_4_), channel_id=1, source_target_pairs={{0,1},{1,0},{2,3},{3,2},{4,5},{5,4},{6,7},{7,6},{8,9},{9,8},{10,11... | collective-permute-start | bytes 319496 | tf_op jit(solution)/shard_map/ppermute | solution.py:432
  111.8 7.7 %collective-permute-start.27 = (bf16[64,704]{1,0:T(8,128)(2,1)S(1)}, bf16[64,704]{1,0:T(8,128)(2,1)S(1)}, u32[]{:S(2)}, u32[]{:S(2)}) collective-permute-start(bf16[64,704]{1,0:T(8,128)(2,1)S(1)} %get-tuple-element.128), channel_id=1, source_target_pairs={{0,2},{1,3},{2,0},{3,1},{4,6},{5,7},{6,4},{7,5},{8,10},{9,11},{10,... | collective-permute-start | bytes 270344 | tf_op jit(solution)/shard_map/ppermute | solution.py:432
  112.6 7.0 %collective-permute-start.28 = (bf16[64,704]{1,0:T(8,128)(2,1)S(1)}, bf16[64,704]{1,0:T(8,128)(2,1)S(1)}, u32[]{:S(2)}, u32[]{:S(2)}) collective-permute-start(bf16[64,704]{1,0:T(8,128)(2,1)S(1)} %get-tuple-element.129), channel_id=1, source_target_pairs={{0,3},{1,2},{2,1},{3,0},{4,7},{5,6},{6,5},{7,4},{8,11},{9,10},{10,... | collective-permute-start | bytes 270344 | tf_op jit(solution)/shard_map/ppermute | solution.py:432
  (12 other events, 50.4 us)

commit v8 on v7

--- a/solution.py
+++ b/solution.py
@@ -42,11 +42,27 @@
 
 
 def route_kernel(
-    group_ref, domain_hbm, slot_hbm, length_hbm, hidden_hbm, target_ref, place_ref, *refs
+    group_ref,
+    domain_hbm,
+    slot_hbm,
+    length_hbm,
+    hidden_hbm,
+    key_hbm,
+    value_hbm,
+    down_hbm,
+    target_ref,
+    place_ref,
+    key_ref,
+    value_ref,
+    down_ref,
+    *refs,
 ):
     groups = len(refs) - 8
     outgoing = refs[:groups]
     count, place, facts, domain_ref, slot_ref, length_ref, hidden_ref, sems = refs[groups:]
+    kinds = down_ref.shape[0]
+    total = down_hbm.shape[0]
+    rank = down_hbm.shape[1] // kinds
     rows, width = hidden_ref.shape
     capacity = outgoing[0].shape[0]
     per_group = slot_ref.shape[0] // groups
@@ -60,6 +76,16 @@
         ],
         sems,
     )
+    pairs = [(key_hbm, key_ref), (value_hbm, value_ref)]
+    for kind in range(kinds):
+        for d in range(total):
+            pairs.append(
+                (
+                    down_hbm.at[d, kind * rank : (kind + 1) * rank, :],
+                    down_ref.at[kind, d * rank : (d + 1) * rank, :],
+                )
+            )
+    later = copy_all(pairs, sems, 4)
     for group in range(groups):
         count[group] = 0
     places = lax.broadcasted_iota(jnp.int32, (1, groups * capacity), 1)
@@ -97,32 +123,17 @@
         block = slice(s * capacity, (s + 1) * capacity)
         outgoing[s][:, :width] = state[block]
         outgoing[s][:, width:] = known[block]
-
-
-def pack_kernel(target_ref, key_hbm, value_hbm, down_hbm, *refs):
-    groups = len(refs) - 5
-    outgoing = refs[:groups]
-    down_ref, packed, key_ref, value_ref, sems = refs[groups:]
+    for copy in later:
+        copy.wait()
+
+
+def pack_kernel(target_ref, key_ref, value_ref, *refs):
+    groups = len(refs) - 1
+    outgoing, packed = refs[:groups], refs[groups]
     rows, kv_local = key_ref.shape[:2]
     capacity = packed.shape[2]
-    kinds = down_ref.shape[0]
-    total = down_hbm.shape[0]
-    rank = down_hbm.shape[1] // kinds
-    copies = copy_all([(key_hbm, key_ref), (value_hbm, value_ref)], sems)
     if groups * capacity > rows:
         packed[...] = jnp.zeros_like(packed)
-    for copy in copies:
-        copy.wait()
-    pairs = []
-    for kind in range(kinds):
-        for d in range(total):
-            pairs.append(
-                (
-                    down_hbm.at[d, kind * rank : (kind + 1) * rank, :],
-                    down_ref.at[kind, d * rank : (d + 1) * rank, :],
-                )
-            )
-    down_copies = copy_all(pairs, sems, len(copies))
 
     def put(row, carry):
         target = target_ref[row]
@@ -136,8 +147,6 @@
     lax.fori_loop(0, rows, put, 0, unroll=4)
     for s in range(groups):
         outgoing[s][...] = packed[s]
-    for copy in down_copies:
-        copy.wait()
 
 
 def load_inputs_kernel(turn, turn_ref, query, key, value, after, *refs):
@@ -476,15 +485,19 @@
     vmem = pl.BlockSpec(memory_space=pltpu.VMEM)
     hbm = pl.BlockSpec(memory_space=pltpu.HBM)
     outgoing_shape = jax.ShapeDtypeStruct((capacity, width + 128), bf16)
-    target, place, *outgoing = pl.pallas_call(
+    kinds = low_width // rank
+    target, place, keys, values, down, *outgoing = pl.pallas_call(
         route_kernel,
         out_shape=[
             jax.ShapeDtypeStruct((row_group,), jnp.int32),
             jax.ShapeDtypeStruct((row_group, rows), bf16),
+            jax.ShapeDtypeStruct(cached_key_rows.shape, bf16),
+            jax.ShapeDtypeStruct(cached_value_rows.shape, bf16),
+            jax.ShapeDtypeStruct((kinds, total * rank, width), bf16),
         ]
         + [outgoing_shape] * groups,
-        in_specs=[smem] + [hbm] * 4,
-        out_specs=[smem] + [vmem] * (groups + 1),
+        in_specs=[smem] + [hbm] * 7,
+        out_specs=[smem] + [vmem] * (groups + 4),
         scratch_shapes=[
             pltpu.SMEM((groups,), jnp.int32),
             pltpu.VMEM((row_group, rows), f32),
@@ -493,9 +506,9 @@
             pltpu.SMEM(slot_of_domain.shape, jnp.int32),
             pltpu.SMEM(cached_length_rows.shape, jnp.int32),
             pltpu.VMEM(hidden.shape, bf16),
-            pltpu.SemaphoreType.DMA((4,)),
+            pltpu.SemaphoreType.DMA((6 + kinds * total,)),
         ],
-        compiler_params=kernel_params(8),
+        compiler_params=kernel_params(16),
         name="route_rows",
     )(
         wide_index.reshape(1),
@@ -503,26 +516,22 @@
         in_hbm(slot_of_domain),
         in_hbm(cached_length_rows),
         in_hbm(hidden),
+        in_hbm(cached_key_rows),
+        in_hbm(cached_value_rows),
+        in_hbm(stacked_down_factors),
     )
     by_group = [0] + list(range(groups - 1, 0, -1))
     arrived = swap_all(outgoing, "wide", by_group)
     packed_shape = (2 * kv_local, capacity, context, head_dim)
-    kinds = low_width // rank
-    *packed, down = pl.pallas_call(
+    packed = pl.pallas_call(
         pack_kernel,
-        out_shape=[jax.ShapeDtypeStruct(packed_shape, bf16)] * groups
-        + [jax.ShapeDtypeStruct((kinds, total * rank, width), bf16)],
-        in_specs=[smem, hbm, hbm, hbm],
-        out_specs=[vmem] * (groups + 1),
-        scratch_shapes=[
-            pltpu.VMEM((groups,) + packed_shape, bf16),
-            pltpu.VMEM(cached_key_rows.shape, bf16),
-            pltpu.VMEM(cached_value_rows.shape, bf16),
-            pltpu.SemaphoreType.DMA((2 + kinds * total,)),
-        ],
+        out_shape=[jax.ShapeDtypeStruct(packed_shape, bf16)] * groups,
+        in_specs=[smem, vmem, vmem],
+        out_specs=[vmem] * groups,
+        scratch_shapes=[pltpu.VMEM((groups,) + packed_shape, bf16)],
         compiler_params=kernel_params(16),
         name="pack_cache",
-    )(target, in_hbm(cached_key_rows), in_hbm(cached_value_rows), in_hbm(stacked_down_factors))
+    )(target, keys, values)
     cache = swap_all(packed, "wide", by_group)
     cache = [block.reshape(2 * kv_local, capacity * context, head_dim) for block in cache]
 

time: 126 us -> 123 us (0.976)
  Pallas kernels: 33.6 us -> 31.7 us
    pallas_call x1, Pallas kernels: 4.59 us -> 1.86 us  [shards(): pl.pallas_call(pack_kernel, out_shape=[jax.ShapeDtypeStruct(packed_shape,...]
  transfers between devices with their start and end apart: 33 -> 33, of which waited for: 21 -> 21; matrix products, arithmetic and copies ran while one was open for 1% -> 1% of each run, Pallas kernels for 13% -> 11%
where the time goes in v8:
time: 123 us
  waiting for transfers between devices  52.9 us (43%)
  starting transfers between devices  36.7 us (30%)
  Pallas kernels  31.7 us (26%)
    ppermute x33, waiting for transfers between devices, swap(): lax.ppermute(block, axis, [(i, i ^ mask) for i in range(lax.axis_size(axi...  52.9 us
    ppermute x33, starting transfers between devices, swap(): lax.ppermute(block, axis, [(i, i ^ mask) for i in range(lax.axis_size(axi...  36.7 us
    pallas_call x4, Pallas kernels, shards(): pl.pallas_call(functools.partial(step_kernel, total, rank, step, parts, l...  11.3 us
    pallas_call x4, Pallas kernels, shards(): pl.pallas_call(functools.partial(early_kernel, early), out_shape=[jax.Sha...  4.64 us
    pallas_call x1, Pallas kernels, load_others(): pl.pallas_call(load_others_kernel, out_shape=[jax.ShapeDtypeStruct(array....  3.44 us
    pallas_call x2, Pallas kernels, load_inputs(): pl.pallas_call(functools.partial(load_inputs_kernel, turn), out_shape=jax...  3.31 us
    pallas_call x1, Pallas kernels, shards(): pl.pallas_call(route_kernel, out_shape=[jax.ShapeDtypeStruct((row_group,)...  2.83 us
  transfers between devices with their start and end apart: 33, of which 21 were waited for; matrix products, arithmetic and copies ran while one was open for 1% of the time, Pallas kernels for 11%

profile of v8, /device:TPU:0, one launch (start us, length us, event | category | flops | bytes accessed | tf_op | source)
XLA Modules:
  0.0 123.3 jit_solution(16273968317483946965)
XLA Ops:
  0.0 2.8 %route_rows.1 = (s32[64]{0:T(128)S(1)}, bf16[64,64]{1,0:T(8,128)(2,1)S(1)}, bf16[64,2,24,128]{3,2,1,0:T(8,128)(2,1)S(1)}, bf16[64,2,24,128]{3,2,1,0:T(8,128)(2,1...) custom-call(s32[1]{0:T(128)} %bitcast.group_ref, ...), custom_call_target="tpu_custom_call" | custom-call | tf_op jit(solution)/shard_map/route_rows/pallas_call | solution.py:489
  3.4 2.6 %collective-permute-start.1 = (bf16[16,768]{1,0:T(8,128)(2,1)S(1)}, bf16[16,768]{1,0:T(8,128)(2,1)S(1)}, u32[]{:S(2)}, u32[]{:S(2)}) collective-permute-start(bf16[16,768]{1,0:T(8,128)(2,1)S(1)} %get-tuple-element.75), channel_id=1, source_target_pairs={{0,12},{4,8},{8,4},{12,0},{1,13},{5,9},{9,5},{13,1},{2,14},{6,10},... | collective-permute-start | bytes 73736 | tf_op jit(solution)/shard_map/ppermute | solution.py:441
  11.8 2.9 %collective-permute-start.3 = (bf16[64,832]{1,0:T(8,128)(2,1)S(1)}, bf16[64,832]{1,0:T(8,128)(2,1)S(1)}, u32[]{:S(2)}, u32[]{:S(2)}) collective-permute-start(bf16[64,832]{1,0:T(8,128)(2,1)S(1)} %get-tuple-element.84.refs_0_.refs_4_), channel_id=1, source_target_pairs={{0,2},{1,3},{2,0},{3,1},{4,6},{5,7},{6,4},{7,5},{8,10},{9,11},{10,... | collective-permute-start | bytes 319496 | tf_op jit(solution)/shard_map/ppermute | solution.py:441
  17.0 3.3 %load_inputs.3.refs_5_.refs_7_ = bf16[2560,1536]{1,0:T(8,128)(2,1)S(1)} custom-call(s32[1]{0:T(128)} %bitcast.1.turn_ref, bf16[2560,1024]{1,0:T(8,128)(2,1)} %query.3, bf16[2560,256]{1,0:T(8,128)(2,1)} %key.3, bf16[2560,256]{1,0:T(8,128)(2,1)} %value.3, f32[64,128]{1,0:T(8,128)S(1)} %get-tuple-element.82.after.refs_5_, bf16[2560,1536]{1,0:T(8,128)(2,1)S(1)} %load_inputs.2.refs_0_), custom_call_target="tpu_custom_call" | custom-call | bytes 20000000 | tf_op jit(solution)/shard_map/load_inputs/pallas_call | solution.py:545
  21.0 3.4 %load_others.1 = (bf16[512,1024]{1,0:T(8,128)(2,1)S(1)}, bf16[512,256]{1,0:T(8,128)(2,1)S(1)}, bf16[512,256]{1,0:T(8,128)(2,1)S(1)}, bf16[1024,2560]{1,0:T(8,128...) custom-call(bf16[512,1024]{1,0:T(8,128)(2,1)} %bitcast.40, ...), custom_call_target="tpu_custom_call" | custom-call | bytes 20000000 | tf_op jit(solution)/shard_map/load_others/pallas_call | solution.py:586
  26.3 2.4 %collective-permute-done.7 = bf16[4,16,24,128]{3,2,1,0:T(8,128)(2,1)S(1)} collective-permute-done((bf16[4,16,24,128]{3,2,1,0:T(8,128)(2,1)}, bf16[4,16,24,128]{3,2,1,0:T(8,128)(2,1)S(1)}, u32[]{:S(2)}, u32[]{:S(2)}) %collective-permute-start.7) | collective-permute-done | bytes 393248 | tf_op jit(solution)/shard_map/ppermute | solution.py:441
  28.7 2.9 %attend_step.4 = (bf16[64,704]{1,0:T(8,128)(2,1)S(1)}, bf16[64,704]{1,0:T(8,128)(2,1)S(1)}, bf16[64,704]{1,0:T(8,128)(2,1)S(1)}, bf16[64,704]{1,0:T(8,128)(2,1)S...) custom-call(bf16[64,832]{1,0:T(8,128)(2,1)S(1)} %collective-permute-done.4.refs_0_, ...), custom_call_target="tpu_custom_call" | custom-call | tf_op jit(solution)/shard_map/attend_step/pallas_call | solution.py:656
  31.6 4.1 %collective-permute-start.10 = (bf16[64,704]{1,0:T(8,128)(2,1)S(1)}, bf16[64,704]{1,0:T(8,128)(2,1)S(1)}, u32[]{:S(2)}, u32[]{:S(2)}) collective-permute-start(bf16[64,704]{1,0:T(8,128)(2,1)S(1)} %get-tuple-element.104), channel_id=1, source_target_pairs={{0,3},{1,2},{2,1},{3,0},{4,7},{5,6},{6,5},{7,4},{8,11},{9,10},{10,... | collective-permute-start | bytes 270344 | tf_op jit(solution)/shard_map/ppermute | solution.py:441
  36.4 3.0 %collective-permute-done.10.refs_2_ = bf16[64,704]{1,0:T(8,128)(2,1)S(1)} collective-permute-done((bf16[64,704]{1,0:T(8,128)(2,1)S(1)}, bf16[64,704]{1,0:T(8,128)(2,1)S(1)}, u32[]{:S(2)}, u32[]{:S(2)}) %collective-permute-start.10) | collective-permute-done | bytes 90144 | tf_op jit(solution)/shard_map/ppermute | solution.py:441
  39.4 2.6 %collective-permute-done.11.refs_3_ = bf16[64,704]{1,0:T(8,128)(2,1)S(1)} collective-permute-done((bf16[64,704]{1,0:T(8,128)(2,1)S(1)}, bf16[64,704]{1,0:T(8,128)(2,1)S(1)}, u32[]{:S(2)}, u32[]{:S(2)}) %collective-permute-start.11) | collective-permute-done | bytes 90144 | tf_op jit(solution)/shard_map/ppermute | solution.py:441
  48.1 4.8 %collective-permute-done.12.refs_2_ = bf16[64,832]{1,0:T(8,128)(2,1)S(1)} collective-permute-done((bf16[64,832]{1,0:T(8,128)(2,1)S(1)}, bf16[64,832]{1,0:T(8,128)(2,1)S(1)}, u32[]{:S(2)}, u32[]{:S(2)}) %collective-permute-start.12) | collective-permute-done | bytes 106528 | tf_op jit(solution)/shard_map/ppermute | solution.py:441
  54.2 3.5 %collective-permute-done.13.refs_0_ = bf16[64,832]{1,0:T(8,128)(2,1)S(1)} collective-permute-done((bf16[64,832]{1,0:T(8,128)(2,1)S(1)}, bf16[64,832]{1,0:T(8,128)(2,1)S(1)}, u32[]{:S(2)}, u32[]{:S(2)}) %collective-permute-start.13) | collective-permute-done | bytes 106528 | tf_op jit(solution)/shard_map/ppermute | solution.py:441
  57.7 2.8 %attend_step.5 = (bf16[64,704]{1,0:T(8,128)(2,1)S(1)}, bf16[64,704]{1,0:T(8,128)(2,1)S(1)}, bf16[64,704]{1,0:T(8,128)(2,1)S(1)}, bf16[64,704]{1,0:T(8,128)(2,1)S...) custom-call(bf16[64,832]{1,0:T(8,128)(2,1)S(1)} %collective-permute-done.13.refs_0_, ...), custom_call_target="tpu_custom_call" | custom-call | tf_op jit(solution)/shard_map/attend_step/pallas_call | solution.py:656
  64.0 5.2 %collective-permute-done.15.refs_1_ = bf16[64,704]{1,0:T(8,128)(2,1)S(1)} collective-permute-done((bf16[64,704]{1,0:T(8,128)(2,1)S(1)}, bf16[64,704]{1,0:T(8,128)(2,1)S(1)}, u32[]{:S(2)}, u32[]{:S(2)}) %collective-permute-start.15) | collective-permute-done | bytes 90144 | tf_op jit(solution)/shard_map/ppermute | solution.py:441
  70.2 2.3 %collective-permute-start.18 = (bf16[64,832]{1,0:T(8,128)(2,1)S(1)}, bf16[64,832]{1,0:T(8,128)(2,1)S(1)}, u32[]{:S(2)}, u32[]{:S(2)}) collective-permute-start(bf16[64,832]{1,0:T(8,128)(2,1)S(1)} %between.4.refs_0_.refs_4_), channel_id=1, source_target_pairs={{0,2},{1,3},{2,0},{3,1},{4,6},{5,7},{6,4},{7,5},{8,10},{9,11},{10,... | collective-permute-start | bytes 319496 | tf_op jit(solution)/shard_map/ppermute | solution.py:441
  72.9 5.0 %collective-permute-done.18.refs_2_ = bf16[64,832]{1,0:T(8,128)(2,1)S(1)} collective-permute-done((bf16[64,832]{1,0:T(8,128)(2,1)S(1)}, bf16[64,832]{1,0:T(8,128)(2,1)S(1)}, u32[]{:S(2)}, u32[]{:S(2)}) %collective-permute-start.18) | collective-permute-done | bytes 106528 | tf_op jit(solution)/shard_map/ppermute | solution.py:441
  79.8 2.9 %collective-permute-done.19.refs_0_ = bf16[64,832]{1,0:T(8,128)(2,1)S(1)} collective-permute-done((bf16[64,832]{1,0:T(8,128)(2,1)S(1)}, bf16[64,832]{1,0:T(8,128)(2,1)S(1)}, u32[]{:S(2)}, u32[]{:S(2)}) %collective-permute-start.19) | collective-permute-done | bytes 106528 | tf_op jit(solution)/shard_map/ppermute | solution.py:441
  82.7 2.8 %attend_step.6 = (bf16[64,704]{1,0:T(8,128)(2,1)S(1)}, bf16[64,704]{1,0:T(8,128)(2,1)S(1)}, bf16[64,704]{1,0:T(8,128)(2,1)S(1)}, bf16[64,704]{1,0:T(8,128)(2,1)S...) custom-call(bf16[64,832]{1,0:T(8,128)(2,1)S(1)} %collective-permute-done.19.refs_0_, ...), custom_call_target="tpu_custom_call" | custom-call | tf_op jit(solution)/shard_map/attend_step/pallas_call | solution.py:656
  89.1 4.5 %collective-permute-done.21.refs_1_ = bf16[64,704]{1,0:T(8,128)(2,1)S(1)} collective-permute-done((bf16[64,704]{1,0:T(8,128)(2,1)S(1)}, bf16[64,704]{1,0:T(8,128)(2,1)S(1)}, u32[]{:S(2)}, u32[]{:S(2)}) %collective-permute-start.21) | collective-permute-done | bytes 90144 | tf_op jit(solution)/shard_map/ppermute | solution.py:441
  97.6 4.3 %collective-permute-done.24.refs_2_ = bf16[64,832]{1,0:T(8,128)(2,1)S(1)} collective-permute-done((bf16[64,832]{1,0:T(8,128)(2,1)S(1)}, bf16[64,832]{1,0:T(8,128)(2,1)S(1)}, u32[]{:S(2)}, u32[]{:S(2)}) %collective-permute-start.24) | collective-permute-done | bytes 106528 | tf_op jit(solution)/shard_map/ppermute | solution.py:441
  103.9 2.8 %collective-permute-done.25.refs_0_ = bf16[64,832]{1,0:T(8,128)(2,1)S(1)} collective-permute-done((bf16[64,832]{1,0:T(8,128)(2,1)S(1)}, bf16[64,832]{1,0:T(8,128)(2,1)S(1)}, u32[]{:S(2)}, u32[]{:S(2)}) %collective-permute-start.25) | collective-permute-done | bytes 106528 | tf_op jit(solution)/shard_map/ppermute | solution.py:441
  106.7 2.8 %attend_step.7 = (bf16[64,704]{1,0:T(8,128)(2,1)S(1)}, bf16[64,704]{1,0:T(8,128)(2,1)S(1)}, bf16[64,704]{1,0:T(8,128)(2,1)S(1)}, bf16[64,704]{1,0:T(8,128)(2,1)S...) custom-call(bf16[64,832]{1,0:T(8,128)(2,1)S(1)} %collective-permute-done.25.refs_0_, ...), custom_call_target="tpu_custom_call" | custom-call | tf_op jit(solution)/shard_map/attend_step/pallas_call | solution.py:656
  110.3 2.5 %collective-permute-start.28 = (bf16[64,704]{1,0:T(8,128)(2,1)S(1)}, bf16[64,704]{1,0:T(8,128)(2,1)S(1)}, u32[]{:S(2)}, u32[]{:S(2)}) collective-permute-start(bf16[64,704]{1,0:T(8,128)(2,1)S(1)} %get-tuple-element.133), channel_id=1, source_target_pairs={{0,3},{1,2},{2,1},{3,0},{4,7},{5,6},{6,5},{7,4},{8,11},{9,10},{10,... | collective-permute-start | bytes 270344 | tf_op jit(solution)/shard_map/ppermute | solution.py:441
  113.1 4.2 %collective-permute-done.27.refs_1_ = bf16[64,704]{1,0:T(8,128)(2,1)S(1)} collective-permute-done((bf16[64,704]{1,0:T(8,128)(2,1)S(1)}, bf16[64,704]{1,0:T(8,128)(2,1)S(1)}, u32[]{:S(2)}, u32[]{:S(2)}) %collective-permute-start.27) | collective-permute-done | bytes 90144 | tf_op jit(solution)/shard_map/ppermute | solution.py:441
  (79 shorter events, 42.5 us)
Async XLA Ops:
  2.8 7.9 %collective-permute-start = (bf16[16,768]{1,0:T(8,128)(2,1)S(1)}, bf16[16,768]{1,0:T(8,128)(2,1)S(1)}, u32[]{:S(2)}, u32[]{:S(2)}) collective-permute-start(bf16[16,768]{1,0:T(8,128)(2,1)S(1)} %get-tuple-element.73), channel_id=1, source_target_pairs={{0,4},{4,0},{8,12},{12,8},{1,5},{5,1},{9,13},{13,9},{2,6},{6,2},{1... | collective-permute-start | bytes 73736 | tf_op jit(solution)/shard_map/ppermute | solution.py:441
  3.4 7.6 %collective-permute-start.1 = (bf16[16,768]{1,0:T(8,128)(2,1)S(1)}, bf16[16,768]{1,0:T(8,128)(2,1)S(1)}, u32[]{:S(2)}, u32[]{:S(2)}) collective-permute-start(bf16[16,768]{1,0:T(8,128)(2,1)S(1)} %get-tuple-element.75), channel_id=1, source_target_pairs={{0,12},{4,8},{8,4},{12,0},{1,13},{5,9},{9,5},{13,1},{2,14},{6,10},... | collective-permute-start | bytes 73736 | tf_op jit(solution)/shard_map/ppermute | solution.py:441
  8.7 17.6 %collective-permute-start.6 = (bf16[4,16,24,128]{3,2,1,0:T(8,128)(2,1)}, bf16[4,16,24,128]{3,2,1,0:T(8,128)(2,1)S(1)}, u32[]{:S(2)}, u32[]{:S(2)}) collective-permute-start(bf16[4,16,24,128]{3,2,1,0:T(8,128)(2,1)} %get-tuple-element.97), channel_id=1, source_target_pairs={{0,12},{4,8},{8,4},{12,0},{1,13},{5,9},{9,5},{13,1},{2,14},{6,10},... | collective-permute-start | bytes 1179656 | tf_op jit(solution)/shard_map/ppermute | solution.py:441
  10.0 18.7 %collective-permute-start.7 = (bf16[4,16,24,128]{3,2,1,0:T(8,128)(2,1)}, bf16[4,16,24,128]{3,2,1,0:T(8,128)(2,1)S(1)}, u32[]{:S(2)}, u32[]{:S(2)}) collective-permute-start(bf16[4,16,24,128]{3,2,1,0:T(8,128)(2,1)} %get-tuple-element.98), channel_id=1, source_target_pairs={{0,8},{4,12},{8,0},{12,4},{1,9},{5,13},{9,1},{13,5},{2,10},{6,14},... | collective-permute-start | bytes 1179656 | tf_op jit(solution)/shard_map/ppermute | solution.py:441
  10.8 17.9 %collective-permute-start.8 = (bf16[4,16,24,128]{3,2,1,0:T(8,128)(2,1)}, bf16[4,16,24,128]{3,2,1,0:T(8,128)(2,1)S(1)}, u32[]{:S(2)}, u32[]{:S(2)}) collective-permute-start(bf16[4,16,24,128]{3,2,1,0:T(8,128)(2,1)} %copy-done.2), channel_id=1, source_target_pairs={{0,4},{4,0},{8,12},{12,8},{1,5},{5,1},{9,13},{13,9},{2,6},{6,2},{1... | collective-permute-start | bytes 1179656 | tf_op jit(solution)/shard_map/ppermute | solution.py:441
  11.8 8.5 %collective-permute-start.3 = (bf16[64,832]{1,0:T(8,128)(2,1)S(1)}, bf16[64,832]{1,0:T(8,128)(2,1)S(1)}, u32[]{:S(2)}, u32[]{:S(2)}) collective-permute-start(bf16[64,832]{1,0:T(8,128)(2,1)S(1)} %get-tuple-element.84.refs_0_.refs_4_), channel_id=1, source_target_pairs={{0,2},{1,3},{2,0},{3,1},{4,6},{5,7},{6,4},{7,5},{8,10},{9,11},{10,... | collective-permute-start | bytes 319496 | tf_op jit(solution)/shard_map/ppermute | solution.py:441
  14.7 9.8 %collective-permute-start.5 = (bf16[64,832]{1,0:T(8,128)(2,1)S(1)}, bf16[64,832]{1,0:T(8,128)(2,1)S(1)}, u32[]{:S(2)}, u32[]{:S(2)}) collective-permute-start(bf16[64,832]{1,0:T(8,128)(2,1)S(1)} %get-tuple-element.84.refs_0_.refs_4_), channel_id=1, source_target_pairs={{0,1},{1,0},{2,3},{3,2},{4,5},{5,4},{6,7},{7,6},{8,9},{9,8},{10,11... | collective-permute-start | bytes 319496 | tf_op jit(solution)/shard_map/ppermute | solution.py:441
  31.6 7.8 %collective-permute-start.10 = (bf16[64,704]{1,0:T(8,128)(2,1)S(1)}, bf16[64,704]{1,0:T(8,128)(2,1)S(1)}, u32[]{:S(2)}, u32[]{:S(2)}) collective-permute-start(bf16[64,704]{1,0:T(8,128)(2,1)S(1)} %get-tuple-element.104), channel_id=1, source_target_pairs={{0,3},{1,2},{2,1},{3,0},{4,7},{5,6},{6,5},{7,4},{8,11},{9,10},{10,... | collective-permute-start | bytes 270344 | tf_op jit(solution)/shard_map/ppermute | solution.py:441
  35.8 6.2 %collective-permute-start.11 = (bf16[64,704]{1,0:T(8,128)(2,1)S(1)}, bf16[64,704]{1,0:T(8,128)(2,1)S(1)}, u32[]{:S(2)}, u32[]{:S(2)}) collective-permute-start(bf16[64,704]{1,0:T(8,128)(2,1)S(1)} %get-tuple-element.105), channel_id=1, source_target_pairs={{0,1},{1,0},{2,3},{3,2},{4,5},{5,4},{6,7},{7,6},{8,9},{9,8},{10,11... | collective-permute-start | bytes 270344 | tf_op jit(solution)/shard_map/ppermute | solution.py:441
  35.8 8.5 %collective-permute-start.9 = (bf16[64,704]{1,0:T(8,128)(2,1)S(1)}, bf16[64,704]{1,0:T(8,128)(2,1)S(1)}, u32[]{:S(2)}, u32[]{:S(2)}) collective-permute-start(bf16[64,704]{1,0:T(8,128)(2,1)S(1)} %get-tuple-element.103), channel_id=1, source_target_pairs={{0,2},{1,3},{2,0},{3,1},{4,6},{5,7},{6,4},{7,5},{8,10},{9,11},{10,... | collective-permute-start | bytes 270344 | tf_op jit(solution)/shard_map/ppermute | solution.py:441
  45.0 7.9 %collective-permute-start.12 = (bf16[64,832]{1,0:T(8,128)(2,1)S(1)}, bf16[64,832]{1,0:T(8,128)(2,1)S(1)}, u32[]{:S(2)}, u32[]{:S(2)}) collective-permute-start(bf16[64,832]{1,0:T(8,128)(2,1)S(1)} %between.3.refs_0_.refs_4_), channel_id=1, source_target_pairs={{0,2},{1,3},{2,0},{3,1},{4,6},{5,7},{6,4},{7,5},{8,10},{9,11},{10,... | collective-permute-start | bytes 319496 | tf_op jit(solution)/shard_map/ppermute | solution.py:441
  46.5 6.6 %collective-permute-start.14 = (bf16[64,832]{1,0:T(8,128)(2,1)S(1)}, bf16[64,832]{1,0:T(8,128)(2,1)S(1)}, u32[]{:S(2)}, u32[]{:S(2)}) collective-permute-start(bf16[64,832]{1,0:T(8,128)(2,1)S(1)} %between.3.refs_0_.refs_4_), channel_id=1, source_target_pairs={{0,1},{1,0},{2,3},{3,2},{4,5},{5,4},{6,7},{7,6},{8,9},{9,8},{10,11... | collective-permute-start | bytes 319496 | tf_op jit(solution)/shard_map/ppermute | solution.py:441
  60.5 8.8 %collective-permute-start.15 = (bf16[64,704]{1,0:T(8,128)(2,1)S(1)}, bf16[64,704]{1,0:T(8,128)(2,1)S(1)}, u32[]{:S(2)}, u32[]{:S(2)}) collective-permute-start(bf16[64,704]{1,0:T(8,128)(2,1)S(1)} %get-tuple-element.114), channel_id=1, source_target_pairs={{0,2},{1,3},{2,0},{3,1},{4,6},{5,7},{6,4},{7,5},{8,10},{9,11},{10,... | collective-permute-start | bytes 270344 | tf_op jit(solution)/shard_map/ppermute | solution.py:441
  61.2 8.0 %collective-permute-start.16 = (bf16[64,704]{1,0:T(8,128)(2,1)S(1)}, bf16[64,704]{1,0:T(8,128)(2,1)S(1)}, u32[]{:S(2)}, u32[]{:S(2)}) collective-permute-start(bf16[64,704]{1,0:T(8,128)(2,1)S(1)} %get-tuple-element.115), channel_id=1, source_target_pairs={{0,3},{1,2},{2,1},{3,0},{4,7},{5,6},{6,5},{7,4},{8,11},{9,10},{10,... | collective-permute-start | bytes 270344 | tf_op jit(solution)/shard_map/ppermute | solution.py:441
  62.9 6.6 %collective-permute-start.17 = (bf16[64,704]{1,0:T(8,128)(2,1)S(1)}, bf16[64,704]{1,0:T(8,128)(2,1)S(1)}, u32[]{:S(2)}, u32[]{:S(2)}) collective-permute-start(bf16[64,704]{1,0:T(8,128)(2,1)S(1)} %get-tuple-element.116), channel_id=1, source_target_pairs={{0,1},{1,0},{2,3},{3,2},{4,5},{5,4},{6,7},{7,6},{8,9},{9,8},{10,11... | collective-permute-start | bytes 270344 | tf_op jit(solution)/shard_map/ppermute | solution.py:441
  70.2 7.7 %collective-permute-start.18 = (bf16[64,832]{1,0:T(8,128)(2,1)S(1)}, bf16[64,832]{1,0:T(8,128)(2,1)S(1)}, u32[]{:S(2)}, u32[]{:S(2)}) collective-permute-start(bf16[64,832]{1,0:T(8,128)(2,1)S(1)} %between.4.refs_0_.refs_4_), channel_id=1, source_target_pairs={{0,2},{1,3},{2,0},{3,1},{4,6},{5,7},{6,4},{7,5},{8,10},{9,11},{10,... | collective-permute-start | bytes 319496 | tf_op jit(solution)/shard_map/ppermute | solution.py:441
  72.5 6.1 %collective-permute-start.20 = (bf16[64,832]{1,0:T(8,128)(2,1)S(1)}, bf16[64,832]{1,0:T(8,128)(2,1)S(1)}, u32[]{:S(2)}, u32[]{:S(2)}) collective-permute-start(bf16[64,832]{1,0:T(8,128)(2,1)S(1)} %between.4.refs_0_.refs_4_), channel_id=1, source_target_pairs={{0,1},{1,0},{2,3},{3,2},{4,5},{5,4},{6,7},{7,6},{8,9},{9,8},{10,11... | collective-permute-start | bytes 319496 | tf_op jit(solution)/shard_map/ppermute | solution.py:441
  85.5 8.0 %collective-permute-start.21 = (bf16[64,704]{1,0:T(8,128)(2,1)S(1)}, bf16[64,704]{1,0:T(8,128)(2,1)S(1)}, u32[]{:S(2)}, u32[]{:S(2)}) collective-permute-start(bf16[64,704]{1,0:T(8,128)(2,1)S(1)} %get-tuple-element.123), channel_id=1, source_target_pairs={{0,2},{1,3},{2,0},{3,1},{4,6},{5,7},{6,4},{7,5},{8,10},{9,11},{10,... | collective-permute-start | bytes 270344 | tf_op jit(solution)/shard_map/ppermute | solution.py:441
  86.9 6.7 %collective-permute-start.22 = (bf16[64,704]{1,0:T(8,128)(2,1)S(1)}, bf16[64,704]{1,0:T(8,128)(2,1)S(1)}, u32[]{:S(2)}, u32[]{:S(2)}) collective-permute-start(bf16[64,704]{1,0:T(8,128)(2,1)S(1)} %get-tuple-element.124), channel_id=1, source_target_pairs={{0,3},{1,2},{2,1},{3,0},{4,7},{5,6},{6,5},{7,4},{8,11},{9,10},{10,... | collective-permute-start | bytes 270344 | tf_op jit(solution)/shard_map/ppermute | solution.py:441
  88.0 6.4 %collective-permute-start.23 = (bf16[64,704]{1,0:T(8,128)(2,1)S(1)}, bf16[64,704]{1,0:T(8,128)(2,1)S(1)}, u32[]{:S(2)}, u32[]{:S(2)}) collective-permute-start(bf16[64,704]{1,0:T(8,128)(2,1)S(1)} %get-tuple-element.125), channel_id=1, source_target_pairs={{0,1},{1,0},{2,3},{3,2},{4,5},{5,4},{6,7},{7,6},{8,9},{9,8},{10,11... | collective-permute-start | bytes 270344 | tf_op jit(solution)/shard_map/ppermute | solution.py:441
  95.2 6.7 %collective-permute-start.24 = (bf16[64,832]{1,0:T(8,128)(2,1)S(1)}, bf16[64,832]{1,0:T(8,128)(2,1)S(1)}, u32[]{:S(2)}, u32[]{:S(2)}) collective-permute-start(bf16[64,832]{1,0:T(8,128)(2,1)S(1)} %between.5.refs_0_.refs_4_), channel_id=1, source_target_pairs={{0,2},{1,3},{2,0},{3,1},{4,6},{5,7},{6,4},{7,5},{8,10},{9,11},{10,... | collective-permute-start | bytes 319496 | tf_op jit(solution)/shard_map/ppermute | solution.py:441
  96.1 6.6 %collective-permute-start.26 = (bf16[64,832]{1,0:T(8,128)(2,1)S(1)}, bf16[64,832]{1,0:T(8,128)(2,1)S(1)}, u32[]{:S(2)}, u32[]{:S(2)}) collective-permute-start(bf16[64,832]{1,0:T(8,128)(2,1)S(1)} %between.5.refs_0_.refs_4_), channel_id=1, source_target_pairs={{0,1},{1,0},{2,3},{3,2},{4,5},{5,4},{6,7},{7,6},{8,9},{9,8},{10,11... | collective-permute-start | bytes 319496 | tf_op jit(solution)/shard_map/ppermute | solution.py:441
  109.6 7.8 %collective-permute-start.27 = (bf16[64,704]{1,0:T(8,128)(2,1)S(1)}, bf16[64,704]{1,0:T(8,128)(2,1)S(1)}, u32[]{:S(2)}, u32[]{:S(2)}) collective-permute-start(bf16[64,704]{1,0:T(8,128)(2,1)S(1)} %get-tuple-element.132), channel_id=1, source_target_pairs={{0,2},{1,3},{2,0},{3,1},{4,6},{5,7},{6,4},{7,5},{8,10},{9,11},{10,... | collective-permute-start | bytes 270344 | tf_op jit(solution)/shard_map/ppermute | solution.py:441
  110.3 7.1 %collective-permute-start.28 = (bf16[64,704]{1,0:T(8,128)(2,1)S(1)}, bf16[64,704]{1,0:T(8,128)(2,1)S(1)}, u32[]{:S(2)}, u32[]{:S(2)}) collective-permute-start(bf16[64,704]{1,0:T(8,128)(2,1)S(1)} %get-tuple-element.133), channel_id=1, source_target_pairs={{0,3},{1,2},{2,1},{3,0},{4,7},{5,6},{6,5},{7,4},{8,11},{9,10},{10,... | collective-permute-start | bytes 270344 | tf_op jit(solution)/shard_map/ppermute | solution.py:441
  (13 other events, 61.2 us)

commit v9 on v8

--- a/solution.py
+++ b/solution.py
@@ -560,7 +560,7 @@
             *held,
         )
 
-    input_weight = load_inputs(1, arrived[-1])
+    input_weight = load_inputs(1, packed[0])
     input_weight, *arrived = lax.optimization_barrier((input_weight, *arrived))
     send, facts_here = pl.pallas_call(
         functools.partial(enter_kernel, total, rank, by_group),

time: 123 us -> 123 us (level)
  waiting for transfers between devices: 52.9 us -> 50 us
  starting transfers between devices: 36.7 us -> 38.2 us
    ppermute x33, waiting for transfers between devices: 52.9 us -> 50 us  [swap(): lax.ppermute(block, axis, [(i, i ^ mask) for i in range(lax.axis_size(axi...]
    ppermute x33, starting transfers between devices: 36.7 us -> 38.2 us  [swap(): lax.ppermute(block, axis, [(i, i ^ mask) for i in range(lax.axis_size(axi...]
where the time goes in v9:
time: 123 us
  waiting for transfers between devices  50 us (41%)
  starting transfers between devices  38.2 us (31%)
  Pallas kernels  31.7 us (26%)
  local copies, waits for them, and re-layouts  1.83 us (1%)
    ppermute x33, waiting for transfers between devices, swap(): lax.ppermute(block, axis, [(i, i ^ mask) for i in range(lax.axis_size(axi...  50 us
    ppermute x33, starting transfers between devices, swap(): lax.ppermute(block, axis, [(i, i ^ mask) for i in range(lax.axis_size(axi...  38.2 us
    pallas_call x4, Pallas kernels, shards(): pl.pallas_call(functools.partial(step_kernel, total, rank, step, parts, l...  11.4 us
    pallas_call x4, Pallas kernels, shards(): pl.pallas_call(functools.partial(early_kernel, early), out_shape=[jax.Sha...  4.63 us
    pallas_call x1, Pallas kernels, load_others(): pl.pallas_call(load_others_kernel, out_shape=[jax.ShapeDtypeStruct(array....  3.44 us
    pallas_call x2, Pallas kernels, load_inputs(): pl.pallas_call(functools.partial(load_inputs_kernel, turn), out_shape=jax...  3.32 us
    pallas_call x1, Pallas kernels, shards(): pl.pallas_call(route_kernel, out_shape=[jax.ShapeDtypeStruct((row_group,)...  2.83 us
  transfers between devices with their start and end apart: 33, of which 21 were waited for; matrix products, arithmetic and copies ran while one was open for 1% of the time, Pallas kernels for 11%

profile of v9, /device:TPU:0, one launch (start us, length us, event | category | flops | bytes accessed | tf_op | source)
XLA Modules:
  0.0 122.8 jit_solution(6048354087869817684)
XLA Ops:
  0.0 2.8 %route_rows.1 = (s32[64]{0:T(128)S(1)}, bf16[64,64]{1,0:T(8,128)(2,1)S(1)}, bf16[64,2,24,128]{3,2,1,0:T(8,128)(2,1)S(1)}, bf16[64,2,24,128]{3,2,1,0:T(8,128)(2,1...) custom-call(s32[1]{0:T(128)} %bitcast.group_ref, ...), custom_call_target="tpu_custom_call" | custom-call | tf_op jit(solution)/shard_map/route_rows/pallas_call | solution.py:489
  2.8 2.5 %collective-permute-start = (bf16[16,768]{1,0:T(8,128)(2,1)S(1)}, bf16[16,768]{1,0:T(8,128)(2,1)S(1)}, u32[]{:S(2)}, u32[]{:S(2)}) collective-permute-start(bf16[16,768]{1,0:T(8,128)(2,1)S(1)} %get-tuple-element.78), channel_id=1, source_target_pairs={{0,12},{4,8},{8,4},{12,0},{1,13},{5,9},{9,5},{13,1},{2,14},{6,10},... | collective-permute-start | bytes 73736 | tf_op jit(solution)/shard_map/ppermute | solution.py:441
  11.8 2.2 %collective-permute-start.8 = (bf16[4,16,24,128]{3,2,1,0:T(8,128)(2,1)S(1)}, bf16[4,16,24,128]{3,2,1,0:T(8,128)(2,1)S(1)}, u32[]{:S(2)}, u32[]{:S(2)}) collective-permute-start(bf16[4,16,24,128]{3,2,1,0:T(8,128)(2,1)S(1)} %copy-done.3), channel_id=1, source_target_pairs={{0,4},{4,0},{8,12},{12,8},{1,5},{5,1},{9,13},{13,9},{2,6},{6,2},{1... | collective-permute-start | bytes 1179656 | tf_op jit(solution)/shard_map/ppermute | solution.py:441
  14.8 2.8 %collective-permute-start.3 = (bf16[64,832]{1,0:T(8,128)(2,1)S(1)}, bf16[64,832]{1,0:T(8,128)(2,1)S(1)}, u32[]{:S(2)}, u32[]{:S(2)}) collective-permute-start(bf16[64,832]{1,0:T(8,128)(2,1)S(1)} %get-tuple-element.88.refs_0_.refs_4_), channel_id=1, source_target_pairs={{0,2},{1,3},{2,0},{3,1},{4,6},{5,7},{6,4},{7,5},{8,10},{9,11},{10,... | collective-permute-start | bytes 319496 | tf_op jit(solution)/shard_map/ppermute | solution.py:441
  20.0 3.3 %load_inputs.3.refs_5_.refs_7_ = bf16[2560,1536]{1,0:T(8,128)(2,1)S(1)} custom-call(s32[1]{0:T(128)} %bitcast.1.turn_ref, bf16[2560,1024]{1,0:T(8,128)(2,1)} %query.3, bf16[2560,256]{1,0:T(8,128)(2,1)} %key.3, bf16[2560,256]{1,0:T(8,128)(2,1)} %value.3, f32[64,128]{1,0:T(8,128)S(1)} %get-tuple-element.86.after.refs_5_, bf16[2560,1536]{1,0:T(8,128)(2,1)S(1)} %load_inputs.2.refs_0_), custom_call_target="tpu_custom_call" | custom-call | bytes 20000000 | tf_op jit(solution)/shard_map/load_inputs/pallas_call | solution.py:545
  24.3 3.4 %load_others.1 = (bf16[512,1024]{1,0:T(8,128)(2,1)S(1)}, bf16[512,256]{1,0:T(8,128)(2,1)S(1)}, bf16[512,256]{1,0:T(8,128)(2,1)S(1)}, bf16[1024,2560]{1,0:T(8,128...) custom-call(bf16[512,1024]{1,0:T(8,128)(2,1)} %bitcast.40, ...), custom_call_target="tpu_custom_call" | custom-call | bytes 20000000 | tf_op jit(solution)/shard_map/load_others/pallas_call | solution.py:586
  29.0 2.9 %attend_step.4 = (bf16[64,704]{1,0:T(8,128)(2,1)S(1)}, bf16[64,704]{1,0:T(8,128)(2,1)S(1)}, bf16[64,704]{1,0:T(8,128)(2,1)S(1)}, bf16[64,704]{1,0:T(8,128)(2,1)S...) custom-call(bf16[64,832]{1,0:T(8,128)(2,1)S(1)} %collective-permute-done.4.refs_0_, ...), custom_call_target="tpu_custom_call" | custom-call | tf_op jit(solution)/shard_map/attend_step/pallas_call | solution.py:656
  31.9 3.5 %collective-permute-start.10 = (bf16[64,704]{1,0:T(8,128)(2,1)S(1)}, bf16[64,704]{1,0:T(8,128)(2,1)S(1)}, u32[]{:S(2)}, u32[]{:S(2)}) collective-permute-start(bf16[64,704]{1,0:T(8,128)(2,1)S(1)} %get-tuple-element.104), channel_id=1, source_target_pairs={{0,3},{1,2},{2,1},{3,0},{4,7},{5,6},{6,5},{7,4},{8,11},{9,10},{10,... | collective-permute-start | bytes 270344 | tf_op jit(solution)/shard_map/ppermute | solution.py:441
  36.4 3.1 %collective-permute-done.10.refs_2_ = bf16[64,704]{1,0:T(8,128)(2,1)S(1)} collective-permute-done((bf16[64,704]{1,0:T(8,128)(2,1)S(1)}, bf16[64,704]{1,0:T(8,128)(2,1)S(1)}, u32[]{:S(2)}, u32[]{:S(2)}) %collective-permute-start.10) | collective-permute-done | bytes 90144 | tf_op jit(solution)/shard_map/ppermute | solution.py:441
  40.7 3.6 %collective-permute-done.9.refs_1_ = bf16[64,704]{1,0:T(8,128)(2,1)S(1)} collective-permute-done((bf16[64,704]{1,0:T(8,128)(2,1)S(1)}, bf16[64,704]{1,0:T(8,128)(2,1)S(1)}, u32[]{:S(2)}, u32[]{:S(2)}) %collective-permute-start.9) | collective-permute-done | bytes 90144 | tf_op jit(solution)/shard_map/ppermute | solution.py:441
  45.9 2.5 %collective-permute-start.14 = (bf16[64,832]{1,0:T(8,128)(2,1)S(1)}, bf16[64,832]{1,0:T(8,128)(2,1)S(1)}, u32[]{:S(2)}, u32[]{:S(2)}) collective-permute-start(bf16[64,832]{1,0:T(8,128)(2,1)S(1)} %between.3.refs_0_.refs_4_), channel_id=1, source_target_pairs={{0,1},{1,0},{2,3},{3,2},{4,5},{5,4},{6,7},{7,6},{8,9},{9,8},{10,11... | collective-permute-start | bytes 319496 | tf_op jit(solution)/shard_map/ppermute | solution.py:441
  48.4 4.0 %collective-permute-done.12.refs_2_ = bf16[64,832]{1,0:T(8,128)(2,1)S(1)} collective-permute-done((bf16[64,832]{1,0:T(8,128)(2,1)S(1)}, bf16[64,832]{1,0:T(8,128)(2,1)S(1)}, u32[]{:S(2)}, u32[]{:S(2)}) %collective-permute-start.12) | collective-permute-done | bytes 106528 | tf_op jit(solution)/shard_map/ppermute | solution.py:441
  54.0 3.3 %collective-permute-done.13.refs_0_ = bf16[64,832]{1,0:T(8,128)(2,1)S(1)} collective-permute-done((bf16[64,832]{1,0:T(8,128)(2,1)S(1)}, bf16[64,832]{1,0:T(8,128)(2,1)S(1)}, u32[]{:S(2)}, u32[]{:S(2)}) %collective-permute-start.13) | collective-permute-done | bytes 106528 | tf_op jit(solution)/shard_map/ppermute | solution.py:441
  57.2 2.8 %attend_step.5 = (bf16[64,704]{1,0:T(8,128)(2,1)S(1)}, bf16[64,704]{1,0:T(8,128)(2,1)S(1)}, bf16[64,704]{1,0:T(8,128)(2,1)S(1)}, bf16[64,704]{1,0:T(8,128)(2,1)S...) custom-call(bf16[64,832]{1,0:T(8,128)(2,1)S(1)} %collective-permute-done.13.refs_0_, ...), custom_call_target="tpu_custom_call" | custom-call | tf_op jit(solution)/shard_map/attend_step/pallas_call | solution.py:656
  63.6 5.2 %collective-permute-done.15.refs_1_ = bf16[64,704]{1,0:T(8,128)(2,1)S(1)} collective-permute-done((bf16[64,704]{1,0:T(8,128)(2,1)S(1)}, bf16[64,704]{1,0:T(8,128)(2,1)S(1)}, u32[]{:S(2)}, u32[]{:S(2)}) %collective-permute-start.15) | collective-permute-done | bytes 90144 | tf_op jit(solution)/shard_map/ppermute | solution.py:441
  69.8 2.3 %collective-permute-start.18 = (bf16[64,832]{1,0:T(8,128)(2,1)S(1)}, bf16[64,832]{1,0:T(8,128)(2,1)S(1)}, u32[]{:S(2)}, u32[]{:S(2)}) collective-permute-start(bf16[64,832]{1,0:T(8,128)(2,1)S(1)} %between.4.refs_0_.refs_4_), channel_id=1, source_target_pairs={{0,2},{1,3},{2,0},{3,1},{4,6},{5,7},{6,4},{7,5},{8,10},{9,11},{10,... | collective-permute-start | bytes 319496 | tf_op jit(solution)/shard_map/ppermute | solution.py:441
  72.5 4.6 %collective-permute-done.18.refs_2_ = bf16[64,832]{1,0:T(8,128)(2,1)S(1)} collective-permute-done((bf16[64,832]{1,0:T(8,128)(2,1)S(1)}, bf16[64,832]{1,0:T(8,128)(2,1)S(1)}, u32[]{:S(2)}, u32[]{:S(2)}) %collective-permute-start.18) | collective-permute-done | bytes 106528 | tf_op jit(solution)/shard_map/ppermute | solution.py:441
  78.7 3.2 %collective-permute-done.19.refs_0_ = bf16[64,832]{1,0:T(8,128)(2,1)S(1)} collective-permute-done((bf16[64,832]{1,0:T(8,128)(2,1)S(1)}, bf16[64,832]{1,0:T(8,128)(2,1)S(1)}, u32[]{:S(2)}, u32[]{:S(2)}) %collective-permute-start.19) | collective-permute-done | bytes 106528 | tf_op jit(solution)/shard_map/ppermute | solution.py:441
  81.9 2.8 %attend_step.6 = (bf16[64,704]{1,0:T(8,128)(2,1)S(1)}, bf16[64,704]{1,0:T(8,128)(2,1)S(1)}, bf16[64,704]{1,0:T(8,128)(2,1)S(1)}, bf16[64,704]{1,0:T(8,128)(2,1)S...) custom-call(bf16[64,832]{1,0:T(8,128)(2,1)S(1)} %collective-permute-done.19.refs_0_, ...), custom_call_target="tpu_custom_call" | custom-call | tf_op jit(solution)/shard_map/attend_step/pallas_call | solution.py:656
  88.3 3.0 %collective-permute-done.21.refs_1_ = bf16[64,704]{1,0:T(8,128)(2,1)S(1)} collective-permute-done((bf16[64,704]{1,0:T(8,128)(2,1)S(1)}, bf16[64,704]{1,0:T(8,128)(2,1)S(1)}, u32[]{:S(2)}, u32[]{:S(2)}) %collective-permute-start.21) | collective-permute-done | bytes 90144 | tf_op jit(solution)/shard_map/ppermute | solution.py:441
  96.7 4.6 %collective-permute-done.24.refs_2_ = bf16[64,832]{1,0:T(8,128)(2,1)S(1)} collective-permute-done((bf16[64,832]{1,0:T(8,128)(2,1)S(1)}, bf16[64,832]{1,0:T(8,128)(2,1)S(1)}, u32[]{:S(2)}, u32[]{:S(2)}) %collective-permute-start.24) | collective-permute-done | bytes 106528 | tf_op jit(solution)/shard_map/ppermute | solution.py:441
  102.8 4.4 %collective-permute-done.25.refs_0_ = bf16[64,832]{1,0:T(8,128)(2,1)S(1)} collective-permute-done((bf16[64,832]{1,0:T(8,128)(2,1)S(1)}, bf16[64,832]{1,0:T(8,128)(2,1)S(1)}, u32[]{:S(2)}, u32[]{:S(2)}) %collective-permute-start.25) | collective-permute-done | bytes 106528 | tf_op jit(solution)/shard_map/ppermute | solution.py:441
  107.2 2.8 %attend_step.7 = (bf16[64,704]{1,0:T(8,128)(2,1)S(1)}, bf16[64,704]{1,0:T(8,128)(2,1)S(1)}, bf16[64,704]{1,0:T(8,128)(2,1)S(1)}, bf16[64,704]{1,0:T(8,128)(2,1)S...) custom-call(bf16[64,832]{1,0:T(8,128)(2,1)S(1)} %collective-permute-done.25.refs_0_, ...), custom_call_target="tpu_custom_call" | custom-call | tf_op jit(solution)/shard_map/attend_step/pallas_call | solution.py:656
  113.6 3.3 %collective-permute-done.27.refs_1_ = bf16[64,704]{1,0:T(8,128)(2,1)S(1)} collective-permute-done((bf16[64,704]{1,0:T(8,128)(2,1)S(1)}, bf16[64,704]{1,0:T(8,128)(2,1)S(1)}, u32[]{:S(2)}, u32[]{:S(2)}) %collective-permute-start.27) | collective-permute-done | bytes 90144 | tf_op jit(solution)/shard_map/ppermute | solution.py:441
  (81 shorter events, 43.4 us)
Async XLA Ops:
  2.8 8.0 %collective-permute-start = (bf16[16,768]{1,0:T(8,128)(2,1)S(1)}, bf16[16,768]{1,0:T(8,128)(2,1)S(1)}, u32[]{:S(2)}, u32[]{:S(2)}) collective-permute-start(bf16[16,768]{1,0:T(8,128)(2,1)S(1)} %get-tuple-element.78), channel_id=1, source_target_pairs={{0,12},{4,8},{8,4},{12,0},{1,13},{5,9},{9,5},{13,1},{2,14},{6,10},... | collective-permute-start | bytes 73736 | tf_op jit(solution)/shard_map/ppermute | solution.py:441
  5.3 8.7 %collective-permute-start.1 = (bf16[16,768]{1,0:T(8,128)(2,1)S(1)}, bf16[16,768]{1,0:T(8,128)(2,1)S(1)}, u32[]{:S(2)}, u32[]{:S(2)}) collective-permute-start(bf16[16,768]{1,0:T(8,128)(2,1)S(1)} %get-tuple-element.79), channel_id=1, source_target_pairs={{0,8},{4,12},{8,0},{12,4},{1,9},{5,13},{9,1},{13,5},{2,10},{6,14},... | collective-permute-start | bytes 73736 | tf_op jit(solution)/shard_map/ppermute | solution.py:441
  6.0 8.0 %collective-permute-start.2 = (bf16[16,768]{1,0:T(8,128)(2,1)S(1)}, bf16[16,768]{1,0:T(8,128)(2,1)S(1)}, u32[]{:S(2)}, u32[]{:S(2)}) collective-permute-start(bf16[16,768]{1,0:T(8,128)(2,1)S(1)} %get-tuple-element.80), channel_id=1, source_target_pairs={{0,4},{4,0},{8,12},{12,8},{1,5},{5,1},{9,13},{13,9},{2,6},{6,2},{1... | collective-permute-start | bytes 73736 | tf_op jit(solution)/shard_map/ppermute | solution.py:441
  8.6 20.4 %collective-permute-start.6 = (bf16[4,16,24,128]{3,2,1,0:T(8,128)(2,1)}, bf16[4,16,24,128]{3,2,1,0:T(8,128)(2,1)S(1)}, u32[]{:S(2)}, u32[]{:S(2)}) collective-permute-start(bf16[4,16,24,128]{3,2,1,0:T(8,128)(2,1)} %get-tuple-element.97), channel_id=1, source_target_pairs={{0,12},{4,8},{8,4},{12,0},{1,13},{5,9},{9,5},{13,1},{2,14},{6,10},... | collective-permute-start | bytes 1179656 | tf_op jit(solution)/shard_map/ppermute | solution.py:441
  10.1 18.9 %collective-permute-start.7 = (bf16[4,16,24,128]{3,2,1,0:T(8,128)(2,1)}, bf16[4,16,24,128]{3,2,1,0:T(8,128)(2,1)S(1)}, u32[]{:S(2)}, u32[]{:S(2)}) collective-permute-start(bf16[4,16,24,128]{3,2,1,0:T(8,128)(2,1)} %get-tuple-element.98), channel_id=1, source_target_pairs={{0,8},{4,12},{8,0},{12,4},{1,9},{5,13},{9,1},{13,5},{2,10},{6,14},... | collective-permute-start | bytes 1179656 | tf_op jit(solution)/shard_map/ppermute | solution.py:441
  11.8 17.2 %collective-permute-start.8 = (bf16[4,16,24,128]{3,2,1,0:T(8,128)(2,1)S(1)}, bf16[4,16,24,128]{3,2,1,0:T(8,128)(2,1)S(1)}, u32[]{:S(2)}, u32[]{:S(2)}) collective-permute-start(bf16[4,16,24,128]{3,2,1,0:T(8,128)(2,1)S(1)} %copy-done.3), channel_id=1, source_target_pairs={{0,4},{4,0},{8,12},{12,8},{1,5},{5,1},{9,13},{13,9},{2,6},{6,2},{1... | collective-permute-start | bytes 1179656 | tf_op jit(solution)/shard_map/ppermute | solution.py:441
  14.8 8.7 %collective-permute-start.3 = (bf16[64,832]{1,0:T(8,128)(2,1)S(1)}, bf16[64,832]{1,0:T(8,128)(2,1)S(1)}, u32[]{:S(2)}, u32[]{:S(2)}) collective-permute-start(bf16[64,832]{1,0:T(8,128)(2,1)S(1)} %get-tuple-element.88.refs_0_.refs_4_), channel_id=1, source_target_pairs={{0,2},{1,3},{2,0},{3,1},{4,6},{5,7},{6,4},{7,5},{8,10},{9,11},{10,... | collective-permute-start | bytes 319496 | tf_op jit(solution)/shard_map/ppermute | solution.py:441
  17.6 10.1 %collective-permute-start.5 = (bf16[64,832]{1,0:T(8,128)(2,1)S(1)}, bf16[64,832]{1,0:T(8,128)(2,1)S(1)}, u32[]{:S(2)}, u32[]{:S(2)}) collective-permute-start(bf16[64,832]{1,0:T(8,128)(2,1)S(1)} %get-tuple-element.88.refs_0_.refs_4_), channel_id=1, source_target_pairs={{0,1},{1,0},{2,3},{3,2},{4,5},{5,4},{6,7},{7,6},{8,9},{9,8},{10,11... | collective-permute-start | bytes 319496 | tf_op jit(solution)/shard_map/ppermute | solution.py:441
  31.9 7.5 %collective-permute-start.10 = (bf16[64,704]{1,0:T(8,128)(2,1)S(1)}, bf16[64,704]{1,0:T(8,128)(2,1)S(1)}, u32[]{:S(2)}, u32[]{:S(2)}) collective-permute-start(bf16[64,704]{1,0:T(8,128)(2,1)S(1)} %get-tuple-element.104), channel_id=1, source_target_pairs={{0,3},{1,2},{2,1},{3,0},{4,7},{5,6},{6,5},{7,4},{8,11},{9,10},{10,... | collective-permute-start | bytes 270344 | tf_op jit(solution)/shard_map/ppermute | solution.py:441
  35.9 8.5 %collective-permute-start.9 = (bf16[64,704]{1,0:T(8,128)(2,1)S(1)}, bf16[64,704]{1,0:T(8,128)(2,1)S(1)}, u32[]{:S(2)}, u32[]{:S(2)}) collective-permute-start(bf16[64,704]{1,0:T(8,128)(2,1)S(1)} %get-tuple-element.103), channel_id=1, source_target_pairs={{0,2},{1,3},{2,0},{3,1},{4,6},{5,7},{6,4},{7,5},{8,10},{9,11},{10,... | collective-permute-start | bytes 270344 | tf_op jit(solution)/shard_map/ppermute | solution.py:441
  45.1 7.3 %collective-permute-start.12 = (bf16[64,832]{1,0:T(8,128)(2,1)S(1)}, bf16[64,832]{1,0:T(8,128)(2,1)S(1)}, u32[]{:S(2)}, u32[]{:S(2)}) collective-permute-start(bf16[64,832]{1,0:T(8,128)(2,1)S(1)} %between.3.refs_0_.refs_4_), channel_id=1, source_target_pairs={{0,2},{1,3},{2,0},{3,1},{4,6},{5,7},{6,4},{7,5},{8,10},{9,11},{10,... | collective-permute-start | bytes 319496 | tf_op jit(solution)/shard_map/ppermute | solution.py:441
  45.9 6.9 %collective-permute-start.14 = (bf16[64,832]{1,0:T(8,128)(2,1)S(1)}, bf16[64,832]{1,0:T(8,128)(2,1)S(1)}, u32[]{:S(2)}, u32[]{:S(2)}) collective-permute-start(bf16[64,832]{1,0:T(8,128)(2,1)S(1)} %between.3.refs_0_.refs_4_), channel_id=1, source_target_pairs={{0,1},{1,0},{2,3},{3,2},{4,5},{5,4},{6,7},{7,6},{8,9},{9,8},{10,11... | collective-permute-start | bytes 319496 | tf_op jit(solution)/shard_map/ppermute | solution.py:441
  60.0 8.7 %collective-permute-start.15 = (bf16[64,704]{1,0:T(8,128)(2,1)S(1)}, bf16[64,704]{1,0:T(8,128)(2,1)S(1)}, u32[]{:S(2)}, u32[]{:S(2)}) collective-permute-start(bf16[64,704]{1,0:T(8,128)(2,1)S(1)} %get-tuple-element.114), channel_id=1, source_target_pairs={{0,2},{1,3},{2,0},{3,1},{4,6},{5,7},{6,4},{7,5},{8,10},{9,11},{10,... | collective-permute-start | bytes 270344 | tf_op jit(solution)/shard_map/ppermute | solution.py:441
  60.9 7.9 %collective-permute-start.16 = (bf16[64,704]{1,0:T(8,128)(2,1)S(1)}, bf16[64,704]{1,0:T(8,128)(2,1)S(1)}, u32[]{:S(2)}, u32[]{:S(2)}) collective-permute-start(bf16[64,704]{1,0:T(8,128)(2,1)S(1)} %get-tuple-element.115), channel_id=1, source_target_pairs={{0,3},{1,2},{2,1},{3,0},{4,7},{5,6},{6,5},{7,4},{8,11},{9,10},{10,... | collective-permute-start | bytes 270344 | tf_op jit(solution)/shard_map/ppermute | solution.py:441
  62.5 6.5 %collective-permute-start.17 = (bf16[64,704]{1,0:T(8,128)(2,1)S(1)}, bf16[64,704]{1,0:T(8,128)(2,1)S(1)}, u32[]{:S(2)}, u32[]{:S(2)}) collective-permute-start(bf16[64,704]{1,0:T(8,128)(2,1)S(1)} %get-tuple-element.116), channel_id=1, source_target_pairs={{0,1},{1,0},{2,3},{3,2},{4,5},{5,4},{6,7},{7,6},{8,9},{9,8},{10,11... | collective-permute-start | bytes 270344 | tf_op jit(solution)/shard_map/ppermute | solution.py:441
  69.8 7.4 %collective-permute-start.18 = (bf16[64,832]{1,0:T(8,128)(2,1)S(1)}, bf16[64,832]{1,0:T(8,128)(2,1)S(1)}, u32[]{:S(2)}, u32[]{:S(2)}) collective-permute-start(bf16[64,832]{1,0:T(8,128)(2,1)S(1)} %between.4.refs_0_.refs_4_), channel_id=1, source_target_pairs={{0,2},{1,3},{2,0},{3,1},{4,6},{5,7},{6,4},{7,5},{8,10},{9,11},{10,... | collective-permute-start | bytes 319496 | tf_op jit(solution)/shard_map/ppermute | solution.py:441
  84.8 6.6 %collective-permute-start.21 = (bf16[64,704]{1,0:T(8,128)(2,1)S(1)}, bf16[64,704]{1,0:T(8,128)(2,1)S(1)}, u32[]{:S(2)}, u32[]{:S(2)}) collective-permute-start(bf16[64,704]{1,0:T(8,128)(2,1)S(1)} %get-tuple-element.123), channel_id=1, source_target_pairs={{0,2},{1,3},{2,0},{3,1},{4,6},{5,7},{6,4},{7,5},{8,10},{9,11},{10,... | collective-permute-start | bytes 270344 | tf_op jit(solution)/shard_map/ppermute | solution.py:441
  86.1 6.6 %collective-permute-start.22 = (bf16[64,704]{1,0:T(8,128)(2,1)S(1)}, bf16[64,704]{1,0:T(8,128)(2,1)S(1)}, u32[]{:S(2)}, u32[]{:S(2)}) collective-permute-start(bf16[64,704]{1,0:T(8,128)(2,1)S(1)} %get-tuple-element.124), channel_id=1, source_target_pairs={{0,3},{1,2},{2,1},{3,0},{4,7},{5,6},{6,5},{7,4},{8,11},{9,10},{10,... | collective-permute-start | bytes 270344 | tf_op jit(solution)/shard_map/ppermute | solution.py:441
  87.3 6.3 %collective-permute-start.23 = (bf16[64,704]{1,0:T(8,128)(2,1)S(1)}, bf16[64,704]{1,0:T(8,128)(2,1)S(1)}, u32[]{:S(2)}, u32[]{:S(2)}) collective-permute-start(bf16[64,704]{1,0:T(8,128)(2,1)S(1)} %get-tuple-element.125), channel_id=1, source_target_pairs={{0,1},{1,0},{2,3},{3,2},{4,5},{5,4},{6,7},{7,6},{8,9},{9,8},{10,11... | collective-permute-start | bytes 270344 | tf_op jit(solution)/shard_map/ppermute | solution.py:441
  94.4 6.9 %collective-permute-start.24 = (bf16[64,832]{1,0:T(8,128)(2,1)S(1)}, bf16[64,832]{1,0:T(8,128)(2,1)S(1)}, u32[]{:S(2)}, u32[]{:S(2)}) collective-permute-start(bf16[64,832]{1,0:T(8,128)(2,1)S(1)} %between.5.refs_0_.refs_4_), channel_id=1, source_target_pairs={{0,2},{1,3},{2,0},{3,1},{4,6},{5,7},{6,4},{7,5},{8,10},{9,11},{10,... | collective-permute-start | bytes 319496 | tf_op jit(solution)/shard_map/ppermute | solution.py:441
  95.3 6.4 %collective-permute-start.26 = (bf16[64,832]{1,0:T(8,128)(2,1)S(1)}, bf16[64,832]{1,0:T(8,128)(2,1)S(1)}, u32[]{:S(2)}, u32[]{:S(2)}) collective-permute-start(bf16[64,832]{1,0:T(8,128)(2,1)S(1)} %between.5.refs_0_.refs_4_), channel_id=1, source_target_pairs={{0,1},{1,0},{2,3},{3,2},{4,5},{5,4},{6,7},{7,6},{8,9},{9,8},{10,11... | collective-permute-start | bytes 319496 | tf_op jit(solution)/shard_map/ppermute | solution.py:441
  101.4 5.8 %collective-permute-start.25 = (bf16[64,832]{1,0:T(8,128)(2,1)S(1)}, bf16[64,832]{1,0:T(8,128)(2,1)S(1)}, u32[]{:S(2)}, u32[]{:S(2)}) collective-permute-start(bf16[64,832]{1,0:T(8,128)(2,1)S(1)} %collective-permute-done.24.refs_2_), channel_id=1, source_target_pairs={{0,1},{1,0},{2,3},{3,2},{4,5},{5,4},{6,7},{7,6},{8,9},{9,8},{10,11... | collective-permute-start | bytes 319496 | tf_op jit(solution)/shard_map/ppermute | solution.py:441
  110.0 6.8 %collective-permute-start.27 = (bf16[64,704]{1,0:T(8,128)(2,1)S(1)}, bf16[64,704]{1,0:T(8,128)(2,1)S(1)}, u32[]{:S(2)}, u32[]{:S(2)}) collective-permute-start(bf16[64,704]{1,0:T(8,128)(2,1)S(1)} %get-tuple-element.132), channel_id=1, source_target_pairs={{0,2},{1,3},{2,0},{3,1},{4,6},{5,7},{6,4},{7,5},{8,10},{9,11},{10,... | collective-permute-start | bytes 270344 | tf_op jit(solution)/shard_map/ppermute | solution.py:441
  110.1 6.7 %collective-permute-start.28 = (bf16[64,704]{1,0:T(8,128)(2,1)S(1)}, bf16[64,704]{1,0:T(8,128)(2,1)S(1)}, u32[]{:S(2)}, u32[]{:S(2)}) collective-permute-start(bf16[64,704]{1,0:T(8,128)(2,1)S(1)} %get-tuple-element.133), channel_id=1, source_target_pairs={{0,3},{1,2},{2,1},{3,0},{4,7},{5,6},{6,5},{7,4},{8,11},{9,10},{10,... | collective-permute-start | bytes 270344 | tf_op jit(solution)/shard_map/ppermute | solution.py:441
  (14 other events, 56.0 us)
